TPU v7x, 128 devices: a whole 4x4x4 slice. The times are simulated.
128 devices in a mesh: vol: 16 (over z, x), col: 8 (over y, core).
Axes of the slice: x: 4, y: 4, z: 4, core: 2. Of those that a mesh axis runs over, the one named last changes fastest.
Arguments:
- face_area: float32 [16, 131072], P('vol', 'col'), may hold values from 0.25 to 2.5
- face_speed: float32 [16, 131072], P('vol', 'col'), may hold values from -6 to 6
- face_node: int32 [16, 131072], P('vol', 'col'), may hold values from 0 to 65535
- face_count: int32 [16, 8], P('vol', 'col'), may hold values from 4096 to 16384, as said below
- surface_metric: float32 [1024, 1024], P('vol'), may hold values from 1 to 10
- displacement: float32 [64, 1024, 1024], P('col', 'vol'), may hold values from -6 to 6
Outputs:
- surface_velocity: float32 [1024, 1024], P('vol')
- displaced: float32 [64, 1024, 1024], P('col', 'vol')
Inputs may be any that keep to these rules, and one draw needn't show every extreme that they name: `face_count`: the live slots of a device are its first slots; some device has all 16384 slots live in every draw.
All inputs are finite; a program needn't handle non-finite values.
Results may differ from a plain program's by a relative error of at most 0.0003.
Values sent between devices are 32-bit elements; how exact they have to be, the bound alone decides.
No kernel may reach another device: no remote copies, remote signals or barrier semaphores. Data moves between devices by JAX's collectives and lax.ppermute only.
A program may use at most 64 MiB of HBM per device.

v0:
```python
import jax
import jax.numpy as jnp
from jax import lax
from jax.sharding import PartitionSpec as P

ITERS = 10
SWEEPS = 4


mass_even = (-1.0 / 15.0, 2.0 / 15.0, 8.0 / 15.0, 2.0 / 15.0, -1.0 / 15.0)
mass_odd = (0.0, 2.0 / 15.0, 16.0 / 15.0, 2.0 / 15.0, 0.0)
stiff_even = (1.0 / 6.0, -8.0 / 6.0, 14.0 / 6.0, -8.0 / 6.0, 1.0 / 6.0)
stiff_odd = (0.0, -8.0 / 6.0, 16.0 / 6.0, -8.0 / 6.0, 0.0)
relaxation = 0.5
step_length = 0.5


def extended(x, sides, width):
    for axis, dim in sides:
        size, length = (lax.axis_size(axis), x.shape[dim])
        up = [(i, (i + 1) % size) for i in range(size - 1)]
        down = [(j, i) for i, j in up]
        last = lax.slice_in_dim(x, length - width, length, axis=dim)
        first = lax.slice_in_dim(x, 0, width, axis=dim)
        before = lax.ppermute(last, axis, up)
        after = lax.ppermute(first, axis, down)
        x = jnp.concatenate([before, x, after], axis=dim)
    return x


def padded_line(padded, along_axis, even_taps, odd_taps):
    line_count = padded.shape[along_axis] - 4
    total_even = None
    total_odd = None
    for tap_index in range(5):
        slab_piece = lax.slice_in_dim(padded, tap_index, tap_index + line_count, axis=along_axis)
        term = even_taps[tap_index] * slab_piece
        total_even = term if total_even is None else total_even + term
        if odd_taps[tap_index] != 0.0:
            term = odd_taps[tap_index] * slab_piece
            total_odd = term if total_odd is None else total_odd + term
    even_mask = lax.broadcasted_iota(jnp.int32, total_even.shape, along_axis) % 2 == 0
    return jnp.where(even_mask, total_even, total_odd)


def surface_lines(padded_rows):
    padded = jnp.pad(padded_rows, ((0, 0), (2, 2)))
    across = padded_line(padded, 1, mass_even, mass_odd)
    return padded_line(across, 0, mass_even, mass_odd)


def diagonal(shape):
    depth_even = lax.broadcasted_iota(jnp.int32, shape, 0) % 2 == 0
    rows_even = lax.broadcasted_iota(jnp.int32, shape, 1) % 2 == 0
    cols_even = lax.broadcasted_iota(jnp.int32, shape, 2) % 2 == 0
    stiff_depth = jnp.where(depth_even, stiff_even[2], stiff_odd[2])
    mass_depth = jnp.where(depth_even, mass_even[2], mass_odd[2])
    stiff_rows = jnp.where(rows_even, stiff_even[2], stiff_odd[2])
    mass_rows = jnp.where(rows_even, mass_even[2], mass_odd[2])
    stiff_cols = jnp.where(cols_even, stiff_even[2], stiff_odd[2])
    mass_cols = jnp.where(cols_even, mass_even[2], mass_odd[2])
    lateral_mass = mass_rows * mass_cols
    lateral_stiff = stiff_rows * mass_cols + mass_rows * stiff_cols
    return stiff_depth * lateral_mass + mass_depth * lateral_stiff


def relax(block, scale):
    padded = jnp.pad(block, ((0, 0), (0, 0), (2, 2)))
    mass_x = padded_line(padded, 2, mass_even, mass_odd)
    stiff_x = padded_line(padded, 2, stiff_even, stiff_odd)
    along = padded_line(mass_x, 1, mass_even, mass_odd)
    cross = padded_line(mass_x, 1, stiff_even, stiff_odd) + padded_line(
        stiff_x, 1, mass_even, mass_odd
    )
    operator_image = padded_line(along, 0, stiff_even, stiff_odd) + padded_line(
        cross, 0, mass_even, mass_odd
    )
    centre = block[2:-2, 2:-2]
    return centre - relaxation * operator_image / scale


def residual_norm(residual):
    return lax.psum(jnp.sum(residual * residual), ("vol", "col"))


def conjugate(flux, apply_mass):
    solution = jnp.zeros_like(flux)
    residual = flux
    direction = flux
    norm_now = residual_norm(residual)
    for iteration in range(ITERS):
        mass_image = apply_mass(direction)
        curvature = lax.psum(jnp.sum(direction * mass_image), ("vol", "col"))
        step_alpha = norm_now / curvature
        solution = solution + step_alpha * direction
        residual = residual - step_alpha * mass_image
        norm_next = residual_norm(residual)
        direction = residual + norm_next / norm_now * direction
        norm_now = norm_next
    return solution


def on_device(face_area, face_speed, face_node, face_count, surface_metric, displacement):
    band_rows, band_cols = surface_metric.shape
    live_slots = jnp.arange(face_node.shape[1], dtype=jnp.int32) < face_count[0, 0]
    contributions = jnp.where(live_slots, face_area[0] * face_speed[0], 0.0)
    band_flux = jax.ops.segment_sum(
        contributions, face_node[0], num_segments=band_rows * band_cols
    ).reshape(band_rows, band_cols)
    flux = lax.psum_scatter(band_flux, "col", scatter_dimension=0, tiled=True)
    strip_rows = flux.shape[0]
    metric_strip = lax.dynamic_slice_in_dim(
        surface_metric, lax.axis_index("col") * strip_rows, strip_rows, 0
    )
    metric_root = jnp.sqrt(metric_strip)

    def apply_mass(values_in):
        weighted = metric_root * values_in
        padded_rows = extended(weighted, ((("vol", "col"), 0),), 2)
        return metric_root * surface_lines(padded_rows)

    solved = conjugate(flux, apply_mass)
    surface_velocity = lax.all_gather(solved, "col", axis=0, tiled=True)
    top_flag = lax.axis_index("col") == 0
    top_plane = displacement[0] + step_length * surface_velocity
    field = displacement.at[0].set(jnp.where(top_flag, top_plane, displacement[0]))
    depth_cells, row_cells, col_cells = displacement.shape
    scale = diagonal((depth_cells, row_cells, col_cells))
    for sweep_index in range(SWEEPS):
        padded_block = extended(field, (("vol", 1), ("col", 0)), 2)
        field = relax(padded_block, scale)
        field = field.at[0].set(jnp.where(top_flag, top_plane, field[0]))
    return (surface_velocity, field)


def solution(mesh):
    in_specs = (
        P("vol", "col"),
        P("vol", "col"),
        P("vol", "col"),
        P("vol", "col"),
        P("vol", None),
        P("col", "vol", None),
    )
    out_specs = (P("vol", None), P("col", "vol", None))
    return jax.shard_map(
        on_device, mesh=mesh, in_specs=in_specs, out_specs=out_specs, check_vma=False
    )
```

profile of v0, /device:TPU:1, one launch (start us, length us, event | category | flops | bytes accessed | tf_op | source)
XLA Modules:
  0.0 1770.0 jit_solution(17285334876468042103)
XLA Ops:
  8.8 86.1 %scatter_custom_fusion = f32[65536]{0:T(1024)S(1)} fusion(s32[16384]{0:T(1024)} %bitcast.41, f32[16384]{0:T(1024)S(1)} %fusion.184, f32[]{:T(128)} %constant.339.clone.1), kind=kCustom, calls=%fused_computation.199 | custom fusion | flops 16384 | bytes 262656 | tf_op jit(solution)/shard_map/scatter-add | solution.py:107
  95.7 31.1 %reduce-scatter.2.cloned.1.call-done = f32[8,1024]{1,0:T(8,128)} async-done(((f32[64,1024]{1,0:T(8,128)}), f32[8,1024]{1,0:T(8,128)}) %reduce-scatter.2.cloned.1.call-update) | async-done | bytes 32784 | tf_op jit(solution)/shard_map/reduce_scatter | solution.py:110
  127.7 3.4 collective-permute-start
  131.0 3.2 collective-permute-start.1
  137.6 72.3 %all-reduce.14 = (f32[]{:T(128)}, f32[]{:T(128)}) all-reduce(f32[]{:T(128)} %get-tuple-element.65, f32[]{:T(128)} %get-tuple-element.64), channel_id=1, replica_groups=mesh['vol'=16,'col'=8] {'vol','col'}, use_global_device_ids=true, to_apply=%region_3.4 | all-reduce | flops 2 | bytes 16 | tf_op jit(solution)/shard_map/psum | solution.py:83
  212.7 63.6 %psum.142 = f32[]{:T(128)} all-reduce(f32[]{:T(128)} %multiply_reduce_fusion.16), channel_id=1, replica_groups=mesh['vol'=16,'col'=8] {'vol','col'}, use_global_device_ids=true, to_apply=%region_7.8 | all-reduce | flops 1 | bytes 8 | tf_op jit(solution)/shard_map/psum | solution.py:83
  282.7 2.9 collective-permute-done.3
  287.2 69.9 %psum.143 = f32[]{:T(128)} all-reduce(f32[]{:T(128)} %get-tuple-element.114), channel_id=1, replica_groups=mesh['vol'=16,'col'=8] {'vol','col'}, use_global_device_ids=true, to_apply=%region_9.10 | all-reduce | flops 1 | bytes 8 | tf_op jit(solution)/shard_map/psum | solution.py:93
  359.8 63.6 %psum.144 = f32[]{:T(128)} all-reduce(f32[]{:T(128)} %get-tuple-element.112), channel_id=1, replica_groups=mesh['vol'=16,'col'=8] {'vol','col'}, use_global_device_ids=true, to_apply=%region_11.12 | all-reduce | flops 1 | bytes 8 | tf_op jit(solution)/shard_map/psum | solution.py:83
  429.8 2.9 collective-permute-done.5
  434.3 69.5 %psum.145 = f32[]{:T(128)} all-reduce(f32[]{:T(128)} %get-tuple-element.108), channel_id=1, replica_groups=mesh['vol'=16,'col'=8] {'vol','col'}, use_global_device_ids=true, to_apply=%region_13.14 | all-reduce | flops 1 | bytes 8 | tf_op jit(solution)/shard_map/psum | solution.py:93
  505.8 64.1 %psum.146 = f32[]{:T(128)} all-reduce(f32[]{:T(128)} %get-tuple-element.106), channel_id=1, replica_groups=mesh['vol'=16,'col'=8] {'vol','col'}, use_global_device_ids=true, to_apply=%region_15.16 | all-reduce | flops 1 | bytes 8 | tf_op jit(solution)/shard_map/psum | solution.py:83
  580.5 69.8 %psum.147 = f32[]{:T(128)} all-reduce(f32[]{:T(128)} %get-tuple-element.102), channel_id=1, replica_groups=mesh['vol'=16,'col'=8] {'vol','col'}, use_global_device_ids=true, to_apply=%region_17.18 | all-reduce | flops 1 | bytes 8 | tf_op jit(solution)/shard_map/psum | solution.py:93
  652.2 63.3 %psum.148 = f32[]{:T(128)} all-reduce(f32[]{:T(128)} %get-tuple-element.100), channel_id=1, replica_groups=mesh['vol'=16,'col'=8] {'vol','col'}, use_global_device_ids=true, to_apply=%region_19.20 | all-reduce | flops 1 | bytes 8 | tf_op jit(solution)/shard_map/psum | solution.py:83
  717.6 3.0 collective-permute-start.8
  722.6 3.0 collective-permute-done.9
  727.3 69.5 %psum.149 = f32[]{:T(128)} all-reduce(f32[]{:T(128)} %get-tuple-element.96), channel_id=1, replica_groups=mesh['vol'=16,'col'=8] {'vol','col'}, use_global_device_ids=true, to_apply=%region_21.22 | all-reduce | flops 1 | bytes 8 | tf_op jit(solution)/shard_map/psum | solution.py:93
  798.8 64.2 %psum.150 = f32[]{:T(128)} all-reduce(f32[]{:T(128)} %get-tuple-element.94), channel_id=1, replica_groups=mesh['vol'=16,'col'=8] {'vol','col'}, use_global_device_ids=true, to_apply=%region_23.24 | all-reduce | flops 1 | bytes 8 | tf_op jit(solution)/shard_map/psum | solution.py:83
  873.6 70.0 %psum.151 = f32[]{:T(128)} all-reduce(f32[]{:T(128)} %get-tuple-element.90), channel_id=1, replica_groups=mesh['vol'=16,'col'=8] {'vol','col'}, use_global_device_ids=true, to_apply=%region_25.26 | all-reduce | flops 1 | bytes 8 | tf_op jit(solution)/shard_map/psum | solution.py:93
  945.6 62.5 %psum.152 = f32[]{:T(128)} all-reduce(f32[]{:T(128)} %get-tuple-element.88), channel_id=1, replica_groups=mesh['vol'=16,'col'=8] {'vol','col'}, use_global_device_ids=true, to_apply=%region_27.28 | all-reduce | flops 1 | bytes 8 | tf_op jit(solution)/shard_map/psum | solution.py:83
  1010.2 3.5 collective-permute-start.12
  1015.7 3.0 collective-permute-done.13
  1020.3 69.1 %psum.153 = f32[]{:T(128)} all-reduce(f32[]{:T(128)} %get-tuple-element.84), channel_id=1, replica_groups=mesh['vol'=16,'col'=8] {'vol','col'}, use_global_device_ids=true, to_apply=%region_29.30 | all-reduce | flops 1 | bytes 8 | tf_op jit(solution)/shard_map/psum | solution.py:93
  1091.4 64.2 %psum.154 = f32[]{:T(128)} all-reduce(f32[]{:T(128)} %get-tuple-element.82), channel_id=1, replica_groups=mesh['vol'=16,'col'=8] {'vol','col'}, use_global_device_ids=true, to_apply=%region_31.32 | all-reduce | flops 1 | bytes 8 | tf_op jit(solution)/shard_map/psum | solution.py:83
  1166.2 70.1 %psum.155 = f32[]{:T(128)} all-reduce(f32[]{:T(128)} %get-tuple-element.78), channel_id=1, replica_groups=mesh['vol'=16,'col'=8] {'vol','col'}, use_global_device_ids=true, to_apply=%region_33.34 | all-reduce | flops 1 | bytes 8 | tf_op jit(solution)/shard_map/psum | solution.py:93
  1238.3 62.5 %psum.156 = f32[]{:T(128)} all-reduce(f32[]{:T(128)} %get-tuple-element.76), channel_id=1, replica_groups=mesh['vol'=16,'col'=8] {'vol','col'}, use_global_device_ids=true, to_apply=%region_35.36 | all-reduce | flops 1 | bytes 8 | tf_op jit(solution)/shard_map/psum | solution.py:83
  1302.9 3.5 collective-permute-start.16
  1313.1 69.1 %psum.157 = f32[]{:T(128)} all-reduce(f32[]{:T(128)} %get-tuple-element.72), channel_id=1, replica_groups=mesh['vol'=16,'col'=8] {'vol','col'}, use_global_device_ids=true, to_apply=%region_37.38 | all-reduce | flops 1 | bytes 8 | tf_op jit(solution)/shard_map/psum | solution.py:93
  1384.1 64.2 %psum.158 = f32[]{:T(128)} all-reduce(f32[]{:T(128)} %multiply_reduce_fusion), channel_id=1, replica_groups=mesh['vol'=16,'col'=8] {'vol','col'}, use_global_device_ids=true, to_apply=%region_39.40 | all-reduce | flops 1 | bytes 8 | tf_op jit(solution)/shard_map/psum | solution.py:83
  1459.0 2.8 copy.8
  1461.8 70.1 %psum.159 = f32[]{:T(128)} all-reduce(f32[]{:T(128)} %fusion.189), channel_id=1, replica_groups=mesh['vol'=16,'col'=8] {'vol','col'}, use_global_device_ids=true, to_apply=%region_41.42 | all-reduce | flops 1 | bytes 8 | tf_op jit(solution)/shard_map/psum | solution.py:93
  1533.3 13.8 all_gather.3
  1553.0 3.8 collective-permute-done.21
  1557.2 3.8 collective-permute-start.22
  1563.2 4.3 collective-permute-done.22
  1567.5 4.4 collective-permute-done.23
  1572.9 9.6 add_select_fusion.7
  1582.6 6.7 add_select_fusion.11
  1589.2 5.2 fusion.75
  1599.8 4.3 collective-permute-done.25
  1604.5 3.2 collective-permute-start.26
  1609.9 4.3 collective-permute-done.26
  1614.2 4.4 collective-permute-done.27
  1619.7 9.6 add_select_fusion.5
  1629.3 6.7 add_select_fusion.10
  1636.0 4.2 fusion.61
  1642.0 6.1 scatter.20
  1649.1 5.5 collective-permute-start.28
  1655.8 3.9 collective-permute-done.29
  1662.5 3.0 collective-permute-start.30
  1667.7 4.3 collective-permute-done.30
  1672.0 4.4 collective-permute-done.31
  1677.6 9.6 add_select_fusion.3
  1687.2 6.7 add_select_fusion.9
  1693.9 5.0 fusion.47
  1700.9 6.1 scatter.21
  1707.9 3.7 collective-permute-start.32
  1712.9 4.0 collective-permute-done.33
  1719.7 2.9 collective-permute-start.34
  1724.8 4.2 collective-permute-done.34
  1729.1 4.4 collective-permute-done.35
  1735.8 9.6 add_select_fusion.1
  1745.4 6.7 add_select_fusion.8
  1752.1 5.2 fusion.33
  (155 shorter events, 124.8 us)
Async XLA Ops:
  7.2 119.7 %reduce-scatter.2.cloned.1.call-start = ((), (), s32[]{:S(2)}) async-start(), calls=%async_computation.1 | async-start | bytes 294912 | tf_op jit(solution)/shard_map/reduce_scatter | solution.py:110
  127.7 6.6 collective-permute-start
  131.0 5.0 collective-permute-start.1
  278.4 4.3 collective-permute-start.2
  280.6 5.0 collective-permute-start.3
  425.5 4.3 collective-permute-start.4
  427.7 5.0 collective-permute-start.5
  572.0 4.3 collective-permute-start.6
  573.9 5.0 collective-permute-start.7
  717.6 5.0 collective-permute-start.8
  720.7 5.0 collective-permute-start.9
  727.3 806.0 %copy-start.3 = (f32[8,1024]{1,0:T(8,128)S(1)}, f32[8,1024]{1,0:T(8,128)}, u32[]{:S(2)}) copy-start(f32[8,1024]{1,0:T(8,128)} %reduce-scatter.2.cloned.1.call-done) | copy-start | bytes 98308
  865.1 4.3 collective-permute-start.10
  867.0 5.0 collective-permute-start.11
  1010.2 5.5 collective-permute-start.12
  1013.8 5.0 collective-permute-start.13
  1157.7 4.3 collective-permute-start.14
  1159.7 5.0 collective-permute-start.15
  1302.9 5.9 collective-permute-start.16
  1306.5 5.0 collective-permute-start.17
  1450.4 4.3 collective-permute-start.18
  1452.4 5.0 collective-permute-start.19
  1550.0 39.2 %copy-start.2 = (f32[8,64,1024]{2,0,1:T(8,128)}, f32[8,64,1024]{2,0,1:T(8,128)S(1)}, u32[]{:S(2)}) copy-start(f32[8,64,1024]{2,0,1:T(8,128)S(1)} %scatter.16) | copy-start | bytes 6291460
  1550.1 2.9 collective-permute-start.20
  1551.4 5.4 collective-permute-start.21
  1557.2 10.3 collective-permute-start.22
  1561.0 10.9 collective-permute-start.23
  1596.7 3.2 collective-permute-start.24
  1598.5 5.6 collective-permute-start.25
  1604.5 9.7 collective-permute-start.26
  1607.8 10.9 collective-permute-start.27
  1640.2 1.3 copy-start
  1648.0 28.3 %copy-start.1 = (f32[8,64,1024]{2,0,1:T(8,128)S(1)}, f32[8,64,1024]{2,0,1:T(8,128)}, u32[]{:S(2)}) copy-start(f32[8,64,1024]{2,0,1:T(8,128)} %scatter.20) | copy-start | bytes 6291460
  1649.1 6.8 collective-permute-start.28
  1654.5 5.2 collective-permute-start.29
  1662.5 9.5 collective-permute-start.30
  1665.5 10.9 collective-permute-start.31
  1707.9 5.1 collective-permute-start.32
  1711.6 5.3 collective-permute-start.33
  1719.7 9.4 collective-permute-start.34
  1722.6 10.9 collective-permute-start.35
Sparse Core Ops, SparseCore 0:
  95.8 31.0 reduce-scatter.1
where the time goes:
time: 1780 us; the launch traced here: 1770 us
  blocking collectives  1290 us (72%)
  other arithmetic  216 us (12%)
  waiting for transfers between devices  109 us (6%)
  starting transfers between devices  87.8 us (5%)
  between operations  41.7 us (2%)
  local copies, waits for them, and re-layouts  30.7 us (2%)
    psum x10, blocking collectives, residual_norm(): return lax.psum(jnp.sum(residual * residual), ('vol', 'col'))  644 us
    psum x9, blocking collectives, conjugate(): curvature = lax.psum(jnp.sum(direction * mass_image), ('vol', 'col'))  627 us
    scatter-add x1, other arithmetic, on_device(): jax.ops.segment_sum(contributions, face_node[0], num_segments=band_rows *...  86.1 us
    select_n x18, other arithmetic, padded_line(): return jnp.where(even_mask, total_even, total_odd)  66.5 us
    ppermute x18, waiting for transfers between devices, extended(): after = lax.ppermute(first, axis, down)  59.9 us
    ppermute x18, starting transfers between devices, extended(): before = lax.ppermute(last, axis, up)  50.9 us
    ppermute x18, starting transfers between devices, extended(): after = lax.ppermute(first, axis, down)  36.9 us
  transfers between devices with their start and end apart: 37, of which 24 were waited for; matrix products, arithmetic and copies ran while one was open for 0% of the time, Pallas kernels for 0%

commit v1 on v0

v1 whole, which is shorter than its diff:
```python
import jax
import jax.numpy as jnp
import numpy as np
from jax import lax
from jax.experimental import pallas as pl
from jax.experimental.pallas import tpu as pltpu
from jax.sharding import PartitionSpec as P

ITERS = 10
SWEEPS = 4
LANES = 128
SUB = 8
MIB = 1024 * 1024

BASIS_LOW = 0.1
BASIS_HIGH = 12.0
CONDITION_MAX = 2000.0


def wrapped_roll(x, shift, axis):
    return pltpu.roll(x, shift % x.shape[axis], axis)


def lane_shift(tiles, offset):
    lane = lax.broadcasted_iota(jnp.int32, tiles[0].shape, 1)
    rolled = [wrapped_roll(tile, -offset, 1) for tile in tiles]
    zero = jnp.zeros_like(tiles[0])
    if offset < 0:
        edge = lane < -offset
        return [
            jnp.where(edge, rolled[t - 1] if t > 0 else zero, rolled[t])
            for t in range(len(tiles))
        ]
    edge = lane >= LANES - offset
    return [
        jnp.where(edge, rolled[t + 1] if t + 1 < len(tiles) else zero, rolled[t])
        for t in range(len(tiles))
    ]


def lane_sums(tiles):
    left, right = lane_shift(tiles, -1), lane_shift(tiles, 1)
    far_left, far_right = lane_shift(tiles, -2), lane_shift(tiles, 2)
    near = [a + b for a, b in zip(left, right)]
    far = [a + b for a, b in zip(far_left, far_right)]
    return near, far


def lane_choice(even, odd):
    lane = lax.broadcasted_iota(jnp.int32, (SUB, LANES), 1)
    return jnp.where(lane % 2 == 0, jnp.float32(even), jnp.float32(odd))


def ring(rows):
    n = len(rows)
    return (
        [wrapped_roll(rows[n - 2], 1, 0), wrapped_roll(rows[n - 1], 1, 0)]
        + list(rows)
        + [wrapped_roll(rows[0], -1, 0), wrapped_roll(rows[1], -1, 0)]
    )


def mass_line(padded, index):
    i = index + 2
    near = padded[i - 1] + padded[i + 1]
    if index % 2:
        return near + 8.0 * padded[i]
    return (near + 4.0 * padded[i]) - 0.5 * (padded[i - 2] + padded[i + 2])


def both_line(padded, index):
    i = index + 2
    near = padded[i - 1] + padded[i + 1]
    return (16.0 / 3.0 if index % 2 else 11.0 / 3.0) * padded[i] - near


def face_kernel(where_ref, count_ref, area_ref, speed_ref, node_ref, keep_ref, send_ref, acc_ref):
    slots = area_ref.shape[1]
    chunk = min(2048, slots)
    core = where_ref[0, 0]
    ids = lax.broadcasted_iota(jnp.int32, (256, chunk), 0)
    ids = ids.astype(jnp.float32).astype(jnp.bfloat16)
    zero = jnp.zeros((), jnp.bfloat16)
    one = jnp.ones((), jnp.bfloat16)
    contract = (((1,), (1,)), ((), ()))
    acc_ref[...] = jnp.zeros_like(acc_ref)

    def wide(x):
        return jnp.broadcast_to(x.astype(jnp.bfloat16), (256, chunk))

    def body(step, carry):
        at = pl.ds(pl.multiple_of(step * chunk, chunk), chunk)
        slot = lax.broadcasted_iota(jnp.int32, (1, chunk), 1) + step * chunk
        value = jnp.where(slot < count_ref[0, 0], area_ref[:, at] * speed_ref[:, at], 0.0)
        node = node_ref[:, at]
        low = (node & 255).astype(jnp.float32)
        high = (((node >> 8) & 3) * 64 + (node >> 10)).astype(jnp.float32)
        first = value.astype(jnp.bfloat16)
        second = value - first.astype(jnp.float32)
        here = wide(high) == ids
        upper = jnp.where(here, wide(first), zero)
        lower = jnp.where(here, wide(second), zero)
        columns = jnp.where(wide(low) == ids, one, zero)
        acc_ref[...] += lax.dot_general(
            upper, columns, contract, preferred_element_type=jnp.float32
        ) + lax.dot_general(lower, columns, contract, preferred_element_type=jnp.float32)
        return carry

    lax.fori_loop(0, slots // chunk, body, 0)
    for j in range(4):
        keep_ref[:, 256 * j : 256 * (j + 1)] = acc_ref[pl.ds(64 * j + 32 * core, 32), :]
        send_ref[:, 256 * j : 256 * (j + 1)] = acc_ref[pl.ds(64 * j + 32 - 32 * core, 32), :]


def face_sums(where, count, area, speed, node):
    half = jax.ShapeDtypeStruct((32, 1024), jnp.float32)
    smem = pl.BlockSpec(memory_space=pltpu.SMEM)
    vmem = pl.BlockSpec(memory_space=pltpu.VMEM)
    return pl.pallas_call(
        face_kernel,
        out_shape=(half, half),
        in_specs=[smem, smem, vmem, vmem, vmem],
        out_specs=(vmem, vmem),
        scratch_shapes=[pltpu.VMEM((256, 256), jnp.float32)],
        compiler_params=pltpu.CompilerParams(vmem_limit_bytes=32 * MIB),
        cost_estimate=pl.CostEstimate(flops=4_000_000_000, bytes_accessed=500_000, transcendentals=0),
        name="face_sums",
    )(where, count, area, speed, node)


HALO = 32
ROWS = 128
GROUPS = 16


def basis_kernel(
    where_ref, own_ref, other_ref, same_ref, cross_ref,
    metric_ref, before_ref, after_ref, basis_ref, sums_ref, root_ref, line_ref,
):
    core = where_ref[0, 0]
    tiles = own_ref.shape[1] // LANES
    for t in range(tiles):
        cols = slice(LANES * t, LANES * (t + 1))
        basis_ref[0, t, pl.ds(32 + 32 * core, 32), :] = own_ref[:, cols]
        basis_ref[0, t, pl.ds(64 - 32 * core, 32), :] = other_ref[:, cols]
        basis_ref[0, t, pl.ds(96 * core, 32), :] = cross_ref[:, cols]
        basis_ref[0, t, pl.ds(96 - 96 * core, 32), :] = same_ref[:, cols]
        root_ref[t, 0:32, :] = jnp.sqrt(before_ref[:, cols])
        root_ref[t, 32:96, :] = jnp.sqrt(metric_ref[:, cols])
        root_ref[t, 96:128, :] = jnp.sqrt(after_ref[:, cols])

    centre = (BASIS_LOW + BASIS_HIGH) / 2
    scale = 2 / (BASIS_HIGH - BASIS_LOW)
    at_centre = lane_choice(4.0, 8.0)
    at_far = lane_choice(-0.5, 0.0)
    group = lax.broadcasted_iota(jnp.int32, (SUB, LANES), 0)
    own_rows = jnp.where((group >= 2) & (group < 6), 1.0, 0.0).astype(jnp.float32)

    def rows_of(ys):
        return pl.ds(ys, SUB, stride=GROUPS)

    def step(k, carry):
        before = jnp.maximum(k - 1, 0)
        first = jnp.where(k == 0, 1.0, 2.0).astype(jnp.float32)
        second = jnp.where(k == 0, 0.0, 1.0).astype(jnp.float32)

        def along_x(ys, carry):
            weighted = []
            for t in range(tiles):
                weighted.append(basis_ref[k, t, rows_of(ys), :] * root_ref[t, rows_of(ys), :])
            near, far = lane_sums(weighted)
            for t in range(tiles):
                line_ref[ys, t] = near[t] + at_centre * weighted[t] + at_far * far[t]
            return carry

        lax.fori_loop(0, GROUPS, along_x, 0)

        square = jnp.zeros((SUB, LANES), jnp.float32)
        shifted = jnp.zeros((SUB, LANES), jnp.float32)
        for t in range(tiles):
            padded = ring([line_ref[ys, t] for ys in range(GROUPS)])
            for ys in range(GROUPS):
                image = (root_ref[t, rows_of(ys), :] * (4.0 / 225.0 * scale)) * mass_line(padded, ys)
                now = basis_ref[k, t, rows_of(ys), :]
                last = basis_ref[before, t, rows_of(ys), :]
                later = first * (image - (centre * scale) * now) - second * last
                basis_ref[k + 1, t, rows_of(ys), :] = later
                square = square + now * now
                shifted = shifted + later * now
        sums_ref[pl.ds(2 * k, 1), :] = jnp.sum(square * own_rows, axis=0, keepdims=True)
        sums_ref[pl.ds(2 * k + 1, 1), :] = jnp.sum(shifted * own_rows, axis=0, keepdims=True)
        return carry

    sums_ref[...] = jnp.zeros_like(sums_ref)
    lax.fori_loop(0, ITERS, step, 0)


def surface_basis(where, own, other, same, cross, metric, before, after):
    cols = own.shape[1]
    smem = pl.BlockSpec(memory_space=pltpu.SMEM)
    vmem = pl.BlockSpec(memory_space=pltpu.VMEM)
    return pl.pallas_call(
        basis_kernel,
        out_shape=(
            jax.ShapeDtypeStruct((ITERS + 1, cols // LANES, ROWS, LANES), jnp.float32),
            jax.ShapeDtypeStruct((24, LANES), jnp.float32),
        ),
        in_specs=[smem] + [vmem] * 7,
        out_specs=(vmem, vmem),
        scratch_shapes=[
            pltpu.VMEM((cols // LANES, ROWS, LANES), jnp.float32),
            pltpu.VMEM((GROUPS, cols // LANES, SUB, LANES), jnp.float32),
        ],
        compiler_params=pltpu.CompilerParams(vmem_limit_bytes=40 * MIB),
        cost_estimate=pl.CostEstimate(flops=40_000_000, bytes_accessed=8_000_000, transcendentals=0),
        name="surface_basis",
    )(where, own, other, same, cross, metric, before, after)


def solve_weights():
    n = ITERS
    moment = np.zeros((2 * n, 2 * n))
    for m in range(2 * n):
        if m < 2:
            moment[m, m] = 1.0
        else:
            moment[m, m] = 2.0
            moment[m, m % 2] = -1.0
    centre, half = (BASIS_LOW + BASIS_HIGH) / 2, (BASIS_HIGH - BASIS_LOW) / 2
    weights = np.zeros((2 * n, 16, LANES))
    for i in range(n):
        for j in range(n):
            lower = abs(j - 1)
            for factor, index in (
                (centre / 2, i + j),
                (centre / 2, abs(i - j)),
                (half / 4, i + j + 1),
                (half / 4, abs(i - j - 1)),
                (half / 4, i + lower),
                (half / 4, abs(i - lower)),
            ):
                weights[:, i, j] += factor * moment[index]
        weights[:, i, n] += moment[i]
    return weights.astype(np.float32)


def solve_kernel(basis_ref, sums_ref, weights_ref, out_ref, flag_ref, part_ref, sem):
    n = ITERS
    first = HALO - 8
    count = out_ref.shape[0]
    copy = pltpu.make_async_copy(basis_ref.at[pl.ds(0, n), :, pl.ds(first, count), :], part_ref, sem)
    copy.start()
    total = sums_ref[0]
    for i in range(1, sums_ref.shape[0]):
        total = total + sums_ref[i]
    total = jnp.broadcast_to(jnp.sum(total, axis=1, keepdims=True), total.shape)
    row = lax.broadcasted_iota(jnp.int32, (16, LANES), 0)
    lane = lax.broadcasted_iota(jnp.int32, (16, LANES), 1)
    system = jnp.where((lane == row + 16) & (row < n), 1.0, 0.0).astype(jnp.float32)
    for m in range(2 * n):
        system = system + weights_ref[m] * total[m : m + 1, :]
    centre = jnp.sum(jnp.where(lane == row, system, 0.0), axis=1, keepdims=True)
    for k in range(n):
        pivot_row = system[k : k + 1, :] / system[k : k + 1, k : k + 1]
        column = system[:, k : k + 1]
        system = jnp.where(row == k, pivot_row, system - column * pivot_row)
    inverse = jnp.sum(jnp.where(lane == row + 16, system, 0.0), axis=1, keepdims=True)
    figure = jnp.broadcast_to(centre * inverse, (16, LANES))
    inside = (row < n) & (lane == 0)
    least = jnp.min(jnp.where(inside, figure, 1.0))
    whole = jnp.sum(jnp.where(inside, figure, 0.0))
    flag_ref[0, 0] = jnp.where((least > 0.5) & (whole < CONDITION_MAX), 1, 0).astype(jnp.int32)
    copy.wait()
    for t in range(out_ref.shape[1] // LANES):
        cols = slice(LANES * t, LANES * (t + 1))
        value = None
        for k in range(n):
            term = system[k : k + 1, n : n + 1] * part_ref[k, t]
            value = term if value is None else value + term
        out_ref[:, cols] = value


def surface_solve(basis, sums):
    tiles = basis.shape[1]
    cols = tiles * LANES
    smem = pl.BlockSpec(memory_space=pltpu.SMEM)
    vmem = pl.BlockSpec(memory_space=pltpu.VMEM)
    return pl.pallas_call(
        solve_kernel,
        out_shape=(
            jax.ShapeDtypeStruct((80, cols), jnp.float32),
            jax.ShapeDtypeStruct((1, 1), jnp.int32),
        ),
        in_specs=[pl.BlockSpec(memory_space=pl.ANY), vmem, vmem],
        out_specs=(vmem, smem),
        scratch_shapes=[pltpu.VMEM((ITERS, tiles, 80, LANES), jnp.float32), pltpu.SemaphoreType.DMA],
        compiler_params=pltpu.CompilerParams(vmem_limit_bytes=32 * MIB),
        cost_estimate=pl.CostEstimate(flops=2_000_000, bytes_accessed=4_000_000, transcendentals=0),
        name="surface_solve",
    )(basis, sums, jnp.asarray(solve_weights()))


DEEP = 2 * SWEEPS
Y_GROUPS = 10
Y_ROWS = 80


def sweep_kernel(
    where_ref, block_ref, ylow_ref, yhigh_ref, zlow_ref, zhigh_ref, speed_ref, out_ref,
    field, along, cross, line_a, line_b, factor, top, sems,
):
    col, cols = where_ref[0, 1], where_ref[0, 2]
    vol, vols = where_ref[0, 3], where_ref[0, 4]
    layers, rows = block_ref.shape[0], block_ref.shape[1]
    tiles = block_ref.shape[2] // LANES
    total = layers + 2 * DEEP
    copies = []
    for t in range(tiles):
        lanes = pl.ds(LANES * t, LANES)
        for source, at_z, nz, at_y, ny in (
            (block_ref, DEEP, layers, DEEP, rows),
            (ylow_ref, DEEP, layers, 0, DEEP),
            (yhigh_ref, DEEP, layers, DEEP + rows, DEEP),
            (zlow_ref, 0, DEEP, 0, Y_ROWS),
            (zhigh_ref, DEEP + layers, DEEP, 0, Y_ROWS),
        ):
            copies.append(
                pltpu.make_async_copy(
                    source.at[:, :, lanes],
                    field.at[pl.ds(at_z, nz), t, pl.ds(at_y, ny), :],
                    sems.at[len(copies)],
                )
            )
    for copy in copies:
        copy.start()

    group = lax.broadcasted_iota(jnp.int32, (SUB, LANES), 0)
    lane = lax.broadcasted_iota(jnp.int32, (SUB, LANES), 1)
    mass, stiff = (8.0, 16.0), (14.0, 16.0)
    for pz in range(2):
        for ys in range(Y_GROUPS):
            py = ys % 2
            values = [
                -12.0
                / (stiff[pz] * mass[py] * mass[px] + mass[pz] * (stiff[py] * mass[px] + mass[py] * stiff[px]))
                for px in range(2)
            ]
            row = group * Y_GROUPS + ys
            outside = ((vol == 0) & (row < DEEP)) | ((vol == vols - 1) & (row >= DEEP + rows))
            factor[pz, ys] = jnp.where(
                outside, 0.0, jnp.where(lane % 2 == 0, jnp.float32(values[0]), jnp.float32(values[1]))
            )
    at_centre = lane_choice(4.0, 8.0)
    at_far = lane_choice(-0.5, 0.0)
    at_both = lane_choice(11.0 / 3.0, 16.0 / 3.0)

    for copy in copies:
        copy.wait()

    @pl.when(col <= 1)
    def _():
        at = DEEP - DEEP * col
        for t in range(tiles):
            lanes = slice(LANES * t, LANES * (t + 1))
            plane = field[at, t] + 0.5 * speed_ref[:, lanes]
            field[at, t] = plane
            top[t] = plane

    def lateral(z, carry):
        def across(ys, carry):
            rows_at = pl.ds(ys, SUB, stride=Y_GROUPS)
            u = [field[z, t, rows_at, :] for t in range(tiles)]
            near, far = lane_sums(u)
            for t in range(tiles):
                m = near[t] + at_centre * u[t] + at_far * far[t]
                line_a[t, ys] = m
                line_b[t, ys] = at_both * u[t] - near[t] - m
            return carry

        lax.fori_loop(0, Y_GROUPS, across, 0)

        def down(t, carry):
            a = ring([line_a[t, ys] for ys in range(Y_GROUPS)])
            b = ring([line_b[t, ys] for ys in range(Y_GROUPS)])
            for ys in range(Y_GROUPS):
                along[z, t, ys] = mass_line(a, ys)
                cross[z, t, ys] = both_line(a, ys) + mass_line(b, ys)
            return carry

        lax.fori_loop(0, tiles, down, 0)
        return carry

    def update(pair, carry):
        for pz in range(2):
            z = 2 * pair + pz

            def one(t, carry):
                for ys in range(Y_GROUPS):
                    w = along[z, t, ys]
                    c = cross[z, t, ys]
                    step = (16.0 / 3.0 if pz else 11.0 / 3.0) * w - (along[z - 1, t, ys] + along[z + 1, t, ys])
                    near = cross[z - 1, t, ys] + cross[z + 1, t, ys]
                    if pz:
                        step = step + (near + 8.0 * c)
                    else:
                        far = cross[z - 2, t, ys] + cross[z + 2, t, ys]
                        step = step + (near + 4.0 * c) - 0.5 * far
                    rows_at = pl.ds(ys, SUB, stride=Y_GROUPS)
                    field[z, t, rows_at, :] += factor[pz, ys] * step
                return carry

            lax.fori_loop(0, tiles, one, 0)
        return carry

    for sweep in range(SWEEPS):
        edge = 2 * sweep
        lax.fori_loop(edge, total - edge, lateral, 0)
        low = jnp.where(col == 0, DEEP // 2, sweep + 1)
        high = jnp.where(col == cols - 1, (DEEP + layers) // 2, total // 2 - sweep - 1)
        lax.fori_loop(low, high, update, 0)

        @pl.when(col == 0)
        def _():
            for t in range(tiles):
                field[DEEP, t] = top[t]

    results = []
    for t in range(tiles):
        results.append(
            pltpu.make_async_copy(
                field.at[pl.ds(DEEP, layers), t, pl.ds(DEEP, rows), :],
                out_ref.at[:, :, pl.ds(LANES * t, LANES)],
                sems.at[t],
            )
        )
    for copy in results:
        copy.start()
    for copy in results:
        copy.wait()


def extend_mesh(where, block, ylow, yhigh, zlow, zhigh, speed):
    layers, rows, cols = block.shape
    tiles = cols // LANES
    total = layers + 2 * DEEP
    smem = pl.BlockSpec(memory_space=pltpu.SMEM)
    vmem = pl.BlockSpec(memory_space=pltpu.VMEM)
    hbm = pl.BlockSpec(memory_space=pl.ANY)
    work = pltpu.VMEM((total, tiles, Y_GROUPS, SUB, LANES), jnp.float32)
    line = pltpu.VMEM((tiles, Y_GROUPS, SUB, LANES), jnp.float32)
    return pl.pallas_call(
        sweep_kernel,
        out_shape=jax.ShapeDtypeStruct(block.shape, jnp.float32),
        in_specs=[smem, hbm, hbm, hbm, hbm, hbm, vmem],
        out_specs=hbm,
        scratch_shapes=[
            pltpu.VMEM((total, tiles, Y_ROWS, LANES), jnp.float32),
            work, work, line, line,
            pltpu.VMEM((2, Y_GROUPS, SUB, LANES), jnp.float32),
            pltpu.VMEM((tiles, Y_ROWS, LANES), jnp.float32),
            pltpu.SemaphoreType.DMA((5 * tiles,)),
        ],
        compiler_params=pltpu.CompilerParams(vmem_limit_bytes=50 * MIB),
        cost_estimate=pl.CostEstimate(flops=200_000_000, bytes_accessed=12_000_000, transcendentals=0),
        name="extend_mesh",
    )(where, block, ylow, yhigh, zlow, zhigh, speed)


mass_even = (-1.0 / 15.0, 2.0 / 15.0, 8.0 / 15.0, 2.0 / 15.0, -1.0 / 15.0)
mass_odd = (0.0, 2.0 / 15.0, 16.0 / 15.0, 2.0 / 15.0, 0.0)


def mass_along(padded, axis):
    count = padded.shape[axis] - 4
    pieces = [lax.slice_in_dim(padded, i, i + count, axis=axis) for i in range(5)]
    even = sum(mass_even[i] * pieces[i] for i in range(5))
    odd = sum(mass_odd[i] * pieces[i] for i in range(1, 4))
    at_even = lax.broadcasted_iota(jnp.int32, even.shape, axis) % 2 == 0
    return jnp.where(at_even, even, odd)


def with_rows(x, width):
    size = lax.axis_size("vol")
    up = [(i, i + 1) for i in range(size - 1)]
    down = [(j, i) for i, j in up]
    before = lax.ppermute(x[-width:], "vol", up)
    after = lax.ppermute(x[:width], "vol", down)
    return jnp.concatenate([before, x, after], axis=0)


def stepwise(flux, metric):
    root = jnp.sqrt(metric)

    def dot(a, b):
        return lax.psum(jnp.sum(a * b), "vol")

    def step(_, state):
        solved, residual, direction, norm = state
        padded = jnp.pad(with_rows(root * direction, 2), ((0, 0), (2, 2)))
        image = root * mass_along(mass_along(padded, 1), 0)
        alpha = norm / dot(direction, image)
        solved = solved + alpha * direction
        residual = residual - alpha * image
        after = dot(residual, residual)
        direction = residual + after / norm * direction
        return solved, residual, direction, after

    state = (jnp.zeros_like(flux), flux, flux, dot(flux, flux))
    return with_rows(lax.fori_loop(0, ITERS, step, state)[0], DEEP)


def on_device(face_area, face_speed, face_node, face_count, surface_metric, displacement):
    vols, cols = lax.axis_size("vol"), lax.axis_size("col")
    vol, col = lax.axis_index("vol"), lax.axis_index("col")
    core = col % 2
    where = jnp.stack([core, col, jnp.int32(cols), vol, jnp.int32(vols)]).astype(jnp.int32).reshape(1, 5)
    up = [(i, i + 1) for i in range(vols - 1)]
    down = [(j, i) for i, j in up]
    col_up = [(i, i + 1) for i in range(cols - 1)]
    col_down = [(j, i) for i, j in col_up]

    with jax.named_scope("volume_halo"):
        ylow = lax.ppermute(displacement[:, -DEEP:], "vol", up)
        yhigh = lax.ppermute(displacement[:, :DEEP], "vol", down)
        wide = jnp.concatenate([ylow, displacement, yhigh], axis=1)
        zlow = lax.ppermute(wide, "col", col_up)
        zhigh = lax.ppermute(wide, "col", col_down)
    with jax.named_scope("metric_halo"):
        metric_before = lax.ppermute(surface_metric[-HALO:], "vol", up)
        metric_after = lax.ppermute(surface_metric[:HALO], "vol", down)

    keep, send = face_sums(where, face_count, face_area, face_speed, face_node)
    with jax.named_scope("flux_sum"):
        keep = keep + lax.ppermute(send, "col", [(j, j ^ 1) for j in range(cols)])
        turned = [
            lax.ppermute(keep, "col", [(j, (j + 2 * k) % cols) for j in range(cols)]) for k in (1, 2, 3)
        ]
        own = (keep + turned[1]) + (turned[0] + turned[2])
    with jax.named_scope("flux_halo"):
        other = lax.ppermute(own, "col", [(j, j ^ 1) for j in range(cols)])
        same_pairs, cross_pairs = [], []
        for i in range(vols):
            for j in range(cols):
                to = i - 1 if j % 2 == 0 else i + 1
                if 0 <= to < vols:
                    same_pairs.append((i * cols + j, to * cols + j))
                    cross_pairs.append((i * cols + j, to * cols + (j ^ 1)))
        same = lax.ppermute(own, ("vol", "col"), same_pairs)
        cross = lax.ppermute(own, ("vol", "col"), cross_pairs)

    basis, sums = surface_basis(
        where, own, other, same, cross, surface_metric, metric_before, metric_after
    )
    with jax.named_scope("gather_sums"):
        spread = jnp.broadcast_to(sums[None], (vols,) + sums.shape)
        gathered = lax.all_to_all(spread, "vol", 0, 0)
    speed, flag = surface_solve(basis, gathered)

    def step_by_step():
        low = jnp.where(core == 0, own, other)
        high = jnp.where(core == 0, other, own)
        return stepwise(jnp.concatenate([low, high], axis=0), surface_metric)

    speed = lax.cond(flag[0, 0] > 0, lambda: speed, step_by_step)
    displaced = extend_mesh(where, displacement, ylow, yhigh, zlow, zhigh, speed)
    return speed[DEEP:-DEEP], displaced


def solution(mesh):
    in_specs = (
        P("vol", "col"),
        P("vol", "col"),
        P("vol", "col"),
        P("vol", "col"),
        P("vol", None),
        P("col", "vol", None),
    )
    out_specs = (P("vol", None), P("col", "vol", None))
    return jax.shard_map(
        on_device, mesh=mesh, in_specs=in_specs, out_specs=out_specs, check_vma=False
    )
```

time: 1780 us -> 250 us (0.14)
  the two profiles are of different devices: /device:TPU:1 before, /device:TPU:8 now
where the time goes in v1:
time: 250 us
  Pallas kernels  150 us (60%)
  waiting for transfers between devices  44.5 us (18%)
  starting transfers between devices  39.2 us (16%)
  local copies, waits for them, and re-layouts  13.5 us (5%)
    pallas_call x1, Pallas kernels, extend_mesh(): pl.pallas_call(sweep_kernel, out_shape=jax.ShapeDtypeStruct(block.shape,...  106 us
    pallas_call x1, Pallas kernels, surface_basis(): pl.pallas_call(basis_kernel, out_shape=(jax.ShapeDtypeStruct((ITERS + 1,...  34.8 us
    ppermute x3, waiting for transfers between devices, on_device(): lax.ppermute(keep, 'col', [(j, (j + 2 * k) % cols) for j in range(cols)])  23.2 us
    all_to_all x1, starting transfers between devices, on_device(): gathered = lax.all_to_all(spread, 'vol', 0, 0)  13.4 us
    unnamed x18, local copies, waits for them, and re-layouts  9.12 us
    all_to_all x1, waiting for transfers between devices, on_device(): gathered = lax.all_to_all(spread, 'vol', 0, 0)  8.34 us
    pallas_call x1, Pallas kernels, face_sums(): pl.pallas_call(face_kernel, out_shape=(half, half), in_specs=[smem, smem,...  6.58 us
    ppermute x1, waiting for transfers between devices, on_device(): same = lax.ppermute(own, ('vol', 'col'), same_pairs)  5.97 us
  transfers between devices with their start and end apart: 14, of which 8 were waited for; matrix products, arithmetic and copies ran while one was open for 3% of the time, Pallas kernels for 18%

profile of v1, /device:TPU:8, one launch (start us, length us, event | category | flops | bytes accessed | tf_op | source)
XLA Modules:
  0.0 249.6 jit_solution(3994884225476121638)
XLA Ops:
  0.6 1.1 fusion.22
  1.7 3.4 %collective-permute-start.13 = (f32[8,8,1024]{2,1,0:T(8,128)S(1)}, f32[8,8,1024]{2,1,0:T(8,128)S(1)}, u32[]{:S(2)}, u32[]{:S(2)}) collective-permute-start(f32[8,8,1024]{2,1,0:T(8,128)S(1)} %get-tuple-element.165), channel_id=1, source_target_pairs={{0,8},{8,16},{16,24},{24,32},{32,40},{40,48},{48,56},{56,64},{64,7... | collective-permute-start | bytes 786440 | tf_op jit(solution)/shard_map/volume_halo/ppermute | solution.py:523
  5.1 0.0 copy-start.4
  5.1 0.0 copy-start.5
  5.1 0.0 copy-start.6
  5.2 1.4 collective-permute-start.14
  6.6 4.1 %collective-permute-done.13.ylow_ref = f32[8,8,1024]{2,1,0:T(8,128)S(1)} collective-permute-done((f32[8,8,1024]{2,1,0:T(8,128)S(1)}, f32[8,8,1024]{2,1,0:T(8,128)S(1)}, u32[]{:S(2)}, u32[]{:S(2)}) %collective-permute-start.13) | collective-permute-done | bytes 262176 | tf_op jit(solution)/shard_map/volume_halo/ppermute | solution.py:523
  10.7 0.7 constant_dynamic-update-slice_fusion.2
  11.4 3.2 %constant_dynamic-update-slice_fusion.1 = f32[8,80,1024]{2,1,0:T(8,128)} fusion(f32[8,80,1024]{2,1,0:T(8,128)} %constant_dynamic-update-slice_fusion.2, f32[8,64,1024]{2,1,0:T(8,128)} %block_ref.1), kind=kLoop, calls=%fused_computation.46 | loop fusion | bytes 4194304
  14.6 0.3 collective-permute-done.14.yhigh_ref
  14.9 0.7 constant_dynamic-update-slice_fusion
  15.7 1.9 collective-permute-start.15
  17.6 3.6 %collective-permute-start.16 = (f32[8,80,1024]{2,1,0:T(8,128)}, f32[8,80,1024]{2,1,0:T(8,128)}, u32[]{:S(2)}, u32[]{:S(2)}) collective-permute-start(f32[8,80,1024]{2,1,0:T(8,128)} %constant_dynamic-update-slice_fusion), channel_id=1, source_target_pairs={{1,0},{2,1},{3,2},{4,3},{5,4},{6,5},{7,6},{9,8},{10,9},{11,10},{12... | collective-permute-start | bytes 7864328 | tf_op jit(solution)/shard_map/volume_halo/ppermute | solution.py:527
  21.9 0.1 stack.15
  22.0 0.0 copy-done.4
  22.0 0.0 copy-done.5
  22.0 0.0 copy-done.6
  22.0 0.0 copy-start.8
  22.0 6.6 %face_sums.1 = (f32[32,1024]{1,0:T(8,128)S(1)}, f32[32,1024]{1,0:T(8,128)S(1)}) custom-call(s32[1,5]{1,0:T(1,128)S(1)} %bitcast.5, s32[1,1]{1,0:T(1,128)S(6)} %copy.30.count_ref, f32[1,16384]{1,0:T(1,128)S(1)} %copy-done.4, f32[1,16384]{1,0:T(1,128)S(1)} %copy-done.5, s32[1,16384]{1,0:T(1,128)S(1)} %copy-done.6), custom_call_target="tpu_custom_call" | custom-call | flops 4000000000 | bytes 500000 | tf_op jit(solution)/shard_map/face_sums/pallas_call | solution.py:119
  28.6 0.0 copy-start.3
  28.6 0.1 collective-permute-start.4
  28.7 1.3 collective-permute-done.4
  30.0 2.4 collective-permute-start.5
  32.4 0.0 collective-permute-start.6
  32.4 2.0 collective-permute-start.7
  34.4 0.0 copy-done.8
  34.5 23.2 %collective-permute-done.5 = f32[32,1024]{1,0:T(8,128)S(1)} collective-permute-done((f32[32,1024]{1,0:T(8,128)S(1)}, f32[32,1024]{1,0:T(8,128)S(1)}, u32[]{:S(2)}, u32[]{:S(2)}) %collective-permute-start.5) | collective-permute-done | bytes 131104 | tf_op jit(solution)/shard_map/flux_sum/ppermute | solution.py:536
  57.7 4.1 %collective-permute-start.11 = (f32[32,1024]{1,0:T(8,128)S(1)}, f32[32,1024]{1,0:T(8,128)S(1)}, u32[]{:S(2)}, u32[]{:S(2)}) collective-permute-start(f32[32,1024]{1,0:T(8,128)S(1)} %get-tuple-element.167), channel_id=1, source_target_pairs={{0,8},{8,16},{16,24},{24,32},{32,40},{40,48},{48,56},{56,64},{64,7... | collective-permute-start | bytes 393224 | tf_op jit(solution)/shard_map/metric_halo/ppermute | solution.py:529
  61.7 0.0 collective-permute-done.6
  61.7 1.3 collective-permute-start.12
  63.0 0.0 collective-permute-done.7
  63.1 0.7 collective-permute-start.10
  63.8 0.5 collective-permute-done.11.before_ref
  64.2 3.6 %collective-permute-start.8 = (f32[32,1024]{1,0:T(8,128)S(1)}, f32[32,1024]{1,0:T(8,128)S(1)}, u32[]{:S(2)}, u32[]{:S(2)}) collective-permute-start(f32[32,1024]{1,0:T(8,128)S(1)} %add_add_fusion.own_ref), channel_id=1, source_target_pairs={{0,1},{1,0},{2,3},{3,2},{4,5},{5,4},{6,7},{7,6},{8,9},{9,8},{10,11... | collective-permute-start | bytes 393224 | tf_op jit(solution)/shard_map/flux_halo/ppermute | solution.py:540
  67.9 0.7 collective-permute-done.12.after_ref
  68.6 1.3 collective-permute-start.9
  69.9 0.0 collective-permute-done.10.cross_ref
  69.9 0.0 collective-permute-done.8.other_ref
  69.9 6.0 %collective-permute-done.9.same_ref = f32[32,1024]{1,0:T(8,128)S(1)} collective-permute-done((f32[32,1024]{1,0:T(8,128)S(1)}, f32[32,1024]{1,0:T(8,128)S(1)}, u32[]{:S(2)}, u32[]{:S(2)}) %collective-permute-start.9) | collective-permute-done | bytes 131104 | tf_op jit(solution)/shard_map/flux_halo/ppermute | solution.py:548
  75.9 34.8 %surface_basis.1 = (f32[11,8,128,128]{3,2,1,0:T(8,128)S(1)}, f32[24,128]{1,0:T(8,128)S(1)}) custom-call(s32[1,5]{1,0:T(1,128)S(1)} %bitcast.6, f32[32,1024]{1,0:T(8,128)S(1)} %add_add_fusion.own_ref, f32[32,1024]{1,0:T(8,128)S(1)} %collective-permute-done.8.other_ref, f32[32,1024]{1,0:T(8,128)S(1)} %collective-permute-done.9.same_ref, ...), custom_call_target="tpu_custom_call" | custom-call | flops 40000000 | bytes 8000000 | tf_op jit(solution)/shard_map/surface_basis/pallas_call | solution.py:202
  110.7 0.0 copy-start.1
  110.7 2.5 copy-done.1
  113.2 0.7 broadcast_in_dim.2
  113.9 13.4 %all-to-all-start = ((f32[16,24,128]{2,1,0:T(8,128)}), f32[16,24,128]{2,1,0:T(8,128)S(1)}, u32[]{:S(2)}, u32[]{:S(2)}) async-start(f32[16,24,128]{2,1,0:T(8,128)} %broadcast_in_dim.2), calls=%async_computation | async-start | bytes 393216 | tf_op jit(solution)/shard_map/gather_sums/all_to_all | solution.py:556
  127.3 8.3 %all-to-all-done.sums_ref = f32[16,24,128]{2,1,0:T(8,128)S(1)} async-done(((f32[16,24,128]{2,1,0:T(8,128)}), f32[16,24,128]{2,1,0:T(8,128)S(1)}, u32[]{:S(2)}, u32[]{:S(2)}) %all-to-all-start) | async-done | bytes 196640 | tf_op jit(solution)/shard_map/gather_sums/all_to_all | solution.py:556
  135.7 0.0 copy-done.3
  135.7 0.0 copy-start.2
  135.7 2.6 %copy-done.2 = f32[11,8,128,128]{3,2,1,0:T(8,128)S(1)} copy-done((f32[11,8,128,128]{3,2,1,0:T(8,128)S(1)}, f32[11,8,128,128]{3,2,1,0:T(8,128)}, u32[]{:S(2)}) %copy-start.2) | copy-done | bytes 5767192
  138.3 2.6 %surface_solve.1 = (f32[80,1024]{1,0:T(8,128)}, s32[1,1]{1,0:T(1,128)}) custom-call(f32[11,8,128,128]{3,2,1,0:T(8,128)S(1)} %copy-done.2, f32[16,24,128]{2,1,0:T(8,128)S(1)} %all-to-all-done.sums_ref, f32[20,16,128]{2,1,0:T(8,128)S(1)} %copy-done.3), custom_call_target="tpu_custom_call" | custom-call | flops 2000000 | bytes 4000000 | tf_op jit(solution)/shard_map/surface_solve/pallas_call | solution.py:288
  141.6 0.0 copy-start
  141.6 1.8 conditional.1
  141.6 1.8 slice.85
  143.4 0.0 collective-permute-done.15.zlow_ref
  143.4 0.0 collective-permute-done.16.zhigh_ref
  143.4 0.0 copy-done
  143.4 106.2 %extend_mesh.1 = f32[8,64,1024]{2,1,0:T(8,128)} custom-call(s32[1,5]{1,0:T(1,128)S(1)} %bitcast.7, f32[8,64,1024]{2,1,0:T(8,128)S(1)} %copy-done, f32[8,8,1024]{2,1,0:T(8,128)S(1)} %collective-permute-done.13.ylow_ref, f32[8,8,1024]{2,1,0:T(8,128)S(1)} %collective-permute-done.14.yhigh_ref, f32[8,80,1024]{2,1,0:T(8,128)} %collective-permute-done.15.zlow_ref, ...), custom_call_target="tpu_custom_call" | custom-call | flops 200000000 | bytes 12000000 | tf_op jit(solution)/shard_map/extend_mesh/pallas_call | solution.py:451
  (3 shorter events, 0.1 us)
Async XLA Ops:
  1.7 8.9 %collective-permute-start.13 = (f32[8,8,1024]{2,1,0:T(8,128)S(1)}, f32[8,8,1024]{2,1,0:T(8,128)S(1)}, u32[]{:S(2)}, u32[]{:S(2)}) collective-permute-start(f32[8,8,1024]{2,1,0:T(8,128)S(1)} %get-tuple-element.165), channel_id=1, source_target_pairs={{0,8},{8,16},{16,24},{24,32},{32,40},{40,48},{48,56},{56,64},{64,7... | collective-permute-start | bytes 786440 | tf_op jit(solution)/shard_map/volume_halo/ppermute | solution.py:523
  5.1 16.9 %copy-start.4 = (f32[1,16384]{1,0:T(1,128)S(1)}, f32[1,16384]{1,0:T(1,128)}, u32[]{:S(2)}) copy-start(f32[1,16384]{1,0:T(1,128)} %area_ref.1) | copy-start | bytes 196612
  5.1 16.8 %copy-start.5 = (f32[1,16384]{1,0:T(1,128)S(1)}, f32[1,16384]{1,0:T(1,128)}, u32[]{:S(2)}) copy-start(f32[1,16384]{1,0:T(1,128)} %speed_ref.1) | copy-start | bytes 196612
  5.1 16.8 %copy-start.6 = (s32[1,16384]{1,0:T(1,128)S(1)}, s32[1,16384]{1,0:T(1,128)}, u32[]{:S(2)}) copy-start(s32[1,16384]{1,0:T(1,128)} %node_ref.1) | copy-start | bytes 196612
  5.2 9.8 %collective-permute-start.14 = (f32[8,8,1024]{2,1,0:T(8,128)S(1)}, f32[8,8,1024]{2,1,0:T(8,128)S(1)}, u32[]{:S(2)}, u32[]{:S(2)}) collective-permute-start(f32[8,8,1024]{2,1,0:T(8,128)S(1)} %get-tuple-element.164), channel_id=1, source_target_pairs={{8,0},{16,8},{24,16},{32,24},{40,32},{48,40},{56,48},{64,56},{72,6... | collective-permute-start | bytes 786440 | tf_op jit(solution)/shard_map/volume_halo/ppermute | solution.py:524
  15.7 127.8 %collective-permute-start.15 = (f32[8,80,1024]{2,1,0:T(8,128)}, f32[8,80,1024]{2,1,0:T(8,128)}, u32[]{:S(2)}, u32[]{:S(2)}) collective-permute-start(f32[8,80,1024]{2,1,0:T(8,128)} %constant_dynamic-update-slice_fusion), channel_id=1, source_target_pairs={{0,1},{1,2},{2,3},{3,4},{4,5},{5,6},{6,7},{8,9},{9,10},{10,11},{11... | collective-permute-start | bytes 7864328 | tf_op jit(solution)/shard_map/volume_halo/ppermute | solution.py:526
  17.6 125.8 %collective-permute-start.16 = (f32[8,80,1024]{2,1,0:T(8,128)}, f32[8,80,1024]{2,1,0:T(8,128)}, u32[]{:S(2)}, u32[]{:S(2)}) collective-permute-start(f32[8,80,1024]{2,1,0:T(8,128)} %constant_dynamic-update-slice_fusion), channel_id=1, source_target_pairs={{1,0},{2,1},{3,2},{4,3},{5,4},{6,5},{7,6},{9,8},{10,9},{11,10},{12... | collective-permute-start | bytes 7864328 | tf_op jit(solution)/shard_map/volume_halo/ppermute | solution.py:527
  22.0 12.5 %copy-start.8 = (f32[64,1024]{1,0:T(8,128)S(1)}, f32[64,1024]{1,0:T(8,128)}, u32[]{:S(2)}) copy-start(f32[64,1024]{1,0:T(8,128)} %metric_ref.1) | copy-start | bytes 786436
  28.6 107.1 %copy-start.3 = (f32[20,16,128]{2,1,0:T(8,128)S(1)}, f32[20,16,128]{2,1,0:T(8,128)}, u32[]{:S(2)}) copy-start(f32[20,16,128]{2,1,0:T(8,128)} %constant.110.clone.weights_ref) | copy-start | bytes 491524
  28.6 1.4 collective-permute-start.4
  30.0 27.6 %collective-permute-start.5 = (f32[32,1024]{1,0:T(8,128)S(1)}, f32[32,1024]{1,0:T(8,128)S(1)}, u32[]{:S(2)}, u32[]{:S(2)}) collective-permute-start(f32[32,1024]{1,0:T(8,128)S(1)} %add.135), channel_id=1, source_target_pairs={{0,4},{1,5},{2,6},{3,7},{4,0},{5,1},{6,2},{7,3},{8,12},{9,13},{10,... | collective-permute-start | bytes 393224 | tf_op jit(solution)/shard_map/flux_sum/ppermute | solution.py:536
  32.4 29.3 %collective-permute-start.6 = (f32[32,1024]{1,0:T(8,128)S(1)}, f32[32,1024]{1,0:T(8,128)S(1)}, u32[]{:S(2)}, u32[]{:S(2)}) collective-permute-start(f32[32,1024]{1,0:T(8,128)S(1)} %add.135), channel_id=1, source_target_pairs={{0,2},{1,3},{2,4},{3,5},{4,6},{5,7},{6,0},{7,1},{8,10},{9,11},{10,... | collective-permute-start | bytes 393224 | tf_op jit(solution)/shard_map/flux_sum/ppermute | solution.py:536
  32.4 30.6 %collective-permute-start.7 = (f32[32,1024]{1,0:T(8,128)S(1)}, f32[32,1024]{1,0:T(8,128)S(1)}, u32[]{:S(2)}, u32[]{:S(2)}) collective-permute-start(f32[32,1024]{1,0:T(8,128)S(1)} %add.135), channel_id=1, source_target_pairs={{0,6},{1,7},{2,0},{3,1},{4,2},{5,3},{6,4},{7,5},{8,14},{9,15},{10,... | collective-permute-start | bytes 393224 | tf_op jit(solution)/shard_map/flux_sum/ppermute | solution.py:536
  57.7 6.6 %collective-permute-start.11 = (f32[32,1024]{1,0:T(8,128)S(1)}, f32[32,1024]{1,0:T(8,128)S(1)}, u32[]{:S(2)}, u32[]{:S(2)}) collective-permute-start(f32[32,1024]{1,0:T(8,128)S(1)} %get-tuple-element.167), channel_id=1, source_target_pairs={{0,8},{8,16},{16,24},{24,32},{32,40},{40,48},{48,56},{56,64},{64,7... | collective-permute-start | bytes 393224 | tf_op jit(solution)/shard_map/metric_halo/ppermute | solution.py:529
  61.7 6.9 %collective-permute-start.12 = (f32[32,1024]{1,0:T(8,128)S(1)}, f32[32,1024]{1,0:T(8,128)S(1)}, u32[]{:S(2)}, u32[]{:S(2)}) collective-permute-start(f32[32,1024]{1,0:T(8,128)S(1)} %get-tuple-element.166), channel_id=1, source_target_pairs={{8,0},{16,8},{24,16},{32,24},{40,32},{48,40},{56,48},{64,56},{72,6... | collective-permute-start | bytes 393224 | tf_op jit(solution)/shard_map/metric_halo/ppermute | solution.py:530
  63.1 6.8 %collective-permute-start.10 = (f32[32,1024]{1,0:T(8,128)S(1)}, f32[32,1024]{1,0:T(8,128)S(1)}, u32[]{:S(2)}, u32[]{:S(2)}) collective-permute-start(f32[32,1024]{1,0:T(8,128)S(1)} %add_add_fusion.own_ref), channel_id=1, source_target_pairs={{1,8},{3,10},{5,12},{7,14},{8,1},{9,16},{10,3},{11,18},{12,5},{13,... | collective-permute-start | bytes 393224 | tf_op jit(solution)/shard_map/flux_halo/ppermute | solution.py:549
  64.2 5.7 %collective-permute-start.8 = (f32[32,1024]{1,0:T(8,128)S(1)}, f32[32,1024]{1,0:T(8,128)S(1)}, u32[]{:S(2)}, u32[]{:S(2)}) collective-permute-start(f32[32,1024]{1,0:T(8,128)S(1)} %add_add_fusion.own_ref), channel_id=1, source_target_pairs={{0,1},{1,0},{2,3},{3,2},{4,5},{5,4},{6,7},{7,6},{8,9},{9,8},{10,11... | collective-permute-start | bytes 393224 | tf_op jit(solution)/shard_map/flux_halo/ppermute | solution.py:540
  68.6 7.3 %collective-permute-start.9 = (f32[32,1024]{1,0:T(8,128)S(1)}, f32[32,1024]{1,0:T(8,128)S(1)}, u32[]{:S(2)}, u32[]{:S(2)}) collective-permute-start(f32[32,1024]{1,0:T(8,128)S(1)} %add_add_fusion.own_ref), channel_id=1, source_target_pairs={{1,9},{3,11},{5,13},{7,15},{8,0},{9,17},{10,2},{11,19},{12,4},{13,... | collective-permute-start | bytes 393224 | tf_op jit(solution)/shard_map/flux_halo/ppermute | solution.py:548
  110.7 2.5 copy-start.1
  113.9 21.7 %all-to-all-start = ((f32[16,24,128]{2,1,0:T(8,128)}), f32[16,24,128]{2,1,0:T(8,128)S(1)}, u32[]{:S(2)}, u32[]{:S(2)}) async-start(f32[16,24,128]{2,1,0:T(8,128)} %broadcast_in_dim.2), calls=%async_computation | async-start | bytes 393216 | tf_op jit(solution)/shard_map/gather_sums/all_to_all | solution.py:556
  135.7 2.6 %copy-start.2 = (f32[11,8,128,128]{3,2,1,0:T(8,128)S(1)}, f32[11,8,128,128]{3,2,1,0:T(8,128)}, u32[]{:S(2)}) copy-start(f32[11,8,128,128]{3,2,1,0:T(8,128)} %copy-done.1) | copy-start | bytes 17301508
  141.6 1.9 copy-start

commit v2 on v1

v2 whole, which is shorter than its diff:
```python
import jax
import jax.numpy as jnp
import numpy as np
from jax import lax
from jax.experimental import pallas as pl
from jax.experimental.pallas import tpu as pltpu
from jax.sharding import PartitionSpec as P

ITERS = 10
SWEEPS = 4
LANES = 128
SUB = 8
MIB = 1024 * 1024
DEEP = 2 * SWEEPS
HALO = 32
ROWS = 128
GROUPS = 16
Y_GROUPS = 10
Y_ROWS = 80

BASIS_LOW = 0.1
BASIS_HIGH = 12.0
CONDITION_MAX = 2000.0


def rolled(x, shift, axis):
    return pltpu.roll(x, shift % x.shape[axis], axis)


def column_ring(tiles):
    n = len(tiles)
    lane = lax.broadcasted_iota(jnp.int32, tiles[0].shape, 1)
    first, last = lane == 0, lane == LANES - 1
    return (
        [jnp.where(first, 0.0, rolled(tiles[j], 1, 1)) for j in (n - 2, n - 1)]
        + list(tiles)
        + [jnp.where(last, 0.0, rolled(tiles[j], -1, 1)) for j in (0, 1)]
    )


def row_ring(rows):
    n = len(rows)
    return (
        [rolled(rows[j], 1, 0) for j in (n - 2, n - 1)]
        + list(rows)
        + [rolled(rows[j], -1, 0) for j in (0, 1)]
    )


def mass_line(padded, index):
    i = index + 2
    near = padded[i - 1] + padded[i + 1]
    if index % 2:
        return near + 8.0 * padded[i]
    return (near + 4.0 * padded[i]) - 0.5 * (padded[i - 2] + padded[i + 2])


def both_line(padded, index):
    i = index + 2
    near = padded[i - 1] + padded[i + 1]
    return (16.0 / 3.0 if index % 2 else 11.0 / 3.0) * padded[i] - near


SMEM = pl.BlockSpec(memory_space=pltpu.SMEM)
VMEM = pl.BlockSpec(memory_space=pltpu.VMEM)
HBM = pl.BlockSpec(memory_space=pl.ANY)


def f32(*shape):
    return jax.ShapeDtypeStruct(shape, jnp.float32)


def params(mib):
    return pltpu.CompilerParams(vmem_limit_bytes=mib * MIB)


def cost(us):
    return pl.CostEstimate(flops=0, bytes_accessed=int(us * 3_000_000), transcendentals=0)


def split(x):
    first = x.astype(jnp.bfloat16)
    return first, (x - first.astype(jnp.float32)).astype(jnp.bfloat16)


def to_blocked(j):
    x = lax.broadcasted_iota(jnp.int32, (1024, 256), 0)
    n = lax.broadcasted_iota(jnp.int32, (1024, 256), 1)
    hit = x == 8 * (n & 127) + j + (n >> 7)
    return jnp.where(hit, 1.0, 0.0).astype(jnp.bfloat16)


def to_plain(q):
    k = lax.broadcasted_iota(jnp.int32, (1024, 256), 0)
    x = lax.broadcasted_iota(jnp.int32, (1024, 256), 1) + 256 * q
    hit = x == 8 * (k & 127) + (k >> 7)
    return jnp.where(hit, 1.0, 0.0).astype(jnp.bfloat16)


def regroup_kernel(block_ref, metric_ref, out_ref, root_ref, up_ref, down_ref, parts_ref):
    layers, rows, _ = block_ref.shape
    total = layers * rows + rows
    for z in range(layers):
        first, second = split(block_ref[z])
        parts_ref[rows * z : rows * (z + 1), :] = first
        parts_ref[total + rows * z : total + rows * (z + 1), :] = second
    first, second = split(jnp.sqrt(metric_ref[...]))
    parts_ref[rows * layers : total, :] = first
    parts_ref[total + rows * layers : 2 * total, :] = second
    for j in range(0, 8, 2):
        pair = jnp.dot(parts_ref[...], to_blocked(j), preferred_element_type=jnp.float32)
        pair = pair[:total] + pair[total:]
        for i in range(2):
            tile = pair[:, LANES * i : LANES * (i + 1)]
            for z in range(layers):
                plane = tile[rows * z : rows * (z + 1)]
                out_ref[z, j + i] = plane
                up_ref[j + i, DEEP * z : DEEP * (z + 1), :] = plane[rows - DEEP :]
                down_ref[j + i, DEEP * z : DEEP * (z + 1), :] = plane[:DEEP]
            plane = tile[rows * layers :]
            root_ref[j + i] = plane
            up_ref[j + i, DEEP * layers :, :] = plane[rows - HALO :]
            down_ref[j + i, DEEP * layers :, :] = plane[:HALO]


def regroup(block, metric):
    layers, rows, cols = block.shape
    packed = f32(8, layers * DEEP + HALO, LANES)
    return pl.pallas_call(
        regroup_kernel,
        out_shape=(f32(layers, 8, rows, LANES), f32(8, rows, LANES), packed, packed),
        in_specs=[VMEM, VMEM],
        out_specs=(VMEM, VMEM, VMEM, VMEM),
        scratch_shapes=[pltpu.VMEM((2 * rows * (layers + 1), cols), jnp.bfloat16)],
        compiler_params=params(40),
        cost_estimate=cost(4),
        name="regroup",
    )(block, metric)


def plain_columns(parts_ref, rows, write):
    for q in range(4):
        value = jnp.dot(parts_ref[...], to_plain(q), preferred_element_type=jnp.float32)
        write(q, value[:rows] + value[rows:])


def face_kernel(where_ref, count_ref, area_ref, speed_ref, node_ref, keep_ref, send_ref, acc_ref):
    slots = area_ref.shape[1]
    chunk = min(2048, slots)
    core = where_ref[0, 0]
    ids = lax.broadcasted_iota(jnp.int32, (256, chunk), 0)
    ids = ids.astype(jnp.float32).astype(jnp.bfloat16)
    zero = jnp.zeros((), jnp.bfloat16)
    one = jnp.ones((), jnp.bfloat16)
    contract = (((1,), (1,)), ((), ()))
    acc_ref[...] = jnp.zeros_like(acc_ref)

    def wide(x):
        return jnp.broadcast_to(x.astype(jnp.bfloat16), (256, chunk))

    def body(step, carry):
        at = pl.ds(pl.multiple_of(step * chunk, chunk), chunk)
        slot = lax.broadcasted_iota(jnp.int32, (1, chunk), 1) + step * chunk
        value = jnp.where(slot < count_ref[0, 0], area_ref[:, at] * speed_ref[:, at], 0.0)
        node = node_ref[:, at]
        low = (((node & 1) << 7) + ((node >> 3) & 127)).astype(jnp.float32)
        high = (((node >> 1) & 3) * 64 + (node >> 10)).astype(jnp.float32)
        first = value.astype(jnp.bfloat16)
        second = value - first.astype(jnp.float32)
        here = wide(high) == ids
        upper = jnp.where(here, wide(first), zero)
        lower = jnp.where(here, wide(second), zero)
        columns = jnp.where(wide(low) == ids, one, zero)
        acc_ref[...] += lax.dot_general(
            upper, columns, contract, preferred_element_type=jnp.float32
        ) + lax.dot_general(lower, columns, contract, preferred_element_type=jnp.float32)
        return carry

    lax.fori_loop(0, slots // chunk, body, 0)
    for j in range(8):
        at, lanes = 64 * (j // 2), slice(LANES * (j % 2), LANES * (j % 2 + 1))
        keep_ref[j] = acc_ref[pl.ds(at + 32 * core, 32), lanes]
        send_ref[j] = acc_ref[pl.ds(at + 32 - 32 * core, 32), lanes]


def face_sums(where, count, area, speed, node):
    half = f32(8, 32, LANES)
    return pl.pallas_call(
        face_kernel,
        out_shape=(half, half),
        in_specs=[SMEM, SMEM, VMEM, VMEM, VMEM],
        out_specs=(VMEM, VMEM),
        scratch_shapes=[pltpu.VMEM((256, 256), jnp.float32)],
        compiler_params=params(32),
        cost_estimate=cost(7),
        name="face_sums",
    )(where, count, area, speed, node)


def basis_kernel(
    where_ref, own_ref, other_ref, same_ref, cross_ref, root_own_ref, before_ref, after_ref,
    basis_ref, sums_ref, field, root, line, sems,
):
    core = where_ref[0, 0]
    packed = before_ref.shape[1]
    for t in range(8):
        field[0, t, pl.ds(32 + 32 * core, 32), :] = own_ref[t]
        field[0, t, pl.ds(64 - 32 * core, 32), :] = other_ref[t]
        field[0, t, pl.ds(96 * core, 32), :] = cross_ref[t]
        field[0, t, pl.ds(96 - 96 * core, 32), :] = same_ref[t]
        root[t, 0:32, :] = before_ref[t, packed - HALO :, :]
        root[t, 32:96, :] = root_own_ref[t]
        root[t, 96:128, :] = after_ref[t, packed - HALO :, :]

    centre = (BASIS_LOW + BASIS_HIGH) / 2
    scale = 2 / (BASIS_HIGH - BASIS_LOW)
    group = lax.broadcasted_iota(jnp.int32, (SUB, LANES), 0)
    own_rows = jnp.where((group >= 2) & (group < 6), 1.0, 0.0).astype(jnp.float32)

    def rows_of(ys):
        return pl.ds(ys, SUB, stride=GROUPS)

    def out_copy(k):
        return pltpu.make_async_copy(
            field.at[k, :, pl.ds(HALO - DEEP, Y_ROWS), :], basis_ref.at[k], sems.at[k]
        )

    def step(k, carry):
        out_copy(k).start()
        before = jnp.maximum(k - 1, 0)
        first = jnp.where(k == 0, 1.0, 2.0).astype(jnp.float32)
        second = jnp.where(k == 0, 0.0, 1.0).astype(jnp.float32)
        for ys in range(GROUPS):
            weighted = [field[k, t, rows_of(ys), :] * root[t, rows_of(ys), :] for t in range(8)]
            padded = column_ring(weighted)
            for t in range(8):
                line[ys, t] = mass_line(padded, t)
        square = jnp.zeros((SUB, LANES), jnp.float32)
        shifted = jnp.zeros((SUB, LANES), jnp.float32)
        for t in range(8):
            padded = row_ring([line[ys, t] for ys in range(GROUPS)])
            for ys in range(GROUPS):
                image = (root[t, rows_of(ys), :] * (4.0 / 225.0 * scale)) * mass_line(padded, ys)
                now = field[k, t, rows_of(ys), :]
                last = field[before, t, rows_of(ys), :]
                later = first * (image - (centre * scale) * now) - second * last
                field[k + 1, t, rows_of(ys), :] = later
                square = square + now * now
                shifted = shifted + later * now
        sums_ref[pl.ds(2 * k, 1), :] = jnp.sum(square * own_rows, axis=0, keepdims=True)
        sums_ref[pl.ds(2 * k + 1, 1), :] = jnp.sum(shifted * own_rows, axis=0, keepdims=True)
        return carry

    sums_ref[...] = jnp.zeros_like(sums_ref)
    lax.fori_loop(0, ITERS, step, 0)
    for k in range(ITERS):
        out_copy(k).wait()


def surface_basis(where, own, other, same, cross, root, before, after):
    return pl.pallas_call(
        basis_kernel,
        out_shape=(f32(ITERS, 8, Y_ROWS, LANES), f32(24, LANES)),
        in_specs=[SMEM] + [VMEM] * 7,
        out_specs=(HBM, VMEM),
        scratch_shapes=[
            pltpu.VMEM((ITERS + 1, 8, ROWS, LANES), jnp.float32),
            pltpu.VMEM((8, ROWS, LANES), jnp.float32),
            pltpu.VMEM((GROUPS, 8, SUB, LANES), jnp.float32),
            pltpu.SemaphoreType.DMA((ITERS,)),
        ],
        compiler_params=params(40),
        cost_estimate=cost(7),
        name="surface_basis",
    )(where, own, other, same, cross, root, before, after)


def solve_weights():
    n = ITERS
    moment = np.zeros((2 * n, 2 * n))
    for m in range(2 * n):
        if m < 2:
            moment[m, m] = 1.0
        else:
            moment[m, m] = 2.0
            moment[m, m % 2] = -1.0
    centre, half = (BASIS_LOW + BASIS_HIGH) / 2, (BASIS_HIGH - BASIS_LOW) / 2
    weights = np.zeros((2 * n, 16, LANES))
    for i in range(n):
        for j in range(n):
            lower = abs(j - 1)
            for factor, index in (
                (centre / 2, i + j),
                (centre / 2, abs(i - j)),
                (half / 4, i + j + 1),
                (half / 4, abs(i - j - 1)),
                (half / 4, i + lower),
                (half / 4, abs(i - lower)),
            ):
                weights[:, i, j] += factor * moment[index]
        weights[:, i, n] += moment[i]
    return weights.astype(np.float32)


def solve_kernel(basis_ref, sums_ref, weights_ref, out_ref, flag_ref, part_ref, sem):
    n = ITERS
    copy = pltpu.make_async_copy(basis_ref, part_ref, sem)
    copy.start()
    total = sums_ref[0]
    for i in range(1, sums_ref.shape[0]):
        total = total + sums_ref[i]
    total = jnp.broadcast_to(jnp.sum(total, axis=1, keepdims=True), total.shape)
    row = lax.broadcasted_iota(jnp.int32, (16, LANES), 0)
    lane = lax.broadcasted_iota(jnp.int32, (16, LANES), 1)
    system = jnp.where((lane == row + 16) & (row < n), 1.0, 0.0).astype(jnp.float32)
    for m in range(2 * n):
        system = system + weights_ref[m] * total[m : m + 1, :]
    centre = jnp.sum(jnp.where(lane == row, system, 0.0), axis=1, keepdims=True)
    for k in range(n):
        pivot_row = system[k : k + 1, :] / system[k : k + 1, k : k + 1]
        column = system[:, k : k + 1]
        system = jnp.where(row == k, pivot_row, system - column * pivot_row)
    inverse = jnp.sum(jnp.where(lane == row + 16, system, 0.0), axis=1, keepdims=True)
    figure = jnp.broadcast_to(centre * inverse, (16, LANES))
    inside = (row < n) & (lane == 0)
    least = jnp.min(jnp.where(inside, figure, 1.0))
    whole = jnp.sum(jnp.where(inside, figure, 0.0))
    flag_ref[0, 0] = jnp.where((least > 0.5) & (whole < CONDITION_MAX), 1, 0).astype(jnp.int32)
    copy.wait()
    for t in range(8):
        value = None
        for k in range(n):
            term = system[k : k + 1, n : n + 1] * part_ref[k, t]
            value = term if value is None else value + term
        out_ref[t] = value


def surface_solve(basis, sums):
    return pl.pallas_call(
        solve_kernel,
        out_shape=(f32(8, Y_ROWS, LANES), jax.ShapeDtypeStruct((1, 1), jnp.int32)),
        in_specs=[HBM, VMEM, VMEM],
        out_specs=(VMEM, SMEM),
        scratch_shapes=[pltpu.VMEM(basis.shape, jnp.float32), pltpu.SemaphoreType.DMA],
        compiler_params=params(32),
        cost_estimate=cost(3),
        name="surface_solve",
    )(basis, sums, jnp.asarray(solve_weights()))


def fill_factors(factor, where_ref, rows):
    vol, vols = where_ref[0, 3], where_ref[0, 4]
    group = lax.broadcasted_iota(jnp.int32, (SUB, LANES), 0)
    mass, stiff = (8.0, 16.0), (14.0, 16.0)
    for ys in range(Y_GROUPS):
        row = group * Y_GROUPS + ys
        outside = ((vol == 0) & (row < DEEP)) | ((vol == vols - 1) & (row >= DEEP + rows))
        py = ys % 2
        for pz in range(2):
            for px in range(2):
                value = -12.0 / (
                    stiff[pz] * mass[py] * mass[px]
                    + mass[pz] * (stiff[py] * mass[px] + mass[py] * stiff[px])
                )
                factor[pz, px, ys] = jnp.where(outside, 0.0, jnp.float32(value))


def lateral_lines(get, line_a, line_b, put):
    for ys in range(Y_GROUPS):
        padded = column_ring([get(t, ys) for t in range(8)])
        for t in range(8):
            m = mass_line(padded, t)
            line_a[t, ys] = m
            line_b[t, ys] = both_line(padded, t) - m
    for t in range(8):
        a = row_ring([line_a[t, ys] for ys in range(Y_GROUPS)])
        b = row_ring([line_b[t, ys] for ys in range(Y_GROUPS)])
        for ys in range(Y_GROUPS):
            put(t, ys, mass_line(a, ys), both_line(a, ys) + mass_line(b, ys))


def pair_steps(w, c):
    near = c[1] + c[3]
    even = (11.0 / 3.0 * w[1] - (w[0] + w[2])) + ((near + 4.0 * c[2]) - 0.5 * (c[0] + c[4]))
    near = c[2] + c[4]
    odd = (16.0 / 3.0 * w[2] - (w[1] + w[3])) + (near + 8.0 * c[3])
    return even, odd


def strided(ys):
    return pl.ds(ys, SUB, stride=Y_GROUPS)


def base_kernel(
    where_ref, block_ref, before_ref, after_ref, zlow_ref, zhigh_ref, corner_low_ref, corner_high_ref,
    out_ref, field, along, cross, line_a, line_b, factor, top, parts, sems,
):
    col, cols = where_ref[0, 1], where_ref[0, 2]
    layers, _, rows, _ = block_ref.shape
    total = layers + 2 * DEEP
    copies = []

    def bring(source, at_z, nz, at_y, ny):
        copies.append(
            pltpu.make_async_copy(
                source, field.at[pl.ds(at_z, nz), :, pl.ds(at_y, ny), :], sems.at[len(copies)]
            )
        )

    bring(block_ref, DEEP, layers, DEEP, rows)
    bring(zlow_ref, 0, DEEP, DEEP, rows)
    bring(zhigh_ref, DEEP + layers, DEEP, DEEP, rows)
    for z in range(layers):
        for source, corner, at_y in ((before_ref, 0, 0), (after_ref, 1, DEEP + rows)):
            at = pl.ds(DEEP * z, DEEP)
            for part, at_z in ((source.at[:, at, :], DEEP + z),
                               (corner_low_ref.at[corner, :, at, :], z),
                               (corner_high_ref.at[corner, :, at, :], DEEP + layers + z)):
                copies.append(
                    pltpu.make_async_copy(
                        part, field.at[at_z, :, pl.ds(at_y, DEEP), :], sems.at[len(copies)]
                    )
                )
    for copy in copies:
        copy.start()
    fill_factors(factor, where_ref, rows)
    for copy in copies:
        copy.wait()

    @pl.when(col == 0)
    def _():
        for t in range(8):
            top[t] = field[DEEP, t]

    def lateral(z, carry):
        def put(t, ys, w, c):
            along[z, t, ys] = w
            cross[z, t, ys] = c

        lateral_lines(lambda t, ys: field[z, t, strided(ys), :], line_a, line_b, put)
        return carry

    def update(pair, carry):
        z = 2 * pair
        for t in range(8):
            for ys in range(Y_GROUPS):
                even, odd = pair_steps(
                    [along[z + i, t, ys] for i in range(-1, 3)], [cross[z + i, t, ys] for i in range(-2, 4)]
                )
                even = field[z, t, strided(ys), :] + factor[0, t % 2, ys] * even
                odd = field[z + 1, t, strided(ys), :] + factor[1, t % 2, ys] * odd
                field[z, t, strided(ys), :] = even
                field[z + 1, t, strided(ys), :] = odd
        return carry

    def one_sweep(sweep, carry):
        edge = 2 * sweep
        lax.fori_loop(edge, total - edge, lateral, 0)
        low = jnp.where(col == 0, DEEP // 2, sweep + 1)
        high = jnp.where(col == cols - 1, (DEEP + layers) // 2, total // 2 - sweep - 1)
        lax.fori_loop(low, high, update, 0)

        @pl.when(col == 0)
        def _():
            for t in range(8):
                field[DEEP, t] = top[t]

        return carry

    lax.fori_loop(0, SWEEPS, one_sweep, 0)
    count = layers * rows
    for z in range(layers):
        for t in range(8):
            first, second = split(field[DEEP + z, t, DEEP : DEEP + rows, :])
            lanes = slice(LANES * t, LANES * (t + 1))
            parts[rows * z : rows * (z + 1), lanes] = first
            parts[count + rows * z : count + rows * (z + 1), lanes] = second

    def write(q, value):
        out_ref[:, :, 256 * q : 256 * (q + 1)] = value.reshape(layers, rows, 256)

    plain_columns(parts, count, write)


def base_sweeps(where, block, before, after, zlow, zhigh, corner_low, corner_high):
    layers, _, rows, _ = block.shape
    total = layers + 2 * DEEP
    work = pltpu.VMEM((total, 8, Y_GROUPS, SUB, LANES), jnp.float32)
    line = pltpu.VMEM((8, Y_GROUPS, SUB, LANES), jnp.float32)
    return pl.pallas_call(
        base_kernel,
        out_shape=f32(layers, rows, 8 * LANES),
        in_specs=[SMEM] + [HBM] * 7,
        out_specs=VMEM,
        scratch_shapes=[
            pltpu.VMEM((total, 8, Y_ROWS, LANES), jnp.float32),
            work, work, line, line,
            pltpu.VMEM((2, 2, Y_GROUPS, SUB, LANES), jnp.float32),
            pltpu.VMEM((8, Y_ROWS, LANES), jnp.float32),
            pltpu.VMEM((2 * layers * rows, 8 * LANES), jnp.bfloat16),
            pltpu.SemaphoreType.DMA((3 + 6 * layers,)),
        ],
        compiler_params=params(50),
        cost_estimate=cost(25),
        name="base_sweeps",
    )(where, block, before, after, zlow, zhigh, corner_low, corner_high)


def top_kernel(
    where_ref, base_ref, speed_ref, velocity_ref, out_ref,
    cells, along, cross, line_a, line_b, factor, plain, parts, parts_speed, shown, sem,
):
    col = where_ref[0, 1]
    layers, rows, _ = out_ref.shape
    for t in range(8):
        lanes = slice(LANES * t, LANES * (t + 1))
        first, second = split(speed_ref[t, DEEP : DEEP + rows, :])
        parts_speed[:rows, lanes] = first
        parts_speed[rows:, lanes] = second

    def write_speed(q, value):
        velocity_ref[:, 256 * q : 256 * (q + 1)] = value

    plain_columns(parts_speed, rows, write_speed)

    def lateral(z, carry):
        def put(t, ys, w, c):
            along[z, t, ys] = w
            cross[z, t, ys] = c

        lateral_lines(lambda t, ys: cells[z, t, ys], line_a, line_b, put)
        return carry

    def start():
        fill_factors(factor, where_ref, rows)
        for t in range(8):
            for ys in range(Y_GROUPS):
                cells[2, t, ys] = 0.5 * speed_ref[t, strided(ys), :]

    @pl.when(col == 0)
    def _():
        copy = pltpu.make_async_copy(base_ref, shown, sem)
        copy.start()
        start()
        clear = jnp.zeros((8, Y_GROUPS, SUB, LANES), jnp.float32)
        for z in range(layers + 4):
            if z != 2:
                cross[z] = clear
                along[z] = clear
                if z < layers + 2:
                    cells[z] = clear

        def update(pair, carry):
            z = 2 * pair + 2
            for t in range(8):
                for ys in range(Y_GROUPS):
                    even, odd = pair_steps(
                        [along[z + i, t, ys] for i in range(-1, 3)],
                        [cross[z + i, t, ys] for i in range(-2, 4)],
                    )
                    cells[z, t, ys] += factor[0, t % 2, ys] * even
                    cells[z + 1, t, ys] += factor[1, t % 2, ys] * odd
            return carry

        def one_sweep(sweep, carry):
            lax.fori_loop(2, 2 * sweep + 3, lateral, 0)
            lax.fori_loop(0, jnp.minimum(sweep + 2, layers // 2), update, 0)
            for t in range(8):
                for ys in range(Y_GROUPS):
                    cells[2, t, ys] = 0.5 * speed_ref[t, strided(ys), :]
            return carry

        lax.fori_loop(0, SWEEPS, one_sweep, 0)
        count = layers * rows
        for z in range(layers):
            for t in range(8):
                for ys in range(Y_GROUPS):
                    plain[strided(ys), :] = cells[z + 2, t, ys]
                first, second = split(plain[DEEP : DEEP + rows, :])
                lanes = slice(LANES * t, LANES * (t + 1))
                parts[rows * z : rows * (z + 1), lanes] = first
                parts[count + rows * z : count + rows * (z + 1), lanes] = second
        copy.wait()

        def write(q, value):
            at = slice(256 * q, 256 * (q + 1))
            shown[:, :, at] = shown[:, :, at] + value.reshape(layers, rows, 256)

        plain_columns(parts, count, write)
        back = pltpu.make_async_copy(shown, out_ref, sem)
        back.start()
        back.wait()

    @pl.when(col == 1)
    def _():
        copy = pltpu.make_async_copy(base_ref.at[pl.ds(0, 1)], shown.at[pl.ds(0, 1)], sem)
        copy.start()
        start()

        def one_sweep(sweep, carry):
            lateral(2, 0)
            for t in range(8):
                for ys in range(Y_GROUPS):
                    cells[2, t, ys] = factor[0, t % 2, ys] * (-0.5 * cross[2, t, ys])
            return carry

        lax.fori_loop(0, SWEEPS, one_sweep, 0)
        for t in range(8):
            for ys in range(Y_GROUPS):
                plain[strided(ys), :] = cells[2, t, ys]
            first, second = split(plain[DEEP : DEEP + rows, :])
            lanes = slice(LANES * t, LANES * (t + 1))
            parts_speed[:rows, lanes] = first
            parts_speed[rows:, lanes] = second
        copy.wait()

        def write(q, value):
            at = slice(256 * q, 256 * (q + 1))
            shown[0, :, at] = shown[0, :, at] + value

        plain_columns(parts_speed, rows, write)
        back = pltpu.make_async_copy(shown.at[pl.ds(0, 1)], out_ref.at[pl.ds(0, 1)], sem)
        back.start()
        back.wait()


def add_top(where, base, speed):
    layers, rows, cols = base.shape
    work = pltpu.VMEM((layers + 4, 8, Y_GROUPS, SUB, LANES), jnp.float32)
    line = pltpu.VMEM((8, Y_GROUPS, SUB, LANES), jnp.float32)
    return pl.pallas_call(
        top_kernel,
        out_shape=(f32(rows, cols), f32(layers, rows, cols)),
        in_specs=[SMEM, HBM, VMEM],
        out_specs=(VMEM, HBM),
        input_output_aliases={1: 1},
        scratch_shapes=[
            pltpu.VMEM((layers + 2, 8, Y_GROUPS, SUB, LANES), jnp.float32),
            work, work, line, line,
            pltpu.VMEM((2, 2, Y_GROUPS, SUB, LANES), jnp.float32),
            pltpu.VMEM((Y_ROWS, LANES), jnp.float32),
            pltpu.VMEM((2 * layers * rows, cols), jnp.bfloat16),
            pltpu.VMEM((2 * rows, cols), jnp.bfloat16),
            pltpu.VMEM((layers, rows, cols), jnp.float32),
            pltpu.SemaphoreType.DMA,
        ],
        compiler_params=params(48),
        cost_estimate=cost(10),
        name="add_top",
    )(where, base, speed)


mass_even = (-1.0 / 15.0, 2.0 / 15.0, 8.0 / 15.0, 2.0 / 15.0, -1.0 / 15.0)
mass_odd = (0.0, 2.0 / 15.0, 16.0 / 15.0, 2.0 / 15.0, 0.0)


def mass_along(padded, axis):
    count = padded.shape[axis] - 4
    pieces = [lax.slice_in_dim(padded, i, i + count, axis=axis) for i in range(5)]
    even = sum(mass_even[i] * pieces[i] for i in range(5))
    odd = sum(mass_odd[i] * pieces[i] for i in range(1, 4))
    at_even = lax.broadcasted_iota(jnp.int32, even.shape, axis) % 2 == 0
    return jnp.where(at_even, even, odd)


def with_rows(x, width):
    size = lax.axis_size("vol")
    up = [(i, i + 1) for i in range(size - 1)]
    down = [(j, i) for i, j in up]
    before = lax.ppermute(x[-width:], "vol", up)
    after = lax.ppermute(x[:width], "vol", down)
    return jnp.concatenate([before, x, after], axis=0)


def stepwise(flux, metric):
    root = jnp.sqrt(metric)

    def dot(a, b):
        return lax.psum(jnp.sum(a * b), "vol")

    def step(_, state):
        solved, residual, direction, norm = state
        padded = jnp.pad(with_rows(root * direction, 2), ((0, 0), (2, 2)))
        image = root * mass_along(mass_along(padded, 1), 0)
        alpha = norm / dot(direction, image)
        solved = solved + alpha * direction
        residual = residual - alpha * image
        after = dot(residual, residual)
        direction = residual + after / norm * direction
        return solved, residual, direction, after

    state = (jnp.zeros_like(flux), flux, flux, dot(flux, flux))
    return with_rows(lax.fori_loop(0, ITERS, step, state)[0], DEEP)


def after(x, *others):
    return lax.optimization_barrier((x,) + others)[0]


def on_device(face_area, face_speed, face_node, face_count, surface_metric, displacement):
    vols, cols = lax.axis_size("vol"), lax.axis_size("col")
    vol, col = lax.axis_index("vol"), lax.axis_index("col")
    core = col % 2
    where = jnp.stack([core, col, jnp.int32(cols), vol, jnp.int32(vols)]).astype(jnp.int32).reshape(1, 5)
    up = [(i, i + 1) for i in range(vols - 1)]
    down = [(j, i) for i, j in up]
    col_up = [(i, i + 1) for i in range(cols - 1)]
    col_down = [(j, i) for i, j in col_up]
    packed = displacement.shape[0] * DEEP

    block, root, rows_up, rows_down = regroup(displacement, surface_metric)
    with jax.named_scope("row_halo"):
        rows_before = lax.ppermute(rows_up, "vol", up)
        rows_after = lax.ppermute(rows_down, "vol", down)
    with jax.named_scope("depth_halo"):
        zlow = lax.ppermute(block, "col", col_up)
        zhigh = lax.ppermute(block, "col", col_down)

    keep, send = face_sums(where, face_count, face_area, face_speed, face_node)
    with jax.named_scope("flux_sum"):
        keep = keep + lax.ppermute(send, "col", [(j, j ^ 1) for j in range(cols)])
        turned = [
            lax.ppermute(keep, "col", [(j, (j + 2 * k) % cols) for j in range(cols)]) for k in (1, 2, 3)
        ]
        own = (keep + turned[1]) + (turned[0] + turned[2])
    with jax.named_scope("flux_halo"):
        other = lax.ppermute(own, "col", [(j, j ^ 1) for j in range(cols)])
        same_pairs, cross_pairs = [], []
        for i in range(vols):
            for j in range(cols):
                to = i - 1 if j % 2 == 0 else i + 1
                if 0 <= to < vols:
                    same_pairs.append((i * cols + j, to * cols + j))
                    cross_pairs.append((i * cols + j, to * cols + (j ^ 1)))
        same = lax.ppermute(own, ("vol", "col"), same_pairs)
        cross = lax.ppermute(own, ("vol", "col"), cross_pairs)

    with jax.named_scope("corner_halo"):
        corners = jnp.stack([rows_before[:, :packed], rows_after[:, :packed]])
        corner_low = lax.ppermute(corners, "col", col_up)
        corner_high = lax.ppermute(corners, "col", col_down)

    basis, sums = surface_basis(where, own, other, same, cross, root, rows_before, rows_after)
    with jax.named_scope("gather_sums"):
        spread = jnp.broadcast_to(sums[None], (vols,) + sums.shape)
        gathered = lax.all_to_all(spread, "vol", 0, 0)
    base = base_sweeps(where, block, rows_before, rows_after, zlow, zhigh, corner_low, corner_high)
    speed, flag = surface_solve(basis, gathered)

    def step_by_step():
        low = jnp.where(core == 0, own, other)
        high = jnp.where(core == 0, other, own)
        flux = jnp.concatenate([low, high], axis=1)
        flux = flux.transpose(1, 2, 0).reshape(surface_metric.shape)
        wide = stepwise(flux, surface_metric)
        return wide.reshape(Y_ROWS, LANES, 8).transpose(2, 0, 1)

    speed = lax.cond(flag[0, 0] > 0, lambda: speed, step_by_step)
    return add_top(where, base, speed)


def solution(mesh):
    in_specs = (
        P("vol", "col"),
        P("vol", "col"),
        P("vol", "col"),
        P("vol", "col"),
        P("vol", None),
        P("col", "vol", None),
    )
    out_specs = (P("vol", None), P("col", "vol", None))
    return jax.shard_map(
        on_device, mesh=mesh, in_specs=in_specs, out_specs=out_specs, check_vma=False
    )
```

time: 250 us -> 160 us (0.64)
  the two profiles are of different devices: /device:TPU:8 before, /device:TPU:1 now
where the time goes in v2:
time: 160 us
  Pallas kernels  69.2 us (43%)
  starting transfers between devices  45.7 us (29%)
  waiting for transfers between devices  35.8 us (22%)
  local copies, waits for them, and re-layouts  5.99 us (4%)
  between operations  2.36 us (1%)
    pallas_call x1, Pallas kernels, base_sweeps(): pl.pallas_call(base_kernel, out_shape=f32(layers, rows, 8 * LANES), in_sp...  31.5 us
    pallas_call x1, Pallas kernels, surface_basis(): pl.pallas_call(basis_kernel, out_shape=(f32(ITERS, 8, Y_ROWS, LANES), f32...  19.3 us
    ppermute x3, waiting for transfers between devices, on_device(): lax.ppermute(keep, 'col', [(j, (j + 2 * k) % cols) for j in range(cols)])  16.4 us
    ppermute x1, waiting for transfers between devices, on_device(): corner_high = lax.ppermute(corners, 'col', col_down)  10.3 us
    all_to_all x1, starting transfers between devices, on_device(): gathered = lax.all_to_all(spread, 'vol', 0, 0)  9.3 us
    ppermute x1, starting transfers between devices, on_device(): cross = lax.ppermute(own, ('vol', 'col'), cross_pairs)  7.5 us
    pallas_call x1, Pallas kernels, face_sums(): pl.pallas_call(face_kernel, out_shape=(half, half), in_specs=[SMEM, SMEM,...  6.59 us
    ppermute x1, starting transfers between devices, on_device(): corner_low = lax.ppermute(corners, 'col', col_up)  6.14 us
  transfers between devices with their start and end apart: 14, of which 6 were waited for; matrix products, arithmetic and copies ran while one was open for 2% of the time, Pallas kernels for 18%

profile of v2, /device:TPU:1, one launch (start us, length us, event | category | flops | bytes accessed | tf_op | source)
XLA Modules:
  0.0 159.9 jit_solution(2234902822616677149)
XLA Ops:
  0.6 0.0 copy-start.4
  0.6 1.6 copy-done.4
  2.2 0.0 copy-start.6
  2.2 0.0 copy-start.7
  2.2 0.0 copy-start.8
  2.2 4.9 %regroup.1 = (f32[8,8,64,128]{3,2,1,0:T(8,128)}, f32[8,64,128]{2,1,0:T(8,128)S(1)}, f32[8,96,128]{2,1,0:T(8,128)S(1)}, f32[8,96,128]{2,1,0:T(8,128)S(1)}) custom-call(f32[8,64,1024]{2,1,0:T(8,128)S(1)} %copy-done.4, f32[64,1024]{1,0:T(8,128)} %metric_ref.1), custom_call_target="tpu_custom_call" | custom-call | bytes 12000000 | tf_op jit(solution)/shard_map/regroup/pallas_call | solution.py:129
  7.2 4.6 %collective-permute-start.6 = (f32[8,8,64,128]{3,2,1,0:T(8,128)}, f32[8,8,64,128]{3,2,1,0:T(8,128)}, u32[]{:S(2)}, u32[]{:S(2)}) collective-permute-start(f32[8,8,64,128]{3,2,1,0:T(8,128)} %get-tuple-element.107.block_ref), channel_id=1, source_target_pairs={{0,1},{1,2},{2,3},{3,4},{4,5},{5,6},{6,7},{8,9},{9,10},{10,11},{11... | collective-permute-start | bytes 6291464 | tf_op jit(solution)/shard_map/depth_halo/ppermute | solution.py:716
  11.7 1.9 %collective-permute-start.7 = (f32[8,8,64,128]{3,2,1,0:T(8,128)}, f32[8,8,64,128]{3,2,1,0:T(8,128)}, u32[]{:S(2)}, u32[]{:S(2)}) collective-permute-start(f32[8,8,64,128]{3,2,1,0:T(8,128)} %get-tuple-element.107.block_ref), channel_id=1, source_target_pairs={{1,0},{2,1},{3,2},{4,3},{5,4},{6,5},{7,6},{9,8},{10,9},{11,10},{12... | collective-permute-start | bytes 6291464 | tf_op jit(solution)/shard_map/depth_halo/ppermute | solution.py:717
  14.3 0.1 stack.24
  14.4 0.0 copy-done.6
  14.4 0.0 copy-done.7
  14.4 0.0 copy-done.8
  14.4 6.6 %face_sums.1 = (f32[8,32,128]{2,1,0:T(8,128)S(1)}, f32[8,32,128]{2,1,0:T(8,128)S(1)}) custom-call(s32[1,5]{1,0:T(1,128)S(1)} %bitcast.19, s32[1,1]{1,0:T(1,128)S(6)} %copy.41.count_ref, f32[1,16384]{1,0:T(1,128)S(1)} %copy-done.6, f32[1,16384]{1,0:T(1,128)S(1)} %copy-done.7, s32[1,16384]{1,0:T(1,128)S(1)} %copy-done.8), custom_call_target="tpu_custom_call" | custom-call | bytes 21000000 | tf_op jit(solution)/shard_map/face_sums/pallas_call | solution.py:188
  21.0 0.1 collective-permute-start.10
  21.1 1.3 collective-permute-done.10
  22.5 1.6 collective-permute-start.12
  24.1 1.5 collective-permute-start.13
  25.6 1.6 collective-permute-start.11
  27.1 12.0 %collective-permute-done.12 = f32[8,32,128]{2,1,0:T(8,128)S(1)} collective-permute-done((f32[8,32,128]{2,1,0:T(8,128)S(1)}, f32[8,32,128]{2,1,0:T(8,128)S(1)}, u32[]{:S(2)}, u32[]{:S(2)}) %collective-permute-start.12) | collective-permute-done | bytes 131104 | tf_op jit(solution)/shard_map/flux_sum/ppermute | solution.py:723
  39.1 0.0 collective-permute-done.13
  39.1 4.5 %collective-permute-done.11 = f32[8,32,128]{2,1,0:T(8,128)S(1)} collective-permute-done((f32[8,32,128]{2,1,0:T(8,128)S(1)}, f32[8,32,128]{2,1,0:T(8,128)S(1)}, u32[]{:S(2)}, u32[]{:S(2)}) %collective-permute-start.11) | collective-permute-done | bytes 131104 | tf_op jit(solution)/shard_map/flux_sum/ppermute | solution.py:723
  43.6 0.0 copy-start.9
  43.6 0.7 collective-permute-start.14
  44.3 3.1 %collective-permute-start.4 = (f32[8,96,128]{2,1,0:T(8,128)S(1)}, f32[8,96,128]{2,1,0:T(8,128)S(1)}, u32[]{:S(2)}, u32[]{:S(2)}) collective-permute-start(f32[8,96,128]{2,1,0:T(8,128)S(1)} %get-tuple-element.108), channel_id=1, source_target_pairs={{0,8},{8,16},{16,24},{24,32},{32,40},{40,48},{48,56},{56,64},{64,7... | collective-permute-start | bytes 1179656 | tf_op jit(solution)/shard_map/row_halo/ppermute | solution.py:713
  47.5 1.3 collective-permute-start.5
  48.8 0.0 collective-permute-done.14.other_ref
  48.8 0.0 copy-start.11
  48.8 4.0 %collective-permute-start.15 = (f32[8,32,128]{2,1,0:T(8,128)S(1)}, f32[8,32,128]{2,1,0:T(8,128)S(1)}, u32[]{:S(2)}, u32[]{:S(2)}) collective-permute-start(f32[8,32,128]{2,1,0:T(8,128)S(1)} %add_add_fusion.own_ref), channel_id=1, source_target_pairs={{1,9},{3,11},{5,13},{7,15},{8,0},{9,17},{10,2},{11,19},{12,4},{13,... | collective-permute-start | bytes 393224 | tf_op jit(solution)/shard_map/flux_halo/ppermute | solution.py:735
  52.8 5.0 %collective-permute-done.15.same_ref = f32[8,32,128]{2,1,0:T(8,128)S(1)} collective-permute-done((f32[8,32,128]{2,1,0:T(8,128)S(1)}, f32[8,32,128]{2,1,0:T(8,128)S(1)}, u32[]{:S(2)}, u32[]{:S(2)}) %collective-permute-start.15) | collective-permute-done | bytes 131104 | tf_op jit(solution)/shard_map/flux_halo/ppermute | solution.py:735
  57.8 7.5 %collective-permute-start.16 = (f32[8,32,128]{2,1,0:T(8,128)S(1)}, f32[8,32,128]{2,1,0:T(8,128)S(1)}, u32[]{:S(2)}, u32[]{:S(2)}) collective-permute-start(f32[8,32,128]{2,1,0:T(8,128)S(1)} %add_add_fusion.own_ref), channel_id=1, source_target_pairs={{1,8},{3,10},{5,12},{7,14},{8,1},{9,16},{10,3},{11,18},{12,5},{13,... | collective-permute-start | bytes 393224 | tf_op jit(solution)/shard_map/flux_halo/ppermute | solution.py:736
  65.3 2.6 %collective-permute-done.16.cross_ref = f32[8,32,128]{2,1,0:T(8,128)S(1)} collective-permute-done((f32[8,32,128]{2,1,0:T(8,128)S(1)}, f32[8,32,128]{2,1,0:T(8,128)S(1)}, u32[]{:S(2)}, u32[]{:S(2)}) %collective-permute-start.16) | collective-permute-done | bytes 131104 | tf_op jit(solution)/shard_map/flux_halo/ppermute | solution.py:736
  67.9 0.0 collective-permute-done.4.before_ref
  67.9 0.0 collective-permute-done.5.after_ref
  67.9 0.0 copy-start.2
  67.9 19.3 %surface_basis.1 = (f32[10,8,80,128]{3,2,1,0:T(8,128)S(1)}, f32[24,128]{1,0:T(8,128)S(1)}) custom-call(s32[1,5]{1,0:T(1,128)S(1)} %bitcast.20, f32[8,32,128]{2,1,0:T(8,128)S(1)} %add_add_fusion.own_ref, f32[8,32,128]{2,1,0:T(8,128)S(1)} %collective-permute-done.14.other_ref, f32[8,32,128]{2,1,0:T(8,128)S(1)} %collective-permute-done.15.same_ref, ...), custom_call_target="tpu_custom_call" | custom-call | bytes 21000000 | tf_op jit(solution)/shard_map/surface_basis/pallas_call | solution.py:261
  87.2 0.0 copy-done.2
  87.3 0.0 copy-start
  87.3 0.7 copy-done
  88.0 0.0 copy-done.9
  88.0 0.0 copy-done.11
  88.0 0.7 broadcast_in_dim.2
  88.7 9.3 %all-to-all-start = ((f32[16,24,128]{2,1,0:T(8,128)}), f32[16,24,128]{2,1,0:T(8,128)S(1)}, u32[]{:S(2)}, u32[]{:S(2)}) async-start(f32[16,24,128]{2,1,0:T(8,128)} %broadcast_in_dim.2), calls=%async_computation | async-start | bytes 393216 | tf_op jit(solution)/shard_map/gather_sums/all_to_all | solution.py:746
  98.0 1.0 slice_bitcast_fusion
  99.0 1.0 slice_bitcast_fusion.1
  100.0 0.8 pad_maximum_fusion.3
  100.8 6.1 %collective-permute-start.8 = (f32[2,8,64,128]{3,2,1,0:T(8,128)}, f32[2,8,64,128]{3,2,1,0:T(8,128)}, u32[]{:S(2)}, u32[]{:S(2)}) collective-permute-start(f32[2,8,64,128]{3,2,1,0:T(8,128)} %pad_maximum_fusion.3), channel_id=1, source_target_pairs={{0,1},{1,2},{2,3},{3,4},{4,5},{5,6},{6,7},{8,9},{9,10},{10,11},{11... | collective-permute-start | bytes 1572872 | tf_op jit(solution)/shard_map/corner_halo/ppermute | solution.py:740
  106.9 0.0 all-to-all-done.sums_ref
  107.0 0.0 copy-start.5
  107.0 0.9 copy-done.5
  107.9 2.6 %surface_solve.1 = (f32[8,80,128]{2,1,0:T(8,128)}, s32[1,1]{1,0:T(1,128)}) custom-call(f32[10,8,80,128]{3,2,1,0:T(8,128)S(1)} %get-tuple-element.113.basis_ref, f32[16,24,128]{2,1,0:T(8,128)S(1)} %all-to-all-done.sums_ref, f32[20,16,128]{2,1,0:T(8,128)S(1)} %copy-done.5), custom_call_target="tpu_custom_call" | custom-call | bytes 9000000 | tf_op jit(solution)/shard_map/surface_solve/pallas_call | solution.py:339
  111.1 0.0 copy-start.1
  111.1 0.0 copy-start.3
  111.1 0.0 copy-start.12
  111.1 2.4 %collective-permute-start.9 = (f32[2,8,64,128]{3,2,1,0:T(8,128)}, f32[2,8,64,128]{3,2,1,0:T(8,128)S(1)}, u32[]{:S(2)}, u32[]{:S(2)}) collective-permute-start(f32[2,8,64,128]{3,2,1,0:T(8,128)} %pad_maximum_fusion.3), channel_id=1, source_target_pairs={{1,0},{2,1},{3,2},{4,3},{5,4},{6,5},{7,6},{9,8},{10,9},{11,10},{12... | collective-permute-start | bytes 1572872 | tf_op jit(solution)/shard_map/corner_halo/ppermute | solution.py:741
  113.5 0.0 collective-permute-done.8.corner_low_ref
  113.5 10.3 %collective-permute-done.9.corner_high_ref = f32[2,8,64,128]{3,2,1,0:T(8,128)S(1)} collective-permute-done((f32[2,8,64,128]{3,2,1,0:T(8,128)}, f32[2,8,64,128]{3,2,1,0:T(8,128)S(1)}, u32[]{:S(2)}, u32[]{:S(2)}) %collective-permute-start.9) | collective-permute-done | bytes 524320 | tf_op jit(solution)/shard_map/corner_halo/ppermute | solution.py:741
  123.9 0.0 collective-permute-done.6.zlow_ref
  123.9 0.0 collective-permute-done.7.zhigh_ref
  123.9 0.0 copy-done.1
  123.9 0.0 copy-done.3
  123.9 31.5 %base_sweeps.1.base_ref = f32[8,64,1024]{2,1,0:T(8,128)} custom-call(s32[1,5]{1,0:T(1,128)S(1)} %bitcast.21, f32[8,8,64,128]{3,2,1,0:T(8,128)} %get-tuple-element.107.block_ref, f32[8,96,128]{2,1,0:T(8,128)S(1)} %copy-done.1, f32[8,96,128]{2,1,0:T(8,128)S(1)} %copy-done.3, f32[8,8,64,128]{3,2,1,0:T(8,128)} %collective-permute-done.6.zlow_ref, ...), custom_call_target="tpu_custom_call" | custom-call | bytes 75000000 | tf_op jit(solution)/shard_map/base_sweeps/pallas_call | solution.py:490
  155.5 0.0 copy-done.12
  155.5 4.2 %add_top.1 = (f32[64,1024]{1,0:T(8,128)}, f32[8,64,1024]{2,1,0:T(8,128)}) custom-call(s32[1,5]{1,0:T(1,128)S(1)} %bitcast.22, f32[8,64,1024]{2,1,0:T(8,128)} %base_sweeps.1.base_ref, f32[8,80,128]{2,1,0:T(8,128)S(1)} %copy-done.12), custom_call_target="tpu_custom_call", output_to_operand_aliasing={{1}: (1, {})} | custom-call | bytes 30000000 | tf_op jit(solution)/shard_map/add_top/pallas_call | solution.py:631
  (3 shorter events, 0.1 us)
Async XLA Ops:
  0.6 1.6 copy-start.4
  2.2 12.2 %copy-start.6 = (f32[1,16384]{1,0:T(1,128)S(1)}, f32[1,16384]{1,0:T(1,128)}, u32[]{:S(2)}) copy-start(f32[1,16384]{1,0:T(1,128)} %area_ref.1) | copy-start | bytes 196612
  2.2 12.2 %copy-start.7 = (f32[1,16384]{1,0:T(1,128)S(1)}, f32[1,16384]{1,0:T(1,128)}, u32[]{:S(2)}) copy-start(f32[1,16384]{1,0:T(1,128)} %speed_ref.1) | copy-start | bytes 196612
  2.2 12.2 %copy-start.8 = (s32[1,16384]{1,0:T(1,128)S(1)}, s32[1,16384]{1,0:T(1,128)}, u32[]{:S(2)}) copy-start(s32[1,16384]{1,0:T(1,128)} %node_ref.1) | copy-start | bytes 196612
  7.2 116.7 %collective-permute-start.6 = (f32[8,8,64,128]{3,2,1,0:T(8,128)}, f32[8,8,64,128]{3,2,1,0:T(8,128)}, u32[]{:S(2)}, u32[]{:S(2)}) collective-permute-start(f32[8,8,64,128]{3,2,1,0:T(8,128)} %get-tuple-element.107.block_ref), channel_id=1, source_target_pairs={{0,1},{1,2},{2,3},{3,4},{4,5},{5,6},{6,7},{8,9},{9,10},{10,11},{11... | collective-permute-start | bytes 6291464 | tf_op jit(solution)/shard_map/depth_halo/ppermute | solution.py:716
  11.7 112.2 %collective-permute-start.7 = (f32[8,8,64,128]{3,2,1,0:T(8,128)}, f32[8,8,64,128]{3,2,1,0:T(8,128)}, u32[]{:S(2)}, u32[]{:S(2)}) collective-permute-start(f32[8,8,64,128]{3,2,1,0:T(8,128)} %get-tuple-element.107.block_ref), channel_id=1, source_target_pairs={{1,0},{2,1},{3,2},{4,3},{5,4},{6,5},{7,6},{9,8},{10,9},{11,10},{12... | collective-permute-start | bytes 6291464 | tf_op jit(solution)/shard_map/depth_halo/ppermute | solution.py:717
  21.0 1.4 collective-permute-start.10
  22.5 16.7 %collective-permute-start.12 = (f32[8,32,128]{2,1,0:T(8,128)S(1)}, f32[8,32,128]{2,1,0:T(8,128)S(1)}, u32[]{:S(2)}, u32[]{:S(2)}) collective-permute-start(f32[8,32,128]{2,1,0:T(8,128)S(1)} %add.135), channel_id=1, source_target_pairs={{0,2},{1,3},{2,4},{3,5},{4,6},{5,7},{6,0},{7,1},{8,10},{9,11},{10,... | collective-permute-start | bytes 393224 | tf_op jit(solution)/shard_map/flux_sum/ppermute | solution.py:723
  24.1 15.1 %collective-permute-start.13 = (f32[8,32,128]{2,1,0:T(8,128)S(1)}, f32[8,32,128]{2,1,0:T(8,128)S(1)}, u32[]{:S(2)}, u32[]{:S(2)}) collective-permute-start(f32[8,32,128]{2,1,0:T(8,128)S(1)} %add.135), channel_id=1, source_target_pairs={{0,6},{1,7},{2,0},{3,1},{4,2},{5,3},{6,4},{7,5},{8,14},{9,15},{10,... | collective-permute-start | bytes 393224 | tf_op jit(solution)/shard_map/flux_sum/ppermute | solution.py:723
  25.6 18.0 %collective-permute-start.11 = (f32[8,32,128]{2,1,0:T(8,128)S(1)}, f32[8,32,128]{2,1,0:T(8,128)S(1)}, u32[]{:S(2)}, u32[]{:S(2)}) collective-permute-start(f32[8,32,128]{2,1,0:T(8,128)S(1)} %add.135), channel_id=1, source_target_pairs={{0,4},{1,5},{2,6},{3,7},{4,0},{5,1},{6,2},{7,3},{8,12},{9,13},{10,... | collective-permute-start | bytes 393224 | tf_op jit(solution)/shard_map/flux_sum/ppermute | solution.py:723
  43.6 44.4 %copy-start.9 = (f32[8,32,128]{2,1,0:T(8,128)}, f32[8,32,128]{2,1,0:T(8,128)S(1)}, u32[]{:S(2)}) copy-start(f32[8,32,128]{2,1,0:T(8,128)S(1)} %add_add_fusion.own_ref) | copy-start | bytes 393220
  43.6 5.1 %collective-permute-start.14 = (f32[8,32,128]{2,1,0:T(8,128)S(1)}, f32[8,32,128]{2,1,0:T(8,128)S(1)}, u32[]{:S(2)}, u32[]{:S(2)}) collective-permute-start(f32[8,32,128]{2,1,0:T(8,128)S(1)} %add_add_fusion.own_ref), channel_id=1, source_target_pairs={{0,1},{1,0},{2,3},{3,2},{4,5},{5,4},{6,7},{7,6},{8,9},{9,8},{10,11... | collective-permute-start | bytes 393224 | tf_op jit(solution)/shard_map/flux_halo/ppermute | solution.py:727
  44.3 23.6 %collective-permute-start.4 = (f32[8,96,128]{2,1,0:T(8,128)S(1)}, f32[8,96,128]{2,1,0:T(8,128)S(1)}, u32[]{:S(2)}, u32[]{:S(2)}) collective-permute-start(f32[8,96,128]{2,1,0:T(8,128)S(1)} %get-tuple-element.108), channel_id=1, source_target_pairs={{0,8},{8,16},{16,24},{24,32},{32,40},{40,48},{48,56},{56,64},{64,7... | collective-permute-start | bytes 1179656 | tf_op jit(solution)/shard_map/row_halo/ppermute | solution.py:713
  47.5 20.4 %collective-permute-start.5 = (f32[8,96,128]{2,1,0:T(8,128)S(1)}, f32[8,96,128]{2,1,0:T(8,128)S(1)}, u32[]{:S(2)}, u32[]{:S(2)}) collective-permute-start(f32[8,96,128]{2,1,0:T(8,128)S(1)} %get-tuple-element.109), channel_id=1, source_target_pairs={{8,0},{16,8},{24,16},{32,24},{40,32},{48,40},{56,48},{64,56},{72,6... | collective-permute-start | bytes 1179656 | tf_op jit(solution)/shard_map/row_halo/ppermute | solution.py:714
  48.8 39.2 %copy-start.11 = (f32[8,32,128]{2,1,0:T(8,128)}, f32[8,32,128]{2,1,0:T(8,128)S(1)}, u32[]{:S(2)}) copy-start(f32[8,32,128]{2,1,0:T(8,128)S(1)} %collective-permute-done.14.other_ref) | copy-start | bytes 393220
  48.8 9.0 %collective-permute-start.15 = (f32[8,32,128]{2,1,0:T(8,128)S(1)}, f32[8,32,128]{2,1,0:T(8,128)S(1)}, u32[]{:S(2)}, u32[]{:S(2)}) collective-permute-start(f32[8,32,128]{2,1,0:T(8,128)S(1)} %add_add_fusion.own_ref), channel_id=1, source_target_pairs={{1,9},{3,11},{5,13},{7,15},{8,0},{9,17},{10,2},{11,19},{12,4},{13,... | collective-permute-start | bytes 393224 | tf_op jit(solution)/shard_map/flux_halo/ppermute | solution.py:735
  57.8 10.1 %collective-permute-start.16 = (f32[8,32,128]{2,1,0:T(8,128)S(1)}, f32[8,32,128]{2,1,0:T(8,128)S(1)}, u32[]{:S(2)}, u32[]{:S(2)}) collective-permute-start(f32[8,32,128]{2,1,0:T(8,128)S(1)} %add_add_fusion.own_ref), channel_id=1, source_target_pairs={{1,8},{3,10},{5,12},{7,14},{8,1},{9,16},{10,3},{11,18},{12,5},{13,... | collective-permute-start | bytes 393224 | tf_op jit(solution)/shard_map/flux_halo/ppermute | solution.py:736
  67.9 19.3 %copy-start.2 = (f32[8,96,128]{2,1,0:T(8,128)}, f32[8,96,128]{2,1,0:T(8,128)S(1)}, u32[]{:S(2)}) copy-start(f32[8,96,128]{2,1,0:T(8,128)S(1)} %collective-permute-done.5.after_ref) | copy-start | bytes 1179652
  87.3 0.7 copy-start
  88.7 18.2 %all-to-all-start = ((f32[16,24,128]{2,1,0:T(8,128)}), f32[16,24,128]{2,1,0:T(8,128)S(1)}, u32[]{:S(2)}, u32[]{:S(2)}) async-start(f32[16,24,128]{2,1,0:T(8,128)} %broadcast_in_dim.2), calls=%async_computation | async-start | bytes 393216 | tf_op jit(solution)/shard_map/gather_sums/all_to_all | solution.py:746
  100.8 12.7 %collective-permute-start.8 = (f32[2,8,64,128]{3,2,1,0:T(8,128)}, f32[2,8,64,128]{3,2,1,0:T(8,128)}, u32[]{:S(2)}, u32[]{:S(2)}) collective-permute-start(f32[2,8,64,128]{3,2,1,0:T(8,128)} %pad_maximum_fusion.3), channel_id=1, source_target_pairs={{0,1},{1,2},{2,3},{3,4},{4,5},{5,6},{6,7},{8,9},{9,10},{10,11},{11... | collective-permute-start | bytes 1572872 | tf_op jit(solution)/shard_map/corner_halo/ppermute | solution.py:740
  107.0 0.9 copy-start.5
  111.1 12.8 %copy-start.1 = (f32[8,96,128]{2,1,0:T(8,128)S(1)}, f32[8,96,128]{2,1,0:T(8,128)}, u32[]{:S(2)}) copy-start(f32[8,96,128]{2,1,0:T(8,128)} %copy-done) | copy-start | bytes 1179652
  111.1 12.8 %copy-start.3 = (f32[8,96,128]{2,1,0:T(8,128)S(1)}, f32[8,96,128]{2,1,0:T(8,128)}, u32[]{:S(2)}) copy-start(f32[8,96,128]{2,1,0:T(8,128)} %copy-done.2) | copy-start | bytes 1179652
  111.1 44.3 %copy-start.12 = (f32[8,80,128]{2,1,0:T(8,128)S(1)}, f32[8,80,128]{2,1,0:T(8,128)}, u32[]{:S(2)}) copy-start(f32[8,80,128]{2,1,0:T(8,128)} %get-tuple-element.152.speed_ref) | copy-start | bytes 983044
  111.1 12.7 %collective-permute-start.9 = (f32[2,8,64,128]{3,2,1,0:T(8,128)}, f32[2,8,64,128]{3,2,1,0:T(8,128)S(1)}, u32[]{:S(2)}, u32[]{:S(2)}) collective-permute-start(f32[2,8,64,128]{3,2,1,0:T(8,128)} %pad_maximum_fusion.3), channel_id=1, source_target_pairs={{1,0},{2,1},{3,2},{4,3},{5,4},{6,5},{7,6},{9,8},{10,9},{11,10},{12... | collective-permute-start | bytes 1572872 | tf_op jit(solution)/shard_map/corner_halo/ppermute | solution.py:741

commit v3 on v2

v3 whole, which is shorter than its diff:
```python
import jax
import jax.numpy as jnp
import numpy as np
from jax import lax
from jax.experimental import pallas as pl
from jax.experimental.pallas import tpu as pltpu
from jax.sharding import PartitionSpec as P

ITERS = 10
SWEEPS = 4
LANES = 128
SUB = 8
MIB = 1024 * 1024
DEEP = 2 * SWEEPS
HALO = 32
ROWS = 128
GROUPS = 16
Y_GROUPS = 10
Y_ROWS = 80

BASIS_LOW = 0.1
BASIS_HIGH = 12.0
CONDITION_MAX = 2000.0


def rolled(x, shift, axis):
    return pltpu.roll(x, shift % x.shape[axis], axis)


def column_ring(tiles):
    n = len(tiles)
    lane = lax.broadcasted_iota(jnp.int32, tiles[0].shape, 1)
    first, last = lane == 0, lane == LANES - 1
    return (
        [jnp.where(first, 0.0, rolled(tiles[j], 1, 1)) for j in (n - 2, n - 1)]
        + list(tiles)
        + [jnp.where(last, 0.0, rolled(tiles[j], -1, 1)) for j in (0, 1)]
    )


def row_ring(rows):
    n = len(rows)
    return (
        [rolled(rows[j], 1, 0) for j in (n - 2, n - 1)]
        + list(rows)
        + [rolled(rows[j], -1, 0) for j in (0, 1)]
    )


def mass_line(padded, index):
    i = index + 2
    near = padded[i - 1] + padded[i + 1]
    if index % 2:
        return near + 8.0 * padded[i]
    return (near + 4.0 * padded[i]) - 0.5 * (padded[i - 2] + padded[i + 2])


def both_line(padded, index):
    i = index + 2
    near = padded[i - 1] + padded[i + 1]
    return (16.0 / 3.0 if index % 2 else 11.0 / 3.0) * padded[i] - near


SMEM = pl.BlockSpec(memory_space=pltpu.SMEM)
VMEM = pl.BlockSpec(memory_space=pltpu.VMEM)
HBM = pl.BlockSpec(memory_space=pl.ANY)


def f32(*shape):
    return jax.ShapeDtypeStruct(shape, jnp.float32)


def params(mib):
    return pltpu.CompilerParams(vmem_limit_bytes=mib * MIB)


def cost(us):
    return pl.CostEstimate(flops=0, bytes_accessed=int(us * 3_000_000), transcendentals=0)


def split(x):
    first = x.astype(jnp.bfloat16)
    return first, (x - first.astype(jnp.float32)).astype(jnp.bfloat16)


def to_blocked(j):
    x = lax.broadcasted_iota(jnp.int32, (1024, 256), 0)
    n = lax.broadcasted_iota(jnp.int32, (1024, 256), 1)
    hit = x == 8 * (n & 127) + j + (n >> 7)
    return jnp.where(hit, 1.0, 0.0).astype(jnp.bfloat16)


def plain_selection():
    k = np.arange(1024)
    out = np.zeros((1024, 1024), np.float32)
    out[k, 8 * (k % LANES) + k // LANES] = 1.0
    return jnp.asarray(out, jnp.bfloat16)


def regroup_kernel(block_ref, metric_ref, before_ref, after_ref, wide_ref, root_ref, parts_ref):
    layers, rows, _ = block_ref.shape
    packed = DEEP * layers
    total = layers * Y_ROWS + ROWS

    def put(at, value):
        first, second = split(value)
        parts_ref[at : at + value.shape[0], :] = first
        parts_ref[total + at : total + at + value.shape[0], :] = second

    for z in range(layers):
        put(Y_ROWS * z, before_ref[DEEP * z : DEEP * (z + 1), :])
        put(Y_ROWS * z + DEEP, block_ref[z])
        put(Y_ROWS * z + DEEP + rows, after_ref[DEEP * z : DEEP * (z + 1), :])
    at = layers * Y_ROWS
    put(at, jnp.sqrt(before_ref[packed:, :]))
    put(at + HALO, jnp.sqrt(metric_ref[...]))
    put(at + HALO + rows, jnp.sqrt(after_ref[packed:, :]))
    for j in range(0, 8, 2):
        pair = jnp.dot(parts_ref[...], to_blocked(j), preferred_element_type=jnp.float32)
        pair = pair[:total] + pair[total:]
        for i in range(2):
            tile = pair[:, LANES * i : LANES * (i + 1)]
            for z in range(layers):
                wide_ref[z, j + i] = tile[Y_ROWS * z : Y_ROWS * (z + 1)]
            root_ref[j + i] = tile[layers * Y_ROWS :]


def regroup(block, metric, before, after):
    layers, rows, cols = block.shape
    return pl.pallas_call(
        regroup_kernel,
        out_shape=(f32(layers, 8, Y_ROWS, LANES), f32(8, ROWS, LANES)),
        in_specs=[VMEM] * 4,
        out_specs=(VMEM, VMEM),
        scratch_shapes=[pltpu.VMEM((2 * (Y_ROWS * layers + ROWS), cols), jnp.bfloat16)],
        compiler_params=params(40),
        cost_estimate=cost(6),
        name="regroup",
    )(block, metric, before, after)


def plain_columns(select_ref, parts, rows, write):
    for q in range(4):
        at = slice(256 * q, 256 * (q + 1))
        value = jnp.dot(parts, select_ref[:, at], preferred_element_type=jnp.float32)
        write(at, value[:rows] + value[rows:])


def face_kernel(
    where_ref, count_ref, area_ref, speed_ref, node_ref, block_ref, metric_ref,
    keep_ref, send_ref, up_ref, down_ref, acc_ref, sems,
):
    slots = area_ref.shape[1]
    layers, rows, _ = block_ref.shape
    copies = []
    for out_ref, row, root_row in ((up_ref, rows - DEEP, rows - HALO), (down_ref, 0, 0)):
        for z in range(layers):
            part = block_ref.at[z, pl.ds(row, DEEP), :]
            copies.append((part, out_ref.at[pl.ds(DEEP * z, DEEP), :]))
        part = metric_ref.at[pl.ds(root_row, HALO), :]
        copies.append((part, out_ref.at[pl.ds(DEEP * layers, HALO), :]))
    copies = [pltpu.make_async_copy(*pair, sems.at[i]) for i, pair in enumerate(copies)]
    for copy in copies:
        copy.start()
    chunk = min(2048, slots)
    core = where_ref[0, 0]
    ids = lax.broadcasted_iota(jnp.int32, (256, chunk), 0)
    ids = ids.astype(jnp.float32).astype(jnp.bfloat16)
    zero = jnp.zeros((), jnp.bfloat16)
    one = jnp.ones((), jnp.bfloat16)
    contract = (((1,), (1,)), ((), ()))
    acc_ref[...] = jnp.zeros_like(acc_ref)

    def wide(x):
        return jnp.broadcast_to(x.astype(jnp.bfloat16), (256, chunk))

    def body(step, carry):
        at = pl.ds(pl.multiple_of(step * chunk, chunk), chunk)
        slot = lax.broadcasted_iota(jnp.int32, (1, chunk), 1) + step * chunk
        value = jnp.where(slot < count_ref[0, 0], area_ref[:, at] * speed_ref[:, at], 0.0)
        node = node_ref[:, at]
        low = (((node & 1) << 7) + ((node >> 3) & 127)).astype(jnp.float32)
        high = (((node >> 1) & 3) * 64 + (node >> 10)).astype(jnp.float32)
        first = value.astype(jnp.bfloat16)
        second = value - first.astype(jnp.float32)
        here = wide(high) == ids
        upper = jnp.where(here, wide(first), zero)
        lower = jnp.where(here, wide(second), zero)
        columns = jnp.where(wide(low) == ids, one, zero)
        acc_ref[...] += lax.dot_general(
            upper, columns, contract, preferred_element_type=jnp.float32
        ) + lax.dot_general(lower, columns, contract, preferred_element_type=jnp.float32)
        return carry

    lax.fori_loop(0, slots // chunk, body, 0)
    for j in range(8):
        at, lanes = 64 * (j // 2), slice(LANES * (j % 2), LANES * (j % 2 + 1))
        keep_ref[j] = acc_ref[pl.ds(at + 32 * core, 32), lanes]
        send_ref[j] = acc_ref[pl.ds(at + 32 - 32 * core, 32), lanes]
    for copy in copies:
        copy.wait()


def face_sums(where, count, area, speed, node, block, metric):
    half = f32(8, 32, LANES)
    layers, _, cols = block.shape
    rows = f32(DEEP * layers + HALO, cols)
    return pl.pallas_call(
        face_kernel,
        out_shape=(half, half, rows, rows),
        in_specs=[SMEM, SMEM, VMEM, VMEM, VMEM, HBM, HBM],
        out_specs=(VMEM, VMEM, HBM, HBM),
        scratch_shapes=[
            pltpu.VMEM((256, 256), jnp.float32),
            pltpu.SemaphoreType.DMA((2 * layers + 2,)),
        ],
        compiler_params=params(32),
        cost_estimate=cost(7),
        name="face_sums",
    )(where, count, area, speed, node, block, metric)


def basis_kernel(
    where_ref, own_ref, other_ref, same_ref, cross_ref, root_ref,
    basis_ref, sums_ref, rows, field, root, outer, line, partial, sems,
):
    core = where_ref[0, 0]
    centre = (BASIS_LOW + BASIS_HIGH) / 2
    scale = 2 / (BASIS_HIGH - BASIS_LOW)
    for t in range(8):
        rows[t, pl.ds(32 + 32 * core, 32), :] = own_ref[t]
        rows[t, pl.ds(64 - 32 * core, 32), :] = other_ref[t]
        rows[t, pl.ds(96 * core, 32), :] = cross_ref[t]
        rows[t, pl.ds(96 - 96 * core, 32), :] = same_ref[t]
    for t in range(8):
        for ys in range(GROUPS):
            field[0, t, ys] = rows[t, pl.ds(ys, SUB, stride=GROUPS), :]
            value = root_ref[t, pl.ds(ys, SUB, stride=GROUPS), :]
            root[t, ys] = value
            outer[t, ys] = value * (2 * scale * 4.0 / 225.0)

    group = lax.broadcasted_iota(jnp.int32, (SUB, LANES), 0)
    own_rows = jnp.where((group >= 2) & (group < 6), 1.0, 0.0).astype(jnp.float32)

    def out_copy(k):
        return pltpu.make_async_copy(field.at[k], basis_ref.at[k], sems.at[k])

    def step(k, begin):
        out_copy(k).start()
        for ys in range(GROUPS):
            padded = column_ring([field[k, t, ys] * root[t, ys] for t in range(8)])
            for t in range(8):
                line[ys, t] = mass_line(padded, t)
        squares, shifts = [], []
        for t in range(8):
            square = jnp.zeros((SUB, LANES), jnp.float32)
            shifted = jnp.zeros((SUB, LANES), jnp.float32)
            padded = row_ring([line[ys, t] for ys in range(GROUPS)])
            for ys in range(GROUPS):
                now = field[k, t, ys]
                later = outer[t, ys] * mass_line(padded, ys) - (2 * centre * scale) * now
                later = 0.5 * later if begin else later - field[k - 1, t, ys]
                field[k + 1, t, ys] = later
                square = square + now * now
                shifted = shifted + later * now
            squares.append(square)
            shifts.append(shifted)

        def add(parts):
            while len(parts) > 1:
                parts = [parts[i] + parts[i + 1] for i in range(0, len(parts), 2)]
            return jnp.sum(parts[0] * own_rows, axis=0, keepdims=True)

        partial[pl.ds(2 * k, 1), :] = add(squares)
        partial[pl.ds(2 * k + 1, 1), :] = add(shifts)

    def later_step(k, carry):
        step(k, False)
        return carry

    partial[...] = jnp.zeros_like(partial)
    step(0, True)
    lax.fori_loop(1, ITERS, later_step, 0)
    whole = jnp.sum(partial[...], axis=1, keepdims=True)
    row = lax.broadcasted_iota(jnp.int32, partial.shape, 0)
    lane = lax.broadcasted_iota(jnp.int32, partial.shape, 1)
    line_of = jnp.sum(jnp.where(row == lane, whole, 0.0), axis=0, keepdims=True)
    sums_ref[...] = jnp.broadcast_to(line_of, sums_ref.shape)
    for k in range(ITERS):
        out_copy(k).wait()


def surface_basis(where, own, other, same, cross, root):
    return pl.pallas_call(
        basis_kernel,
        out_shape=(f32(ITERS, 8, GROUPS, SUB, LANES), f32(SUB, LANES)),
        in_specs=[SMEM] + [VMEM] * 5,
        out_specs=(HBM, VMEM),
        scratch_shapes=[
            pltpu.VMEM((8, ROWS, LANES), jnp.float32),
            pltpu.VMEM((ITERS + 1, 8, GROUPS, SUB, LANES), jnp.float32),
            pltpu.VMEM((8, GROUPS, SUB, LANES), jnp.float32),
            pltpu.VMEM((8, GROUPS, SUB, LANES), jnp.float32),
            pltpu.VMEM((GROUPS, 8, SUB, LANES), jnp.float32),
            pltpu.VMEM((24, LANES), jnp.float32),
            pltpu.SemaphoreType.DMA((ITERS,)),
        ],
        compiler_params=params(40),
        cost_estimate=cost(7),
        name="surface_basis",
    )(where, own, other, same, cross, root)


def solve_weights():
    n = ITERS
    moment = np.zeros((2 * n, 2 * n))
    for m in range(2 * n):
        if m < 2:
            moment[m, m] = 1.0
        else:
            moment[m, m] = 2.0
            moment[m, m % 2] = -1.0
    centre, half = (BASIS_LOW + BASIS_HIGH) / 2, (BASIS_HIGH - BASIS_LOW) / 2
    weights = np.zeros((2 * n, 16, LANES))
    for i in range(n):
        for j in range(n):
            lower = abs(j - 1)
            for factor, index in (
                (centre / 2, i + j),
                (centre / 2, abs(i - j)),
                (half / 4, i + j + 1),
                (half / 4, abs(i - j - 1)),
                (half / 4, i + lower),
                (half / 4, abs(i - lower)),
            ):
                weights[:, i, j] += factor * moment[index]
        weights[:, i, n] += moment[i]
    return weights.astype(np.float32)


def solve_kernel(basis_ref, sums_ref, weights_ref, out_ref, flag_ref, part_ref, rows, sem):
    n = ITERS
    copy = pltpu.make_async_copy(basis_ref, part_ref, sem)
    copy.start()
    total = sums_ref[0]
    for i in range(1, sums_ref.shape[0]):
        total = total + sums_ref[i]
    row = lax.broadcasted_iota(jnp.int32, (16, LANES), 0)
    lane = lax.broadcasted_iota(jnp.int32, (16, LANES), 1)
    system = jnp.where((lane == row + 16) & (row < n), 1.0, 0.0).astype(jnp.float32)
    for m in range(2 * n):
        system = system + weights_ref[m] * total[0:1, m : m + 1]
    centre = jnp.sum(jnp.where(lane == row, system, 0.0), axis=1, keepdims=True)
    for k in range(n):
        pivot_row = system[k : k + 1, :] / system[k : k + 1, k : k + 1]
        column = system[:, k : k + 1]
        system = jnp.where(row == k, pivot_row, system - column * pivot_row)
    inverse = jnp.sum(jnp.where(lane == row + 16, system, 0.0), axis=1, keepdims=True)
    figure = jnp.broadcast_to(centre * inverse, (16, LANES))
    inside = (row < n) & (lane == 0)
    least = jnp.min(jnp.where(inside, figure, 1.0))
    whole = jnp.sum(jnp.where(inside, figure, 0.0))
    flag_ref[0, 0] = jnp.where((least > 0.5) & (whole < CONDITION_MAX), 1, 0).astype(jnp.int32)
    copy.wait()
    weights = [jnp.broadcast_to(system[k : k + 1, n : n + 1], (SUB, LANES)) for k in range(n)]
    for t in range(8):
        for ys in range(GROUPS):
            value = weights[0] * part_ref[0, t, ys]
            for k in range(1, n):
                value = value + weights[k] * part_ref[k, t, ys]
            rows[t, pl.ds(ys, SUB, stride=GROUPS), :] = value
        out_ref[t] = rows[t, HALO - DEEP : HALO - DEEP + Y_ROWS, :]


def surface_solve(basis, sums):
    return pl.pallas_call(
        solve_kernel,
        out_shape=(f32(8, Y_ROWS, LANES), jax.ShapeDtypeStruct((1, 1), jnp.int32)),
        in_specs=[HBM, VMEM, VMEM],
        out_specs=(VMEM, SMEM),
        scratch_shapes=[
            pltpu.VMEM(basis.shape, jnp.float32),
            pltpu.VMEM((8, ROWS, LANES), jnp.float32),
            pltpu.SemaphoreType.DMA,
        ],
        compiler_params=params(32),
        cost_estimate=cost(3),
        name="surface_solve",
    )(basis, sums, jnp.asarray(solve_weights()))


def fill_factors(factor, where_ref, rows):
    vol, vols = where_ref[0, 3], where_ref[0, 4]
    group = lax.broadcasted_iota(jnp.int32, (SUB, LANES), 0)
    mass, stiff = (8.0, 16.0), (14.0, 16.0)
    for ys in range(Y_GROUPS):
        row = group * Y_GROUPS + ys
        outside = ((vol == 0) & (row < DEEP)) | ((vol == vols - 1) & (row >= DEEP + rows))
        py = ys % 2
        for pz in range(2):
            for px in range(2):
                value = -12.0 / (
                    stiff[pz] * mass[py] * mass[px]
                    + mass[pz] * (stiff[py] * mass[px] + mass[py] * stiff[px])
                )
                factor[pz, px, ys] = jnp.where(outside, 0.0, jnp.float32(value))


def lateral_lines(get, line_a, line_b, put):
    for ys in range(Y_GROUPS):
        padded = column_ring([get(t, ys) for t in range(8)])
        for t in range(8):
            m = mass_line(padded, t)
            line_a[t, ys] = m
            line_b[t, ys] = both_line(padded, t) - m
    for t in range(8):
        a = row_ring([line_a[t, ys] for ys in range(Y_GROUPS)])
        b = row_ring([line_b[t, ys] for ys in range(Y_GROUPS)])
        for ys in range(Y_GROUPS):
            put(t, ys, mass_line(a, ys), both_line(a, ys) + mass_line(b, ys))


def pair_steps(w, c):
    near = c[1] + c[3]
    even = (11.0 / 3.0 * w[1] - (w[0] + w[2])) + ((near + 4.0 * c[2]) - 0.5 * (c[0] + c[4]))
    near = c[2] + c[4]
    odd = (16.0 / 3.0 * w[2] - (w[1] + w[3])) + (near + 8.0 * c[3])
    return even, odd


def strided(ys):
    return pl.ds(ys, SUB, stride=Y_GROUPS)


def change_kernel(
    where_ref, speed_ref, out_ref, cells, along, cross, line_a, line_b, factor, plain, sem,
):
    col = where_ref[0, 1]
    layers, _, rows, _ = out_ref.shape

    def lateral(z, carry):
        def put(t, ys, w, c):
            along[z, t, ys] = w
            cross[z, t, ys] = c

        lateral_lines(lambda t, ys: cells[z, t, ys], line_a, line_b, put)
        return carry

    def set_top():
        for t in range(8):
            for ys in range(Y_GROUPS):
                cells[2, t, ys] = 0.5 * speed_ref[t, strided(ys), :]

    def send(count):
        for z in range(count):
            for t in range(8):
                for ys in range(Y_GROUPS):
                    plain[z, t, strided(ys), :] = cells[z + 2, t, ys]
        copy = pltpu.make_async_copy(
            plain.at[pl.ds(0, count), :, pl.ds(DEEP, rows), :], out_ref.at[pl.ds(0, count)], sem
        )
        copy.start()
        copy.wait()

    @pl.when(col == 0)
    def _():
        fill_factors(factor, where_ref, rows)
        set_top()
        clear = jnp.zeros((8, Y_GROUPS, SUB, LANES), jnp.float32)
        for z in range(layers + 3):
            if z != 2:
                cross[z] = clear
                if z:
                    along[z] = clear
        for z in range(3, layers + 2):
            cells[z] = clear

        def update(pair, carry):
            z = 2 * pair + 2
            for ys in range(Y_GROUPS):
                factors = [[factor[pz, px, ys] for px in range(2)] for pz in range(2)]
                for t in range(8):
                    even, odd = pair_steps(
                        [along[z + i, t, ys] for i in range(-1, 3)],
                        [cross[z + i, t, ys] for i in range(-2, 3)],
                    )
                    cells[z, t, ys] += factors[0][t % 2] * even
                    cells[z + 1, t, ys] += factors[1][t % 2] * odd
            return carry

        def one_sweep(sweep, carry):
            lax.fori_loop(2, 2 * sweep + 3, lateral, 0)
            lax.fori_loop(0, jnp.minimum(sweep + 2, layers // 2), update, 0)
            set_top()
            return carry

        lax.fori_loop(0, SWEEPS, one_sweep, 0)
        send(layers)

    @pl.when(col == 1)
    def _():
        fill_factors(factor, where_ref, rows)
        set_top()

        def one_sweep(sweep, carry):
            lateral(2, 0)
            for t in range(8):
                for ys in range(Y_GROUPS):
                    cells[2, t, ys] = factor[0, t % 2, ys] * (-0.5 * cross[2, t, ys])
            return carry

        lax.fori_loop(0, SWEEPS, one_sweep, 0)
        send(1)


def surface_change(where, speed, layers, rows):
    work = pltpu.VMEM((layers + 4, 8, Y_GROUPS, SUB, LANES), jnp.float32)
    line = pltpu.VMEM((8, Y_GROUPS, SUB, LANES), jnp.float32)
    return pl.pallas_call(
        change_kernel,
        out_shape=f32(layers, 8, rows, LANES),
        in_specs=[SMEM, VMEM],
        out_specs=HBM,
        scratch_shapes=[
            pltpu.VMEM((layers + 2, 8, Y_GROUPS, SUB, LANES), jnp.float32),
            work, work, line, line,
            pltpu.VMEM((2, 2, Y_GROUPS, SUB, LANES), jnp.float32),
            pltpu.VMEM((layers, 8, Y_ROWS, LANES), jnp.float32),
            pltpu.SemaphoreType.DMA,
        ],
        compiler_params=params(40),
        cost_estimate=cost(8),
        name="surface_change",
    )(where, speed)


def base_kernel(
    where_ref, wide_ref, zlow_ref, zhigh_ref, change_ref, speed_ref, select_ref,
    velocity_ref, out_ref, field, along, cross, line_a, line_b, factor, change, parts, sems,
):
    col, cols = where_ref[0, 1], where_ref[0, 2]
    layers, _, rows, _ = change_ref.shape
    total = layers + 2 * DEEP
    own = pltpu.make_async_copy(wide_ref, field.at[pl.ds(DEEP, layers)], sems.at[0])
    low = pltpu.make_async_copy(zlow_ref, field.at[pl.ds(0, DEEP)], sems.at[1])
    high = pltpu.make_async_copy(zhigh_ref, field.at[pl.ds(DEEP + layers, DEEP)], sems.at[2])
    all_change = pltpu.make_async_copy(change_ref, change, sems.at[3])
    one_change = pltpu.make_async_copy(
        change_ref.at[pl.ds(0, 1)], change.at[pl.ds(0, 1)], sems.at[4]
    )
    own.start()
    low.start()
    high.start()
    pl.when(col == 0)(all_change.start)
    pl.when(col == 1)(one_change.start)
    fill_factors(factor, where_ref, rows)
    count = (layers + 1) * rows

    def cut(value, at, t):
        first, second = split(value)
        lanes = slice(LANES * t, LANES * (t + 1))
        parts[at : at + rows, lanes] = first
        parts[count + at : count + at + rows, lanes] = second

    for t in range(8):
        cut(speed_ref[t, DEEP : DEEP + rows, :], 0, t)

    def lateral(z, carry):
        def put(t, ys, w, c):
            along[z, t, ys] = w
            cross[z, t, ys] = c

        lateral_lines(lambda t, ys: field[z, t, strided(ys), :], line_a, line_b, put)
        return carry

    def update(pair, carry):
        z = 2 * pair
        for ys in range(Y_GROUPS):
            factors = [[factor[pz, px, ys] for px in range(2)] for pz in range(2)]
            for t in range(8):
                even, odd = pair_steps(
                    [along[z + i, t, ys] for i in range(-1, 3)], [cross[z + i, t, ys] for i in range(-2, 3)]
                )
                scale = jnp.where((col == 0) & (z == DEEP), 0.0, factors[0][t % 2])
                even = field[z, t, strided(ys), :] + scale * even
                odd = field[z + 1, t, strided(ys), :] + factors[1][t % 2] * odd
                field[z, t, strided(ys), :] = even
                field[z + 1, t, strided(ys), :] = odd
        return carry

    begin = jnp.where(col == 0, DEEP, 0)
    end = jnp.where(col == cols - 1, DEEP + layers + 1, total - 1)

    def one_sweep(sweep, carry):
        first = jnp.maximum(begin, 2 * sweep)
        last = jnp.minimum(end, total - 2 * sweep - 1)

        @pl.when(sweep == 0)
        def _():
            own.wait()

        lax.fori_loop(jnp.where(sweep == 0, DEEP, first), jnp.where(sweep == 0, DEEP + layers, last), lateral, 0)

        @pl.when(sweep == 0)
        def _():
            low.wait()
            high.wait()

        lax.fori_loop(jnp.where(sweep == 0, first, DEEP), DEEP, lateral, 0)
        lax.fori_loop(jnp.where(sweep == 0, DEEP + layers, last), last, lateral, 0)
        low_pair = jnp.where(col == 0, DEEP // 2, sweep + 1)
        high_pair = jnp.where(col == cols - 1, (DEEP + layers) // 2, total // 2 - sweep - 1)
        lax.fori_loop(low_pair, high_pair, update, 0)
        return carry

    @pl.when(col == 0)
    def _():
        clear = jnp.zeros((8, Y_GROUPS, SUB, LANES), jnp.float32)
        for z in (DEEP - 2, DEEP - 1):
            along[z] = clear
            cross[z] = clear

    lax.fori_loop(0, SWEEPS, one_sweep, 0)

    @pl.when(col == 0)
    def _():
        all_change.wait()
        for z in range(layers):
            for t in range(8):
                field[DEEP + z, t, DEEP : DEEP + rows, :] += change[z, t]

    @pl.when(col == 1)
    def _():
        one_change.wait()
        for t in range(8):
            field[DEEP, t, DEEP : DEEP + rows, :] += change[0, t]

    for z in range(layers):
        for t in range(8):
            cut(field[DEEP + z, t, DEEP : DEEP + rows, :], rows * (z + 1), t)

    def write(at, value):
        velocity_ref[:, at] = value[:rows]
        out_ref[:, :, at] = value[rows:].reshape(layers, rows, 256)

    plain_columns(select_ref, parts[...], count, write)


def base_sweeps(where, wide, zlow, zhigh, change, speed, select):
    layers, _, rows, _ = change.shape
    total = layers + 2 * DEEP
    work = pltpu.VMEM((total, 8, Y_GROUPS, SUB, LANES), jnp.float32)
    line = pltpu.VMEM((8, Y_GROUPS, SUB, LANES), jnp.float32)
    return pl.pallas_call(
        base_kernel,
        out_shape=(f32(rows, 8 * LANES), f32(layers, rows, 8 * LANES)),
        in_specs=[SMEM] + [HBM] * 4 + [VMEM] * 2,
        out_specs=(VMEM, VMEM),
        scratch_shapes=[
            pltpu.VMEM((total, 8, Y_ROWS, LANES), jnp.float32),
            work, work, line, line,
            pltpu.VMEM((2, 2, Y_GROUPS, SUB, LANES), jnp.float32),
            pltpu.VMEM((layers, 8, rows, LANES), jnp.float32),
            pltpu.VMEM((2 * (layers + 1) * rows, 8 * LANES), jnp.bfloat16),
            pltpu.SemaphoreType.DMA((5,)),
        ],
        compiler_params=params(50),
        cost_estimate=cost(25),
        name="base_sweeps",
    )(where, wide, zlow, zhigh, change, speed, select)


mass_even = (-1.0 / 15.0, 2.0 / 15.0, 8.0 / 15.0, 2.0 / 15.0, -1.0 / 15.0)
mass_odd = (0.0, 2.0 / 15.0, 16.0 / 15.0, 2.0 / 15.0, 0.0)


def mass_along(padded, axis):
    count = padded.shape[axis] - 4
    pieces = [lax.slice_in_dim(padded, i, i + count, axis=axis) for i in range(5)]
    even = sum(mass_even[i] * pieces[i] for i in range(5))
    odd = sum(mass_odd[i] * pieces[i] for i in range(1, 4))
    at_even = lax.broadcasted_iota(jnp.int32, even.shape, axis) % 2 == 0
    return jnp.where(at_even, even, odd)


def with_rows(x, width):
    size = lax.axis_size("vol")
    up = [(i, i + 1) for i in range(size - 1)]
    down = [(j, i) for i, j in up]
    before = lax.ppermute(x[-width:], "vol", up)
    after = lax.ppermute(x[:width], "vol", down)
    return jnp.concatenate([before, x, after], axis=0)


def stepwise(flux, metric):
    root = jnp.sqrt(metric)

    def dot(a, b):
        return lax.psum(jnp.sum(a * b), "vol")

    def step(_, state):
        solved, residual, direction, norm = state
        padded = jnp.pad(with_rows(root * direction, 2), ((0, 0), (2, 2)))
        image = root * mass_along(mass_along(padded, 1), 0)
        alpha = norm / dot(direction, image)
        solved = solved + alpha * direction
        residual = residual - alpha * image
        after = dot(residual, residual)
        direction = residual + after / norm * direction
        return solved, residual, direction, after

    state = (jnp.zeros_like(flux), flux, flux, dot(flux, flux))
    return with_rows(lax.fori_loop(0, ITERS, step, state)[0], DEEP)


def after(x, *others):
    return lax.optimization_barrier((x,) + others)[0]


def on_device(face_area, face_speed, face_node, face_count, surface_metric, displacement):
    vols, cols = lax.axis_size("vol"), lax.axis_size("col")
    vol, col = lax.axis_index("vol"), lax.axis_index("col")
    core = col % 2
    where = jnp.stack([core, col, jnp.int32(cols), vol, jnp.int32(vols)]).astype(jnp.int32).reshape(1, 5)
    up = [(i, i + 1) for i in range(vols - 1)]
    down = [(j, i) for i, j in up]
    col_up = [(i, i + 1) for i in range(cols - 1)]
    col_down = [(j, i) for i, j in col_up]
    packed = displacement.shape[0] * DEEP

    select = plain_selection()

    def moved(x, steps):
        dv, dc = steps
        pairs = [
            (i * cols + j, (i + dv) * cols + j + dc)
            for i in range(vols)
            for j in range(cols)
            if 0 <= i + dv < vols and 0 <= j + dc < cols
        ]
        return lax.ppermute(x, ("vol", "col"), pairs)

    keep, send, rows_up, rows_down = face_sums(
        where, face_count, face_area, face_speed, face_node, displacement, surface_metric
    )
    with jax.named_scope("flux_sum"):
        keep = keep + lax.ppermute(send, "col", [(j, j ^ 1) for j in range(cols)])
        turned = [
            lax.ppermute(keep, "col", [(j, (j + 2 * k) % cols) for j in range(cols)]) for k in (1, 2, 3)
        ]
        own = (keep + turned[1]) + (turned[0] + turned[2])
    with jax.named_scope("row_halo"):
        rows_before, rows_after = moved(rows_up, (1, 0)), moved(rows_down, (-1, 0))
    wide, root = regroup(displacement, surface_metric, rows_before, rows_after)
    own = after(own, wide)
    with jax.named_scope("flux_halo"):
        other = lax.ppermute(own, "col", [(j, j ^ 1) for j in range(cols)])
        same_pairs, cross_pairs = [], []
        for i in range(vols):
            for j in range(cols):
                to = i - 1 if j % 2 == 0 else i + 1
                if 0 <= to < vols:
                    same_pairs.append((i * cols + j, to * cols + j))
                    cross_pairs.append((i * cols + j, to * cols + (j ^ 1)))
        same = lax.ppermute(own, ("vol", "col"), same_pairs)
        cross = lax.ppermute(own, ("vol", "col"), cross_pairs)

    with jax.named_scope("depth_halo"):
        sent = after(wide, other)
        zlow, zhigh = moved(sent, (0, 1)), moved(sent, (0, -1))
    basis, sums = surface_basis(where, own, other, same, cross, root)
    with jax.named_scope("gather_sums"):
        spread = jnp.broadcast_to(sums[None], (vols,) + sums.shape)
        gathered = lax.all_to_all(spread, "vol", 0, 0)
    speed, flag = surface_solve(basis, gathered)

    def step_by_step(state):
        low = jnp.where(core == 0, own, other)
        high = jnp.where(core == 0, other, own)
        flux = jnp.concatenate([low, high], axis=1)
        flux = flux.transpose(1, 2, 0).reshape(surface_metric.shape)
        wide = stepwise(flux, surface_metric)
        return jnp.int32(1), wide.reshape(Y_ROWS, LANES, 8).transpose(2, 0, 1)

    _, speed = lax.while_loop(lambda state: state[0] == 0, step_by_step, (flag[0, 0], speed))
    change = surface_change(where, speed, displacement.shape[0], displacement.shape[1])
    return base_sweeps(where, wide, zlow, zhigh, change, speed, select)


def solution(mesh):
    in_specs = (
        P("vol", "col"),
        P("vol", "col"),
        P("vol", "col"),
        P("vol", "col"),
        P("vol", None),
        P("col", "vol", None),
    )
    out_specs = (P("vol", None), P("col", "vol", None))
    return jax.shard_map(
        on_device, mesh=mesh, in_specs=in_specs, out_specs=out_specs, check_vma=False
    )
```

time: 160 us -> 135 us (0.84)
  Pallas kernels: 69.2 us -> 54 us
  starting transfers between devices: 45.7 us -> 35.2 us
  local copies, waits for them, and re-layouts: 5.99 us -> 13.9 us
  waiting for transfers between devices: 35.8 us -> 29.2 us
    pallas_call x5, Pallas kernels: 66.6 us -> 52 us  [the longest x1 30.9 us: base_sweeps(): pl.pallas_call(base_kernel, out_shape=(f32(rows, 8 * LANES), f32(layers,...]
    ppermute x3, waiting for transfers between devices: 16.4 us -> 3.9 us  [on_device(): lax.ppermute(keep, 'col', [(j, (j + 2 * k) % cols) for j in range(cols)])]
    ppermute x6 -> x4, waiting for transfers between devices: 10.4 us -> 21.4 us  [moved(): return lax.ppermute(x, ('vol', 'col'), pairs)]
    ppermute x6 -> x4, starting transfers between devices: 19.4 us -> 10.4 us  [moved(): return lax.ppermute(x, ('vol', 'col'), pairs)]
    unnamed x24 -> x20, local copies, waits for them, and re-layouts: 3.27 us -> 8.96 us
    ppermute x1, starting transfers between devices: 7.5 us -> 2.37 us  [on_device(): cross = lax.ppermute(own, ('vol', 'col'), cross_pairs)]
    ppermute x1, waiting for transfers between devices: 4.97 us -> 0.01 us  [on_device(): same = lax.ppermute(own, ('vol', 'col'), same_pairs)]
    while x0 -> x4, local copies, waits for them, and re-layouts: none -> 4.23 us  [on_device(): lax.while_loop(lambda state: state[0] == 0, step_by_step, (flag[0, 0], sp...]
  transfers between devices with their start and end apart: 14 -> 12, of which waited for: 6 -> 6; matrix products, arithmetic and copies ran while one was open for 2% -> 3% of each run, Pallas kernels for 18% -> 3%
where the time goes in v3:
time: 135 us
  Pallas kernels  54 us (40%)
  starting transfers between devices  35.2 us (26%)
  waiting for transfers between devices  29.2 us (22%)
  local copies, waits for them, and re-layouts  13.9 us (10%)
  between operations  1.64 us (1%)
    pallas_call x1, Pallas kernels, base_sweeps(): pl.pallas_call(base_kernel, out_shape=(f32(rows, 8 * LANES), f32(layers,...  30.9 us
    ppermute x4, waiting for transfers between devices, moved(): return lax.ppermute(x, ('vol', 'col'), pairs)  21.4 us
    all_to_all x1, starting transfers between devices, on_device(): gathered = lax.all_to_all(spread, 'vol', 0, 0)  11 us
    ppermute x4, starting transfers between devices, moved(): return lax.ppermute(x, ('vol', 'col'), pairs)  10.4 us
    unnamed x20, local copies, waits for them, and re-layouts  8.96 us
    pallas_call x1, Pallas kernels, surface_basis(): pl.pallas_call(basis_kernel, out_shape=(f32(ITERS, 8, GROUPS, SUB, LANES)...  8.4 us
    pallas_call x1, Pallas kernels, face_sums(): pl.pallas_call(face_kernel, out_shape=(half, half, rows, rows), in_specs=...  7.46 us
    ppermute x3, starting transfers between devices, on_device(): lax.ppermute(keep, 'col', [(j, (j + 2 * k) % cols) for j in range(cols)])  5.69 us
  transfers between devices with their start and end apart: 12, of which 6 were waited for; matrix products, arithmetic and copies ran while one was open for 3% of the time, Pallas kernels for 3%

profile of v3, /device:TPU:1, one launch (start us, length us, event | category | flops | bytes accessed | tf_op | source)
XLA Modules:
  0.0 134.7 jit_solution(8660522888522837848)
XLA Ops:
  1.3 0.1 stack.15
  1.4 0.0 copy-start
  1.4 1.6 %copy-done = f32[8,64,1024]{2,1,0:T(8,128)S(1)} copy-done((f32[8,64,1024]{2,1,0:T(8,128)S(1)}, f32[8,64,1024]{2,1,0:T(8,128)}, u32[]{:S(2)}) %copy-start) | copy-done | bytes 2097176
  3.0 0.0 copy-start.6
  3.0 0.8 copy-done.6
  3.8 0.0 copy-start.7
  3.8 0.8 copy-done.7
  4.6 0.0 copy-start.8
  4.6 0.8 copy-done.8
  5.5 0.0 copy-start.1
  5.5 0.0 copy-start.10
  5.5 7.5 %face_sums.1 = (f32[8,32,128]{2,1,0:T(8,128)S(1)}, f32[8,32,128]{2,1,0:T(8,128)S(1)}, f32[96,1024]{1,0:T(8,128)S(1)}, f32[96,1024]{1,0:T(8,128)S(1)}) custom-call(s32[1,5]{1,0:T(1,128)S(1)} %bitcast.15, s32[1,1]{1,0:T(1,128)S(6)} %copy.45.count_ref, f32[1,16384]{1,0:T(1,128)S(1)} %copy-done.6, f32[1,16384]{1,0:T(1,128)S(1)} %copy-done.7, ...), custom_call_target="tpu_custom_call" | custom-call | bytes 21000000 | tf_op jit(solution)/shard_map/face_sums/pallas_call | solution.py:208
  13.0 1.5 %collective-permute-start.6 = (f32[8,32,128]{2,1,0:T(8,128)S(1)}, f32[8,32,128]{2,1,0:T(8,128)S(1)}, u32[]{:S(2)}, u32[]{:S(2)}) collective-permute-start(f32[8,32,128]{2,1,0:T(8,128)S(1)} %get-tuple-element.144), channel_id=1, source_target_pairs={{0,1},{1,0},{2,3},{3,2},{4,5},{5,4},{6,7},{7,6},{8,9},{9,8},{10,11... | collective-permute-start | bytes 393224 | tf_op jit(solution)/shard_map/flux_sum/ppermute | solution.py:747
  14.5 3.2 %collective-permute-start.4 = (f32[96,1024]{1,0:T(8,128)S(1)}, f32[96,1024]{1,0:T(8,128)S(1)}, u32[]{:S(2)}, u32[]{:S(2)}) collective-permute-start(f32[96,1024]{1,0:T(8,128)S(1)} %get-tuple-element.140), channel_id=1, source_target_pairs={{0,8},{1,9},{2,10},{3,11},{4,12},{5,13},{6,14},{7,15},{8,16},{9,17... | collective-permute-start | bytes 1179656 | tf_op jit(solution)/shard_map/row_halo/ppermute | solution.py:741
  17.7 1.3 collective-permute-start.5
  19.0 0.0 collective-permute-done.6
  19.0 3.0 %collective-permute-start.7 = (f32[8,32,128]{2,1,0:T(8,128)S(1)}, f32[8,32,128]{2,1,0:T(8,128)S(1)}, u32[]{:S(2)}, u32[]{:S(2)}) collective-permute-start(f32[8,32,128]{2,1,0:T(8,128)S(1)} %add.153), channel_id=1, source_target_pairs={{0,4},{1,5},{2,6},{3,7},{4,0},{5,1},{6,2},{7,3},{8,12},{9,13},{10,... | collective-permute-start | bytes 393224 | tf_op jit(solution)/shard_map/flux_sum/ppermute | solution.py:749
  22.0 0.4 collective-permute-start.8
  22.4 2.3 %collective-permute-start.9 = (f32[8,32,128]{2,1,0:T(8,128)S(1)}, f32[8,32,128]{2,1,0:T(8,128)S(1)}, u32[]{:S(2)}, u32[]{:S(2)}) collective-permute-start(f32[8,32,128]{2,1,0:T(8,128)S(1)} %add.153), channel_id=1, source_target_pairs={{0,6},{1,7},{2,0},{3,1},{4,2},{5,3},{6,4},{7,5},{8,14},{9,15},{10,... | collective-permute-start | bytes 393224 | tf_op jit(solution)/shard_map/flux_sum/ppermute | solution.py:749
  24.7 0.7 collective-permute-done.7
  25.4 3.2 %collective-permute-done.8 = f32[8,32,128]{2,1,0:T(8,128)S(1)} collective-permute-done((f32[8,32,128]{2,1,0:T(8,128)S(1)}, f32[8,32,128]{2,1,0:T(8,128)S(1)}, u32[]{:S(2)}, u32[]{:S(2)}) %collective-permute-start.8) | collective-permute-done | bytes 131104 | tf_op jit(solution)/shard_map/flux_sum/ppermute | solution.py:749
  28.6 0.0 collective-permute-done.9
  28.6 0.0 copy-start.5
  28.7 0.0 collective-permute-done.4.before_ref
  28.7 1.3 collective-permute-done.5.after_ref
  30.0 0.0 copy-done.1
  30.0 0.0 copy-done.10
  30.0 3.4 %regroup.1 = (f32[8,8,80,128]{3,2,1,0:T(8,128)S(1)}, f32[8,128,128]{2,1,0:T(8,128)S(1)}) custom-call(f32[8,64,1024]{2,1,0:T(8,128)S(1)} %copy-done.1, f32[64,1024]{1,0:T(8,128)S(1)} %copy-done.10, f32[96,1024]{1,0:T(8,128)S(1)} %collective-permute-done.4.before_ref, f32[96,1024]{1,0:T(8,128)S(1)} %collective-permute-done.5.after_ref), custom_call_target="tpu_custom_call" | custom-call | bytes 18000000 | tf_op jit(solution)/shard_map/regroup/pallas_call | solution.py:130
  33.4 0.0 copy-start.4
  33.4 1.2 collective-permute-start.10
  34.6 3.1 %collective-permute-start.13 = (f32[8,32,128]{2,1,0:T(8,128)S(1)}, f32[8,32,128]{2,1,0:T(8,128)S(1)}, u32[]{:S(2)}, u32[]{:S(2)}) collective-permute-start(f32[8,32,128]{2,1,0:T(8,128)S(1)} %add_add_fusion.own_ref), channel_id=1, source_target_pairs={{1,9},{3,11},{5,13},{7,15},{8,0},{9,17},{10,2},{11,19},{12,4},{13,... | collective-permute-start | bytes 393224 | tf_op jit(solution)/shard_map/flux_halo/ppermute | solution.py:765
  37.7 2.4 %collective-permute-start.14 = (f32[8,32,128]{2,1,0:T(8,128)S(1)}, f32[8,32,128]{2,1,0:T(8,128)S(1)}, u32[]{:S(2)}, u32[]{:S(2)}) collective-permute-start(f32[8,32,128]{2,1,0:T(8,128)S(1)} %add_add_fusion.own_ref), channel_id=1, source_target_pairs={{1,8},{3,10},{5,12},{7,14},{8,1},{9,16},{10,3},{11,18},{12,5},{13,... | collective-permute-start | bytes 393224 | tf_op jit(solution)/shard_map/flux_halo/ppermute | solution.py:766
  40.1 0.0 collective-permute-done.10.other_ref
  40.1 0.0 collective-permute-done.13.same_ref
  40.1 3.9 %collective-permute-done.14.cross_ref = f32[8,32,128]{2,1,0:T(8,128)S(1)} collective-permute-done((f32[8,32,128]{2,1,0:T(8,128)S(1)}, f32[8,32,128]{2,1,0:T(8,128)S(1)}, u32[]{:S(2)}, u32[]{:S(2)}) %collective-permute-start.14) | collective-permute-done | bytes 131104 | tf_op jit(solution)/shard_map/flux_halo/ppermute | solution.py:766
  44.0 8.4 %surface_basis.1 = (f32[10,8,16,8,128]{4,3,2,1,0:T(8,128)S(1)}, f32[8,128]{1,0:T(8,128)S(1)}) custom-call(s32[1,5]{1,0:T(1,128)S(1)} %bitcast.16, f32[8,32,128]{2,1,0:T(8,128)S(1)} %add_add_fusion.own_ref, f32[8,32,128]{2,1,0:T(8,128)S(1)} %collective-permute-done.10.other_ref, f32[8,32,128]{2,1,0:T(8,128)S(1)} %collective-permute-done.13.same_ref, ...), custom_call_target="tpu_custom_call" | custom-call | bytes 21000000 | tf_op jit(solution)/shard_map/surface_basis/pallas_call | solution.py:294
  52.4 0.0 copy-start.2
  52.4 2.3 %copy-done.2 = f32[10,8,16,8,128]{4,3,2,1,0:T(8,128)} copy-done((f32[10,8,16,8,128]{4,3,2,1,0:T(8,128)}, f32[10,8,16,8,128]{4,3,2,1,0:T(8,128)S(1)}, u32[]{:S(2)}) %copy-start.2) | copy-done | bytes 5242904
  54.8 0.6 broadcast_in_dim.2
  55.4 11.0 %all-to-all-start = ((f32[16,8,128]{2,1,0:T(8,128)}), f32[16,8,128]{2,1,0:T(8,128)S(1)}, u32[]{:S(2)}, u32[]{:S(2)}) async-start(f32[16,8,128]{2,1,0:T(8,128)} %broadcast_in_dim.2), calls=%async_computation | async-start | bytes 131072 | tf_op jit(solution)/shard_map/gather_sums/all_to_all | solution.py:774
  66.4 1.0 copy.19
  67.4 3.2 %collective-permute-start.11 = (f32[8,8,80,128]{3,2,1,0:T(8,128)S(1)}, f32[8,8,80,128]{3,2,1,0:T(8,128)}, u32[]{:S(2)}, u32[]{:S(2)}) collective-permute-start(f32[8,8,80,128]{3,2,1,0:T(8,128)S(1)} %get-tuple-element.146.wide_ref), channel_id=1, source_target_pairs={{0,1},{1,2},{2,3},{3,4},{4,5},{5,6},{6,7},{8,9},{9,10},{10,11},{11... | collective-permute-start | bytes 7864328 | tf_op jit(solution)/shard_map/depth_halo/ppermute | solution.py:741
  70.6 2.7 %collective-permute-start.12 = (f32[8,8,80,128]{3,2,1,0:T(8,128)S(1)}, f32[8,8,80,128]{3,2,1,0:T(8,128)}, u32[]{:S(2)}, u32[]{:S(2)}) collective-permute-start(f32[8,8,80,128]{3,2,1,0:T(8,128)S(1)} %get-tuple-element.146.wide_ref), channel_id=1, source_target_pairs={{1,0},{2,1},{3,2},{4,3},{5,4},{6,5},{7,6},{9,8},{10,9},{11,10},{12... | collective-permute-start | bytes 7864328 | tf_op jit(solution)/shard_map/depth_halo/ppermute | solution.py:741
  73.3 1.0 copy.20
  74.3 0.0 all-to-all-done.sums_ref
  74.3 0.0 copy-done.5
  74.3 0.0 copy-start.3
  74.3 2.5 %copy-done.3 = f32[10,8,16,8,128]{4,3,2,1,0:T(8,128)S(1)} copy-done((f32[10,8,16,8,128]{4,3,2,1,0:T(8,128)S(1)}, f32[10,8,16,8,128]{4,3,2,1,0:T(8,128)}, u32[]{:S(2)}) %copy-start.3) | copy-done | bytes 5242904
  76.8 2.0 %surface_solve.1 = (f32[8,80,128]{2,1,0:T(8,128)S(1)}, s32[1,1]{1,0:T(1,128)}) custom-call(f32[10,8,16,8,128]{4,3,2,1,0:T(8,128)S(1)} %copy-done.3, f32[16,8,128]{2,1,0:T(8,128)S(1)} %all-to-all-done.sums_ref, f32[20,16,128]{2,1,0:T(8,128)S(1)} %copy-done.5), custom_call_target="tpu_custom_call" | custom-call | bytes 9000000 | tf_op jit(solution)/shard_map/surface_solve/pallas_call | solution.py:376
  78.8 1.0 copy.18
  79.8 0.0 copy-done.4
  79.8 0.7 while.28
  80.5 1.2 copy.21.speed_ref
  81.7 1.9 %surface_change.1.change_ref = f32[8,8,64,128]{3,2,1,0:T(8,128)S(1)} custom-call(s32[1,5]{1,0:T(1,128)S(1)} %bitcast.17, f32[8,80,128]{2,1,0:T(8,128)S(1)} %copy.21.speed_ref), custom_call_target="tpu_custom_call" | custom-call | bytes 24000000 | tf_op jit(solution)/shard_map/surface_change/pallas_call | solution.py:519
  83.6 15.6 %collective-permute-done.11.zlow_ref = f32[8,8,80,128]{3,2,1,0:T(8,128)} collective-permute-done((f32[8,8,80,128]{3,2,1,0:T(8,128)S(1)}, f32[8,8,80,128]{3,2,1,0:T(8,128)}, u32[]{:S(2)}, u32[]{:S(2)}) %collective-permute-start.11) | collective-permute-done | bytes 2621472 | tf_op jit(solution)/shard_map/depth_halo/ppermute | solution.py:741
  99.2 4.5 %collective-permute-done.12.zhigh_ref = f32[8,8,80,128]{3,2,1,0:T(8,128)} collective-permute-done((f32[8,8,80,128]{3,2,1,0:T(8,128)S(1)}, f32[8,8,80,128]{3,2,1,0:T(8,128)}, u32[]{:S(2)}, u32[]{:S(2)}) %collective-permute-start.12) | collective-permute-done | bytes 2621472 | tf_op jit(solution)/shard_map/depth_halo/ppermute | solution.py:741
  103.7 30.9 %base_sweeps.1 = (f32[64,1024]{1,0:T(8,128)}, f32[8,64,1024]{2,1,0:T(8,128)}) custom-call(s32[1,5]{1,0:T(1,128)S(1)} %bitcast.18, f32[8,8,80,128]{3,2,1,0:T(8,128)} %copy-done.4, f32[8,8,80,128]{3,2,1,0:T(8,128)} %collective-permute-done.11.zlow_ref, f32[8,8,80,128]{3,2,1,0:T(8,128)} %collective-permute-done.12.zhigh_ref, ...), custom_call_target="tpu_custom_call" | custom-call | bytes 75000000 | tf_op jit(solution)/shard_map/base_sweeps/pallas_call | solution.py:654
  (2 shorter events, 0.1 us)
Async XLA Ops:
  1.4 1.6 %copy-start = (f32[8,64,1024]{2,1,0:T(8,128)S(1)}, f32[8,64,1024]{2,1,0:T(8,128)}, u32[]{:S(2)}) copy-start(f32[8,64,1024]{2,1,0:T(8,128)} %block_ref.3) | copy-start | bytes 6291460
  3.0 0.8 copy-start.6
  3.8 0.8 copy-start.7
  4.6 0.8 copy-start.8
  5.5 24.5 %copy-start.1 = (f32[8,64,1024]{2,1,0:T(8,128)S(1)}, f32[8,64,1024]{2,1,0:T(8,128)}, u32[]{:S(2)}) copy-start(f32[8,64,1024]{2,1,0:T(8,128)} %block_ref.3) | copy-start | bytes 6291460
  5.5 24.5 %copy-start.10 = (f32[64,1024]{1,0:T(8,128)S(1)}, f32[64,1024]{1,0:T(8,128)}, u32[]{:S(2)}) copy-start(f32[64,1024]{1,0:T(8,128)} %metric_ref.3) | copy-start | bytes 786436
  13.0 6.0 %collective-permute-start.6 = (f32[8,32,128]{2,1,0:T(8,128)S(1)}, f32[8,32,128]{2,1,0:T(8,128)S(1)}, u32[]{:S(2)}, u32[]{:S(2)}) collective-permute-start(f32[8,32,128]{2,1,0:T(8,128)S(1)} %get-tuple-element.144), channel_id=1, source_target_pairs={{0,1},{1,0},{2,3},{3,2},{4,5},{5,4},{6,7},{7,6},{8,9},{9,8},{10,11... | collective-permute-start | bytes 393224 | tf_op jit(solution)/shard_map/flux_sum/ppermute | solution.py:747
  14.5 14.2 %collective-permute-start.4 = (f32[96,1024]{1,0:T(8,128)S(1)}, f32[96,1024]{1,0:T(8,128)S(1)}, u32[]{:S(2)}, u32[]{:S(2)}) collective-permute-start(f32[96,1024]{1,0:T(8,128)S(1)} %get-tuple-element.140), channel_id=1, source_target_pairs={{0,8},{1,9},{2,10},{3,11},{4,12},{5,13},{6,14},{7,15},{8,16},{9,17... | collective-permute-start | bytes 1179656 | tf_op jit(solution)/shard_map/row_halo/ppermute | solution.py:741
  17.7 12.3 %collective-permute-start.5 = (f32[96,1024]{1,0:T(8,128)S(1)}, f32[96,1024]{1,0:T(8,128)S(1)}, u32[]{:S(2)}, u32[]{:S(2)}) collective-permute-start(f32[96,1024]{1,0:T(8,128)S(1)} %get-tuple-element.141), channel_id=1, source_target_pairs={{8,0},{9,1},{10,2},{11,3},{12,4},{13,5},{14,6},{15,7},{16,8},{17,9... | collective-permute-start | bytes 1179656 | tf_op jit(solution)/shard_map/row_halo/ppermute | solution.py:741
  19.0 6.4 %collective-permute-start.7 = (f32[8,32,128]{2,1,0:T(8,128)S(1)}, f32[8,32,128]{2,1,0:T(8,128)S(1)}, u32[]{:S(2)}, u32[]{:S(2)}) collective-permute-start(f32[8,32,128]{2,1,0:T(8,128)S(1)} %add.153), channel_id=1, source_target_pairs={{0,4},{1,5},{2,6},{3,7},{4,0},{5,1},{6,2},{7,3},{8,12},{9,13},{10,... | collective-permute-start | bytes 393224 | tf_op jit(solution)/shard_map/flux_sum/ppermute | solution.py:749
  22.0 6.6 %collective-permute-start.8 = (f32[8,32,128]{2,1,0:T(8,128)S(1)}, f32[8,32,128]{2,1,0:T(8,128)S(1)}, u32[]{:S(2)}, u32[]{:S(2)}) collective-permute-start(f32[8,32,128]{2,1,0:T(8,128)S(1)} %add.153), channel_id=1, source_target_pairs={{0,2},{1,3},{2,4},{3,5},{4,6},{5,7},{6,0},{7,1},{8,10},{9,11},{10,... | collective-permute-start | bytes 393224 | tf_op jit(solution)/shard_map/flux_sum/ppermute | solution.py:749
  22.4 6.2 %collective-permute-start.9 = (f32[8,32,128]{2,1,0:T(8,128)S(1)}, f32[8,32,128]{2,1,0:T(8,128)S(1)}, u32[]{:S(2)}, u32[]{:S(2)}) collective-permute-start(f32[8,32,128]{2,1,0:T(8,128)S(1)} %add.153), channel_id=1, source_target_pairs={{0,6},{1,7},{2,0},{3,1},{4,2},{5,3},{6,4},{7,5},{8,14},{9,15},{10,... | collective-permute-start | bytes 393224 | tf_op jit(solution)/shard_map/flux_sum/ppermute | solution.py:749
  28.6 45.7 %copy-start.5 = (f32[20,16,128]{2,1,0:T(8,128)S(1)}, f32[20,16,128]{2,1,0:T(8,128)}, u32[]{:S(2)}) copy-start(f32[20,16,128]{2,1,0:T(8,128)} %constant.123.clone.weights_ref) | copy-start | bytes 491524
  33.4 46.4 %copy-start.4 = (f32[8,8,80,128]{3,2,1,0:T(8,128)}, f32[8,8,80,128]{3,2,1,0:T(8,128)S(1)}, u32[]{:S(2)}) copy-start(f32[8,8,80,128]{3,2,1,0:T(8,128)S(1)} %get-tuple-element.146.wide_ref) | copy-start | bytes 7864324
  33.4 6.7 %collective-permute-start.10 = (f32[8,32,128]{2,1,0:T(8,128)S(1)}, f32[8,32,128]{2,1,0:T(8,128)S(1)}, u32[]{:S(2)}, u32[]{:S(2)}) collective-permute-start(f32[8,32,128]{2,1,0:T(8,128)S(1)} %add_add_fusion.own_ref), channel_id=1, source_target_pairs={{0,1},{1,0},{2,3},{3,2},{4,5},{5,4},{6,7},{7,6},{8,9},{9,8},{10,11... | collective-permute-start | bytes 393224 | tf_op jit(solution)/shard_map/flux_halo/ppermute | solution.py:757
  34.6 5.5 %collective-permute-start.13 = (f32[8,32,128]{2,1,0:T(8,128)S(1)}, f32[8,32,128]{2,1,0:T(8,128)S(1)}, u32[]{:S(2)}, u32[]{:S(2)}) collective-permute-start(f32[8,32,128]{2,1,0:T(8,128)S(1)} %add_add_fusion.own_ref), channel_id=1, source_target_pairs={{1,9},{3,11},{5,13},{7,15},{8,0},{9,17},{10,2},{11,19},{12,4},{13,... | collective-permute-start | bytes 393224 | tf_op jit(solution)/shard_map/flux_halo/ppermute | solution.py:765
  37.7 6.3 %collective-permute-start.14 = (f32[8,32,128]{2,1,0:T(8,128)S(1)}, f32[8,32,128]{2,1,0:T(8,128)S(1)}, u32[]{:S(2)}, u32[]{:S(2)}) collective-permute-start(f32[8,32,128]{2,1,0:T(8,128)S(1)} %add_add_fusion.own_ref), channel_id=1, source_target_pairs={{1,8},{3,10},{5,12},{7,14},{8,1},{9,16},{10,3},{11,18},{12,5},{13,... | collective-permute-start | bytes 393224 | tf_op jit(solution)/shard_map/flux_halo/ppermute | solution.py:766
  52.4 2.4 %copy-start.2 = (f32[10,8,16,8,128]{4,3,2,1,0:T(8,128)}, f32[10,8,16,8,128]{4,3,2,1,0:T(8,128)S(1)}, u32[]{:S(2)}) copy-start(f32[10,8,16,8,128]{4,3,2,1,0:T(8,128)S(1)} %get-tuple-element.148.basis_ref) | copy-start | bytes 15728644
  55.4 18.9 %all-to-all-start = ((f32[16,8,128]{2,1,0:T(8,128)}), f32[16,8,128]{2,1,0:T(8,128)S(1)}, u32[]{:S(2)}, u32[]{:S(2)}) async-start(f32[16,8,128]{2,1,0:T(8,128)} %broadcast_in_dim.2), calls=%async_computation | async-start | bytes 131072 | tf_op jit(solution)/shard_map/gather_sums/all_to_all | solution.py:774
  67.4 31.8 %collective-permute-start.11 = (f32[8,8,80,128]{3,2,1,0:T(8,128)S(1)}, f32[8,8,80,128]{3,2,1,0:T(8,128)}, u32[]{:S(2)}, u32[]{:S(2)}) collective-permute-start(f32[8,8,80,128]{3,2,1,0:T(8,128)S(1)} %get-tuple-element.146.wide_ref), channel_id=1, source_target_pairs={{0,1},{1,2},{2,3},{3,4},{4,5},{5,6},{6,7},{8,9},{9,10},{10,11},{11... | collective-permute-start | bytes 7864328 | tf_op jit(solution)/shard_map/depth_halo/ppermute | solution.py:741
  70.6 33.1 %collective-permute-start.12 = (f32[8,8,80,128]{3,2,1,0:T(8,128)S(1)}, f32[8,8,80,128]{3,2,1,0:T(8,128)}, u32[]{:S(2)}, u32[]{:S(2)}) collective-permute-start(f32[8,8,80,128]{3,2,1,0:T(8,128)S(1)} %get-tuple-element.146.wide_ref), channel_id=1, source_target_pairs={{1,0},{2,1},{3,2},{4,3},{5,4},{6,5},{7,6},{9,8},{10,9},{11,10},{12... | collective-permute-start | bytes 7864328 | tf_op jit(solution)/shard_map/depth_halo/ppermute | solution.py:741
  74.3 2.5 %copy-start.3 = (f32[10,8,16,8,128]{4,3,2,1,0:T(8,128)S(1)}, f32[10,8,16,8,128]{4,3,2,1,0:T(8,128)}, u32[]{:S(2)}) copy-start(f32[10,8,16,8,128]{4,3,2,1,0:T(8,128)} %copy-done.2) | copy-start | bytes 15728644

commit v4 on v3

--- a/solution.py
+++ b/solution.py
@@ -75,7 +75,7 @@
 
 
 def cost(us):
-    return pl.CostEstimate(flops=0, bytes_accessed=int(us * 3_000_000), transcendentals=0)
+    return pl.CostEstimate(flops=0, bytes_accessed=int(us * 100_000), transcendentals=0)
 
 
 def split(x):
@@ -162,7 +162,7 @@
     copies = [pltpu.make_async_copy(*pair, sems.at[i]) for i, pair in enumerate(copies)]
     for copy in copies:
         copy.start()
-    chunk = min(2048, slots)
+    chunk = min(4096, slots)
     core = where_ref[0, 0]
     ids = lax.broadcasted_iota(jnp.int32, (256, chunk), 0)
     ids = ids.astype(jnp.float32).astype(jnp.bfloat16)
@@ -187,16 +187,16 @@
         upper = jnp.where(here, wide(first), zero)
         lower = jnp.where(here, wide(second), zero)
         columns = jnp.where(wide(low) == ids, one, zero)
-        acc_ref[...] += lax.dot_general(
-            upper, columns, contract, preferred_element_type=jnp.float32
-        ) + lax.dot_general(lower, columns, contract, preferred_element_type=jnp.float32)
+        both = jnp.concatenate([upper, lower], axis=0)
+        acc_ref[...] += lax.dot_general(both, columns, contract, preferred_element_type=jnp.float32)
         return carry
 
     lax.fori_loop(0, slots // chunk, body, 0)
     for j in range(8):
         at, lanes = 64 * (j // 2), slice(LANES * (j % 2), LANES * (j % 2 + 1))
-        keep_ref[j] = acc_ref[pl.ds(at + 32 * core, 32), lanes]
-        send_ref[j] = acc_ref[pl.ds(at + 32 - 32 * core, 32), lanes]
+        near, far = at + 32 * core, at + 32 - 32 * core
+        keep_ref[j] = acc_ref[pl.ds(near, 32), lanes] + acc_ref[pl.ds(256 + near, 32), lanes]
+        send_ref[j] = acc_ref[pl.ds(far, 32), lanes] + acc_ref[pl.ds(256 + far, 32), lanes]
     for copy in copies:
         copy.wait()
 
@@ -209,12 +209,12 @@
         face_kernel,
         out_shape=(half, half, rows, rows),
         in_specs=[SMEM, SMEM, VMEM, VMEM, VMEM, HBM, HBM],
-        out_specs=(VMEM, VMEM, HBM, HBM),
+        out_specs=(VMEM, VMEM, VMEM, VMEM),
         scratch_shapes=[
-            pltpu.VMEM((256, 256), jnp.float32),
+            pltpu.VMEM((512, 256), jnp.float32),
             pltpu.SemaphoreType.DMA((2 * layers + 2,)),
         ],
-        compiler_params=params(32),
+        compiler_params=params(58),
         cost_estimate=cost(7),
         name="face_sums",
     )(where, count, area, speed, node, block, metric)
@@ -305,7 +305,7 @@
             pltpu.VMEM((24, LANES), jnp.float32),
             pltpu.SemaphoreType.DMA((ITERS,)),
         ],
-        compiler_params=params(40),
+        compiler_params=params(58),
         cost_estimate=cost(7),
         name="surface_basis",
     )(where, own, other, same, cross, root)
@@ -383,7 +383,7 @@
             pltpu.VMEM((8, ROWS, LANES), jnp.float32),
             pltpu.SemaphoreType.DMA,
         ],
-        compiler_params=params(32),
+        compiler_params=params(58),
         cost_estimate=cost(3),
         name="surface_solve",
     )(basis, sums, jnp.asarray(solve_weights()))
@@ -528,7 +528,7 @@
             pltpu.VMEM((layers, 8, Y_ROWS, LANES), jnp.float32),
             pltpu.SemaphoreType.DMA,
         ],
-        compiler_params=params(40),
+        compiler_params=params(58),
         cost_estimate=cost(8),
         name="surface_change",
     )(where, speed)
@@ -664,7 +664,7 @@
             pltpu.VMEM((2 * (layers + 1) * rows, 8 * LANES), jnp.bfloat16),
             pltpu.SemaphoreType.DMA((5,)),
         ],
-        compiler_params=params(50),
+        compiler_params=params(58),
         cost_estimate=cost(25),
         name="base_sweeps",
     )(where, wide, zlow, zhigh, change, speed, select)
@@ -766,7 +766,7 @@
         cross = lax.ppermute(own, ("vol", "col"), cross_pairs)
 
     with jax.named_scope("depth_halo"):
-        sent = after(wide, other)
+        sent = after(wide, own)
         zlow, zhigh = moved(sent, (0, 1)), moved(sent, (0, -1))
     basis, sums = surface_basis(where, own, other, same, cross, root)
     with jax.named_scope("gather_sums"):
@@ -774,17 +774,19 @@
         gathered = lax.all_to_all(spread, "vol", 0, 0)
     speed, flag = surface_solve(basis, gathered)
 
-    def step_by_step(state):
+    def finish(speed):
+        change = surface_change(where, speed, displacement.shape[0], displacement.shape[1])
+        return base_sweeps(where, wide, zlow, zhigh, change, speed, select)
+
+    def step_by_step():
         low = jnp.where(core == 0, own, other)
         high = jnp.where(core == 0, other, own)
         flux = jnp.concatenate([low, high], axis=1)
         flux = flux.transpose(1, 2, 0).reshape(surface_metric.shape)
-        wide = stepwise(flux, surface_metric)
-        return jnp.int32(1), wide.reshape(Y_ROWS, LANES, 8).transpose(2, 0, 1)
-
-    _, speed = lax.while_loop(lambda state: state[0] == 0, step_by_step, (flag[0, 0], speed))
-    change = surface_change(where, speed, displacement.shape[0], displacement.shape[1])
-    return base_sweeps(where, wide, zlow, zhigh, change, speed, select)
+        solved = stepwise(flux, surface_metric)
+        return finish(solved.reshape(Y_ROWS, LANES, 8).transpose(2, 0, 1))
+
+    return lax.cond(flag[0, 0] > 0, lambda: finish(speed), step_by_step)
 
 
 def solution(mesh):

time: 135 us -> 116 us (0.86)
  waiting for transfers between devices: 29.2 us -> 9.73 us
  blocking collectives: 0 us -> 18.4 us
  starting transfers between devices: 35.2 us -> 22.6 us
  local copies, waits for them, and re-layouts: 13.9 us -> 2.23 us
  Pallas kernels: 54 us -> 58.9 us
    ppermute x4, waiting for transfers between devices: 21.4 us -> 0.11 us  [moved(): return lax.ppermute(x, ('vol', 'col'), pairs)]
    all_to_all x0 -> x1, blocking collectives: none -> 18.4 us  [on_device(): gathered = lax.all_to_all(spread, 'vol', 0, 0)]
    all_to_all x1 -> x0, starting transfers between devices: 11 us -> none  [on_device(): gathered = lax.all_to_all(spread, 'vol', 0, 0)]
    unnamed x20 -> x14, local copies, waits for them, and re-layouts: 8.96 us -> 1.46 us
    while x4 -> x0, local copies, waits for them, and re-layouts: 4.23 us -> none  [on_device(): lax.while_loop(lambda state: state[0] == 0, step_by_step, (flag[0, 0], sp...]
    pallas_call x1, Pallas kernels: 1.99 us -> 4.84 us  [surface_solve(): pl.pallas_call(solve_kernel, out_shape=(f32(8, Y_ROWS, LANES), jax.ShapeD...]
    ppermute x3, waiting for transfers between devices: 3.9 us -> 5.66 us  [on_device(): lax.ppermute(keep, 'col', [(j, (j + 2 * k) % cols) for j in range(cols)])]
    pallas_call x1, Pallas kernels: 3.41 us -> 4.86 us  [regroup(): pl.pallas_call(regroup_kernel, out_shape=(f32(layers, 8, Y_ROWS, LANES),...]
  transfers between devices with their start and end apart: 12 -> 11, of which waited for: 6 -> 4; matrix products, arithmetic and copies ran while one was open for 3% -> 1% of each run, Pallas kernels for 3% -> 12%
where the time goes in v4:
time: 116 us
  Pallas kernels  58.9 us (51%)
  starting transfers between devices  22.6 us (19%)
  blocking collectives  18.4 us (16%)
  waiting for transfers between devices  9.73 us (8%)
  between operations  2.45 us (2%)
  local copies, waits for them, and re-layouts  2.23 us (2%)
    pallas_call x1, Pallas kernels, base_sweeps(): pl.pallas_call(base_kernel, out_shape=(f32(rows, 8 * LANES), f32(layers,...  29.8 us
    all_to_all x1, blocking collectives, on_device(): gathered = lax.all_to_all(spread, 'vol', 0, 0)  18.4 us
    ppermute x4, starting transfers between devices, moved(): return lax.ppermute(x, ('vol', 'col'), pairs)  10.6 us
    pallas_call x1, Pallas kernels, surface_basis(): pl.pallas_call(basis_kernel, out_shape=(f32(ITERS, 8, GROUPS, SUB, LANES)...  9.19 us
    pallas_call x1, Pallas kernels, face_sums(): pl.pallas_call(face_kernel, out_shape=(half, half, rows, rows), in_specs=...  7.32 us
    ppermute x3, waiting for transfers between devices, on_device(): lax.ppermute(keep, 'col', [(j, (j + 2 * k) % cols) for j in range(cols)])  5.66 us
    pallas_call x1, Pallas kernels, regroup(): pl.pallas_call(regroup_kernel, out_shape=(f32(layers, 8, Y_ROWS, LANES),...  4.86 us
    pallas_call x1, Pallas kernels, surface_solve(): pl.pallas_call(solve_kernel, out_shape=(f32(8, Y_ROWS, LANES), jax.ShapeD...  4.84 us
  transfers between devices with their start and end apart: 11, of which 4 were waited for; matrix products, arithmetic and copies ran while one was open for 1% of the time, Pallas kernels for 12%

profile of v4, /device:TPU:1, one launch (start us, length us, event | category | flops | bytes accessed | tf_op | source)
XLA Modules:
  0.0 115.6 jit_solution(760348275524072784)
XLA Ops:
  0.6 0.0 copy-start
  0.6 0.0 copy-start.3
  1.5 0.1 stack.15
  1.5 7.3 %face_sums.1 = (f32[8,32,128]{2,1,0:T(8,128)}, f32[8,32,128]{2,1,0:T(8,128)}, f32[96,1024]{1,0:T(8,128)}, f32[96,1024]{1,0:T(8,128)}) custom-call(s32[1,5]{1,0:T(1,128)S(1)} %bitcast.17, s32[1,1]{1,0:T(1,128)S(6)} %copy.41.count_ref, f32[1,16384]{1,0:T(1,128)} %area_ref.1, f32[1,16384]{1,0:T(1,128)} %speed_ref.1, s32[1,16384]{1,0:T(1,128)} %node_ref.1, ...), custom_call_target="tpu_custom_call" | custom-call | bytes 700000 | tf_op jit(solution)/shard_map/face_sums/pallas_call | solution.py:208
  8.9 1.5 %collective-permute-start.4 = (f32[8,32,128]{2,1,0:T(8,128)}, f32[8,32,128]{2,1,0:T(8,128)S(1)}, u32[]{:S(2)}, u32[]{:S(2)}) collective-permute-start(f32[8,32,128]{2,1,0:T(8,128)} %get-tuple-element.139), channel_id=1, source_target_pairs={{0,1},{1,0},{2,3},{3,2},{4,5},{5,4},{6,7},{7,6},{8,9},{9,8},{10,11... | collective-permute-start | bytes 393224 | tf_op jit(solution)/shard_map/flux_sum/ppermute | solution.py:747
  10.4 3.2 %collective-permute-start.8 = (f32[96,1024]{1,0:T(8,128)}, f32[96,1024]{1,0:T(8,128)S(1)}, u32[]{:S(2)}, u32[]{:S(2)}) collective-permute-start(f32[96,1024]{1,0:T(8,128)} %get-tuple-element.140), channel_id=1, source_target_pairs={{0,8},{1,9},{2,10},{3,11},{4,12},{5,13},{6,14},{7,15},{8,16},{9,17... | collective-permute-start | bytes 1179656 | tf_op jit(solution)/shard_map/row_halo/ppermute | solution.py:741
  13.6 1.3 %collective-permute-start.9 = (f32[96,1024]{1,0:T(8,128)}, f32[96,1024]{1,0:T(8,128)S(1)}, u32[]{:S(2)}, u32[]{:S(2)}) collective-permute-start(f32[96,1024]{1,0:T(8,128)} %get-tuple-element.141), channel_id=1, source_target_pairs={{8,0},{9,1},{10,2},{11,3},{12,4},{13,5},{14,6},{15,7},{16,8},{17,9... | collective-permute-start | bytes 1179656 | tf_op jit(solution)/shard_map/row_halo/ppermute | solution.py:741
  14.9 0.0 collective-permute-done.4
  14.9 0.9 add.135
  15.8 1.4 %collective-permute-start.6 = (f32[8,32,128]{2,1,0:T(8,128)S(1)}, f32[8,32,128]{2,1,0:T(8,128)S(1)}, u32[]{:S(2)}, u32[]{:S(2)}) collective-permute-start(f32[8,32,128]{2,1,0:T(8,128)S(1)} %add.135), channel_id=1, source_target_pairs={{0,2},{1,3},{2,4},{3,5},{4,6},{5,7},{6,0},{7,1},{8,10},{9,11},{10,... | collective-permute-start | bytes 393224 | tf_op jit(solution)/shard_map/flux_sum/ppermute | solution.py:749
  17.2 1.5 %collective-permute-start.7 = (f32[8,32,128]{2,1,0:T(8,128)S(1)}, f32[8,32,128]{2,1,0:T(8,128)S(1)}, u32[]{:S(2)}, u32[]{:S(2)}) collective-permute-start(f32[8,32,128]{2,1,0:T(8,128)S(1)} %add.135), channel_id=1, source_target_pairs={{0,6},{1,7},{2,0},{3,1},{4,2},{5,3},{6,4},{7,5},{8,14},{9,15},{10,... | collective-permute-start | bytes 393224 | tf_op jit(solution)/shard_map/flux_sum/ppermute | solution.py:749
  18.7 1.6 %collective-permute-start.5 = (f32[8,32,128]{2,1,0:T(8,128)S(1)}, f32[8,32,128]{2,1,0:T(8,128)S(1)}, u32[]{:S(2)}, u32[]{:S(2)}) collective-permute-start(f32[8,32,128]{2,1,0:T(8,128)S(1)} %add.135), channel_id=1, source_target_pairs={{0,4},{1,5},{2,6},{3,7},{4,0},{5,1},{6,2},{7,3},{8,12},{9,13},{10,... | collective-permute-start | bytes 393224 | tf_op jit(solution)/shard_map/flux_sum/ppermute | solution.py:749
  20.3 1.8 %collective-permute-done.6 = f32[8,32,128]{2,1,0:T(8,128)S(1)} collective-permute-done((f32[8,32,128]{2,1,0:T(8,128)S(1)}, f32[8,32,128]{2,1,0:T(8,128)S(1)}, u32[]{:S(2)}, u32[]{:S(2)}) %collective-permute-start.6) | collective-permute-done | bytes 131104 | tf_op jit(solution)/shard_map/flux_sum/ppermute | solution.py:749
  22.0 0.0 collective-permute-done.7
  22.0 3.9 %collective-permute-done.5 = f32[8,32,128]{2,1,0:T(8,128)S(1)} collective-permute-done((f32[8,32,128]{2,1,0:T(8,128)S(1)}, f32[8,32,128]{2,1,0:T(8,128)S(1)}, u32[]{:S(2)}, u32[]{:S(2)}) %collective-permute-start.5) | collective-permute-done | bytes 131104 | tf_op jit(solution)/shard_map/flux_sum/ppermute | solution.py:749
  26.0 0.0 collective-permute-done.8.before_ref
  26.0 0.1 collective-permute-done.9.after_ref
  26.1 0.0 copy-done
  26.1 0.0 copy-done.3
  26.1 4.9 %regroup.1 = (f32[8,8,80,128]{3,2,1,0:T(8,128)}, f32[8,128,128]{2,1,0:T(8,128)S(1)}) custom-call(f32[8,64,1024]{2,1,0:T(8,128)S(1)} %copy-done, f32[64,1024]{1,0:T(8,128)S(1)} %copy-done.3, f32[96,1024]{1,0:T(8,128)S(1)} %collective-permute-done.8.before_ref, f32[96,1024]{1,0:T(8,128)S(1)} %collective-permute-done.9.after_ref), custom_call_target="tpu_custom_call" | custom-call | bytes 600000 | tf_op jit(solution)/shard_map/regroup/pallas_call | solution.py:130
  31.0 0.0 copy-start.1
  31.0 0.8 copy-done.1
  31.8 4.2 %collective-permute-start.13 = (f32[8,8,80,128]{3,2,1,0:T(8,128)}, f32[8,8,80,128]{3,2,1,0:T(8,128)}, u32[]{:S(2)}, u32[]{:S(2)}) collective-permute-start(f32[8,8,80,128]{3,2,1,0:T(8,128)} %get-tuple-element.148), channel_id=1, source_target_pairs={{0,1},{1,2},{2,3},{3,4},{4,5},{5,6},{6,7},{8,9},{9,10},{10,11},{11... | collective-permute-start | bytes 7864328 | tf_op jit(solution)/shard_map/depth_halo/ppermute | solution.py:741
  36.0 1.9 %collective-permute-start.14 = (f32[8,8,80,128]{3,2,1,0:T(8,128)}, f32[8,8,80,128]{3,2,1,0:T(8,128)}, u32[]{:S(2)}, u32[]{:S(2)}) collective-permute-start(f32[8,8,80,128]{3,2,1,0:T(8,128)} %get-tuple-element.148), channel_id=1, source_target_pairs={{1,0},{2,1},{3,2},{4,3},{5,4},{6,5},{7,6},{9,8},{10,9},{11,10},{12... | collective-permute-start | bytes 7864328 | tf_op jit(solution)/shard_map/depth_halo/ppermute | solution.py:741
  37.9 0.1 collective-permute-start.10
  38.0 3.7 %collective-permute-start.11 = (f32[8,32,128]{2,1,0:T(8,128)S(1)}, f32[8,32,128]{2,1,0:T(8,128)S(1)}, u32[]{:S(2)}, u32[]{:S(2)}) collective-permute-start(f32[8,32,128]{2,1,0:T(8,128)S(1)} %add_add_fusion.own_ref), channel_id=1, source_target_pairs={{1,9},{3,11},{5,13},{7,15},{8,0},{9,17},{10,2},{11,19},{12,4},{13,... | collective-permute-start | bytes 393224 | tf_op jit(solution)/shard_map/flux_halo/ppermute | solution.py:765
  41.7 2.3 %collective-permute-start.12 = (f32[8,32,128]{2,1,0:T(8,128)S(1)}, f32[8,32,128]{2,1,0:T(8,128)S(1)}, u32[]{:S(2)}, u32[]{:S(2)}) collective-permute-start(f32[8,32,128]{2,1,0:T(8,128)S(1)} %add_add_fusion.own_ref), channel_id=1, source_target_pairs={{1,8},{3,10},{5,12},{7,14},{8,1},{9,16},{10,3},{11,18},{12,5},{13,... | collective-permute-start | bytes 393224 | tf_op jit(solution)/shard_map/flux_halo/ppermute | solution.py:766
  44.0 0.0 collective-permute-done.10.other_ref
  44.0 0.0 collective-permute-done.11.same_ref
  44.0 0.0 copy-start.6
  44.0 4.0 %collective-permute-done.12.cross_ref = f32[8,32,128]{2,1,0:T(8,128)S(1)} collective-permute-done((f32[8,32,128]{2,1,0:T(8,128)S(1)}, f32[8,32,128]{2,1,0:T(8,128)S(1)}, u32[]{:S(2)}, u32[]{:S(2)}) %collective-permute-start.12) | collective-permute-done | bytes 131104 | tf_op jit(solution)/shard_map/flux_halo/ppermute | solution.py:766
  48.0 0.0 copy-start.7
  48.0 0.0 copy-done.6
  48.0 0.6 copy-done.7
  48.6 9.2 %surface_basis.1 = (f32[10,8,16,8,128]{4,3,2,1,0:T(8,128)}, f32[8,128]{1,0:T(8,128)}) custom-call(s32[1,5]{1,0:T(1,128)S(1)} %bitcast.18, f32[8,32,128]{2,1,0:T(8,128)S(1)} %add_add_fusion.own_ref, f32[8,32,128]{2,1,0:T(8,128)S(1)} %collective-permute-done.10.other_ref, f32[8,32,128]{2,1,0:T(8,128)} %copy-done.6, f32[8,32,128]{2,1,0:T(8,128)} %copy-done.7, ...), custom_call_target="tpu_custom_call" | custom-call | bytes 700000 | tf_op jit(solution)/shard_map/surface_basis/pallas_call | solution.py:294
  57.8 0.7 broadcast_in_dim.2
  58.5 18.4 %all_to_all.5.sums_ref = f32[16,8,128]{2,1,0:T(8,128)} all-to-all(f32[16,8,128]{2,1,0:T(8,128)S(1)} %broadcast_in_dim.2), channel_id=1, replica_groups=mesh['vol'=16,'col'=8] {'vol'}, dimensions={0} | all-to-all | bytes 131072 | tf_op jit(solution)/shard_map/gather_sums/all_to_all | solution.py:774
  76.9 0.0 copy-start.2
  76.9 0.0 copy-start.4
  76.9 4.8 %surface_solve.1 = (f32[8,80,128]{2,1,0:T(8,128)}, s32[1,1]{1,0:T(1,128)}) custom-call(f32[10,8,16,8,128]{4,3,2,1,0:T(8,128)} %get-tuple-element.145.basis_ref, f32[16,8,128]{2,1,0:T(8,128)} %all_to_all.5.sums_ref, f32[20,16,128]{2,1,0:T(8,128)} %constant.113.clone.weights_ref), custom_call_target="tpu_custom_call" | custom-call | bytes 300000 | tf_op jit(solution)/shard_map/surface_solve/pallas_call | solution.py:376
  82.4 0.0 collective-permute-done.13
  82.4 0.0 collective-permute-done.14
  82.4 0.0 copy-done.2
  82.4 0.0 copy-done.4
  82.5 33.0 %conditional.1 = ((f32[64,1024]{1,0:T(8,128)}, f32[8,64,1024]{2,1,0:T(8,128)})) conditional(s32[]{:T(128)} %bitcast.9, (s32[]{:T(128)}, f32[8,32,128]{2,1,0:T(8,128)S(1)}, f32[8,32,128]{2,1,0:T(8,128)S(1)}, f32[64,1024]{1,0:T(8,128)S(1)}, s32[1,5]{1,0:T(1,128)S(1)}, /*index=5*/f32[8,8,80,128]{3,2,1,0:T(8,128)}, f32[8,8,80,128]{3,2,1,0:T(8,128)}, ...), branch_computations={%region_0.9_spmd, %region_9.10_spmd} | conditional | flops 3516806 | bytes 15280337 | solution.py:789
  82.7 0.0 copy-start.5
  82.7 2.8 %surface_change.3.change_ref = f32[8,8,64,128]{3,2,1,0:T(8,128)} custom-call(s32[1,5]{1,0:T(1,128)S(1)} %get-tuple-element.118.where_ref, f32[8,80,128]{2,1,0:T(8,128)} %get-tuple-element.122.speed_ref), custom_call_target="tpu_custom_call" | custom-call | bytes 800000 | tf_op jit(solution)/shard_map/cond/branch_1_fun/surface_change/pallas_call | solution.py:519
  85.6 0.0 copy-done.5
  85.6 29.8 %base_sweeps.3 = (f32[64,1024]{1,0:T(8,128)}, f32[8,64,1024]{2,1,0:T(8,128)}) custom-call(s32[1,5]{1,0:T(1,128)S(1)} %get-tuple-element.118.where_ref, f32[8,8,80,128]{3,2,1,0:T(8,128)} %get-tuple-element.119.wide_ref, f32[8,8,80,128]{3,2,1,0:T(8,128)} %get-tuple-element.120.zlow_ref, f32[8,8,80,128]{3,2,1,0:T(8,128)} %get-tuple-element.121.zhigh_ref, ...), custom_call_target="tpu_custom_call" | custom-call | bytes 2500000 | tf_op jit(solution)/shard_map/cond/branch_1_fun/base_sweeps/pallas_call | solution.py:654
  (1 shorter events, 0.0 us)
Async XLA Ops:
  0.6 25.5 %copy-start = (f32[8,64,1024]{2,1,0:T(8,128)S(1)}, f32[8,64,1024]{2,1,0:T(8,128)}, u32[]{:S(2)}) copy-start(f32[8,64,1024]{2,1,0:T(8,128)} %block_ref.3) | copy-start | bytes 6291460
  0.6 25.5 %copy-start.3 = (f32[64,1024]{1,0:T(8,128)S(1)}, f32[64,1024]{1,0:T(8,128)}, u32[]{:S(2)}) copy-start(f32[64,1024]{1,0:T(8,128)} %metric_ref.3) | copy-start | bytes 786436
  8.9 6.0 %collective-permute-start.4 = (f32[8,32,128]{2,1,0:T(8,128)}, f32[8,32,128]{2,1,0:T(8,128)S(1)}, u32[]{:S(2)}, u32[]{:S(2)}) collective-permute-start(f32[8,32,128]{2,1,0:T(8,128)} %get-tuple-element.139), channel_id=1, source_target_pairs={{0,1},{1,0},{2,3},{3,2},{4,5},{5,4},{6,7},{7,6},{8,9},{9,8},{10,11... | collective-permute-start | bytes 393224 | tf_op jit(solution)/shard_map/flux_sum/ppermute | solution.py:747
  10.4 15.6 %collective-permute-start.8 = (f32[96,1024]{1,0:T(8,128)}, f32[96,1024]{1,0:T(8,128)S(1)}, u32[]{:S(2)}, u32[]{:S(2)}) collective-permute-start(f32[96,1024]{1,0:T(8,128)} %get-tuple-element.140), channel_id=1, source_target_pairs={{0,8},{1,9},{2,10},{3,11},{4,12},{5,13},{6,14},{7,15},{8,16},{9,17... | collective-permute-start | bytes 1179656 | tf_op jit(solution)/shard_map/row_halo/ppermute | solution.py:741
  13.6 12.5 %collective-permute-start.9 = (f32[96,1024]{1,0:T(8,128)}, f32[96,1024]{1,0:T(8,128)S(1)}, u32[]{:S(2)}, u32[]{:S(2)}) collective-permute-start(f32[96,1024]{1,0:T(8,128)} %get-tuple-element.141), channel_id=1, source_target_pairs={{8,0},{9,1},{10,2},{11,3},{12,4},{13,5},{14,6},{15,7},{16,8},{17,9... | collective-permute-start | bytes 1179656 | tf_op jit(solution)/shard_map/row_halo/ppermute | solution.py:741
  15.8 6.2 %collective-permute-start.6 = (f32[8,32,128]{2,1,0:T(8,128)S(1)}, f32[8,32,128]{2,1,0:T(8,128)S(1)}, u32[]{:S(2)}, u32[]{:S(2)}) collective-permute-start(f32[8,32,128]{2,1,0:T(8,128)S(1)} %add.135), channel_id=1, source_target_pairs={{0,2},{1,3},{2,4},{3,5},{4,6},{5,7},{6,0},{7,1},{8,10},{9,11},{10,... | collective-permute-start | bytes 393224 | tf_op jit(solution)/shard_map/flux_sum/ppermute | solution.py:749
  17.2 4.8 %collective-permute-start.7 = (f32[8,32,128]{2,1,0:T(8,128)S(1)}, f32[8,32,128]{2,1,0:T(8,128)S(1)}, u32[]{:S(2)}, u32[]{:S(2)}) collective-permute-start(f32[8,32,128]{2,1,0:T(8,128)S(1)} %add.135), channel_id=1, source_target_pairs={{0,6},{1,7},{2,0},{3,1},{4,2},{5,3},{6,4},{7,5},{8,14},{9,15},{10,... | collective-permute-start | bytes 393224 | tf_op jit(solution)/shard_map/flux_sum/ppermute | solution.py:749
  18.7 7.2 %collective-permute-start.5 = (f32[8,32,128]{2,1,0:T(8,128)S(1)}, f32[8,32,128]{2,1,0:T(8,128)S(1)}, u32[]{:S(2)}, u32[]{:S(2)}) collective-permute-start(f32[8,32,128]{2,1,0:T(8,128)S(1)} %add.135), channel_id=1, source_target_pairs={{0,4},{1,5},{2,6},{3,7},{4,0},{5,1},{6,2},{7,3},{8,12},{9,13},{10,... | collective-permute-start | bytes 393224 | tf_op jit(solution)/shard_map/flux_sum/ppermute | solution.py:749
  31.0 0.8 copy-start.1
  31.8 50.7 %collective-permute-start.13 = (f32[8,8,80,128]{3,2,1,0:T(8,128)}, f32[8,8,80,128]{3,2,1,0:T(8,128)}, u32[]{:S(2)}, u32[]{:S(2)}) collective-permute-start(f32[8,8,80,128]{3,2,1,0:T(8,128)} %get-tuple-element.148), channel_id=1, source_target_pairs={{0,1},{1,2},{2,3},{3,4},{4,5},{5,6},{6,7},{8,9},{9,10},{10,11},{11... | collective-permute-start | bytes 7864328 | tf_op jit(solution)/shard_map/depth_halo/ppermute | solution.py:741
  36.0 46.5 %collective-permute-start.14 = (f32[8,8,80,128]{3,2,1,0:T(8,128)}, f32[8,8,80,128]{3,2,1,0:T(8,128)}, u32[]{:S(2)}, u32[]{:S(2)}) collective-permute-start(f32[8,8,80,128]{3,2,1,0:T(8,128)} %get-tuple-element.148), channel_id=1, source_target_pairs={{1,0},{2,1},{3,2},{4,3},{5,4},{6,5},{7,6},{9,8},{10,9},{11,10},{12... | collective-permute-start | bytes 7864328 | tf_op jit(solution)/shard_map/depth_halo/ppermute | solution.py:741
  37.9 6.1 %collective-permute-start.10 = (f32[8,32,128]{2,1,0:T(8,128)S(1)}, f32[8,32,128]{2,1,0:T(8,128)S(1)}, u32[]{:S(2)}, u32[]{:S(2)}) collective-permute-start(f32[8,32,128]{2,1,0:T(8,128)S(1)} %add_add_fusion.own_ref), channel_id=1, source_target_pairs={{0,1},{1,0},{2,3},{3,2},{4,5},{5,4},{6,7},{7,6},{8,9},{9,8},{10,11... | collective-permute-start | bytes 393224 | tf_op jit(solution)/shard_map/flux_halo/ppermute | solution.py:757
  38.0 6.0 %collective-permute-start.11 = (f32[8,32,128]{2,1,0:T(8,128)S(1)}, f32[8,32,128]{2,1,0:T(8,128)S(1)}, u32[]{:S(2)}, u32[]{:S(2)}) collective-permute-start(f32[8,32,128]{2,1,0:T(8,128)S(1)} %add_add_fusion.own_ref), channel_id=1, source_target_pairs={{1,9},{3,11},{5,13},{7,15},{8,0},{9,17},{10,2},{11,19},{12,4},{13,... | collective-permute-start | bytes 393224 | tf_op jit(solution)/shard_map/flux_halo/ppermute | solution.py:765
  41.7 6.3 %collective-permute-start.12 = (f32[8,32,128]{2,1,0:T(8,128)S(1)}, f32[8,32,128]{2,1,0:T(8,128)S(1)}, u32[]{:S(2)}, u32[]{:S(2)}) collective-permute-start(f32[8,32,128]{2,1,0:T(8,128)S(1)} %add_add_fusion.own_ref), channel_id=1, source_target_pairs={{1,8},{3,10},{5,12},{7,14},{8,1},{9,16},{10,3},{11,18},{12,5},{13,... | collective-permute-start | bytes 393224 | tf_op jit(solution)/shard_map/flux_halo/ppermute | solution.py:766
  44.0 4.0 %copy-start.6 = (f32[8,32,128]{2,1,0:T(8,128)}, f32[8,32,128]{2,1,0:T(8,128)S(1)}, u32[]{:S(2)}) copy-start(f32[8,32,128]{2,1,0:T(8,128)S(1)} %collective-permute-done.11.same_ref) | copy-start | bytes 393220
  48.0 0.6 copy-start.7
  76.9 5.5 %copy-start.2 = (bf16[1024,1024]{1,0:T(8,128)(2,1)S(1)}, bf16[1024,1024]{1,0:T(8,128)(2,1)}, u32[]{:S(2)}) copy-start(bf16[1024,1024]{1,0:T(8,128)(2,1)} %constant.112.clone) | copy-start | bytes 6291460
  76.9 5.5 %copy-start.4 = (f32[64,1024]{1,0:T(8,128)S(1)}, f32[64,1024]{1,0:T(8,128)}, u32[]{:S(2)}) copy-start(f32[64,1024]{1,0:T(8,128)} %metric_ref.3) | copy-start | bytes 786436
  82.7 2.9 %copy-start.5 = (f32[8,80,128]{2,1,0:T(8,128)S(1)}, f32[8,80,128]{2,1,0:T(8,128)}, u32[]{:S(2)}) copy-start(f32[8,80,128]{2,1,0:T(8,128)} %get-tuple-element.122.speed_ref) | copy-start | bytes 983044 | tf_op jit(solution)/shard_map/cond

commit v5 on v4

--- a/solution.py
+++ b/solution.py
@@ -63,7 +63,7 @@
 
 SMEM = pl.BlockSpec(memory_space=pltpu.SMEM)
 VMEM = pl.BlockSpec(memory_space=pltpu.VMEM)
-HBM = pl.BlockSpec(memory_space=pl.ANY)
+HBM = pl.BlockSpec(memory_space=pltpu.HBM)
 
 
 def f32(*shape):
@@ -133,7 +133,7 @@
         in_specs=[VMEM] * 4,
         out_specs=(VMEM, VMEM),
         scratch_shapes=[pltpu.VMEM((2 * (Y_ROWS * layers + ROWS), cols), jnp.bfloat16)],
-        compiler_params=params(40),
+        compiler_params=params(32),
         cost_estimate=cost(6),
         name="regroup",
     )(block, metric, before, after)
@@ -148,9 +148,15 @@
 
 def face_kernel(
     where_ref, count_ref, area_ref, speed_ref, node_ref, block_ref, metric_ref,
-    keep_ref, send_ref, up_ref, down_ref, acc_ref, sems,
+    keep_ref, send_ref, up_ref, down_ref, area, speed, nodes, acc_ref, sems,
 ):
     slots = area_ref.shape[1]
+    fetches = [
+        pltpu.make_async_copy(source, target, sems.at[i])
+        for i, (source, target) in enumerate(((area_ref, area), (speed_ref, speed), (node_ref, nodes)))
+    ]
+    for fetch in fetches:
+        fetch.start()
     layers, rows, _ = block_ref.shape
     copies = []
     for out_ref, row, root_row in ((up_ref, rows - DEEP, rows - HALO), (down_ref, 0, 0)):
@@ -159,7 +165,7 @@
             copies.append((part, out_ref.at[pl.ds(DEEP * z, DEEP), :]))
         part = metric_ref.at[pl.ds(root_row, HALO), :]
         copies.append((part, out_ref.at[pl.ds(DEEP * layers, HALO), :]))
-    copies = [pltpu.make_async_copy(*pair, sems.at[i]) for i, pair in enumerate(copies)]
+    copies = [pltpu.make_async_copy(*pair, sems.at[i + 3]) for i, pair in enumerate(copies)]
     for copy in copies:
         copy.start()
     chunk = min(4096, slots)
@@ -170,6 +176,8 @@
     one = jnp.ones((), jnp.bfloat16)
     contract = (((1,), (1,)), ((), ()))
     acc_ref[...] = jnp.zeros_like(acc_ref)
+    for fetch in fetches:
+        fetch.wait()
 
     def wide(x):
         return jnp.broadcast_to(x.astype(jnp.bfloat16), (256, chunk))
@@ -177,8 +185,8 @@
     def body(step, carry):
         at = pl.ds(pl.multiple_of(step * chunk, chunk), chunk)
         slot = lax.broadcasted_iota(jnp.int32, (1, chunk), 1) + step * chunk
-        value = jnp.where(slot < count_ref[0, 0], area_ref[:, at] * speed_ref[:, at], 0.0)
-        node = node_ref[:, at]
+        value = jnp.where(slot < count_ref[0, 0], area[:, at] * speed[:, at], 0.0)
+        node = nodes[:, at]
         low = (((node & 1) << 7) + ((node >> 3) & 127)).astype(jnp.float32)
         high = (((node >> 1) & 3) * 64 + (node >> 10)).astype(jnp.float32)
         first = value.astype(jnp.bfloat16)
@@ -208,13 +216,16 @@
     return pl.pallas_call(
         face_kernel,
         out_shape=(half, half, rows, rows),
-        in_specs=[SMEM, SMEM, VMEM, VMEM, VMEM, HBM, HBM],
+        in_specs=[SMEM, SMEM] + [HBM] * 5,
         out_specs=(VMEM, VMEM, VMEM, VMEM),
         scratch_shapes=[
+            pltpu.VMEM(area.shape, jnp.float32),
+            pltpu.VMEM(area.shape, jnp.float32),
+            pltpu.VMEM(area.shape, jnp.int32),
             pltpu.VMEM((512, 256), jnp.float32),
-            pltpu.SemaphoreType.DMA((2 * layers + 2,)),
+            pltpu.SemaphoreType.DMA((2 * layers + 5,)),
         ],
-        compiler_params=params(58),
+        compiler_params=params(56),
         cost_estimate=cost(7),
         name="face_sums",
     )(where, count, area, speed, node, block, metric)
@@ -222,7 +233,7 @@
 
 def basis_kernel(
     where_ref, own_ref, other_ref, same_ref, cross_ref, root_ref,
-    basis_ref, sums_ref, rows, field, root, outer, line, partial, sems,
+    field, sums_ref, rows, root, outer, line, partial,
 ):
     core = where_ref[0, 0]
     centre = (BASIS_LOW + BASIS_HIGH) / 2
@@ -242,11 +253,11 @@
     group = lax.broadcasted_iota(jnp.int32, (SUB, LANES), 0)
     own_rows = jnp.where((group >= 2) & (group < 6), 1.0, 0.0).astype(jnp.float32)
 
-    def out_copy(k):
-        return pltpu.make_async_copy(field.at[k], basis_ref.at[k], sems.at[k])
-
-    def step(k, begin):
-        out_copy(k).start()
+    def step(k, begin, end):
+        def put(k, t, ys, value):
+            if not end:
+                field[k, t, ys] = value
+
         for ys in range(GROUPS):
             padded = column_ring([field[k, t, ys] * root[t, ys] for t in range(8)])
             for t in range(8):
@@ -260,7 +271,7 @@
                 now = field[k, t, ys]
                 later = outer[t, ys] * mass_line(padded, ys) - (2 * centre * scale) * now
                 later = 0.5 * later if begin else later - field[k - 1, t, ys]
-                field[k + 1, t, ys] = later
+                put(k + 1, t, ys, later)
                 square = square + now * now
                 shifted = shifted + later * now
             squares.append(square)
@@ -275,37 +286,34 @@
         partial[pl.ds(2 * k + 1, 1), :] = add(shifts)
 
     def later_step(k, carry):
-        step(k, False)
+        step(k, False, False)
         return carry
 
     partial[...] = jnp.zeros_like(partial)
-    step(0, True)
-    lax.fori_loop(1, ITERS, later_step, 0)
+    step(0, True, False)
+    lax.fori_loop(1, ITERS - 1, later_step, 0)
+    step(ITERS - 1, False, True)
     whole = jnp.sum(partial[...], axis=1, keepdims=True)
     row = lax.broadcasted_iota(jnp.int32, partial.shape, 0)
     lane = lax.broadcasted_iota(jnp.int32, partial.shape, 1)
     line_of = jnp.sum(jnp.where(row == lane, whole, 0.0), axis=0, keepdims=True)
-    sums_ref[...] = jnp.broadcast_to(line_of, sums_ref.shape)
-    for k in range(ITERS):
-        out_copy(k).wait()
-
-
-def surface_basis(where, own, other, same, cross, root):
+    sums_ref[...] = jnp.broadcast_to(line_of[None], sums_ref.shape)
+
+
+def surface_basis(where, vols, own, other, same, cross, root):
     return pl.pallas_call(
         basis_kernel,
-        out_shape=(f32(ITERS, 8, GROUPS, SUB, LANES), f32(SUB, LANES)),
+        out_shape=(f32(ITERS, 8, GROUPS, SUB, LANES), f32(vols, SUB, LANES)),
         in_specs=[SMEM] + [VMEM] * 5,
-        out_specs=(HBM, VMEM),
+        out_specs=(VMEM, VMEM),
         scratch_shapes=[
             pltpu.VMEM((8, ROWS, LANES), jnp.float32),
-            pltpu.VMEM((ITERS + 1, 8, GROUPS, SUB, LANES), jnp.float32),
             pltpu.VMEM((8, GROUPS, SUB, LANES), jnp.float32),
             pltpu.VMEM((8, GROUPS, SUB, LANES), jnp.float32),
             pltpu.VMEM((GROUPS, 8, SUB, LANES), jnp.float32),
             pltpu.VMEM((24, LANES), jnp.float32),
-            pltpu.SemaphoreType.DMA((ITERS,)),
         ],
-        compiler_params=params(58),
+        compiler_params=params(24),
         cost_estimate=cost(7),
         name="surface_basis",
     )(where, own, other, same, cross, root)
@@ -338,10 +346,8 @@
     return weights.astype(np.float32)
 
 
-def solve_kernel(basis_ref, sums_ref, weights_ref, out_ref, flag_ref, part_ref, rows, sem):
+def solve_kernel(part_ref, sums_ref, weights_ref, out_ref, flag_ref, rows):
     n = ITERS
-    copy = pltpu.make_async_copy(basis_ref, part_ref, sem)
-    copy.start()
     total = sums_ref[0]
     for i in range(1, sums_ref.shape[0]):
         total = total + sums_ref[i]
@@ -361,7 +367,6 @@
     least = jnp.min(jnp.where(inside, figure, 1.0))
     whole = jnp.sum(jnp.where(inside, figure, 0.0))
     flag_ref[0, 0] = jnp.where((least > 0.5) & (whole < CONDITION_MAX), 1, 0).astype(jnp.int32)
-    copy.wait()
     weights = [jnp.broadcast_to(system[k : k + 1, n : n + 1], (SUB, LANES)) for k in range(n)]
     for t in range(8):
         for ys in range(GROUPS):
@@ -376,14 +381,10 @@
     return pl.pallas_call(
         solve_kernel,
         out_shape=(f32(8, Y_ROWS, LANES), jax.ShapeDtypeStruct((1, 1), jnp.int32)),
-        in_specs=[HBM, VMEM, VMEM],
+        in_specs=[VMEM, VMEM, VMEM],
         out_specs=(VMEM, SMEM),
-        scratch_shapes=[
-            pltpu.VMEM(basis.shape, jnp.float32),
-            pltpu.VMEM((8, ROWS, LANES), jnp.float32),
-            pltpu.SemaphoreType.DMA,
-        ],
-        compiler_params=params(58),
+        scratch_shapes=[pltpu.VMEM((8, ROWS, LANES), jnp.float32)],
+        compiler_params=params(24),
         cost_estimate=cost(3),
         name="surface_solve",
     )(basis, sums, jnp.asarray(solve_weights()))
@@ -528,7 +529,7 @@
             pltpu.VMEM((layers, 8, Y_ROWS, LANES), jnp.float32),
             pltpu.SemaphoreType.DMA,
         ],
-        compiler_params=params(58),
+        compiler_params=params(32),
         cost_estimate=cost(8),
         name="surface_change",
     )(where, speed)
@@ -664,7 +665,7 @@
             pltpu.VMEM((2 * (layers + 1) * rows, 8 * LANES), jnp.bfloat16),
             pltpu.SemaphoreType.DMA((5,)),
         ],
-        compiler_params=params(58),
+        compiler_params=params(50),
         cost_estimate=cost(25),
         name="base_sweeps",
     )(where, wide, zlow, zhigh, change, speed, select)
@@ -748,29 +749,28 @@
         turned = [
             lax.ppermute(keep, "col", [(j, (j + 2 * k) % cols) for j in range(cols)]) for k in (1, 2, 3)
         ]
-        own = (keep + turned[1]) + (turned[0] + turned[2])
     with jax.named_scope("row_halo"):
         rows_before, rows_after = moved(rows_up, (1, 0)), moved(rows_down, (-1, 0))
     wide, root = regroup(displacement, surface_metric, rows_before, rows_after)
-    own = after(own, wide)
+    with jax.named_scope("flux_sum"):
+        turned = lax.optimization_barrier((*turned, wide))
+        own = (keep + turned[1]) + (turned[0] + turned[2])
     with jax.named_scope("flux_halo"):
         other = lax.ppermute(own, "col", [(j, j ^ 1) for j in range(cols)])
-        same_pairs, cross_pairs = [], []
+        pairs = []
         for i in range(vols):
             for j in range(cols):
                 to = i - 1 if j % 2 == 0 else i + 1
                 if 0 <= to < vols:
-                    same_pairs.append((i * cols + j, to * cols + j))
-                    cross_pairs.append((i * cols + j, to * cols + (j ^ 1)))
-        same = lax.ppermute(own, ("vol", "col"), same_pairs)
-        cross = lax.ppermute(own, ("vol", "col"), cross_pairs)
+                    pairs.append((i * cols + j, to * cols + j))
+        same = lax.ppermute(own, ("vol", "col"), pairs)
+        cross = lax.ppermute(same, "col", [(j, j ^ 1) for j in range(cols)])
 
     with jax.named_scope("depth_halo"):
-        sent = after(wide, own)
+        sent = after(wide, other)
         zlow, zhigh = moved(sent, (0, 1)), moved(sent, (0, -1))
-    basis, sums = surface_basis(where, own, other, same, cross, root)
+    basis, spread = surface_basis(where, vols, own, other, same, cross, root)
     with jax.named_scope("gather_sums"):
-        spread = jnp.broadcast_to(sums[None], (vols,) + sums.shape)
         gathered = lax.all_to_all(spread, "vol", 0, 0)
     speed, flag = surface_solve(basis, gathered)
 

time: 116 us -> 108 us (0.931)
  Pallas kernels: 58.9 us -> 54.6 us
  waiting for transfers between devices: 9.73 us -> 7.34 us
  local copies, waits for them, and re-layouts: 2.23 us -> 0.12 us
    ppermute x3, waiting for transfers between devices: 5.66 us -> 0.01 us  [on_device(): lax.ppermute(keep, 'col', [(j, (j + 2 * k) % cols) for j in range(cols)])]
    pallas_call x1, Pallas kernels: 4.84 us -> 2.28 us  [surface_solve(): pl.pallas_call(solve_kernel, out_shape=(f32(8, Y_ROWS, LANES), jax.ShapeD...]
    ppermute x4, waiting for transfers between devices: 0.11 us -> 2.24 us  [moved(): return lax.ppermute(x, ('vol', 'col'), pairs)]
    ppermute x1, starting transfers between devices: 0.09 us -> 1.95 us  [on_device(): other = lax.ppermute(own, 'col', [(j, j ^ 1) for j in range(cols)])]
    ppermute x2, starting transfers between devices: 5.97 us -> 4.31 us  [the longest x1 3.1 us: on_device(): same = lax.ppermute(own, ('vol', 'col'), pairs)]
    pallas_call x1, Pallas kernels: 9.19 us -> 7.54 us  [surface_basis(): pl.pallas_call(basis_kernel, out_shape=(f32(ITERS, 8, GROUPS, SUB, LANES)...]
    unnamed x14 -> x10, local copies, waits for them, and re-layouts: 1.46 us -> 0.03 us
    ppermute x1, waiting for transfers between devices: 0.01 us -> 1.2 us  [on_device(): keep = keep + lax.ppermute(send, 'col', [(j, j ^ 1) for j in range(cols)])]
  transfers between devices with their start and end apart: 11 -> 11, of which waited for: 4 -> 5; matrix products, arithmetic and copies ran while one was open for 1% -> 1% of each run, Pallas kernels for 12% -> 14%
where the time goes in v5:
time: 108 us; the launch traced here: 107 us
  Pallas kernels  54.6 us (51%)
  starting transfers between devices  23.4 us (22%)
  blocking collectives  17.7 us (16%)
  waiting for transfers between devices  7.34 us (7%)
  between operations  2.4 us (2%)
    pallas_call x1, Pallas kernels, base_sweeps(): pl.pallas_call(base_kernel, out_shape=(f32(rows, 8 * LANES), f32(layers,...  29.9 us
    all_to_all x1, blocking collectives, on_device(): gathered = lax.all_to_all(spread, 'vol', 0, 0)  17.7 us
    ppermute x4, starting transfers between devices, moved(): return lax.ppermute(x, ('vol', 'col'), pairs)  11.1 us
    pallas_call x1, Pallas kernels, face_sums(): pl.pallas_call(face_kernel, out_shape=(half, half, rows, rows), in_specs=...  7.84 us
    pallas_call x1, Pallas kernels, surface_basis(): pl.pallas_call(basis_kernel, out_shape=(f32(ITERS, 8, GROUPS, SUB, LANES)...  7.54 us
    ppermute x3, starting transfers between devices, on_device(): lax.ppermute(keep, 'col', [(j, (j + 2 * k) % cols) for j in range(cols)])  5.06 us
    pallas_call x1, Pallas kernels, regroup(): pl.pallas_call(regroup_kernel, out_shape=(f32(layers, 8, Y_ROWS, LANES),...  4.88 us
    ppermute x1, starting transfers between devices, on_device(): same = lax.ppermute(own, ('vol', 'col'), pairs)  3.1 us
  transfers between devices with their start and end apart: 11, of which 5 were waited for; matrix products, arithmetic and copies ran while one was open for 1% of the time, Pallas kernels for 14%

profile of v5, /device:TPU:1, one launch (start us, length us, event | category | flops | bytes accessed | tf_op | source)
XLA Modules:
  0.0 106.8 jit_solution(14383187732701054188)
XLA Ops:
  0.6 0.0 copy-start
  0.6 0.0 copy-start.3
  1.5 0.1 stack.15
  1.5 7.8 %face_sums.1 = (f32[8,32,128]{2,1,0:T(8,128)}, f32[8,32,128]{2,1,0:T(8,128)}, f32[96,1024]{1,0:T(8,128)}, f32[96,1024]{1,0:T(8,128)}) custom-call(s32[1,5]{1,0:T(1,128)S(1)} %bitcast.17, s32[1,1]{1,0:T(1,128)S(6)} %copy.41.count_ref, f32[1,16384]{1,0:T(1,128)} %area_ref.1, f32[1,16384]{1,0:T(1,128)} %speed_ref.1, s32[1,16384]{1,0:T(1,128)} %node_ref.1, ...), custom_call_target="tpu_custom_call" | custom-call | bytes 700000 | tf_op jit(solution)/shard_map/face_sums/pallas_call | solution.py:216
  9.4 4.0 %collective-permute-start.8 = (f32[96,1024]{1,0:T(8,128)}, f32[96,1024]{1,0:T(8,128)S(1)}, u32[]{:S(2)}, u32[]{:S(2)}) collective-permute-start(f32[96,1024]{1,0:T(8,128)} %get-tuple-element.142), channel_id=1, source_target_pairs={{0,8},{1,9},{2,10},{3,11},{4,12},{5,13},{6,14},{7,15},{8,16},{9,17... | collective-permute-start | bytes 1179656 | tf_op jit(solution)/shard_map/row_halo/ppermute | solution.py:742
  13.4 1.3 %collective-permute-start.9 = (f32[96,1024]{1,0:T(8,128)}, f32[96,1024]{1,0:T(8,128)S(1)}, u32[]{:S(2)}, u32[]{:S(2)}) collective-permute-start(f32[96,1024]{1,0:T(8,128)} %get-tuple-element.143), channel_id=1, source_target_pairs={{8,0},{9,1},{10,2},{11,3},{12,4},{13,5},{14,6},{15,7},{16,8},{17,9... | collective-permute-start | bytes 1179656 | tf_op jit(solution)/shard_map/row_halo/ppermute | solution.py:742
  14.7 1.0 collective-permute-start.4
  15.7 1.2 %collective-permute-done.4 = f32[8,32,128]{2,1,0:T(8,128)S(1)} collective-permute-done((f32[8,32,128]{2,1,0:T(8,128)}, f32[8,32,128]{2,1,0:T(8,128)S(1)}, u32[]{:S(2)}, u32[]{:S(2)}) %collective-permute-start.4) | collective-permute-done | bytes 131104 | tf_op jit(solution)/shard_map/flux_sum/ppermute | solution.py:748
  16.9 0.9 add.135
  17.8 0.0 copy-start.1
  17.8 1.4 %collective-permute-start.5 = (f32[8,32,128]{2,1,0:T(8,128)S(1)}, f32[8,32,128]{2,1,0:T(8,128)S(1)}, u32[]{:S(2)}, u32[]{:S(2)}) collective-permute-start(f32[8,32,128]{2,1,0:T(8,128)S(1)} %add.135), channel_id=1, source_target_pairs={{0,2},{1,3},{2,4},{3,5},{4,6},{5,7},{6,0},{7,1},{8,10},{9,11},{10,... | collective-permute-start | bytes 393224 | tf_op jit(solution)/shard_map/flux_sum/ppermute | solution.py:750
  19.2 2.6 %collective-permute-start.6 = (f32[8,32,128]{2,1,0:T(8,128)S(1)}, f32[8,32,128]{2,1,0:T(8,128)S(1)}, u32[]{:S(2)}, u32[]{:S(2)}) collective-permute-start(f32[8,32,128]{2,1,0:T(8,128)S(1)} %add.135), channel_id=1, source_target_pairs={{0,4},{1,5},{2,6},{3,7},{4,0},{5,1},{6,2},{7,3},{8,12},{9,13},{10,... | collective-permute-start | bytes 393224 | tf_op jit(solution)/shard_map/flux_sum/ppermute | solution.py:750
  21.8 1.1 %collective-permute-start.7 = (f32[8,32,128]{2,1,0:T(8,128)S(1)}, f32[8,32,128]{2,1,0:T(8,128)S(1)}, u32[]{:S(2)}, u32[]{:S(2)}) collective-permute-start(f32[8,32,128]{2,1,0:T(8,128)S(1)} %add.135), channel_id=1, source_target_pairs={{0,6},{1,7},{2,0},{3,1},{4,2},{5,3},{6,4},{7,5},{8,14},{9,15},{10,... | collective-permute-start | bytes 393224 | tf_op jit(solution)/shard_map/flux_sum/ppermute | solution.py:750
  22.9 0.0 collective-permute-done.8.before_ref
  22.9 2.2 %collective-permute-done.9.after_ref = f32[96,1024]{1,0:T(8,128)S(1)} collective-permute-done((f32[96,1024]{1,0:T(8,128)}, f32[96,1024]{1,0:T(8,128)S(1)}, u32[]{:S(2)}, u32[]{:S(2)}) %collective-permute-start.9) | collective-permute-done | bytes 393248 | tf_op jit(solution)/shard_map/row_halo/ppermute | solution.py:742
  25.1 0.0 copy-done
  25.1 0.0 copy-done.3
  25.1 4.9 %regroup.1 = (f32[8,8,80,128]{3,2,1,0:T(8,128)}, f32[8,128,128]{2,1,0:T(8,128)S(1)}) custom-call(f32[8,64,1024]{2,1,0:T(8,128)S(1)} %copy-done, f32[64,1024]{1,0:T(8,128)S(1)} %copy-done.3, f32[96,1024]{1,0:T(8,128)S(1)} %collective-permute-done.8.before_ref, f32[96,1024]{1,0:T(8,128)S(1)} %collective-permute-done.9.after_ref), custom_call_target="tpu_custom_call" | custom-call | bytes 600000 | tf_op jit(solution)/shard_map/regroup/pallas_call | solution.py:130
  30.0 0.0 collective-permute-done.5
  30.0 0.0 collective-permute-done.6
  30.0 0.0 collective-permute-done.7
  30.1 1.9 %collective-permute-start.10 = (f32[8,32,128]{2,1,0:T(8,128)S(1)}, f32[8,32,128]{2,1,0:T(8,128)S(1)}, u32[]{:S(2)}, u32[]{:S(2)}) collective-permute-start(f32[8,32,128]{2,1,0:T(8,128)S(1)} %add_add_fusion.own_ref), channel_id=1, source_target_pairs={{0,1},{1,0},{2,3},{3,2},{4,5},{5,4},{6,7},{7,6},{8,9},{9,8},{10,11... | collective-permute-start | bytes 393224 | tf_op jit(solution)/shard_map/flux_halo/ppermute | solution.py:759
  32.0 1.0 collective-permute-done.10.other_ref
  33.0 3.4 %collective-permute-start.13 = (f32[8,8,80,128]{3,2,1,0:T(8,128)}, f32[8,8,80,128]{3,2,1,0:T(8,128)}, u32[]{:S(2)}, u32[]{:S(2)}) collective-permute-start(f32[8,8,80,128]{3,2,1,0:T(8,128)} %get-tuple-element.152), channel_id=1, source_target_pairs={{0,1},{1,2},{2,3},{3,4},{4,5},{5,6},{6,7},{8,9},{9,10},{10,11},{11... | collective-permute-start | bytes 7864328 | tf_op jit(solution)/shard_map/depth_halo/ppermute | solution.py:742
  36.5 2.4 %collective-permute-start.14 = (f32[8,8,80,128]{3,2,1,0:T(8,128)}, f32[8,8,80,128]{3,2,1,0:T(8,128)}, u32[]{:S(2)}, u32[]{:S(2)}) collective-permute-start(f32[8,8,80,128]{3,2,1,0:T(8,128)} %get-tuple-element.152), channel_id=1, source_target_pairs={{1,0},{2,1},{3,2},{4,3},{5,4},{6,5},{7,6},{9,8},{10,9},{11,10},{12... | collective-permute-start | bytes 7864328 | tf_op jit(solution)/shard_map/depth_halo/ppermute | solution.py:742
  38.8 3.1 %collective-permute-start.11 = (f32[8,32,128]{2,1,0:T(8,128)S(1)}, f32[8,32,128]{2,1,0:T(8,128)S(1)}, u32[]{:S(2)}, u32[]{:S(2)}) collective-permute-start(f32[8,32,128]{2,1,0:T(8,128)S(1)} %add_add_fusion.own_ref), channel_id=1, source_target_pairs={{1,9},{3,11},{5,13},{7,15},{8,0},{9,17},{10,2},{11,19},{12,4},{13,... | collective-permute-start | bytes 393224 | tf_op jit(solution)/shard_map/flux_halo/ppermute | solution.py:766
  42.0 1.9 %collective-permute-done.11.same_ref = f32[8,32,128]{2,1,0:T(8,128)S(1)} collective-permute-done((f32[8,32,128]{2,1,0:T(8,128)S(1)}, f32[8,32,128]{2,1,0:T(8,128)S(1)}, u32[]{:S(2)}, u32[]{:S(2)}) %collective-permute-start.11) | collective-permute-done | bytes 131104 | tf_op jit(solution)/shard_map/flux_halo/ppermute | solution.py:766
  43.9 1.2 %collective-permute-start.12 = (f32[8,32,128]{2,1,0:T(8,128)S(1)}, f32[8,32,128]{2,1,0:T(8,128)S(1)}, u32[]{:S(2)}, u32[]{:S(2)}) collective-permute-start(f32[8,32,128]{2,1,0:T(8,128)S(1)} %collective-permute-done.11.same_ref), channel_id=1, source_target_pairs={{0,1},{1,0},{2,3},{3,2},{4,5},{5,4},{6,7},{7,6},{8,9},{9,8},{10,11... | collective-permute-start | bytes 393224 | tf_op jit(solution)/shard_map/flux_halo/ppermute | solution.py:767
  45.1 1.0 collective-permute-done.12.cross_ref
  46.1 7.5 %surface_basis.1 = (f32[10,8,16,8,128]{4,3,2,1,0:T(8,128)S(1)}, f32[16,8,128]{2,1,0:T(8,128)S(1)}) custom-call(s32[1,5]{1,0:T(1,128)S(1)} %bitcast.18, f32[8,32,128]{2,1,0:T(8,128)S(1)} %add_add_fusion.own_ref, f32[8,32,128]{2,1,0:T(8,128)S(1)} %collective-permute-done.10.other_ref, f32[8,32,128]{2,1,0:T(8,128)S(1)} %collective-permute-done.11.same_ref, ...), custom_call_target="tpu_custom_call" | custom-call | bytes 700000 | tf_op jit(solution)/shard_map/surface_basis/pallas_call | solution.py:304
  53.6 17.7 %all_to_all.5.sums_ref = f32[16,8,128]{2,1,0:T(8,128)S(1)} all-to-all(f32[16,8,128]{2,1,0:T(8,128)S(1)} %get-tuple-element.150), channel_id=1, replica_groups=mesh['vol'=16,'col'=8] {'vol'}, dimensions={0} | all-to-all | bytes 131072 | tf_op jit(solution)/shard_map/gather_sums/all_to_all | solution.py:774
  71.3 0.0 copy-done.1
  71.3 0.0 copy-start.2
  71.3 0.0 copy-start.4
  71.4 2.3 %surface_solve.1 = (f32[8,80,128]{2,1,0:T(8,128)}, s32[1,1]{1,0:T(1,128)}) custom-call(f32[10,8,16,8,128]{4,3,2,1,0:T(8,128)S(1)} %get-tuple-element.149.part_ref, f32[16,8,128]{2,1,0:T(8,128)S(1)} %all_to_all.5.sums_ref, f32[20,16,128]{2,1,0:T(8,128)S(1)} %copy-done.1), custom_call_target="tpu_custom_call" | custom-call | bytes 300000 | tf_op jit(solution)/shard_map/surface_solve/pallas_call | solution.py:381
  74.3 0.0 collective-permute-done.13
  74.3 0.0 collective-permute-done.14
  74.3 0.0 copy-done.2
  74.3 0.0 copy-done.4
  74.3 32.3 %conditional.1 = ((f32[64,1024]{1,0:T(8,128)}, f32[8,64,1024]{2,1,0:T(8,128)})) conditional(s32[]{:T(128)} %bitcast.9, (s32[]{:T(128)}, f32[8,32,128]{2,1,0:T(8,128)S(1)}, f32[8,32,128]{2,1,0:T(8,128)S(1)}, f32[64,1024]{1,0:T(8,128)S(1)}, s32[1,5]{1,0:T(1,128)S(1)}, /*index=5*/f32[8,8,80,128]{3,2,1,0:T(8,128)}, f32[8,8,80,128]{3,2,1,0:T(8,128)}, ...), branch_computations={%region_0.9_spmd, %region_9.10_spmd} | conditional | flops 3516806 | bytes 15280337 | solution.py:789
  74.6 0.0 copy-start.5
  74.6 2.2 %surface_change.3.change_ref = f32[8,8,64,128]{3,2,1,0:T(8,128)S(1)} custom-call(s32[1,5]{1,0:T(1,128)S(1)} %get-tuple-element.118.where_ref, f32[8,80,128]{2,1,0:T(8,128)} %get-tuple-element.122.speed_ref), custom_call_target="tpu_custom_call" | custom-call | bytes 800000 | tf_op jit(solution)/shard_map/cond/branch_1_fun/surface_change/pallas_call | solution.py:520
  76.8 0.0 copy-done.5
  76.8 29.9 %base_sweeps.3 = (f32[64,1024]{1,0:T(8,128)}, f32[8,64,1024]{2,1,0:T(8,128)}) custom-call(s32[1,5]{1,0:T(1,128)S(1)} %get-tuple-element.118.where_ref, f32[8,8,80,128]{3,2,1,0:T(8,128)} %get-tuple-element.119.wide_ref, f32[8,8,80,128]{3,2,1,0:T(8,128)} %get-tuple-element.120.zlow_ref, f32[8,8,80,128]{3,2,1,0:T(8,128)} %get-tuple-element.121.zhigh_ref, ...), custom_call_target="tpu_custom_call" | custom-call | bytes 2500000 | tf_op jit(solution)/shard_map/cond/branch_1_fun/base_sweeps/pallas_call | solution.py:655
  (1 shorter events, 0.0 us)
Async XLA Ops:
  0.6 24.5 %copy-start = (f32[8,64,1024]{2,1,0:T(8,128)S(1)}, f32[8,64,1024]{2,1,0:T(8,128)}, u32[]{:S(2)}) copy-start(f32[8,64,1024]{2,1,0:T(8,128)} %block_ref.3) | copy-start | bytes 6291460
  0.6 24.5 %copy-start.3 = (f32[64,1024]{1,0:T(8,128)S(1)}, f32[64,1024]{1,0:T(8,128)}, u32[]{:S(2)}) copy-start(f32[64,1024]{1,0:T(8,128)} %metric_ref.3) | copy-start | bytes 786436
  9.4 13.5 %collective-permute-start.8 = (f32[96,1024]{1,0:T(8,128)}, f32[96,1024]{1,0:T(8,128)S(1)}, u32[]{:S(2)}, u32[]{:S(2)}) collective-permute-start(f32[96,1024]{1,0:T(8,128)} %get-tuple-element.142), channel_id=1, source_target_pairs={{0,8},{1,9},{2,10},{3,11},{4,12},{5,13},{6,14},{7,15},{8,16},{9,17... | collective-permute-start | bytes 1179656 | tf_op jit(solution)/shard_map/row_halo/ppermute | solution.py:742
  13.4 11.8 %collective-permute-start.9 = (f32[96,1024]{1,0:T(8,128)}, f32[96,1024]{1,0:T(8,128)S(1)}, u32[]{:S(2)}, u32[]{:S(2)}) collective-permute-start(f32[96,1024]{1,0:T(8,128)} %get-tuple-element.143), channel_id=1, source_target_pairs={{8,0},{9,1},{10,2},{11,3},{12,4},{13,5},{14,6},{15,7},{16,8},{17,9... | collective-permute-start | bytes 1179656 | tf_op jit(solution)/shard_map/row_halo/ppermute | solution.py:742
  14.7 2.2 %collective-permute-start.4 = (f32[8,32,128]{2,1,0:T(8,128)}, f32[8,32,128]{2,1,0:T(8,128)S(1)}, u32[]{:S(2)}, u32[]{:S(2)}) collective-permute-start(f32[8,32,128]{2,1,0:T(8,128)} %get-tuple-element.141), channel_id=1, source_target_pairs={{0,1},{1,0},{2,3},{3,2},{4,5},{5,4},{6,7},{7,6},{8,9},{9,8},{10,11... | collective-permute-start | bytes 393224 | tf_op jit(solution)/shard_map/flux_sum/ppermute | solution.py:748
  17.8 53.5 %copy-start.1 = (f32[20,16,128]{2,1,0:T(8,128)S(1)}, f32[20,16,128]{2,1,0:T(8,128)}, u32[]{:S(2)}) copy-start(f32[20,16,128]{2,1,0:T(8,128)} %constant.113.clone.weights_ref) | copy-start | bytes 491524
  17.8 12.2 %collective-permute-start.5 = (f32[8,32,128]{2,1,0:T(8,128)S(1)}, f32[8,32,128]{2,1,0:T(8,128)S(1)}, u32[]{:S(2)}, u32[]{:S(2)}) collective-permute-start(f32[8,32,128]{2,1,0:T(8,128)S(1)} %add.135), channel_id=1, source_target_pairs={{0,2},{1,3},{2,4},{3,5},{4,6},{5,7},{6,0},{7,1},{8,10},{9,11},{10,... | collective-permute-start | bytes 393224 | tf_op jit(solution)/shard_map/flux_sum/ppermute | solution.py:750
  19.2 10.8 %collective-permute-start.6 = (f32[8,32,128]{2,1,0:T(8,128)S(1)}, f32[8,32,128]{2,1,0:T(8,128)S(1)}, u32[]{:S(2)}, u32[]{:S(2)}) collective-permute-start(f32[8,32,128]{2,1,0:T(8,128)S(1)} %add.135), channel_id=1, source_target_pairs={{0,4},{1,5},{2,6},{3,7},{4,0},{5,1},{6,2},{7,3},{8,12},{9,13},{10,... | collective-permute-start | bytes 393224 | tf_op jit(solution)/shard_map/flux_sum/ppermute | solution.py:750
  21.8 8.2 %collective-permute-start.7 = (f32[8,32,128]{2,1,0:T(8,128)S(1)}, f32[8,32,128]{2,1,0:T(8,128)S(1)}, u32[]{:S(2)}, u32[]{:S(2)}) collective-permute-start(f32[8,32,128]{2,1,0:T(8,128)S(1)} %add.135), channel_id=1, source_target_pairs={{0,6},{1,7},{2,0},{3,1},{4,2},{5,3},{6,4},{7,5},{8,14},{9,15},{10,... | collective-permute-start | bytes 393224 | tf_op jit(solution)/shard_map/flux_sum/ppermute | solution.py:750
  30.1 2.9 %collective-permute-start.10 = (f32[8,32,128]{2,1,0:T(8,128)S(1)}, f32[8,32,128]{2,1,0:T(8,128)S(1)}, u32[]{:S(2)}, u32[]{:S(2)}) collective-permute-start(f32[8,32,128]{2,1,0:T(8,128)S(1)} %add_add_fusion.own_ref), channel_id=1, source_target_pairs={{0,1},{1,0},{2,3},{3,2},{4,5},{5,4},{6,7},{7,6},{8,9},{9,8},{10,11... | collective-permute-start | bytes 393224 | tf_op jit(solution)/shard_map/flux_halo/ppermute | solution.py:759
  33.0 41.3 %collective-permute-start.13 = (f32[8,8,80,128]{3,2,1,0:T(8,128)}, f32[8,8,80,128]{3,2,1,0:T(8,128)}, u32[]{:S(2)}, u32[]{:S(2)}) collective-permute-start(f32[8,8,80,128]{3,2,1,0:T(8,128)} %get-tuple-element.152), channel_id=1, source_target_pairs={{0,1},{1,2},{2,3},{3,4},{4,5},{5,6},{6,7},{8,9},{9,10},{10,11},{11... | collective-permute-start | bytes 7864328 | tf_op jit(solution)/shard_map/depth_halo/ppermute | solution.py:742
  36.5 37.9 %collective-permute-start.14 = (f32[8,8,80,128]{3,2,1,0:T(8,128)}, f32[8,8,80,128]{3,2,1,0:T(8,128)}, u32[]{:S(2)}, u32[]{:S(2)}) collective-permute-start(f32[8,8,80,128]{3,2,1,0:T(8,128)} %get-tuple-element.152), channel_id=1, source_target_pairs={{1,0},{2,1},{3,2},{4,3},{5,4},{6,5},{7,6},{9,8},{10,9},{11,10},{12... | collective-permute-start | bytes 7864328 | tf_op jit(solution)/shard_map/depth_halo/ppermute | solution.py:742
  38.8 5.0 %collective-permute-start.11 = (f32[8,32,128]{2,1,0:T(8,128)S(1)}, f32[8,32,128]{2,1,0:T(8,128)S(1)}, u32[]{:S(2)}, u32[]{:S(2)}) collective-permute-start(f32[8,32,128]{2,1,0:T(8,128)S(1)} %add_add_fusion.own_ref), channel_id=1, source_target_pairs={{1,9},{3,11},{5,13},{7,15},{8,0},{9,17},{10,2},{11,19},{12,4},{13,... | collective-permute-start | bytes 393224 | tf_op jit(solution)/shard_map/flux_halo/ppermute | solution.py:766
  43.9 2.2 %collective-permute-start.12 = (f32[8,32,128]{2,1,0:T(8,128)S(1)}, f32[8,32,128]{2,1,0:T(8,128)S(1)}, u32[]{:S(2)}, u32[]{:S(2)}) collective-permute-start(f32[8,32,128]{2,1,0:T(8,128)S(1)} %collective-permute-done.11.same_ref), channel_id=1, source_target_pairs={{0,1},{1,0},{2,3},{3,2},{4,5},{5,4},{6,7},{7,6},{8,9},{9,8},{10,11... | collective-permute-start | bytes 393224 | tf_op jit(solution)/shard_map/flux_halo/ppermute | solution.py:767
  71.3 3.0 %copy-start.2 = (bf16[1024,1024]{1,0:T(8,128)(2,1)S(1)}, bf16[1024,1024]{1,0:T(8,128)(2,1)}, u32[]{:S(2)}) copy-start(bf16[1024,1024]{1,0:T(8,128)(2,1)} %constant.112.clone) | copy-start | bytes 6291460
  71.3 3.0 %copy-start.4 = (f32[64,1024]{1,0:T(8,128)S(1)}, f32[64,1024]{1,0:T(8,128)}, u32[]{:S(2)}) copy-start(f32[64,1024]{1,0:T(8,128)} %metric_ref.3) | copy-start | bytes 786436
  74.6 2.2 %copy-start.5 = (f32[8,80,128]{2,1,0:T(8,128)S(1)}, f32[8,80,128]{2,1,0:T(8,128)}, u32[]{:S(2)}) copy-start(f32[8,80,128]{2,1,0:T(8,128)} %get-tuple-element.122.speed_ref) | copy-start | bytes 983044 | tf_op jit(solution)/shard_map/cond

commit v6 on v5

--- a/solution.py
+++ b/solution.py
@@ -51,14 +51,22 @@
     i = index + 2
     near = padded[i - 1] + padded[i + 1]
     if index % 2:
-        return near + 8.0 * padded[i]
-    return (near + 4.0 * padded[i]) - 0.5 * (padded[i - 2] + padded[i + 2])
+        return near + 4.0 * padded[i]
+    return (near + 8.0 * padded[i]) - (padded[i - 2] + padded[i + 2])
 
 
 def both_line(padded, index):
     i = index + 2
     near = padded[i - 1] + padded[i + 1]
-    return (16.0 / 3.0 if index % 2 else 11.0 / 3.0) * padded[i] - near
+    return (8.0 / 3.0 if index % 2 else 22.0 / 3.0) * padded[i] - near
+
+
+def stored(parity):
+    return 1.0 if parity else 0.5
+
+
+def given(parity):
+    return 0.5 if parity else 1.0
 
 
 SMEM = pl.BlockSpec(memory_space=pltpu.SMEM)
@@ -111,6 +119,8 @@
         put(Y_ROWS * z, before_ref[DEEP * z : DEEP * (z + 1), :])
         put(Y_ROWS * z + DEEP, block_ref[z])
         put(Y_ROWS * z + DEEP + rows, after_ref[DEEP * z : DEEP * (z + 1), :])
+    row = lax.broadcasted_iota(jnp.int32, (Y_ROWS, LANES), 0)
+    by_row = jnp.where(row % 2 == 0, stored(0), stored(1)).astype(jnp.float32)
     at = layers * Y_ROWS
     put(at, jnp.sqrt(before_ref[packed:, :]))
     put(at + HALO, jnp.sqrt(metric_ref[...]))
@@ -121,7 +131,7 @@
         for i in range(2):
             tile = pair[:, LANES * i : LANES * (i + 1)]
             for z in range(layers):
-                wide_ref[z, j + i] = tile[Y_ROWS * z : Y_ROWS * (z + 1)]
+                wide_ref[z, j + i] = tile[Y_ROWS * z : Y_ROWS * (z + 1)] * (by_row * (stored(z % 2) * stored(i)))
             root_ref[j + i] = tile[layers * Y_ROWS :]
 
 
@@ -247,8 +257,8 @@
         for ys in range(GROUPS):
             field[0, t, ys] = rows[t, pl.ds(ys, SUB, stride=GROUPS), :]
             value = root_ref[t, pl.ds(ys, SUB, stride=GROUPS), :]
-            root[t, ys] = value
-            outer[t, ys] = value * (2 * scale * 4.0 / 225.0)
+            root[t, ys] = value * (stored(t % 2) * stored(ys % 2))
+            outer[t, ys] = value * (2 * scale * 4.0 / 225.0 / (given(t % 2) * given(ys % 2)))
 
     group = lax.broadcasted_iota(jnp.int32, (SUB, LANES), 0)
     own_rows = jnp.where((group >= 2) & (group < 6), 1.0, 0.0).astype(jnp.float32)
@@ -390,8 +400,8 @@
     )(basis, sums, jnp.asarray(solve_weights()))
 
 
-def fill_factors(factor, where_ref, rows):
-    vol, vols = where_ref[0, 3], where_ref[0, 4]
+def factor_kernel(where_ref, factor):
+    vol, vols, rows = where_ref[0, 3], where_ref[0, 4], where_ref[0, 5]
     group = lax.broadcasted_iota(jnp.int32, (SUB, LANES), 0)
     mass, stiff = (8.0, 16.0), (14.0, 16.0)
     for ys in range(Y_GROUPS):
@@ -404,7 +414,21 @@
                     stiff[pz] * mass[py] * mass[px]
                     + mass[pz] * (stiff[py] * mass[px] + mass[py] * stiff[px])
                 )
+                for p in (pz, py, px):
+                    value = value * stored(p) / given(p)
                 factor[pz, px, ys] = jnp.where(outside, 0.0, jnp.float32(value))
+
+
+def relaxation_factors(where):
+    return pl.pallas_call(
+        factor_kernel,
+        out_shape=f32(2, 2, Y_GROUPS, SUB, LANES),
+        in_specs=[SMEM],
+        out_specs=VMEM,
+        compiler_params=params(16),
+        cost_estimate=cost(1),
+        name="relaxation_factors",
+    )(where)
 
 
 def lateral_lines(get, line_a, line_b, put):
@@ -421,12 +445,13 @@
             put(t, ys, mass_line(a, ys), both_line(a, ys) + mass_line(b, ys))
 
 
-def pair_steps(w, c):
+def even_step(w, c):
     near = c[1] + c[3]
-    even = (11.0 / 3.0 * w[1] - (w[0] + w[2])) + ((near + 4.0 * c[2]) - 0.5 * (c[0] + c[4]))
-    near = c[2] + c[4]
-    odd = (16.0 / 3.0 * w[2] - (w[1] + w[3])) + (near + 8.0 * c[3])
-    return even, odd
+    return (22.0 / 3.0 * w[1] - (w[0] + w[2])) + ((near + 8.0 * c[2]) - (c[0] + c[4]))
+
+
+def odd_step(w, c):
+    return (8.0 / 3.0 * w[1] - (w[0] + w[2])) + ((c[0] + c[2]) + 4.0 * c[1])
 
 
 def strided(ys):
@@ -434,7 +459,7 @@
 
 
 def change_kernel(
-    where_ref, speed_ref, out_ref, cells, along, cross, line_a, line_b, factor, plain, sem,
+    where_ref, factor, speed_ref, out_ref, cells, along, cross, line_a, line_b, plain, sems,
 ):
     col = where_ref[0, 1]
     layers, _, rows, _ = out_ref.shape
@@ -450,94 +475,99 @@
     def set_top():
         for t in range(8):
             for ys in range(Y_GROUPS):
-                cells[2, t, ys] = 0.5 * speed_ref[t, strided(ys), :]
-
-    def send(count):
-        for z in range(count):
+                scale = 0.5 * stored(0) * stored(t % 2) * stored(ys % 2)
+                cells[2, t, ys] = scale * speed_ref[t, strided(ys), :]
+
+    def send(first, count):
+        copies = []
+        for z in range(first, first + count):
             for t in range(8):
                 for ys in range(Y_GROUPS):
                     plain[z, t, strided(ys), :] = cells[z + 2, t, ys]
-        copy = pltpu.make_async_copy(
-            plain.at[pl.ds(0, count), :, pl.ds(DEEP, rows), :], out_ref.at[pl.ds(0, count)], sem
-        )
-        copy.start()
-        copy.wait()
+            copy = pltpu.make_async_copy(
+                plain.at[z, :, pl.ds(DEEP, rows), :], out_ref.at[z], sems.at[z]
+            )
+            copy.start()
+            copies.append(copy)
+        for copy in copies:
+            copy.wait()
 
     @pl.when(col == 0)
     def _():
-        fill_factors(factor, where_ref, rows)
         set_top()
         clear = jnp.zeros((8, Y_GROUPS, SUB, LANES), jnp.float32)
-        for z in range(layers + 3):
-            if z != 2:
-                cross[z] = clear
-                if z:
-                    along[z] = clear
-        for z in range(3, layers + 2):
-            cells[z] = clear
+        for z in range(2):
+            cross[z] = clear
+            along[z] = clear
 
         def update(pair, carry):
             z = 2 * pair + 2
             for ys in range(Y_GROUPS):
                 factors = [[factor[pz, px, ys] for px in range(2)] for pz in range(2)]
                 for t in range(8):
-                    even, odd = pair_steps(
-                        [along[z + i, t, ys] for i in range(-1, 3)],
-                        [cross[z + i, t, ys] for i in range(-2, 3)],
-                    )
-                    cells[z, t, ys] += factors[0][t % 2] * even
-                    cells[z + 1, t, ys] += factors[1][t % 2] * odd
+                    w = [along[z + i, t, ys] for i in range(-1, 3)]
+                    c = [cross[z + i, t, ys] for i in range(-2, 3)]
+                    cells[z, t, ys] += factors[0][t % 2] * even_step(w, c)
+                    cells[z + 1, t, ys] += factors[1][t % 2] * odd_step(w[1:], c[2:])
             return carry
 
         def one_sweep(sweep, carry):
-            lax.fori_loop(2, 2 * sweep + 3, lateral, 0)
-            lax.fori_loop(0, jnp.minimum(sweep + 2, layers // 2), update, 0)
+            front = 2 * sweep + 2
+            lax.fori_loop(2, front + 1, lateral, 0)
+            lax.fori_loop(0, sweep, update, 0)
+            for ys in range(Y_GROUPS):
+                factors = [[factor[pz, px, ys] for px in range(2)] for pz in range(2)]
+                for t in range(8):
+                    w0, w1 = along[front - 1, t, ys], along[front, t, ys]
+                    c0, c1, c2 = [cross[front + i, t, ys] for i in range(-2, 1)]
+                    step = (22.0 / 3.0 * w1 - w0) + ((c1 + 8.0 * c2) - c0)
+                    cells[front, t, ys] += factors[0][t % 2] * step
+                    cells[front + 1, t, ys] = factors[1][t % 2] * (c2 - w1)
+                    cells[front + 2, t, ys] = -factors[0][t % 2] * c2
             set_top()
             return carry
 
         lax.fori_loop(0, SWEEPS, one_sweep, 0)
-        send(layers)
+        send(1, layers - 1)
 
     @pl.when(col == 1)
     def _():
-        fill_factors(factor, where_ref, rows)
         set_top()
 
         def one_sweep(sweep, carry):
             lateral(2, 0)
             for t in range(8):
                 for ys in range(Y_GROUPS):
-                    cells[2, t, ys] = factor[0, t % 2, ys] * (-0.5 * cross[2, t, ys])
+                    cells[2, t, ys] = -factor[0, t % 2, ys] * cross[2, t, ys]
             return carry
 
         lax.fori_loop(0, SWEEPS, one_sweep, 0)
-        send(1)
-
-
-def surface_change(where, speed, layers, rows):
-    work = pltpu.VMEM((layers + 4, 8, Y_GROUPS, SUB, LANES), jnp.float32)
+        send(0, 1)
+
+
+def surface_change(where, factor, speed, layers, rows):
+    work = pltpu.VMEM((layers + 2, 8, Y_GROUPS, SUB, LANES), jnp.float32)
     line = pltpu.VMEM((8, Y_GROUPS, SUB, LANES), jnp.float32)
     return pl.pallas_call(
         change_kernel,
         out_shape=f32(layers, 8, rows, LANES),
-        in_specs=[SMEM, VMEM],
+        in_specs=[SMEM, VMEM, VMEM],
         out_specs=HBM,
         scratch_shapes=[
-            pltpu.VMEM((layers + 2, 8, Y_GROUPS, SUB, LANES), jnp.float32),
+            pltpu.VMEM((layers + 3, 8, Y_GROUPS, SUB, LANES), jnp.float32),
             work, work, line, line,
-            pltpu.VMEM((2, 2, Y_GROUPS, SUB, LANES), jnp.float32),
             pltpu.VMEM((layers, 8, Y_ROWS, LANES), jnp.float32),
-            pltpu.SemaphoreType.DMA,
+            pltpu.SemaphoreType.DMA((layers,)),
         ],
         compiler_params=params(32),
         cost_estimate=cost(8),
         name="surface_change",
-    )(where, speed)
+    )(where, factor, speed)
 
 
 def base_kernel(
-    where_ref, wide_ref, zlow_ref, zhigh_ref, change_ref, speed_ref, select_ref,
-    velocity_ref, out_ref, field, along, cross, line_a, line_b, factor, change, parts, sems,
+    where_ref, factor, wide_ref, zlow_ref, zhigh_ref, change_ref, speed_ref, select_ref,
+    velocity_ref, out_ref, field, along, cross, line_a, line_b, change, parts, sems,
 ):
     col, cols = where_ref[0, 1], where_ref[0, 2]
     layers, _, rows, _ = change_ref.shape
@@ -545,7 +575,9 @@
     own = pltpu.make_async_copy(wide_ref, field.at[pl.ds(DEEP, layers)], sems.at[0])
     low = pltpu.make_async_copy(zlow_ref, field.at[pl.ds(0, DEEP)], sems.at[1])
     high = pltpu.make_async_copy(zhigh_ref, field.at[pl.ds(DEEP + layers, DEEP)], sems.at[2])
-    all_change = pltpu.make_async_copy(change_ref, change, sems.at[3])
+    all_change = pltpu.make_async_copy(
+        change_ref.at[pl.ds(1, layers - 1)], change.at[pl.ds(1, layers - 1)], sems.at[3]
+    )
     one_change = pltpu.make_async_copy(
         change_ref.at[pl.ds(0, 1)], change.at[pl.ds(0, 1)], sems.at[4]
     )
@@ -554,7 +586,6 @@
     high.start()
     pl.when(col == 0)(all_change.start)
     pl.when(col == 1)(one_change.start)
-    fill_factors(factor, where_ref, rows)
     count = (layers + 1) * rows
 
     def cut(value, at, t):
@@ -579,9 +610,9 @@
         for ys in range(Y_GROUPS):
             factors = [[factor[pz, px, ys] for px in range(2)] for pz in range(2)]
             for t in range(8):
-                even, odd = pair_steps(
-                    [along[z + i, t, ys] for i in range(-1, 3)], [cross[z + i, t, ys] for i in range(-2, 3)]
-                )
+                w = [along[z + i, t, ys] for i in range(-1, 3)]
+                c = [cross[z + i, t, ys] for i in range(-2, 3)]
+                even, odd = even_step(w, c), odd_step(w[1:], c[2:])
                 scale = jnp.where((col == 0) & (z == DEEP), 0.0, factors[0][t % 2])
                 even = field[z, t, strided(ys), :] + scale * even
                 odd = field[z + 1, t, strided(ys), :] + factors[1][t % 2] * odd
@@ -623,11 +654,17 @@
 
     lax.fori_loop(0, SWEEPS, one_sweep, 0)
 
+    row = lax.broadcasted_iota(jnp.int32, (rows, LANES), 0)
+    by_row = jnp.where(row % 2 == 0, stored(0), stored(1)).astype(jnp.float32)
+    back_row = jnp.where(row % 2 == 0, 1 / stored(0), 1 / stored(1)).astype(jnp.float32)
+
     @pl.when(col == 0)
     def _():
         all_change.wait()
-        for z in range(layers):
-            for t in range(8):
+        for t in range(8):
+            top = speed_ref[t, DEEP : DEEP + rows, :] * (by_row * (0.5 * stored(0) * stored(t % 2)))
+            field[DEEP, t, DEEP : DEEP + rows, :] += top
+            for z in range(1, layers):
                 field[DEEP + z, t, DEEP : DEEP + rows, :] += change[z, t]
 
     @pl.when(col == 1)
@@ -638,7 +675,8 @@
 
     for z in range(layers):
         for t in range(8):
-            cut(field[DEEP + z, t, DEEP : DEEP + rows, :], rows * (z + 1), t)
+            value = field[DEEP + z, t, DEEP : DEEP + rows, :]
+            cut(value * (back_row * (1 / (stored(z % 2) * stored(t % 2)))), rows * (z + 1), t)
 
     def write(at, value):
         velocity_ref[:, at] = value[:rows]
@@ -647,7 +685,7 @@
     plain_columns(select_ref, parts[...], count, write)
 
 
-def base_sweeps(where, wide, zlow, zhigh, change, speed, select):
+def base_sweeps(where, factor, wide, zlow, zhigh, change, speed, select):
     layers, _, rows, _ = change.shape
     total = layers + 2 * DEEP
     work = pltpu.VMEM((total, 8, Y_GROUPS, SUB, LANES), jnp.float32)
@@ -655,12 +693,11 @@
     return pl.pallas_call(
         base_kernel,
         out_shape=(f32(rows, 8 * LANES), f32(layers, rows, 8 * LANES)),
-        in_specs=[SMEM] + [HBM] * 4 + [VMEM] * 2,
+        in_specs=[SMEM, VMEM] + [HBM] * 4 + [VMEM] * 2,
         out_specs=(VMEM, VMEM),
         scratch_shapes=[
             pltpu.VMEM((total, 8, Y_ROWS, LANES), jnp.float32),
             work, work, line, line,
-            pltpu.VMEM((2, 2, Y_GROUPS, SUB, LANES), jnp.float32),
             pltpu.VMEM((layers, 8, rows, LANES), jnp.float32),
             pltpu.VMEM((2 * (layers + 1) * rows, 8 * LANES), jnp.bfloat16),
             pltpu.SemaphoreType.DMA((5,)),
@@ -668,7 +705,7 @@
         compiler_params=params(50),
         cost_estimate=cost(25),
         name="base_sweeps",
-    )(where, wide, zlow, zhigh, change, speed, select)
+    )(where, factor, wide, zlow, zhigh, change, speed, select)
 
 
 mass_even = (-1.0 / 15.0, 2.0 / 15.0, 8.0 / 15.0, 2.0 / 15.0, -1.0 / 15.0)
@@ -722,7 +759,8 @@
     vols, cols = lax.axis_size("vol"), lax.axis_size("col")
     vol, col = lax.axis_index("vol"), lax.axis_index("col")
     core = col % 2
-    where = jnp.stack([core, col, jnp.int32(cols), vol, jnp.int32(vols)]).astype(jnp.int32).reshape(1, 5)
+    where = [core, col, jnp.int32(cols), vol, jnp.int32(vols), jnp.int32(displacement.shape[1])]
+    where = jnp.stack(where).astype(jnp.int32).reshape(1, 6)
     up = [(i, i + 1) for i in range(vols - 1)]
     down = [(j, i) for i, j in up]
     col_up = [(i, i + 1) for i in range(cols - 1)]
@@ -767,16 +805,17 @@
         cross = lax.ppermute(same, "col", [(j, j ^ 1) for j in range(cols)])
 
     with jax.named_scope("depth_halo"):
-        sent = after(wide, other)
+        sent = after(wide, own)
         zlow, zhigh = moved(sent, (0, 1)), moved(sent, (0, -1))
     basis, spread = surface_basis(where, vols, own, other, same, cross, root)
     with jax.named_scope("gather_sums"):
         gathered = lax.all_to_all(spread, "vol", 0, 0)
+    factor = relaxation_factors(after(where, spread))
     speed, flag = surface_solve(basis, gathered)
 
     def finish(speed):
-        change = surface_change(where, speed, displacement.shape[0], displacement.shape[1])
-        return base_sweeps(where, wide, zlow, zhigh, change, speed, select)
+        change = surface_change(where, factor, speed, displacement.shape[0], displacement.shape[1])
+        return base_sweeps(where, factor, wide, zlow, zhigh, change, speed, select)
 
     def step_by_step():
         low = jnp.where(core == 0, own, other)

time: 108 us -> 110 us (1.019)
  blocking collectives: 17.7 us -> 0 us
  starting transfers between devices: 23.4 us -> 33.8 us
  waiting for transfers between devices: 7.34 us -> 12.2 us
  local copies, waits for them, and re-layouts: 0.12 us -> 4.93 us
    all_to_all x1 -> x0, blocking collectives: 17.7 us -> none  [on_device(): gathered = lax.all_to_all(spread, 'vol', 0, 0)]
    all_to_all x0 -> x1, starting transfers between devices: none -> 11.4 us  [on_device(): gathered = lax.all_to_all(spread, 'vol', 0, 0)]
    all_to_all x0 -> x1, waiting for transfers between devices: none -> 5.93 us  [on_device(): gathered = lax.all_to_all(spread, 'vol', 0, 0)]
    unnamed x10, local copies, waits for them, and re-layouts: 0.03 us -> 4.84 us
    ppermute x1, starting transfers between devices: 1.95 us -> 0.09 us  [on_device(): other = lax.ppermute(own, 'col', [(j, j ^ 1) for j in range(cols)])]
    pallas_call x1, Pallas kernels: 29.9 us -> 28.7 us  [base_sweeps(): pl.pallas_call(base_kernel, out_shape=(f32(rows, 8 * LANES), f32(layers,...]
  transfers between devices with their start and end apart: 11 -> 12, of which waited for: 5 -> 5; matrix products, arithmetic and copies ran while one was open for 1% -> 1% of each run, Pallas kernels for 14% -> 14%
where the time goes in v6:
time: 110 us; the launch traced here: 108 us
  Pallas kernels  53.6 us (49%)
  starting transfers between devices  33.8 us (31%)
  waiting for transfers between devices  12.2 us (11%)
  local copies, waits for them, and re-layouts  4.93 us (4%)
  between operations  2.41 us (2%)
    pallas_call x1, Pallas kernels, base_sweeps(): pl.pallas_call(base_kernel, out_shape=(f32(rows, 8 * LANES), f32(layers,...  28.7 us
    ppermute x4, starting transfers between devices, moved(): return lax.ppermute(x, ('vol', 'col'), pairs)  12.1 us
    all_to_all x1, starting transfers between devices, on_device(): gathered = lax.all_to_all(spread, 'vol', 0, 0)  11.4 us
    pallas_call x1, Pallas kernels, surface_basis(): pl.pallas_call(basis_kernel, out_shape=(f32(ITERS, 8, GROUPS, SUB, LANES)...  8.11 us
    pallas_call x1, Pallas kernels, face_sums(): pl.pallas_call(face_kernel, out_shape=(half, half, rows, rows), in_specs=...  7.85 us
    all_to_all x1, waiting for transfers between devices, on_device(): gathered = lax.all_to_all(spread, 'vol', 0, 0)  5.93 us
    ppermute x3, starting transfers between devices, on_device(): lax.ppermute(keep, 'col', [(j, (j + 2 * k) % cols) for j in range(cols)])  5.06 us
    pallas_call x1, Pallas kernels, regroup(): pl.pallas_call(regroup_kernel, out_shape=(f32(layers, 8, Y_ROWS, LANES),...  4.87 us
  transfers between devices with their start and end apart: 12, of which 5 were waited for; matrix products, arithmetic and copies ran while one was open for 1% of the time, Pallas kernels for 14%

profile of v6, /device:TPU:1, one launch (start us, length us, event | category | flops | bytes accessed | tf_op | source)
XLA Modules:
  0.0 108.1 jit_solution(12437100346847776538)
XLA Ops:
  0.6 0.0 copy-start
  0.6 0.0 copy-start.6
  1.5 0.1 stack.15
  1.5 7.8 %face_sums.1 = (f32[8,32,128]{2,1,0:T(8,128)}, f32[8,32,128]{2,1,0:T(8,128)}, f32[96,1024]{1,0:T(8,128)}, f32[96,1024]{1,0:T(8,128)}) custom-call(s32[1,6]{1,0:T(1,128)S(1)} %bitcast.17, s32[1,1]{1,0:T(1,128)S(6)} %copy.41.count_ref, f32[1,16384]{1,0:T(1,128)} %area_ref.1, f32[1,16384]{1,0:T(1,128)} %speed_ref.1, s32[1,16384]{1,0:T(1,128)} %node_ref.1, ...), custom_call_target="tpu_custom_call" | custom-call | bytes 700000 | tf_op jit(solution)/shard_map/face_sums/pallas_call | solution.py:226
  9.4 4.0 %collective-permute-start.8 = (f32[96,1024]{1,0:T(8,128)}, f32[96,1024]{1,0:T(8,128)S(1)}, u32[]{:S(2)}, u32[]{:S(2)}) collective-permute-start(f32[96,1024]{1,0:T(8,128)} %get-tuple-element.149), channel_id=1, source_target_pairs={{0,8},{1,9},{2,10},{3,11},{4,12},{5,13},{6,14},{7,15},{8,16},{9,17... | collective-permute-start | bytes 1179656 | tf_op jit(solution)/shard_map/row_halo/ppermute | solution.py:780
  13.4 1.3 %collective-permute-start.9 = (f32[96,1024]{1,0:T(8,128)}, f32[96,1024]{1,0:T(8,128)S(1)}, u32[]{:S(2)}, u32[]{:S(2)}) collective-permute-start(f32[96,1024]{1,0:T(8,128)} %get-tuple-element.150), channel_id=1, source_target_pairs={{8,0},{9,1},{10,2},{11,3},{12,4},{13,5},{14,6},{15,7},{16,8},{17,9... | collective-permute-start | bytes 1179656 | tf_op jit(solution)/shard_map/row_halo/ppermute | solution.py:780
  14.7 1.0 collective-permute-start.4
  15.7 1.2 %collective-permute-done.4 = f32[8,32,128]{2,1,0:T(8,128)S(1)} collective-permute-done((f32[8,32,128]{2,1,0:T(8,128)}, f32[8,32,128]{2,1,0:T(8,128)S(1)}, u32[]{:S(2)}, u32[]{:S(2)}) %collective-permute-start.4) | collective-permute-done | bytes 131104 | tf_op jit(solution)/shard_map/flux_sum/ppermute | solution.py:786
  16.9 0.9 add.135
  17.8 0.0 copy-start.3
  17.8 1.4 %collective-permute-start.5 = (f32[8,32,128]{2,1,0:T(8,128)S(1)}, f32[8,32,128]{2,1,0:T(8,128)S(1)}, u32[]{:S(2)}, u32[]{:S(2)}) collective-permute-start(f32[8,32,128]{2,1,0:T(8,128)S(1)} %add.135), channel_id=1, source_target_pairs={{0,2},{1,3},{2,4},{3,5},{4,6},{5,7},{6,0},{7,1},{8,10},{9,11},{10,... | collective-permute-start | bytes 393224 | tf_op jit(solution)/shard_map/flux_sum/ppermute | solution.py:788
  19.2 2.6 %collective-permute-start.6 = (f32[8,32,128]{2,1,0:T(8,128)S(1)}, f32[8,32,128]{2,1,0:T(8,128)S(1)}, u32[]{:S(2)}, u32[]{:S(2)}) collective-permute-start(f32[8,32,128]{2,1,0:T(8,128)S(1)} %add.135), channel_id=1, source_target_pairs={{0,4},{1,5},{2,6},{3,7},{4,0},{5,1},{6,2},{7,3},{8,12},{9,13},{10,... | collective-permute-start | bytes 393224 | tf_op jit(solution)/shard_map/flux_sum/ppermute | solution.py:788
  21.8 1.1 collective-permute-start.7
  22.9 0.0 collective-permute-done.8.before_ref
  22.9 2.2 %collective-permute-done.9.after_ref = f32[96,1024]{1,0:T(8,128)S(1)} collective-permute-done((f32[96,1024]{1,0:T(8,128)}, f32[96,1024]{1,0:T(8,128)S(1)}, u32[]{:S(2)}, u32[]{:S(2)}) %collective-permute-start.9) | collective-permute-done | bytes 393248 | tf_op jit(solution)/shard_map/row_halo/ppermute | solution.py:780
  25.2 0.0 copy-done
  25.2 0.0 copy-done.6
  25.2 4.9 %regroup.1 = (f32[8,8,80,128]{3,2,1,0:T(8,128)}, f32[8,128,128]{2,1,0:T(8,128)S(1)}) custom-call(f32[8,64,1024]{2,1,0:T(8,128)S(1)} %copy-done, f32[64,1024]{1,0:T(8,128)S(1)} %copy-done.6, f32[96,1024]{1,0:T(8,128)S(1)} %collective-permute-done.8.before_ref, f32[96,1024]{1,0:T(8,128)S(1)} %collective-permute-done.9.after_ref), custom_call_target="tpu_custom_call" | custom-call | bytes 600000 | tf_op jit(solution)/shard_map/regroup/pallas_call | solution.py:140
  30.0 0.0 collective-permute-done.5
  30.0 0.0 collective-permute-done.6
  30.0 0.0 collective-permute-done.7
  30.1 5.0 %collective-permute-start.13 = (f32[8,8,80,128]{3,2,1,0:T(8,128)}, f32[8,8,80,128]{3,2,1,0:T(8,128)}, u32[]{:S(2)}, u32[]{:S(2)}) collective-permute-start(f32[8,8,80,128]{3,2,1,0:T(8,128)} %get-tuple-element.160), channel_id=1, source_target_pairs={{0,1},{1,2},{2,3},{3,4},{4,5},{5,6},{6,7},{8,9},{9,10},{10,11},{11... | collective-permute-start | bytes 7864328 | tf_op jit(solution)/shard_map/depth_halo/ppermute | solution.py:780
  35.0 1.9 %collective-permute-start.14 = (f32[8,8,80,128]{3,2,1,0:T(8,128)}, f32[8,8,80,128]{3,2,1,0:T(8,128)}, u32[]{:S(2)}, u32[]{:S(2)}) collective-permute-start(f32[8,8,80,128]{3,2,1,0:T(8,128)} %get-tuple-element.160), channel_id=1, source_target_pairs={{1,0},{2,1},{3,2},{4,3},{5,4},{6,5},{7,6},{9,8},{10,9},{11,10},{12... | collective-permute-start | bytes 7864328 | tf_op jit(solution)/shard_map/depth_halo/ppermute | solution.py:780
  37.0 3.1 %collective-permute-start.11 = (f32[8,32,128]{2,1,0:T(8,128)S(1)}, f32[8,32,128]{2,1,0:T(8,128)S(1)}, u32[]{:S(2)}, u32[]{:S(2)}) collective-permute-start(f32[8,32,128]{2,1,0:T(8,128)S(1)} %add_add_fusion.own_ref), channel_id=1, source_target_pairs={{1,9},{3,11},{5,13},{7,15},{8,0},{9,17},{10,2},{11,19},{12,4},{13,... | collective-permute-start | bytes 393224 | tf_op jit(solution)/shard_map/flux_halo/ppermute | solution.py:804
  40.1 0.1 collective-permute-start.10
  40.2 1.8 %collective-permute-done.11.same_ref = f32[8,32,128]{2,1,0:T(8,128)S(1)} collective-permute-done((f32[8,32,128]{2,1,0:T(8,128)S(1)}, f32[8,32,128]{2,1,0:T(8,128)S(1)}, u32[]{:S(2)}, u32[]{:S(2)}) %collective-permute-start.11) | collective-permute-done | bytes 131104 | tf_op jit(solution)/shard_map/flux_halo/ppermute | solution.py:804
  42.0 1.0 collective-permute-start.12
  43.0 0.0 collective-permute-done.10.other_ref
  43.0 1.0 collective-permute-done.12.cross_ref
  44.0 8.1 %surface_basis.1 = (f32[10,8,16,8,128]{4,3,2,1,0:T(8,128)S(1)}, f32[16,8,128]{2,1,0:T(8,128)}) custom-call(s32[1,6]{1,0:T(1,128)S(1)} %bitcast.18, f32[8,32,128]{2,1,0:T(8,128)S(1)} %add_add_fusion.own_ref, f32[8,32,128]{2,1,0:T(8,128)S(1)} %collective-permute-done.10.other_ref, f32[8,32,128]{2,1,0:T(8,128)S(1)} %collective-permute-done.11.same_ref, ...), custom_call_target="tpu_custom_call" | custom-call | bytes 700000 | tf_op jit(solution)/shard_map/surface_basis/pallas_call | solution.py:314
  52.1 0.0 copy-start.1
  52.1 2.3 %copy-done.1 = f32[10,8,16,8,128]{4,3,2,1,0:T(8,128)} copy-done((f32[10,8,16,8,128]{4,3,2,1,0:T(8,128)}, f32[10,8,16,8,128]{4,3,2,1,0:T(8,128)S(1)}, u32[]{:S(2)}) %copy-start.1) | copy-done | bytes 5242904
  54.4 11.4 %all-to-all-start = ((f32[16,8,128]{2,1,0:T(8,128)}), f32[16,8,128]{2,1,0:T(8,128)S(1)}, u32[]{:S(2)}, u32[]{:S(2)}) async-start(f32[16,8,128]{2,1,0:T(8,128)} %get-tuple-element.157), calls=%async_computation | async-start | bytes 131072 | tf_op jit(solution)/shard_map/gather_sums/all_to_all | solution.py:812
  65.8 0.6 relaxation_factors.1
  66.4 5.9 %all-to-all-done.sums_ref = f32[16,8,128]{2,1,0:T(8,128)S(1)} async-done(((f32[16,8,128]{2,1,0:T(8,128)}), f32[16,8,128]{2,1,0:T(8,128)S(1)}, u32[]{:S(2)}, u32[]{:S(2)}) %all-to-all-start) | async-done | bytes 65568 | tf_op jit(solution)/shard_map/gather_sums/all_to_all | solution.py:812
  72.4 0.0 copy-done.3
  72.4 0.0 copy-start.2
  72.4 2.5 %copy-done.2 = f32[10,8,16,8,128]{4,3,2,1,0:T(8,128)S(1)} copy-done((f32[10,8,16,8,128]{4,3,2,1,0:T(8,128)S(1)}, f32[10,8,16,8,128]{4,3,2,1,0:T(8,128)}, u32[]{:S(2)}) %copy-start.2) | copy-done | bytes 5242904
  74.8 1.8 %surface_solve.1 = (f32[8,80,128]{2,1,0:T(8,128)S(1)}, s32[1,1]{1,0:T(1,128)}) custom-call(f32[10,8,16,8,128]{4,3,2,1,0:T(8,128)S(1)} %copy-done.2, f32[16,8,128]{2,1,0:T(8,128)S(1)} %all-to-all-done.sums_ref, f32[20,16,128]{2,1,0:T(8,128)S(1)} %copy-done.3), custom_call_target="tpu_custom_call" | custom-call | bytes 300000 | tf_op jit(solution)/shard_map/surface_solve/pallas_call | solution.py:391
  77.3 0.0 collective-permute-done.13
  77.3 0.0 collective-permute-done.14
  77.4 30.6 %conditional.1 = ((f32[64,1024]{1,0:T(8,128)}, f32[8,64,1024]{2,1,0:T(8,128)})) conditional(s32[]{:T(128)} %bitcast.9, (s32[]{:T(128)}, f32[8,32,128]{2,1,0:T(8,128)S(1)}, f32[8,32,128]{2,1,0:T(8,128)S(1)}, f32[64,1024]{1,0:T(8,128)S(1)}, s32[1,6]{1,0:T(1,128)S(1)}, /*index=5*/f32[2,2,10,8,128]{4,3,2,1,0:T(8,128)S(1)}, f32[8,8,80,128]{3,2,1,0:T(8,128)}, ...), branch_computations={%region_0.9_spmd, %region_9.10_spmd} | conditional | flops 3516806 | bytes 23668972 | solution.py:828
  77.6 0.0 copy-start.5
  77.6 1.7 %surface_change.3.change_ref = f32[8,8,64,128]{3,2,1,0:T(8,128)S(1)} custom-call(s32[1,6]{1,0:T(1,128)S(1)} %get-tuple-element.123.where_ref, f32[2,2,10,8,128]{4,3,2,1,0:T(8,128)S(1)} %get-tuple-element.124.factor, f32[8,80,128]{2,1,0:T(8,128)S(1)} %get-tuple-element.128.speed_ref), custom_call_target="tpu_custom_call" | custom-call | bytes 800000 | tf_op jit(solution)/shard_map/cond/branch_1_fun/surface_change/pallas_call | solution.py:551
  79.3 0.0 copy-done.5
  79.3 28.7 %base_sweeps.3 = (f32[64,1024]{1,0:T(8,128)}, f32[8,64,1024]{2,1,0:T(8,128)}) custom-call(s32[1,6]{1,0:T(1,128)S(1)} %get-tuple-element.123.where_ref, f32[2,2,10,8,128]{4,3,2,1,0:T(8,128)S(1)} %get-tuple-element.124.factor, f32[8,8,80,128]{3,2,1,0:T(8,128)} %get-tuple-element.125.wide_ref, f32[8,8,80,128]{3,2,1,0:T(8,128)} %get-tuple-element.126.zlow_ref, ...), custom_call_target="tpu_custom_call" | custom-call | bytes 2500000 | tf_op jit(solution)/shard_map/cond/branch_1_fun/base_sweeps/pallas_call | solution.py:693
  (1 shorter events, 0.0 us)
Async XLA Ops:
  0.6 24.5 %copy-start = (f32[8,64,1024]{2,1,0:T(8,128)S(1)}, f32[8,64,1024]{2,1,0:T(8,128)}, u32[]{:S(2)}) copy-start(f32[8,64,1024]{2,1,0:T(8,128)} %block_ref.3) | copy-start | bytes 6291460
  0.6 24.5 %copy-start.6 = (f32[64,1024]{1,0:T(8,128)S(1)}, f32[64,1024]{1,0:T(8,128)}, u32[]{:S(2)}) copy-start(f32[64,1024]{1,0:T(8,128)} %metric_ref.3) | copy-start | bytes 786436
  9.4 13.5 %collective-permute-start.8 = (f32[96,1024]{1,0:T(8,128)}, f32[96,1024]{1,0:T(8,128)S(1)}, u32[]{:S(2)}, u32[]{:S(2)}) collective-permute-start(f32[96,1024]{1,0:T(8,128)} %get-tuple-element.149), channel_id=1, source_target_pairs={{0,8},{1,9},{2,10},{3,11},{4,12},{5,13},{6,14},{7,15},{8,16},{9,17... | collective-permute-start | bytes 1179656 | tf_op jit(solution)/shard_map/row_halo/ppermute | solution.py:780
  13.4 11.8 %collective-permute-start.9 = (f32[96,1024]{1,0:T(8,128)}, f32[96,1024]{1,0:T(8,128)S(1)}, u32[]{:S(2)}, u32[]{:S(2)}) collective-permute-start(f32[96,1024]{1,0:T(8,128)} %get-tuple-element.150), channel_id=1, source_target_pairs={{8,0},{9,1},{10,2},{11,3},{12,4},{13,5},{14,6},{15,7},{16,8},{17,9... | collective-permute-start | bytes 1179656 | tf_op jit(solution)/shard_map/row_halo/ppermute | solution.py:780
  14.7 2.2 %collective-permute-start.4 = (f32[8,32,128]{2,1,0:T(8,128)}, f32[8,32,128]{2,1,0:T(8,128)S(1)}, u32[]{:S(2)}, u32[]{:S(2)}) collective-permute-start(f32[8,32,128]{2,1,0:T(8,128)} %get-tuple-element.148), channel_id=1, source_target_pairs={{0,1},{1,0},{2,3},{3,2},{4,5},{5,4},{6,7},{7,6},{8,9},{9,8},{10,11... | collective-permute-start | bytes 393224 | tf_op jit(solution)/shard_map/flux_sum/ppermute | solution.py:786
  17.8 54.5 %copy-start.3 = (f32[20,16,128]{2,1,0:T(8,128)S(1)}, f32[20,16,128]{2,1,0:T(8,128)}, u32[]{:S(2)}) copy-start(f32[20,16,128]{2,1,0:T(8,128)} %constant.115.clone.weights_ref) | copy-start | bytes 491524
  17.8 12.2 %collective-permute-start.5 = (f32[8,32,128]{2,1,0:T(8,128)S(1)}, f32[8,32,128]{2,1,0:T(8,128)S(1)}, u32[]{:S(2)}, u32[]{:S(2)}) collective-permute-start(f32[8,32,128]{2,1,0:T(8,128)S(1)} %add.135), channel_id=1, source_target_pairs={{0,2},{1,3},{2,4},{3,5},{4,6},{5,7},{6,0},{7,1},{8,10},{9,11},{10,... | collective-permute-start | bytes 393224 | tf_op jit(solution)/shard_map/flux_sum/ppermute | solution.py:788
  19.2 10.8 %collective-permute-start.6 = (f32[8,32,128]{2,1,0:T(8,128)S(1)}, f32[8,32,128]{2,1,0:T(8,128)S(1)}, u32[]{:S(2)}, u32[]{:S(2)}) collective-permute-start(f32[8,32,128]{2,1,0:T(8,128)S(1)} %add.135), channel_id=1, source_target_pairs={{0,4},{1,5},{2,6},{3,7},{4,0},{5,1},{6,2},{7,3},{8,12},{9,13},{10,... | collective-permute-start | bytes 393224 | tf_op jit(solution)/shard_map/flux_sum/ppermute | solution.py:788
  21.8 8.2 %collective-permute-start.7 = (f32[8,32,128]{2,1,0:T(8,128)S(1)}, f32[8,32,128]{2,1,0:T(8,128)S(1)}, u32[]{:S(2)}, u32[]{:S(2)}) collective-permute-start(f32[8,32,128]{2,1,0:T(8,128)S(1)} %add.135), channel_id=1, source_target_pairs={{0,6},{1,7},{2,0},{3,1},{4,2},{5,3},{6,4},{7,5},{8,14},{9,15},{10,... | collective-permute-start | bytes 393224 | tf_op jit(solution)/shard_map/flux_sum/ppermute | solution.py:788
  30.1 47.2 %collective-permute-start.13 = (f32[8,8,80,128]{3,2,1,0:T(8,128)}, f32[8,8,80,128]{3,2,1,0:T(8,128)}, u32[]{:S(2)}, u32[]{:S(2)}) collective-permute-start(f32[8,8,80,128]{3,2,1,0:T(8,128)} %get-tuple-element.160), channel_id=1, source_target_pairs={{0,1},{1,2},{2,3},{3,4},{4,5},{5,6},{6,7},{8,9},{9,10},{10,11},{11... | collective-permute-start | bytes 7864328 | tf_op jit(solution)/shard_map/depth_halo/ppermute | solution.py:780
  35.0 42.3 %collective-permute-start.14 = (f32[8,8,80,128]{3,2,1,0:T(8,128)}, f32[8,8,80,128]{3,2,1,0:T(8,128)}, u32[]{:S(2)}, u32[]{:S(2)}) collective-permute-start(f32[8,8,80,128]{3,2,1,0:T(8,128)} %get-tuple-element.160), channel_id=1, source_target_pairs={{1,0},{2,1},{3,2},{4,3},{5,4},{6,5},{7,6},{9,8},{10,9},{11,10},{12... | collective-permute-start | bytes 7864328 | tf_op jit(solution)/shard_map/depth_halo/ppermute | solution.py:780
  37.0 5.0 %collective-permute-start.11 = (f32[8,32,128]{2,1,0:T(8,128)S(1)}, f32[8,32,128]{2,1,0:T(8,128)S(1)}, u32[]{:S(2)}, u32[]{:S(2)}) collective-permute-start(f32[8,32,128]{2,1,0:T(8,128)S(1)} %add_add_fusion.own_ref), channel_id=1, source_target_pairs={{1,9},{3,11},{5,13},{7,15},{8,0},{9,17},{10,2},{11,19},{12,4},{13,... | collective-permute-start | bytes 393224 | tf_op jit(solution)/shard_map/flux_halo/ppermute | solution.py:804
  40.1 2.9 %collective-permute-start.10 = (f32[8,32,128]{2,1,0:T(8,128)S(1)}, f32[8,32,128]{2,1,0:T(8,128)S(1)}, u32[]{:S(2)}, u32[]{:S(2)}) collective-permute-start(f32[8,32,128]{2,1,0:T(8,128)S(1)} %add_add_fusion.own_ref), channel_id=1, source_target_pairs={{0,1},{1,0},{2,3},{3,2},{4,5},{5,4},{6,7},{7,6},{8,9},{9,8},{10,11... | collective-permute-start | bytes 393224 | tf_op jit(solution)/shard_map/flux_halo/ppermute | solution.py:797
  42.0 2.0 %collective-permute-start.12 = (f32[8,32,128]{2,1,0:T(8,128)S(1)}, f32[8,32,128]{2,1,0:T(8,128)S(1)}, u32[]{:S(2)}, u32[]{:S(2)}) collective-permute-start(f32[8,32,128]{2,1,0:T(8,128)S(1)} %collective-permute-done.11.same_ref), channel_id=1, source_target_pairs={{0,1},{1,0},{2,3},{3,2},{4,5},{5,4},{6,7},{7,6},{8,9},{9,8},{10,11... | collective-permute-start | bytes 393224 | tf_op jit(solution)/shard_map/flux_halo/ppermute | solution.py:805
  52.1 2.3 %copy-start.1 = (f32[10,8,16,8,128]{4,3,2,1,0:T(8,128)}, f32[10,8,16,8,128]{4,3,2,1,0:T(8,128)S(1)}, u32[]{:S(2)}) copy-start(f32[10,8,16,8,128]{4,3,2,1,0:T(8,128)S(1)} %get-tuple-element.156.part_ref) | copy-start | bytes 15728644
  54.4 17.9 %all-to-all-start = ((f32[16,8,128]{2,1,0:T(8,128)}), f32[16,8,128]{2,1,0:T(8,128)S(1)}, u32[]{:S(2)}, u32[]{:S(2)}) async-start(f32[16,8,128]{2,1,0:T(8,128)} %get-tuple-element.157), calls=%async_computation | async-start | bytes 131072 | tf_op jit(solution)/shard_map/gather_sums/all_to_all | solution.py:812
  72.4 2.5 %copy-start.2 = (f32[10,8,16,8,128]{4,3,2,1,0:T(8,128)S(1)}, f32[10,8,16,8,128]{4,3,2,1,0:T(8,128)}, u32[]{:S(2)}) copy-start(f32[10,8,16,8,128]{4,3,2,1,0:T(8,128)} %copy-done.1) | copy-start | bytes 15728644
  77.6 1.7 %copy-start.5 = (bf16[1024,1024]{1,0:T(8,128)(2,1)S(1)}, bf16[1024,1024]{1,0:T(8,128)(2,1)}, u32[]{:S(2)}) copy-start(bf16[1024,1024]{1,0:T(8,128)(2,1)} %get-tuple-element.129.select_ref) | copy-start | bytes 6291460 | tf_op jit(solution)/shard_map/cond

commit v7 on v6

--- a/solution.py
+++ b/solution.py
@@ -144,7 +144,7 @@
         out_specs=(VMEM, VMEM),
         scratch_shapes=[pltpu.VMEM((2 * (Y_ROWS * layers + ROWS), cols), jnp.bfloat16)],
         compiler_params=params(32),
-        cost_estimate=cost(6),
+        cost_estimate=cost(150),
         name="regroup",
     )(block, metric, before, after)
 
@@ -432,17 +432,17 @@
 
 
 def lateral_lines(get, line_a, line_b, put):
+    for t in range(8):
+        u = row_ring([get(t, ys) for ys in range(Y_GROUPS)])
+        for ys in range(Y_GROUPS):
+            m = mass_line(u, ys)
+            line_a[t, ys] = m
+            line_b[t, ys] = both_line(u, ys) - m
     for ys in range(Y_GROUPS):
-        padded = column_ring([get(t, ys) for t in range(8)])
+        a = column_ring([line_a[t, ys] for t in range(8)])
+        b = column_ring([line_b[t, ys] for t in range(8)])
         for t in range(8):
-            m = mass_line(padded, t)
-            line_a[t, ys] = m
-            line_b[t, ys] = both_line(padded, t) - m
-    for t in range(8):
-        a = row_ring([line_a[t, ys] for ys in range(Y_GROUPS)])
-        b = row_ring([line_b[t, ys] for ys in range(Y_GROUPS)])
-        for ys in range(Y_GROUPS):
-            put(t, ys, mass_line(a, ys), both_line(a, ys) + mass_line(b, ys))
+            put(t, ys, mass_line(a, t), both_line(a, t) + mass_line(b, t))
 
 
 def even_step(w, c):
@@ -787,12 +787,10 @@
         turned = [
             lax.ppermute(keep, "col", [(j, (j + 2 * k) % cols) for j in range(cols)]) for k in (1, 2, 3)
         ]
+        own = (keep + turned[1]) + (turned[0] + turned[2])
     with jax.named_scope("row_halo"):
-        rows_before, rows_after = moved(rows_up, (1, 0)), moved(rows_down, (-1, 0))
-    wide, root = regroup(displacement, surface_metric, rows_before, rows_after)
-    with jax.named_scope("flux_sum"):
-        turned = lax.optimization_barrier((*turned, wide))
-        own = (keep + turned[1]) + (turned[0] + turned[2])
+        rows_before, rows_after = moved(after(rows_up, keep), (1, 0)), moved(after(rows_down, keep), (-1, 0))
+    wide, root = regroup(displacement, surface_metric, after(rows_before, own), rows_after)
     with jax.named_scope("flux_halo"):
         other = lax.ppermute(own, "col", [(j, j ^ 1) for j in range(cols)])
         pairs = []
@@ -805,12 +803,11 @@
         cross = lax.ppermute(same, "col", [(j, j ^ 1) for j in range(cols)])
 
     with jax.named_scope("depth_halo"):
-        sent = after(wide, own)
-        zlow, zhigh = moved(sent, (0, 1)), moved(sent, (0, -1))
+        zlow, zhigh = moved(wide, (0, 1)), moved(wide, (0, -1))
     basis, spread = surface_basis(where, vols, own, other, same, cross, root)
     with jax.named_scope("gather_sums"):
         gathered = lax.all_to_all(spread, "vol", 0, 0)
-    factor = relaxation_factors(after(where, spread))
+    factor = relaxation_factors(after(where, own))
     speed, flag = surface_solve(basis, gathered)
 
     def finish(speed):

time: 110 us -> 112 us (1.018)
  waiting for transfers between devices: 12.2 us -> 15 us
  Pallas kernels: 53.6 us -> 52.2 us
    ppermute x3, waiting for transfers between devices: 0.01 us -> 3.73 us  [on_device(): lax.ppermute(keep, 'col', [(j, (j + 2 * k) % cols) for j in range(cols)])]
    pallas_call x1, Pallas kernels: 28.7 us -> 27.3 us  [base_sweeps(): pl.pallas_call(base_kernel, out_shape=(f32(rows, 8 * LANES), f32(layers,...]
  transfers between devices with their start and end apart: 12 -> 12, of which waited for: 5 -> 7; matrix products, arithmetic and copies ran while one was open for 1% -> 0% of each run, Pallas kernels for 14% -> 10%
where the time goes in v7:
time: 112 us; the launch traced here: 110 us
  Pallas kernels  52.2 us (47%)
  starting transfers between devices  33.8 us (30%)
  waiting for transfers between devices  15 us (13%)
  local copies, waits for them, and re-layouts  4.93 us (4%)
  between operations  2.41 us (2%)
    pallas_call x1, Pallas kernels, base_sweeps(): pl.pallas_call(base_kernel, out_shape=(f32(rows, 8 * LANES), f32(layers,...  27.3 us
    all_to_all x1, starting transfers between devices, on_device(): gathered = lax.all_to_all(spread, 'vol', 0, 0)  11.4 us
    ppermute x4, starting transfers between devices, moved(): return lax.ppermute(x, ('vol', 'col'), pairs)  11 us
    pallas_call x1, Pallas kernels, surface_basis(): pl.pallas_call(basis_kernel, out_shape=(f32(ITERS, 8, GROUPS, SUB, LANES)...  8.11 us
    pallas_call x1, Pallas kernels, face_sums(): pl.pallas_call(face_kernel, out_shape=(half, half, rows, rows), in_specs=...  7.85 us
    all_to_all x1, waiting for transfers between devices, on_device(): gathered = lax.all_to_all(spread, 'vol', 0, 0)  5.93 us
    ppermute x3, starting transfers between devices, on_device(): lax.ppermute(keep, 'col', [(j, (j + 2 * k) % cols) for j in range(cols)])  5.68 us
    pallas_call x1, Pallas kernels, regroup(): pl.pallas_call(regroup_kernel, out_shape=(f32(layers, 8, Y_ROWS, LANES),...  4.87 us
  transfers between devices with their start and end apart: 12, of which 7 were waited for; matrix products, arithmetic and copies ran while one was open for 0% of the time, Pallas kernels for 10%

profile of v7, /device:TPU:1, one launch (start us, length us, event | category | flops | bytes accessed | tf_op | source)
XLA Modules:
  0.0 109.5 jit_solution(4897685603326822551)
XLA Ops:
  0.6 0.0 copy-start.6
  0.6 0.0 copy-start
  1.5 0.1 stack.15
  1.5 7.8 %face_sums.1 = (f32[8,32,128]{2,1,0:T(8,128)}, f32[8,32,128]{2,1,0:T(8,128)}, f32[96,1024]{1,0:T(8,128)}, f32[96,1024]{1,0:T(8,128)}) custom-call(s32[1,6]{1,0:T(1,128)S(1)} %bitcast.17, s32[1,1]{1,0:T(1,128)S(6)} %copy.41.count_ref, f32[1,16384]{1,0:T(1,128)} %area_ref.1, f32[1,16384]{1,0:T(1,128)} %speed_ref.1, s32[1,16384]{1,0:T(1,128)} %node_ref.1, ...), custom_call_target="tpu_custom_call" | custom-call | bytes 700000 | tf_op jit(solution)/shard_map/face_sums/pallas_call | solution.py:226
  9.4 1.5 %collective-permute-start.4 = (f32[8,32,128]{2,1,0:T(8,128)}, f32[8,32,128]{2,1,0:T(8,128)S(1)}, u32[]{:S(2)}, u32[]{:S(2)}) collective-permute-start(f32[8,32,128]{2,1,0:T(8,128)} %get-tuple-element.147), channel_id=1, source_target_pairs={{0,1},{1,0},{2,3},{3,2},{4,5},{5,4},{6,7},{7,6},{8,9},{9,8},{10,11... | collective-permute-start | bytes 393224 | tf_op jit(solution)/shard_map/flux_sum/ppermute | solution.py:786
  10.9 1.2 %collective-permute-done.4 = f32[8,32,128]{2,1,0:T(8,128)S(1)} collective-permute-done((f32[8,32,128]{2,1,0:T(8,128)}, f32[8,32,128]{2,1,0:T(8,128)S(1)}, u32[]{:S(2)}, u32[]{:S(2)}) %collective-permute-start.4) | collective-permute-done | bytes 131104 | tf_op jit(solution)/shard_map/flux_sum/ppermute | solution.py:786
  12.1 0.9 add.135
  13.0 3.2 %collective-permute-start.11 = (f32[96,1024]{1,0:T(8,128)}, f32[96,1024]{1,0:T(8,128)S(1)}, u32[]{:S(2)}, u32[]{:S(2)}) collective-permute-start(f32[96,1024]{1,0:T(8,128)} %get-tuple-element.149), channel_id=1, source_target_pairs={{0,8},{1,9},{2,10},{3,11},{4,12},{5,13},{6,14},{7,15},{8,16},{9,17... | collective-permute-start | bytes 1179656 | tf_op jit(solution)/shard_map/row_halo/ppermute | solution.py:780
  16.2 1.3 %collective-permute-start.12 = (f32[96,1024]{1,0:T(8,128)}, f32[96,1024]{1,0:T(8,128)S(1)}, u32[]{:S(2)}, u32[]{:S(2)}) collective-permute-start(f32[96,1024]{1,0:T(8,128)} %get-tuple-element.152), channel_id=1, source_target_pairs={{8,0},{9,1},{10,2},{11,3},{12,4},{13,5},{14,6},{15,7},{16,8},{17,9... | collective-permute-start | bytes 1179656 | tf_op jit(solution)/shard_map/row_halo/ppermute | solution.py:780
  17.5 3.0 %collective-permute-start.5 = (f32[8,32,128]{2,1,0:T(8,128)S(1)}, f32[8,32,128]{2,1,0:T(8,128)S(1)}, u32[]{:S(2)}, u32[]{:S(2)}) collective-permute-start(f32[8,32,128]{2,1,0:T(8,128)S(1)} %add.135), channel_id=1, source_target_pairs={{0,4},{1,5},{2,6},{3,7},{4,0},{5,1},{6,2},{7,3},{8,12},{9,13},{10,... | collective-permute-start | bytes 393224 | tf_op jit(solution)/shard_map/flux_sum/ppermute | solution.py:788
  20.5 0.4 collective-permute-start.6
  20.9 2.3 %collective-permute-start.7 = (f32[8,32,128]{2,1,0:T(8,128)S(1)}, f32[8,32,128]{2,1,0:T(8,128)S(1)}, u32[]{:S(2)}, u32[]{:S(2)}) collective-permute-start(f32[8,32,128]{2,1,0:T(8,128)S(1)} %add.135), channel_id=1, source_target_pairs={{0,6},{1,7},{2,0},{3,1},{4,2},{5,3},{6,4},{7,5},{8,14},{9,15},{10,... | collective-permute-start | bytes 393224 | tf_op jit(solution)/shard_map/flux_sum/ppermute | solution.py:788
  23.2 0.3 collective-permute-done.5
  23.5 3.4 %collective-permute-done.6 = f32[8,32,128]{2,1,0:T(8,128)S(1)} collective-permute-done((f32[8,32,128]{2,1,0:T(8,128)S(1)}, f32[8,32,128]{2,1,0:T(8,128)S(1)}, u32[]{:S(2)}, u32[]{:S(2)}) %collective-permute-start.6) | collective-permute-done | bytes 131104 | tf_op jit(solution)/shard_map/flux_sum/ppermute | solution.py:788
  27.0 0.0 collective-permute-done.7
  27.0 0.0 copy-start.3
  27.0 0.0 collective-permute-done.11.before_ref
  27.0 1.4 %collective-permute-done.12.after_ref = f32[96,1024]{1,0:T(8,128)S(1)} collective-permute-done((f32[96,1024]{1,0:T(8,128)}, f32[96,1024]{1,0:T(8,128)S(1)}, u32[]{:S(2)}, u32[]{:S(2)}) %collective-permute-start.12) | collective-permute-done | bytes 393248 | tf_op jit(solution)/shard_map/row_halo/ppermute | solution.py:780
  28.4 0.0 copy-done.6
  28.4 0.0 copy-done
  28.4 4.9 %regroup.1 = (f32[8,8,80,128]{3,2,1,0:T(8,128)}, f32[8,128,128]{2,1,0:T(8,128)S(1)}) custom-call(f32[8,64,1024]{2,1,0:T(8,128)S(1)} %copy-done, f32[64,1024]{1,0:T(8,128)S(1)} %copy-done.6, f32[96,1024]{1,0:T(8,128)S(1)} %collective-permute-done.11.before_ref, f32[96,1024]{1,0:T(8,128)S(1)} %collective-permute-done.12.after_ref), custom_call_target="tpu_custom_call" | custom-call | bytes 15000000 | tf_op jit(solution)/shard_map/regroup/pallas_call | solution.py:140
  33.3 4.6 %collective-permute-start.13 = (f32[8,8,80,128]{3,2,1,0:T(8,128)}, f32[8,8,80,128]{3,2,1,0:T(8,128)}, u32[]{:S(2)}, u32[]{:S(2)}) collective-permute-start(f32[8,8,80,128]{3,2,1,0:T(8,128)} %get-tuple-element.158), channel_id=1, source_target_pairs={{0,1},{1,2},{2,3},{3,4},{4,5},{5,6},{6,7},{8,9},{9,10},{10,11},{11... | collective-permute-start | bytes 7864328 | tf_op jit(solution)/shard_map/depth_halo/ppermute | solution.py:780
  37.9 1.9 %collective-permute-start.14 = (f32[8,8,80,128]{3,2,1,0:T(8,128)}, f32[8,8,80,128]{3,2,1,0:T(8,128)}, u32[]{:S(2)}, u32[]{:S(2)}) collective-permute-start(f32[8,8,80,128]{3,2,1,0:T(8,128)} %get-tuple-element.158), channel_id=1, source_target_pairs={{1,0},{2,1},{3,2},{4,3},{5,4},{6,5},{7,6},{9,8},{10,9},{11,10},{12... | collective-permute-start | bytes 7864328 | tf_op jit(solution)/shard_map/depth_halo/ppermute | solution.py:780
  39.8 3.1 %collective-permute-start.9 = (f32[8,32,128]{2,1,0:T(8,128)S(1)}, f32[8,32,128]{2,1,0:T(8,128)S(1)}, u32[]{:S(2)}, u32[]{:S(2)}) collective-permute-start(f32[8,32,128]{2,1,0:T(8,128)S(1)} %add_add_fusion.own_ref), channel_id=1, source_target_pairs={{1,9},{3,11},{5,13},{7,15},{8,0},{9,17},{10,2},{11,19},{12,4},{13,... | collective-permute-start | bytes 393224 | tf_op jit(solution)/shard_map/flux_halo/ppermute | solution.py:802
  42.9 0.1 collective-permute-start.8
  43.0 1.8 %collective-permute-done.9.same_ref = f32[8,32,128]{2,1,0:T(8,128)S(1)} collective-permute-done((f32[8,32,128]{2,1,0:T(8,128)S(1)}, f32[8,32,128]{2,1,0:T(8,128)S(1)}, u32[]{:S(2)}, u32[]{:S(2)}) %collective-permute-start.9) | collective-permute-done | bytes 131104 | tf_op jit(solution)/shard_map/flux_halo/ppermute | solution.py:802
  44.8 1.0 collective-permute-start.10
  45.8 0.0 collective-permute-done.8.other_ref
  45.8 1.0 collective-permute-done.10.cross_ref
  46.8 8.1 %surface_basis.1 = (f32[10,8,16,8,128]{4,3,2,1,0:T(8,128)S(1)}, f32[16,8,128]{2,1,0:T(8,128)}) custom-call(s32[1,6]{1,0:T(1,128)S(1)} %bitcast.18, f32[8,32,128]{2,1,0:T(8,128)S(1)} %add_add_fusion.own_ref, f32[8,32,128]{2,1,0:T(8,128)S(1)} %collective-permute-done.8.other_ref, f32[8,32,128]{2,1,0:T(8,128)S(1)} %collective-permute-done.9.same_ref, ...), custom_call_target="tpu_custom_call" | custom-call | bytes 700000 | tf_op jit(solution)/shard_map/surface_basis/pallas_call | solution.py:314
  54.9 0.0 copy-start.1
  54.9 2.3 %copy-done.1 = f32[10,8,16,8,128]{4,3,2,1,0:T(8,128)} copy-done((f32[10,8,16,8,128]{4,3,2,1,0:T(8,128)}, f32[10,8,16,8,128]{4,3,2,1,0:T(8,128)S(1)}, u32[]{:S(2)}) %copy-start.1) | copy-done | bytes 5242904
  57.2 11.4 %all-to-all-start = ((f32[16,8,128]{2,1,0:T(8,128)}), f32[16,8,128]{2,1,0:T(8,128)S(1)}, u32[]{:S(2)}, u32[]{:S(2)}) async-start(f32[16,8,128]{2,1,0:T(8,128)} %get-tuple-element.155), calls=%async_computation | async-start | bytes 131072 | tf_op jit(solution)/shard_map/gather_sums/all_to_all | solution.py:809
  68.6 0.6 relaxation_factors.1
  69.2 5.9 %all-to-all-done.sums_ref = f32[16,8,128]{2,1,0:T(8,128)S(1)} async-done(((f32[16,8,128]{2,1,0:T(8,128)}), f32[16,8,128]{2,1,0:T(8,128)S(1)}, u32[]{:S(2)}, u32[]{:S(2)}) %all-to-all-start) | async-done | bytes 65568 | tf_op jit(solution)/shard_map/gather_sums/all_to_all | solution.py:809
  75.2 0.0 copy-done.3
  75.2 0.0 copy-start.2
  75.2 2.5 %copy-done.2 = f32[10,8,16,8,128]{4,3,2,1,0:T(8,128)S(1)} copy-done((f32[10,8,16,8,128]{4,3,2,1,0:T(8,128)S(1)}, f32[10,8,16,8,128]{4,3,2,1,0:T(8,128)}, u32[]{:S(2)}) %copy-start.2) | copy-done | bytes 5242904
  77.6 1.8 %surface_solve.1 = (f32[8,80,128]{2,1,0:T(8,128)S(1)}, s32[1,1]{1,0:T(1,128)}) custom-call(f32[10,8,16,8,128]{4,3,2,1,0:T(8,128)S(1)} %copy-done.2, f32[16,8,128]{2,1,0:T(8,128)S(1)} %all-to-all-done.sums_ref, f32[20,16,128]{2,1,0:T(8,128)S(1)} %copy-done.3), custom_call_target="tpu_custom_call" | custom-call | bytes 300000 | tf_op jit(solution)/shard_map/surface_solve/pallas_call | solution.py:391
  80.1 0.0 collective-permute-done.13
  80.1 0.0 collective-permute-done.14
  80.2 29.2 %conditional.1 = ((f32[64,1024]{1,0:T(8,128)}, f32[8,64,1024]{2,1,0:T(8,128)})) conditional(s32[]{:T(128)} %bitcast.9, (s32[]{:T(128)}, f32[8,32,128]{2,1,0:T(8,128)S(1)}, f32[8,32,128]{2,1,0:T(8,128)S(1)}, f32[64,1024]{1,0:T(8,128)S(1)}, s32[1,6]{1,0:T(1,128)S(1)}, /*index=5*/f32[2,2,10,8,128]{4,3,2,1,0:T(8,128)S(1)}, f32[8,8,80,128]{3,2,1,0:T(8,128)}, ...), branch_computations={%region_0.9_spmd, %region_9.10_spmd} | conditional | flops 3516806 | bytes 23668964 | solution.py:825
  80.4 0.0 copy-start.5
  80.4 1.6 %surface_change.3.change_ref = f32[8,8,64,128]{3,2,1,0:T(8,128)S(1)} custom-call(s32[1,6]{1,0:T(1,128)S(1)} %get-tuple-element.123.where_ref, f32[2,2,10,8,128]{4,3,2,1,0:T(8,128)S(1)} %get-tuple-element.124.factor, f32[8,80,128]{2,1,0:T(8,128)S(1)} %get-tuple-element.128.speed_ref), custom_call_target="tpu_custom_call" | custom-call | bytes 800000 | tf_op jit(solution)/shard_map/cond/branch_1_fun/surface_change/pallas_call | solution.py:551
  82.0 0.0 copy-done.5
  82.0 27.3 %base_sweeps.3 = (f32[64,1024]{1,0:T(8,128)}, f32[8,64,1024]{2,1,0:T(8,128)}) custom-call(s32[1,6]{1,0:T(1,128)S(1)} %get-tuple-element.123.where_ref, f32[2,2,10,8,128]{4,3,2,1,0:T(8,128)S(1)} %get-tuple-element.124.factor, f32[8,8,80,128]{3,2,1,0:T(8,128)} %get-tuple-element.125.wide_ref, f32[8,8,80,128]{3,2,1,0:T(8,128)} %get-tuple-element.126.zlow_ref, ...), custom_call_target="tpu_custom_call" | custom-call | bytes 2500000 | tf_op jit(solution)/shard_map/cond/branch_1_fun/base_sweeps/pallas_call | solution.py:693
  (1 shorter events, 0.0 us)
Async XLA Ops:
  0.6 27.7 %copy-start.6 = (f32[64,1024]{1,0:T(8,128)S(1)}, f32[64,1024]{1,0:T(8,128)}, u32[]{:S(2)}) copy-start(f32[64,1024]{1,0:T(8,128)} %metric_ref.3) | copy-start | bytes 786436
  0.6 27.7 %copy-start = (f32[8,64,1024]{2,1,0:T(8,128)S(1)}, f32[8,64,1024]{2,1,0:T(8,128)}, u32[]{:S(2)}) copy-start(f32[8,64,1024]{2,1,0:T(8,128)} %block_ref.3) | copy-start | bytes 6291460
  9.4 2.7 %collective-permute-start.4 = (f32[8,32,128]{2,1,0:T(8,128)}, f32[8,32,128]{2,1,0:T(8,128)S(1)}, u32[]{:S(2)}, u32[]{:S(2)}) collective-permute-start(f32[8,32,128]{2,1,0:T(8,128)} %get-tuple-element.147), channel_id=1, source_target_pairs={{0,1},{1,0},{2,3},{3,2},{4,5},{5,4},{6,7},{7,6},{8,9},{9,8},{10,11... | collective-permute-start | bytes 393224 | tf_op jit(solution)/shard_map/flux_sum/ppermute | solution.py:786
  13.0 14.0 %collective-permute-start.11 = (f32[96,1024]{1,0:T(8,128)}, f32[96,1024]{1,0:T(8,128)S(1)}, u32[]{:S(2)}, u32[]{:S(2)}) collective-permute-start(f32[96,1024]{1,0:T(8,128)} %get-tuple-element.149), channel_id=1, source_target_pairs={{0,8},{1,9},{2,10},{3,11},{4,12},{5,13},{6,14},{7,15},{8,16},{9,17... | collective-permute-start | bytes 1179656 | tf_op jit(solution)/shard_map/row_halo/ppermute | solution.py:780
  16.2 12.1 %collective-permute-start.12 = (f32[96,1024]{1,0:T(8,128)}, f32[96,1024]{1,0:T(8,128)S(1)}, u32[]{:S(2)}, u32[]{:S(2)}) collective-permute-start(f32[96,1024]{1,0:T(8,128)} %get-tuple-element.152), channel_id=1, source_target_pairs={{8,0},{9,1},{10,2},{11,3},{12,4},{13,5},{14,6},{15,7},{16,8},{17,9... | collective-permute-start | bytes 1179656 | tf_op jit(solution)/shard_map/row_halo/ppermute | solution.py:780
  17.5 6.0 %collective-permute-start.5 = (f32[8,32,128]{2,1,0:T(8,128)S(1)}, f32[8,32,128]{2,1,0:T(8,128)S(1)}, u32[]{:S(2)}, u32[]{:S(2)}) collective-permute-start(f32[8,32,128]{2,1,0:T(8,128)S(1)} %add.135), channel_id=1, source_target_pairs={{0,4},{1,5},{2,6},{3,7},{4,0},{5,1},{6,2},{7,3},{8,12},{9,13},{10,... | collective-permute-start | bytes 393224 | tf_op jit(solution)/shard_map/flux_sum/ppermute | solution.py:788
  20.5 6.4 %collective-permute-start.6 = (f32[8,32,128]{2,1,0:T(8,128)S(1)}, f32[8,32,128]{2,1,0:T(8,128)S(1)}, u32[]{:S(2)}, u32[]{:S(2)}) collective-permute-start(f32[8,32,128]{2,1,0:T(8,128)S(1)} %add.135), channel_id=1, source_target_pairs={{0,2},{1,3},{2,4},{3,5},{4,6},{5,7},{6,0},{7,1},{8,10},{9,11},{10,... | collective-permute-start | bytes 393224 | tf_op jit(solution)/shard_map/flux_sum/ppermute | solution.py:788
  20.9 6.0 %collective-permute-start.7 = (f32[8,32,128]{2,1,0:T(8,128)S(1)}, f32[8,32,128]{2,1,0:T(8,128)S(1)}, u32[]{:S(2)}, u32[]{:S(2)}) collective-permute-start(f32[8,32,128]{2,1,0:T(8,128)S(1)} %add.135), channel_id=1, source_target_pairs={{0,6},{1,7},{2,0},{3,1},{4,2},{5,3},{6,4},{7,5},{8,14},{9,15},{10,... | collective-permute-start | bytes 393224 | tf_op jit(solution)/shard_map/flux_sum/ppermute | solution.py:788
  27.0 48.2 %copy-start.3 = (f32[20,16,128]{2,1,0:T(8,128)S(1)}, f32[20,16,128]{2,1,0:T(8,128)}, u32[]{:S(2)}) copy-start(f32[20,16,128]{2,1,0:T(8,128)} %constant.115.clone.weights_ref) | copy-start | bytes 491524
  33.3 46.9 %collective-permute-start.13 = (f32[8,8,80,128]{3,2,1,0:T(8,128)}, f32[8,8,80,128]{3,2,1,0:T(8,128)}, u32[]{:S(2)}, u32[]{:S(2)}) collective-permute-start(f32[8,8,80,128]{3,2,1,0:T(8,128)} %get-tuple-element.158), channel_id=1, source_target_pairs={{0,1},{1,2},{2,3},{3,4},{4,5},{5,6},{6,7},{8,9},{9,10},{10,11},{11... | collective-permute-start | bytes 7864328 | tf_op jit(solution)/shard_map/depth_halo/ppermute | solution.py:780
  37.9 42.3 %collective-permute-start.14 = (f32[8,8,80,128]{3,2,1,0:T(8,128)}, f32[8,8,80,128]{3,2,1,0:T(8,128)}, u32[]{:S(2)}, u32[]{:S(2)}) collective-permute-start(f32[8,8,80,128]{3,2,1,0:T(8,128)} %get-tuple-element.158), channel_id=1, source_target_pairs={{1,0},{2,1},{3,2},{4,3},{5,4},{6,5},{7,6},{9,8},{10,9},{11,10},{12... | collective-permute-start | bytes 7864328 | tf_op jit(solution)/shard_map/depth_halo/ppermute | solution.py:780
  39.8 5.0 %collective-permute-start.9 = (f32[8,32,128]{2,1,0:T(8,128)S(1)}, f32[8,32,128]{2,1,0:T(8,128)S(1)}, u32[]{:S(2)}, u32[]{:S(2)}) collective-permute-start(f32[8,32,128]{2,1,0:T(8,128)S(1)} %add_add_fusion.own_ref), channel_id=1, source_target_pairs={{1,9},{3,11},{5,13},{7,15},{8,0},{9,17},{10,2},{11,19},{12,4},{13,... | collective-permute-start | bytes 393224 | tf_op jit(solution)/shard_map/flux_halo/ppermute | solution.py:802
  42.9 2.9 %collective-permute-start.8 = (f32[8,32,128]{2,1,0:T(8,128)S(1)}, f32[8,32,128]{2,1,0:T(8,128)S(1)}, u32[]{:S(2)}, u32[]{:S(2)}) collective-permute-start(f32[8,32,128]{2,1,0:T(8,128)S(1)} %add_add_fusion.own_ref), channel_id=1, source_target_pairs={{0,1},{1,0},{2,3},{3,2},{4,5},{5,4},{6,7},{7,6},{8,9},{9,8},{10,11... | collective-permute-start | bytes 393224 | tf_op jit(solution)/shard_map/flux_halo/ppermute | solution.py:795
  44.8 1.9 %collective-permute-start.10 = (f32[8,32,128]{2,1,0:T(8,128)S(1)}, f32[8,32,128]{2,1,0:T(8,128)S(1)}, u32[]{:S(2)}, u32[]{:S(2)}) collective-permute-start(f32[8,32,128]{2,1,0:T(8,128)S(1)} %collective-permute-done.9.same_ref), channel_id=1, source_target_pairs={{0,1},{1,0},{2,3},{3,2},{4,5},{5,4},{6,7},{7,6},{8,9},{9,8},{10,11... | collective-permute-start | bytes 393224 | tf_op jit(solution)/shard_map/flux_halo/ppermute | solution.py:803
  54.9 2.3 %copy-start.1 = (f32[10,8,16,8,128]{4,3,2,1,0:T(8,128)}, f32[10,8,16,8,128]{4,3,2,1,0:T(8,128)S(1)}, u32[]{:S(2)}) copy-start(f32[10,8,16,8,128]{4,3,2,1,0:T(8,128)S(1)} %get-tuple-element.154.part_ref) | copy-start | bytes 15728644
  57.2 17.9 %all-to-all-start = ((f32[16,8,128]{2,1,0:T(8,128)}), f32[16,8,128]{2,1,0:T(8,128)S(1)}, u32[]{:S(2)}, u32[]{:S(2)}) async-start(f32[16,8,128]{2,1,0:T(8,128)} %get-tuple-element.155), calls=%async_computation | async-start | bytes 131072 | tf_op jit(solution)/shard_map/gather_sums/all_to_all | solution.py:809
  75.2 2.5 %copy-start.2 = (f32[10,8,16,8,128]{4,3,2,1,0:T(8,128)S(1)}, f32[10,8,16,8,128]{4,3,2,1,0:T(8,128)}, u32[]{:S(2)}) copy-start(f32[10,8,16,8,128]{4,3,2,1,0:T(8,128)} %copy-done.1) | copy-start | bytes 15728644
  80.4 1.6 %copy-start.5 = (bf16[1024,1024]{1,0:T(8,128)(2,1)S(1)}, bf16[1024,1024]{1,0:T(8,128)(2,1)}, u32[]{:S(2)}) copy-start(bf16[1024,1024]{1,0:T(8,128)(2,1)} %get-tuple-element.129.select_ref) | copy-start | bytes 6291460 | tf_op jit(solution)/shard_map/cond

commit v8 on v7

--- a/solution.py
+++ b/solution.py
@@ -400,7 +400,7 @@
     )(basis, sums, jnp.asarray(solve_weights()))
 
 
-def factor_kernel(where_ref, factor):
+def fill_factors(where_ref, factor):
     vol, vols, rows = where_ref[0, 3], where_ref[0, 4], where_ref[0, 5]
     group = lax.broadcasted_iota(jnp.int32, (SUB, LANES), 0)
     mass, stiff = (8.0, 16.0), (14.0, 16.0)
@@ -419,18 +419,6 @@
                 factor[pz, px, ys] = jnp.where(outside, 0.0, jnp.float32(value))
 
 
-def relaxation_factors(where):
-    return pl.pallas_call(
-        factor_kernel,
-        out_shape=f32(2, 2, Y_GROUPS, SUB, LANES),
-        in_specs=[SMEM],
-        out_specs=VMEM,
-        compiler_params=params(16),
-        cost_estimate=cost(1),
-        name="relaxation_factors",
-    )(where)
-
-
 def lateral_lines(get, line_a, line_b, put):
     for t in range(8):
         u = row_ring([get(t, ys) for ys in range(Y_GROUPS)])
@@ -459,7 +447,7 @@
 
 
 def change_kernel(
-    where_ref, factor, speed_ref, out_ref, cells, along, cross, line_a, line_b, plain, sems,
+    where_ref, speed_ref, out_ref, cells, along, cross, line_a, line_b, factor, plain, sems,
 ):
     col = where_ref[0, 1]
     layers, _, rows, _ = out_ref.shape
@@ -494,6 +482,7 @@
 
     @pl.when(col == 0)
     def _():
+        fill_factors(where_ref, factor)
         set_top()
         clear = jnp.zeros((8, Y_GROUPS, SUB, LANES), jnp.float32)
         for z in range(2):
@@ -532,6 +521,7 @@
 
     @pl.when(col == 1)
     def _():
+        fill_factors(where_ref, factor)
         set_top()
 
         def one_sweep(sweep, carry):
@@ -545,47 +535,52 @@
         send(0, 1)
 
 
-def surface_change(where, factor, speed, layers, rows):
+def surface_change(where, speed, layers, rows):
     work = pltpu.VMEM((layers + 2, 8, Y_GROUPS, SUB, LANES), jnp.float32)
     line = pltpu.VMEM((8, Y_GROUPS, SUB, LANES), jnp.float32)
     return pl.pallas_call(
         change_kernel,
         out_shape=f32(layers, 8, rows, LANES),
-        in_specs=[SMEM, VMEM, VMEM],
+        in_specs=[SMEM, VMEM],
         out_specs=HBM,
         scratch_shapes=[
             pltpu.VMEM((layers + 3, 8, Y_GROUPS, SUB, LANES), jnp.float32),
             work, work, line, line,
+            pltpu.VMEM((2, 2, Y_GROUPS, SUB, LANES), jnp.float32),
             pltpu.VMEM((layers, 8, Y_ROWS, LANES), jnp.float32),
             pltpu.SemaphoreType.DMA((layers,)),
         ],
         compiler_params=params(32),
         cost_estimate=cost(8),
         name="surface_change",
-    )(where, factor, speed)
+    )(where, speed)
 
 
 def base_kernel(
-    where_ref, factor, wide_ref, zlow_ref, zhigh_ref, change_ref, speed_ref, select_ref,
-    velocity_ref, out_ref, field, along, cross, line_a, line_b, change, parts, sems,
+    where_ref, wide_ref, zlow_ref, zhigh_ref, change_ref, speed_ref, select_hbm_ref,
+    velocity_ref, out_ref, field, along, cross, line_a, line_b, factor, change, select, parts, sems,
 ):
     col, cols = where_ref[0, 1], where_ref[0, 2]
     layers, _, rows, _ = change_ref.shape
     total = layers + 2 * DEEP
-    own = pltpu.make_async_copy(wide_ref, field.at[pl.ds(DEEP, layers)], sems.at[0])
-    low = pltpu.make_async_copy(zlow_ref, field.at[pl.ds(0, DEEP)], sems.at[1])
-    high = pltpu.make_async_copy(zhigh_ref, field.at[pl.ds(DEEP + layers, DEEP)], sems.at[2])
+    arrivals = []
+    for i in range(total):
+        z = (i + DEEP) % total
+        source = wide_ref if i < layers else zhigh_ref if i < layers + DEEP else zlow_ref
+        arrivals.append(pltpu.make_async_copy(source.at[i % DEEP], field.at[z], sems.at[z]))
+    for arrival in arrivals:
+        arrival.start()
+    choose = pltpu.make_async_copy(select_hbm_ref, select, sems.at[total + 2])
+    choose.start()
     all_change = pltpu.make_async_copy(
-        change_ref.at[pl.ds(1, layers - 1)], change.at[pl.ds(1, layers - 1)], sems.at[3]
+        change_ref.at[pl.ds(1, layers - 1)], change.at[pl.ds(1, layers - 1)], sems.at[total]
     )
     one_change = pltpu.make_async_copy(
-        change_ref.at[pl.ds(0, 1)], change.at[pl.ds(0, 1)], sems.at[4]
+        change_ref.at[pl.ds(0, 1)], change.at[pl.ds(0, 1)], sems.at[total + 1]
     )
-    own.start()
-    low.start()
-    high.start()
     pl.when(col == 0)(all_change.start)
     pl.when(col == 1)(one_change.start)
+    fill_factors(where_ref, factor)
     count = (layers + 1) * rows
 
     def cut(value, at, t):
@@ -620,29 +615,29 @@
                 field[z + 1, t, strided(ys), :] = odd
         return carry
 
-    begin = jnp.where(col == 0, DEEP, 0)
-    end = jnp.where(col == cols - 1, DEEP + layers + 1, total - 1)
-
-    def one_sweep(sweep, carry):
-        first = jnp.maximum(begin, 2 * sweep)
-        last = jnp.minimum(end, total - 2 * sweep - 1)
-
-        @pl.when(sweep == 0)
-        def _():
-            own.wait()
-
-        lax.fori_loop(jnp.where(sweep == 0, DEEP, first), jnp.where(sweep == 0, DEEP + layers, last), lateral, 0)
-
-        @pl.when(sweep == 0)
-        def _():
-            low.wait()
-            high.wait()
-
-        lax.fori_loop(jnp.where(sweep == 0, first, DEEP), DEEP, lateral, 0)
-        lax.fori_loop(jnp.where(sweep == 0, DEEP + layers, last), last, lateral, 0)
+    def update_all(sweep):
         low_pair = jnp.where(col == 0, DEEP // 2, sweep + 1)
         high_pair = jnp.where(col == cols - 1, (DEEP + layers) // 2, total // 2 - sweep - 1)
         lax.fori_loop(low_pair, high_pair, update, 0)
+
+    begin = jnp.where(col == 0, DEEP, 0)
+    end = jnp.where(col == cols - 1, DEEP + layers + 1, total - 1)
+
+    def first_lateral(i, carry):
+        z = lax.rem(i + DEEP, total)
+        pltpu.make_async_copy(wide_ref.at[0], field.at[z], sems.at[z]).wait()
+
+        @pl.when((z >= begin) & (z < end))
+        def _():
+            lateral(z, 0)
+
+        return carry
+
+    def later_sweep(sweep, carry):
+        lax.fori_loop(
+            jnp.maximum(begin, 2 * sweep), jnp.minimum(end, total - 2 * sweep - 1), lateral, 0
+        )
+        update_all(sweep)
         return carry
 
     @pl.when(col == 0)
@@ -652,7 +647,9 @@
             along[z] = clear
             cross[z] = clear
 
-    lax.fori_loop(0, SWEEPS, one_sweep, 0)
+    lax.fori_loop(0, total, first_lateral, 0)
+    update_all(0)
+    lax.fori_loop(1, SWEEPS, later_sweep, 0)
 
     row = lax.broadcasted_iota(jnp.int32, (rows, LANES), 0)
     by_row = jnp.where(row % 2 == 0, stored(0), stored(1)).astype(jnp.float32)
@@ -682,10 +679,11 @@
         velocity_ref[:, at] = value[:rows]
         out_ref[:, :, at] = value[rows:].reshape(layers, rows, 256)
 
-    plain_columns(select_ref, parts[...], count, write)
-
-
-def base_sweeps(where, factor, wide, zlow, zhigh, change, speed, select):
+    choose.wait()
+    plain_columns(select, parts[...], count, write)
+
+
+def base_sweeps(where, wide, zlow, zhigh, change, speed, select):
     layers, _, rows, _ = change.shape
     total = layers + 2 * DEEP
     work = pltpu.VMEM((total, 8, Y_GROUPS, SUB, LANES), jnp.float32)
@@ -693,19 +691,21 @@
     return pl.pallas_call(
         base_kernel,
         out_shape=(f32(rows, 8 * LANES), f32(layers, rows, 8 * LANES)),
-        in_specs=[SMEM, VMEM] + [HBM] * 4 + [VMEM] * 2,
+        in_specs=[SMEM] + [HBM] * 4 + [VMEM, HBM],
         out_specs=(VMEM, VMEM),
         scratch_shapes=[
             pltpu.VMEM((total, 8, Y_ROWS, LANES), jnp.float32),
             work, work, line, line,
+            pltpu.VMEM((2, 2, Y_GROUPS, SUB, LANES), jnp.float32),
             pltpu.VMEM((layers, 8, rows, LANES), jnp.float32),
+            pltpu.VMEM(select.shape, jnp.bfloat16),
             pltpu.VMEM((2 * (layers + 1) * rows, 8 * LANES), jnp.bfloat16),
-            pltpu.SemaphoreType.DMA((5,)),
+            pltpu.SemaphoreType.DMA((total + 3,)),
         ],
         compiler_params=params(50),
         cost_estimate=cost(25),
         name="base_sweeps",
-    )(where, factor, wide, zlow, zhigh, change, speed, select)
+    )(where, wide, zlow, zhigh, change, speed, select)
 
 
 mass_even = (-1.0 / 15.0, 2.0 / 15.0, 8.0 / 15.0, 2.0 / 15.0, -1.0 / 15.0)
@@ -787,10 +787,12 @@
         turned = [
             lax.ppermute(keep, "col", [(j, (j + 2 * k) % cols) for j in range(cols)]) for k in (1, 2, 3)
         ]
+    with jax.named_scope("row_halo"):
+        rows_before, rows_after = moved(rows_up, (1, 0)), moved(rows_down, (-1, 0))
+    wide, root = regroup(displacement, surface_metric, rows_before, rows_after)
+    with jax.named_scope("flux_sum"):
+        turned = lax.optimization_barrier((*turned, wide))
         own = (keep + turned[1]) + (turned[0] + turned[2])
-    with jax.named_scope("row_halo"):
-        rows_before, rows_after = moved(after(rows_up, keep), (1, 0)), moved(after(rows_down, keep), (-1, 0))
-    wide, root = regroup(displacement, surface_metric, after(rows_before, own), rows_after)
     with jax.named_scope("flux_halo"):
         other = lax.ppermute(own, "col", [(j, j ^ 1) for j in range(cols)])
         pairs = []
@@ -803,16 +805,16 @@
         cross = lax.ppermute(same, "col", [(j, j ^ 1) for j in range(cols)])
 
     with jax.named_scope("depth_halo"):
-        zlow, zhigh = moved(wide, (0, 1)), moved(wide, (0, -1))
+        sent = after(wide, own)
+        zlow, zhigh = moved(sent, (0, 1)), moved(sent, (0, -1))
     basis, spread = surface_basis(where, vols, own, other, same, cross, root)
     with jax.named_scope("gather_sums"):
         gathered = lax.all_to_all(spread, "vol", 0, 0)
-    factor = relaxation_factors(after(where, own))
     speed, flag = surface_solve(basis, gathered)
 
     def finish(speed):
-        change = surface_change(where, factor, speed, displacement.shape[0], displacement.shape[1])
-        return base_sweeps(where, factor, wide, zlow, zhigh, change, speed, select)
+        change = surface_change(where, speed, displacement.shape[0], displacement.shape[1])
+        return base_sweeps(where, wide, zlow, zhigh, change, speed, select)
 
     def step_by_step():
         low = jnp.where(core == 0, own, other)

time: 112 us -> 104 us (0.929)
  blocking collectives: 0 us -> 17.7 us
  starting transfers between devices: 33.8 us -> 22.3 us
  waiting for transfers between devices: 15 us -> 6.27 us
  local copies, waits for them, and re-layouts: 4.93 us -> 0.11 us
    all_to_all x0 -> x1, blocking collectives: none -> 17.7 us  [on_device(): gathered = lax.all_to_all(spread, 'vol', 0, 0)]
    all_to_all x1 -> x0, starting transfers between devices: 11.4 us -> none  [on_device(): gathered = lax.all_to_all(spread, 'vol', 0, 0)]
    all_to_all x1 -> x0, waiting for transfers between devices: 5.93 us -> none  [on_device(): gathered = lax.all_to_all(spread, 'vol', 0, 0)]
    unnamed x10, local copies, waits for them, and re-layouts: 4.84 us -> 0.02 us
    ppermute x3, waiting for transfers between devices: 3.73 us -> 0.01 us  [on_device(): lax.ppermute(keep, 'col', [(j, (j + 2 * k) % cols) for j in range(cols)])]
  transfers between devices with their start and end apart: 12 -> 11, of which waited for: 7 -> 4; matrix products, arithmetic and copies ran while one was open for 0% -> 1% of each run, Pallas kernels for 10% -> 14%
where the time goes in v8:
time: 104 us; the launch traced here: 102 us
  Pallas kernels  52.4 us (50%)
  starting transfers between devices  22.3 us (21%)
  blocking collectives  17.7 us (17%)
  waiting for transfers between devices  6.27 us (6%)
  between operations  2.41 us (2%)
    pallas_call x1, Pallas kernels, base_sweeps(): pl.pallas_call(base_kernel, out_shape=(f32(rows, 8 * LANES), f32(layers,...  27.8 us
    all_to_all x1, blocking collectives, on_device(): gathered = lax.all_to_all(spread, 'vol', 0, 0)  17.7 us
    ppermute x4, starting transfers between devices, moved(): return lax.ppermute(x, ('vol', 'col'), pairs)  12.1 us
    pallas_call x1, Pallas kernels, face_sums(): pl.pallas_call(face_kernel, out_shape=(half, half, rows, rows), in_specs=...  7.84 us
    pallas_call x1, Pallas kernels, surface_basis(): pl.pallas_call(basis_kernel, out_shape=(f32(ITERS, 8, GROUPS, SUB, LANES)...  7.48 us
    ppermute x3, starting transfers between devices, on_device(): lax.ppermute(keep, 'col', [(j, (j + 2 * k) % cols) for j in range(cols)])  5.06 us
    pallas_call x1, Pallas kernels, regroup(): pl.pallas_call(regroup_kernel, out_shape=(f32(layers, 8, Y_ROWS, LANES),...  4.88 us
    ppermute x1, starting transfers between devices, on_device(): same = lax.ppermute(own, ('vol', 'col'), pairs)  3.1 us
  transfers between devices with their start and end apart: 11, of which 4 were waited for; matrix products, arithmetic and copies ran while one was open for 1% of the time, Pallas kernels for 14%

profile of v8, /device:TPU:1, one launch (start us, length us, event | category | flops | bytes accessed | tf_op | source)
XLA Modules:
  0.0 102.4 jit_solution(1850017596911662840)
XLA Ops:
  0.6 0.0 copy-start
  0.6 0.0 copy-start.3
  1.5 0.1 stack.15
  1.5 7.8 %face_sums.1 = (f32[8,32,128]{2,1,0:T(8,128)}, f32[8,32,128]{2,1,0:T(8,128)}, f32[96,1024]{1,0:T(8,128)}, f32[96,1024]{1,0:T(8,128)}) custom-call(s32[1,6]{1,0:T(1,128)S(1)} %bitcast.17, s32[1,1]{1,0:T(1,128)S(6)} %copy.41.count_ref, f32[1,16384]{1,0:T(1,128)} %area_ref.1, f32[1,16384]{1,0:T(1,128)} %speed_ref.1, s32[1,16384]{1,0:T(1,128)} %node_ref.1, ...), custom_call_target="tpu_custom_call" | custom-call | bytes 700000 | tf_op jit(solution)/shard_map/face_sums/pallas_call | solution.py:226
  9.4 4.0 %collective-permute-start.8 = (f32[96,1024]{1,0:T(8,128)}, f32[96,1024]{1,0:T(8,128)S(1)}, u32[]{:S(2)}, u32[]{:S(2)}) collective-permute-start(f32[96,1024]{1,0:T(8,128)} %get-tuple-element.142), channel_id=1, source_target_pairs={{0,8},{1,9},{2,10},{3,11},{4,12},{5,13},{6,14},{7,15},{8,16},{9,17... | collective-permute-start | bytes 1179656 | tf_op jit(solution)/shard_map/row_halo/ppermute | solution.py:780
  13.4 1.3 %collective-permute-start.9 = (f32[96,1024]{1,0:T(8,128)}, f32[96,1024]{1,0:T(8,128)S(1)}, u32[]{:S(2)}, u32[]{:S(2)}) collective-permute-start(f32[96,1024]{1,0:T(8,128)} %get-tuple-element.143), channel_id=1, source_target_pairs={{8,0},{9,1},{10,2},{11,3},{12,4},{13,5},{14,6},{15,7},{16,8},{17,9... | collective-permute-start | bytes 1179656 | tf_op jit(solution)/shard_map/row_halo/ppermute | solution.py:780
  14.7 1.0 %collective-permute-start.4 = (f32[8,32,128]{2,1,0:T(8,128)}, f32[8,32,128]{2,1,0:T(8,128)S(1)}, u32[]{:S(2)}, u32[]{:S(2)}) collective-permute-start(f32[8,32,128]{2,1,0:T(8,128)} %get-tuple-element.141), channel_id=1, source_target_pairs={{0,1},{1,0},{2,3},{3,2},{4,5},{5,4},{6,7},{7,6},{8,9},{9,8},{10,11... | collective-permute-start | bytes 393224 | tf_op jit(solution)/shard_map/flux_sum/ppermute | solution.py:786
  15.7 1.2 %collective-permute-done.4 = f32[8,32,128]{2,1,0:T(8,128)S(1)} collective-permute-done((f32[8,32,128]{2,1,0:T(8,128)}, f32[8,32,128]{2,1,0:T(8,128)S(1)}, u32[]{:S(2)}, u32[]{:S(2)}) %collective-permute-start.4) | collective-permute-done | bytes 131104 | tf_op jit(solution)/shard_map/flux_sum/ppermute | solution.py:786
  16.9 0.9 add.135
  17.8 0.0 copy-start.1
  17.8 1.4 %collective-permute-start.5 = (f32[8,32,128]{2,1,0:T(8,128)S(1)}, f32[8,32,128]{2,1,0:T(8,128)S(1)}, u32[]{:S(2)}, u32[]{:S(2)}) collective-permute-start(f32[8,32,128]{2,1,0:T(8,128)S(1)} %add.135), channel_id=1, source_target_pairs={{0,2},{1,3},{2,4},{3,5},{4,6},{5,7},{6,0},{7,1},{8,10},{9,11},{10,... | collective-permute-start | bytes 393224 | tf_op jit(solution)/shard_map/flux_sum/ppermute | solution.py:788
  19.2 2.6 %collective-permute-start.6 = (f32[8,32,128]{2,1,0:T(8,128)S(1)}, f32[8,32,128]{2,1,0:T(8,128)S(1)}, u32[]{:S(2)}, u32[]{:S(2)}) collective-permute-start(f32[8,32,128]{2,1,0:T(8,128)S(1)} %add.135), channel_id=1, source_target_pairs={{0,4},{1,5},{2,6},{3,7},{4,0},{5,1},{6,2},{7,3},{8,12},{9,13},{10,... | collective-permute-start | bytes 393224 | tf_op jit(solution)/shard_map/flux_sum/ppermute | solution.py:788
  21.8 1.1 %collective-permute-start.7 = (f32[8,32,128]{2,1,0:T(8,128)S(1)}, f32[8,32,128]{2,1,0:T(8,128)S(1)}, u32[]{:S(2)}, u32[]{:S(2)}) collective-permute-start(f32[8,32,128]{2,1,0:T(8,128)S(1)} %add.135), channel_id=1, source_target_pairs={{0,6},{1,7},{2,0},{3,1},{4,2},{5,3},{6,4},{7,5},{8,14},{9,15},{10,... | collective-permute-start | bytes 393224 | tf_op jit(solution)/shard_map/flux_sum/ppermute | solution.py:788
  22.9 0.0 collective-permute-done.8.before_ref
  22.9 2.2 %collective-permute-done.9.after_ref = f32[96,1024]{1,0:T(8,128)S(1)} collective-permute-done((f32[96,1024]{1,0:T(8,128)}, f32[96,1024]{1,0:T(8,128)S(1)}, u32[]{:S(2)}, u32[]{:S(2)}) %collective-permute-start.9) | collective-permute-done | bytes 393248 | tf_op jit(solution)/shard_map/row_halo/ppermute | solution.py:780
  25.1 0.0 copy-done
  25.1 0.0 copy-done.3
  25.1 4.9 %regroup.1 = (f32[8,8,80,128]{3,2,1,0:T(8,128)}, f32[8,128,128]{2,1,0:T(8,128)S(1)}) custom-call(f32[8,64,1024]{2,1,0:T(8,128)S(1)} %copy-done, f32[64,1024]{1,0:T(8,128)S(1)} %copy-done.3, f32[96,1024]{1,0:T(8,128)S(1)} %collective-permute-done.8.before_ref, f32[96,1024]{1,0:T(8,128)S(1)} %collective-permute-done.9.after_ref), custom_call_target="tpu_custom_call" | custom-call | bytes 15000000 | tf_op jit(solution)/shard_map/regroup/pallas_call | solution.py:140
  30.0 0.0 collective-permute-done.5
  30.0 0.0 collective-permute-done.6
  30.0 0.0 collective-permute-done.7
  30.1 4.9 %collective-permute-start.13 = (f32[8,8,80,128]{3,2,1,0:T(8,128)}, f32[8,8,80,128]{3,2,1,0:T(8,128)}, u32[]{:S(2)}, u32[]{:S(2)}) collective-permute-start(f32[8,8,80,128]{3,2,1,0:T(8,128)} %get-tuple-element.152), channel_id=1, source_target_pairs={{0,1},{1,2},{2,3},{3,4},{4,5},{5,6},{6,7},{8,9},{9,10},{10,11},{11... | collective-permute-start | bytes 7864328 | tf_op jit(solution)/shard_map/depth_halo/ppermute | solution.py:780
  35.0 1.9 %collective-permute-start.14 = (f32[8,8,80,128]{3,2,1,0:T(8,128)}, f32[8,8,80,128]{3,2,1,0:T(8,128)}, u32[]{:S(2)}, u32[]{:S(2)}) collective-permute-start(f32[8,8,80,128]{3,2,1,0:T(8,128)} %get-tuple-element.152), channel_id=1, source_target_pairs={{1,0},{2,1},{3,2},{4,3},{5,4},{6,5},{7,6},{9,8},{10,9},{11,10},{12... | collective-permute-start | bytes 7864328 | tf_op jit(solution)/shard_map/depth_halo/ppermute | solution.py:780
  37.0 3.1 %collective-permute-start.11 = (f32[8,32,128]{2,1,0:T(8,128)S(1)}, f32[8,32,128]{2,1,0:T(8,128)S(1)}, u32[]{:S(2)}, u32[]{:S(2)}) collective-permute-start(f32[8,32,128]{2,1,0:T(8,128)S(1)} %add_add_fusion.own_ref), channel_id=1, source_target_pairs={{1,9},{3,11},{5,13},{7,15},{8,0},{9,17},{10,2},{11,19},{12,4},{13,... | collective-permute-start | bytes 393224 | tf_op jit(solution)/shard_map/flux_halo/ppermute | solution.py:804
  40.1 0.1 collective-permute-start.10
  40.2 1.8 %collective-permute-done.11.same_ref = f32[8,32,128]{2,1,0:T(8,128)S(1)} collective-permute-done((f32[8,32,128]{2,1,0:T(8,128)S(1)}, f32[8,32,128]{2,1,0:T(8,128)S(1)}, u32[]{:S(2)}, u32[]{:S(2)}) %collective-permute-start.11) | collective-permute-done | bytes 131104 | tf_op jit(solution)/shard_map/flux_halo/ppermute | solution.py:804
  42.0 0.9 collective-permute-start.12
  42.9 0.0 collective-permute-done.10.other_ref
  42.9 1.0 collective-permute-done.12.cross_ref
  43.9 7.5 %surface_basis.1 = (f32[10,8,16,8,128]{4,3,2,1,0:T(8,128)S(1)}, f32[16,8,128]{2,1,0:T(8,128)S(1)}) custom-call(s32[1,6]{1,0:T(1,128)S(1)} %bitcast.18, f32[8,32,128]{2,1,0:T(8,128)S(1)} %add_add_fusion.own_ref, f32[8,32,128]{2,1,0:T(8,128)S(1)} %collective-permute-done.10.other_ref, f32[8,32,128]{2,1,0:T(8,128)S(1)} %collective-permute-done.11.same_ref, ...), custom_call_target="tpu_custom_call" | custom-call | bytes 700000 | tf_op jit(solution)/shard_map/surface_basis/pallas_call | solution.py:314
  51.4 17.7 %all_to_all.5.sums_ref = f32[16,8,128]{2,1,0:T(8,128)S(1)} all-to-all(f32[16,8,128]{2,1,0:T(8,128)S(1)} %get-tuple-element.150), channel_id=1, replica_groups=mesh['vol'=16,'col'=8] {'vol'}, dimensions={0} | all-to-all | bytes 131072 | tf_op jit(solution)/shard_map/gather_sums/all_to_all | solution.py:812
  69.1 0.0 copy-done.1
  69.1 0.0 copy-start.2
  69.1 0.0 copy-start.4
  69.1 2.3 %surface_solve.1 = (f32[8,80,128]{2,1,0:T(8,128)}, s32[1,1]{1,0:T(1,128)}) custom-call(f32[10,8,16,8,128]{4,3,2,1,0:T(8,128)S(1)} %get-tuple-element.149.part_ref, f32[16,8,128]{2,1,0:T(8,128)S(1)} %all_to_all.5.sums_ref, f32[20,16,128]{2,1,0:T(8,128)S(1)} %copy-done.1), custom_call_target="tpu_custom_call" | custom-call | bytes 300000 | tf_op jit(solution)/shard_map/surface_solve/pallas_call | solution.py:391
  72.1 0.0 collective-permute-done.13
  72.1 0.0 collective-permute-done.14
  72.1 0.0 copy-done.2
  72.1 0.0 copy-done.4
  72.1 30.2 %conditional.1 = ((f32[64,1024]{1,0:T(8,128)}, f32[8,64,1024]{2,1,0:T(8,128)})) conditional(s32[]{:T(128)} %bitcast.9, (s32[]{:T(128)}, f32[8,32,128]{2,1,0:T(8,128)S(1)}, f32[8,32,128]{2,1,0:T(8,128)S(1)}, f32[64,1024]{1,0:T(8,128)S(1)}, s32[1,6]{1,0:T(1,128)S(1)}, /*index=5*/f32[8,8,80,128]{3,2,1,0:T(8,128)}, f32[8,8,80,128]{3,2,1,0:T(8,128)}, ...), branch_computations={%region_0.9_spmd, %region_9.10_spmd} | conditional | flops 3516806 | bytes 15280337 | solution.py:827
  72.3 0.0 copy-start.5
  72.4 2.1 %surface_change.3.change_ref = f32[8,8,64,128]{3,2,1,0:T(8,128)S(1)} custom-call(s32[1,6]{1,0:T(1,128)S(1)} %get-tuple-element.118.where_ref, f32[8,80,128]{2,1,0:T(8,128)} %get-tuple-element.122.speed_ref), custom_call_target="tpu_custom_call" | custom-call | bytes 800000 | tf_op jit(solution)/shard_map/cond/branch_1_fun/surface_change/pallas_call | solution.py:541
  74.5 0.0 copy-done.5
  74.5 27.8 %base_sweeps.3 = (f32[64,1024]{1,0:T(8,128)}, f32[8,64,1024]{2,1,0:T(8,128)}) custom-call(s32[1,6]{1,0:T(1,128)S(1)} %get-tuple-element.118.where_ref, f32[8,8,80,128]{3,2,1,0:T(8,128)} %get-tuple-element.119.wide_ref, f32[8,8,80,128]{3,2,1,0:T(8,128)} %get-tuple-element.120.zlow_ref, f32[8,8,80,128]{3,2,1,0:T(8,128)} %get-tuple-element.121.zhigh_ref, ...), custom_call_target="tpu_custom_call" | custom-call | bytes 2500000 | tf_op jit(solution)/shard_map/cond/branch_1_fun/base_sweeps/pallas_call | solution.py:691
  (1 shorter events, 0.0 us)
Async XLA Ops:
  0.6 24.5 %copy-start = (f32[8,64,1024]{2,1,0:T(8,128)S(1)}, f32[8,64,1024]{2,1,0:T(8,128)}, u32[]{:S(2)}) copy-start(f32[8,64,1024]{2,1,0:T(8,128)} %block_ref.3) | copy-start | bytes 6291460
  0.6 24.5 %copy-start.3 = (f32[64,1024]{1,0:T(8,128)S(1)}, f32[64,1024]{1,0:T(8,128)}, u32[]{:S(2)}) copy-start(f32[64,1024]{1,0:T(8,128)} %metric_ref.3) | copy-start | bytes 786436
  9.4 13.5 %collective-permute-start.8 = (f32[96,1024]{1,0:T(8,128)}, f32[96,1024]{1,0:T(8,128)S(1)}, u32[]{:S(2)}, u32[]{:S(2)}) collective-permute-start(f32[96,1024]{1,0:T(8,128)} %get-tuple-element.142), channel_id=1, source_target_pairs={{0,8},{1,9},{2,10},{3,11},{4,12},{5,13},{6,14},{7,15},{8,16},{9,17... | collective-permute-start | bytes 1179656 | tf_op jit(solution)/shard_map/row_halo/ppermute | solution.py:780
  13.4 11.8 %collective-permute-start.9 = (f32[96,1024]{1,0:T(8,128)}, f32[96,1024]{1,0:T(8,128)S(1)}, u32[]{:S(2)}, u32[]{:S(2)}) collective-permute-start(f32[96,1024]{1,0:T(8,128)} %get-tuple-element.143), channel_id=1, source_target_pairs={{8,0},{9,1},{10,2},{11,3},{12,4},{13,5},{14,6},{15,7},{16,8},{17,9... | collective-permute-start | bytes 1179656 | tf_op jit(solution)/shard_map/row_halo/ppermute | solution.py:780
  14.7 2.2 %collective-permute-start.4 = (f32[8,32,128]{2,1,0:T(8,128)}, f32[8,32,128]{2,1,0:T(8,128)S(1)}, u32[]{:S(2)}, u32[]{:S(2)}) collective-permute-start(f32[8,32,128]{2,1,0:T(8,128)} %get-tuple-element.141), channel_id=1, source_target_pairs={{0,1},{1,0},{2,3},{3,2},{4,5},{5,4},{6,7},{7,6},{8,9},{9,8},{10,11... | collective-permute-start | bytes 393224 | tf_op jit(solution)/shard_map/flux_sum/ppermute | solution.py:786
  17.8 51.3 %copy-start.1 = (f32[20,16,128]{2,1,0:T(8,128)S(1)}, f32[20,16,128]{2,1,0:T(8,128)}, u32[]{:S(2)}) copy-start(f32[20,16,128]{2,1,0:T(8,128)} %constant.115.clone.weights_ref) | copy-start | bytes 491524
  17.8 12.2 %collective-permute-start.5 = (f32[8,32,128]{2,1,0:T(8,128)S(1)}, f32[8,32,128]{2,1,0:T(8,128)S(1)}, u32[]{:S(2)}, u32[]{:S(2)}) collective-permute-start(f32[8,32,128]{2,1,0:T(8,128)S(1)} %add.135), channel_id=1, source_target_pairs={{0,2},{1,3},{2,4},{3,5},{4,6},{5,7},{6,0},{7,1},{8,10},{9,11},{10,... | collective-permute-start | bytes 393224 | tf_op jit(solution)/shard_map/flux_sum/ppermute | solution.py:788
  19.2 10.8 %collective-permute-start.6 = (f32[8,32,128]{2,1,0:T(8,128)S(1)}, f32[8,32,128]{2,1,0:T(8,128)S(1)}, u32[]{:S(2)}, u32[]{:S(2)}) collective-permute-start(f32[8,32,128]{2,1,0:T(8,128)S(1)} %add.135), channel_id=1, source_target_pairs={{0,4},{1,5},{2,6},{3,7},{4,0},{5,1},{6,2},{7,3},{8,12},{9,13},{10,... | collective-permute-start | bytes 393224 | tf_op jit(solution)/shard_map/flux_sum/ppermute | solution.py:788
  21.8 8.2 %collective-permute-start.7 = (f32[8,32,128]{2,1,0:T(8,128)S(1)}, f32[8,32,128]{2,1,0:T(8,128)S(1)}, u32[]{:S(2)}, u32[]{:S(2)}) collective-permute-start(f32[8,32,128]{2,1,0:T(8,128)S(1)} %add.135), channel_id=1, source_target_pairs={{0,6},{1,7},{2,0},{3,1},{4,2},{5,3},{6,4},{7,5},{8,14},{9,15},{10,... | collective-permute-start | bytes 393224 | tf_op jit(solution)/shard_map/flux_sum/ppermute | solution.py:788
  30.1 42.0 %collective-permute-start.13 = (f32[8,8,80,128]{3,2,1,0:T(8,128)}, f32[8,8,80,128]{3,2,1,0:T(8,128)}, u32[]{:S(2)}, u32[]{:S(2)}) collective-permute-start(f32[8,8,80,128]{3,2,1,0:T(8,128)} %get-tuple-element.152), channel_id=1, source_target_pairs={{0,1},{1,2},{2,3},{3,4},{4,5},{5,6},{6,7},{8,9},{9,10},{10,11},{11... | collective-permute-start | bytes 7864328 | tf_op jit(solution)/shard_map/depth_halo/ppermute | solution.py:780
  35.0 37.0 %collective-permute-start.14 = (f32[8,8,80,128]{3,2,1,0:T(8,128)}, f32[8,8,80,128]{3,2,1,0:T(8,128)}, u32[]{:S(2)}, u32[]{:S(2)}) collective-permute-start(f32[8,8,80,128]{3,2,1,0:T(8,128)} %get-tuple-element.152), channel_id=1, source_target_pairs={{1,0},{2,1},{3,2},{4,3},{5,4},{6,5},{7,6},{9,8},{10,9},{11,10},{12... | collective-permute-start | bytes 7864328 | tf_op jit(solution)/shard_map/depth_halo/ppermute | solution.py:780
  37.0 5.0 %collective-permute-start.11 = (f32[8,32,128]{2,1,0:T(8,128)S(1)}, f32[8,32,128]{2,1,0:T(8,128)S(1)}, u32[]{:S(2)}, u32[]{:S(2)}) collective-permute-start(f32[8,32,128]{2,1,0:T(8,128)S(1)} %add_add_fusion.own_ref), channel_id=1, source_target_pairs={{1,9},{3,11},{5,13},{7,15},{8,0},{9,17},{10,2},{11,19},{12,4},{13,... | collective-permute-start | bytes 393224 | tf_op jit(solution)/shard_map/flux_halo/ppermute | solution.py:804
  40.1 2.8 %collective-permute-start.10 = (f32[8,32,128]{2,1,0:T(8,128)S(1)}, f32[8,32,128]{2,1,0:T(8,128)S(1)}, u32[]{:S(2)}, u32[]{:S(2)}) collective-permute-start(f32[8,32,128]{2,1,0:T(8,128)S(1)} %add_add_fusion.own_ref), channel_id=1, source_target_pairs={{0,1},{1,0},{2,3},{3,2},{4,5},{5,4},{6,7},{7,6},{8,9},{9,8},{10,11... | collective-permute-start | bytes 393224 | tf_op jit(solution)/shard_map/flux_halo/ppermute | solution.py:797
  42.0 1.9 %collective-permute-start.12 = (f32[8,32,128]{2,1,0:T(8,128)S(1)}, f32[8,32,128]{2,1,0:T(8,128)S(1)}, u32[]{:S(2)}, u32[]{:S(2)}) collective-permute-start(f32[8,32,128]{2,1,0:T(8,128)S(1)} %collective-permute-done.11.same_ref), channel_id=1, source_target_pairs={{0,1},{1,0},{2,3},{3,2},{4,5},{5,4},{6,7},{7,6},{8,9},{9,8},{10,11... | collective-permute-start | bytes 393224 | tf_op jit(solution)/shard_map/flux_halo/ppermute | solution.py:805
  69.1 3.0 %copy-start.2 = (bf16[1024,1024]{1,0:T(8,128)(2,1)S(1)}, bf16[1024,1024]{1,0:T(8,128)(2,1)}, u32[]{:S(2)}) copy-start(bf16[1024,1024]{1,0:T(8,128)(2,1)} %constant.114.clone) | copy-start | bytes 6291460
  69.1 3.0 %copy-start.4 = (f32[64,1024]{1,0:T(8,128)S(1)}, f32[64,1024]{1,0:T(8,128)}, u32[]{:S(2)}) copy-start(f32[64,1024]{1,0:T(8,128)} %metric_ref.3) | copy-start | bytes 786436
  72.3 2.1 %copy-start.5 = (f32[8,80,128]{2,1,0:T(8,128)S(1)}, f32[8,80,128]{2,1,0:T(8,128)}, u32[]{:S(2)}) copy-start(f32[8,80,128]{2,1,0:T(8,128)} %get-tuple-element.122.speed_ref) | copy-start | bytes 983044 | tf_op jit(solution)/shard_map/cond

commit v9 on v8

--- a/solution.py
+++ b/solution.py
@@ -157,8 +157,8 @@
 
 
 def face_kernel(
-    where_ref, count_ref, area_ref, speed_ref, node_ref, block_ref, metric_ref,
-    keep_ref, send_ref, up_ref, down_ref, area, speed, nodes, acc_ref, sems,
+    where_ref, count_ref, area_ref, speed_ref, node_ref,
+    keep_ref, send_ref, area, speed, nodes, acc_ref, sems,
 ):
     slots = area_ref.shape[1]
     fetches = [
@@ -167,17 +167,6 @@
     ]
     for fetch in fetches:
         fetch.start()
-    layers, rows, _ = block_ref.shape
-    copies = []
-    for out_ref, row, root_row in ((up_ref, rows - DEEP, rows - HALO), (down_ref, 0, 0)):
-        for z in range(layers):
-            part = block_ref.at[z, pl.ds(row, DEEP), :]
-            copies.append((part, out_ref.at[pl.ds(DEEP * z, DEEP), :]))
-        part = metric_ref.at[pl.ds(root_row, HALO), :]
-        copies.append((part, out_ref.at[pl.ds(DEEP * layers, HALO), :]))
-    copies = [pltpu.make_async_copy(*pair, sems.at[i + 3]) for i, pair in enumerate(copies)]
-    for copy in copies:
-        copy.start()
     chunk = min(4096, slots)
     core = where_ref[0, 0]
     ids = lax.broadcasted_iota(jnp.int32, (256, chunk), 0)
@@ -215,30 +204,57 @@
         near, far = at + 32 * core, at + 32 - 32 * core
         keep_ref[j] = acc_ref[pl.ds(near, 32), lanes] + acc_ref[pl.ds(256 + near, 32), lanes]
         send_ref[j] = acc_ref[pl.ds(far, 32), lanes] + acc_ref[pl.ds(256 + far, 32), lanes]
-    for copy in copies:
-        copy.wait()
-
-
-def face_sums(where, count, area, speed, node, block, metric):
+
+
+def face_sums(where, count, area, speed, node):
     half = f32(8, 32, LANES)
-    layers, _, cols = block.shape
-    rows = f32(DEEP * layers + HALO, cols)
     return pl.pallas_call(
         face_kernel,
-        out_shape=(half, half, rows, rows),
-        in_specs=[SMEM, SMEM] + [HBM] * 5,
-        out_specs=(VMEM, VMEM, VMEM, VMEM),
+        out_shape=(half, half),
+        in_specs=[SMEM, SMEM] + [HBM] * 3,
+        out_specs=(VMEM, VMEM),
         scratch_shapes=[
             pltpu.VMEM(area.shape, jnp.float32),
             pltpu.VMEM(area.shape, jnp.float32),
             pltpu.VMEM(area.shape, jnp.int32),
             pltpu.VMEM((512, 256), jnp.float32),
-            pltpu.SemaphoreType.DMA((2 * layers + 5,)),
+            pltpu.SemaphoreType.DMA((3,)),
         ],
         compiler_params=params(56),
         cost_estimate=cost(7),
         name="face_sums",
-    )(where, count, area, speed, node, block, metric)
+    )(where, count, area, speed, node)
+
+
+def cut_kernel(block_ref, metric_ref, up_ref, down_ref, sems):
+    layers, rows, _ = block_ref.shape
+    copies = []
+    for out_ref, row, root_row in ((up_ref, rows - DEEP, rows - HALO), (down_ref, 0, 0)):
+        for z in range(layers):
+            part = block_ref.at[z, pl.ds(row, DEEP), :]
+            copies.append((part, out_ref.at[pl.ds(DEEP * z, DEEP), :]))
+        part = metric_ref.at[pl.ds(root_row, HALO), :]
+        copies.append((part, out_ref.at[pl.ds(DEEP * layers, HALO), :]))
+    copies = [pltpu.make_async_copy(*pair, sems.at[i]) for i, pair in enumerate(copies)]
+    for copy in copies:
+        copy.start()
+    for copy in copies:
+        copy.wait()
+
+
+def outgoing_rows(block, metric):
+    layers, _, cols = block.shape
+    rows = f32(DEEP * layers + HALO, cols)
+    return pl.pallas_call(
+        cut_kernel,
+        out_shape=(rows, rows),
+        in_specs=[HBM, HBM],
+        out_specs=(VMEM, VMEM),
+        scratch_shapes=[pltpu.SemaphoreType.DMA((2 * layers + 2,))],
+        compiler_params=params(56),
+        cost_estimate=cost(1),
+        name="outgoing_rows",
+    )(block, metric)
 
 
 def basis_kernel(
@@ -779,9 +795,8 @@
         ]
         return lax.ppermute(x, ("vol", "col"), pairs)
 
-    keep, send, rows_up, rows_down = face_sums(
-        where, face_count, face_area, face_speed, face_node, displacement, surface_metric
-    )
+    rows_up, rows_down = outgoing_rows(displacement, surface_metric)
+    keep, send = face_sums(where, face_count, after(face_area, rows_up), face_speed, face_node)
     with jax.named_scope("flux_sum"):
         keep = keep + lax.ppermute(send, "col", [(j, j ^ 1) for j in range(cols)])
         turned = [

time: 104 us -> 101 us (0.971)
  waiting for transfers between devices: 6.27 us -> 4.12 us
  Pallas kernels: 52.4 us -> 54.3 us
  blocking collectives: 17.7 us -> 16.1 us
    ppermute x4, waiting for transfers between devices: 2.25 us -> 0.01 us  [moved(): return lax.ppermute(x, ('vol', 'col'), pairs)]
    pallas_call x1 -> x2, Pallas kernels: 7.84 us -> 9.76 us  [the longest x1 7.38 us: face_sums(): pl.pallas_call(face_kernel, out_shape=(half, half), in_specs=[SMEM, SMEM]...]
    all_to_all x1, blocking collectives: 17.7 us -> 16.1 us  [on_device(): gathered = lax.all_to_all(spread, 'vol', 0, 0)]
    ppermute x1, starting transfers between devices: 3.1 us -> 4.27 us  [on_device(): same = lax.ppermute(own, ('vol', 'col'), pairs)]
  transfers between devices with their start and end apart: 11 -> 11, of which waited for: 4 -> 4; matrix products, arithmetic and copies ran while one was open for 1% -> 1% of each run, Pallas kernels for 14% -> 22%
where the time goes in v9:
time: 101 us; the launch traced here: 100 us
  Pallas kernels  54.3 us (54%)
  starting transfers between devices  22.3 us (22%)
  blocking collectives  16.1 us (16%)
  waiting for transfers between devices  4.12 us (4%)
  between operations  2.27 us (2%)
    pallas_call x1, Pallas kernels, base_sweeps(): pl.pallas_call(base_kernel, out_shape=(f32(rows, 8 * LANES), f32(layers,...  27.8 us
    all_to_all x1, blocking collectives, on_device(): gathered = lax.all_to_all(spread, 'vol', 0, 0)  16.1 us
    ppermute x4, starting transfers between devices, moved(): return lax.ppermute(x, ('vol', 'col'), pairs)  11.2 us
    pallas_call x1, Pallas kernels, surface_basis(): pl.pallas_call(basis_kernel, out_shape=(f32(ITERS, 8, GROUPS, SUB, LANES)...  7.48 us
    pallas_call x1, Pallas kernels, face_sums(): pl.pallas_call(face_kernel, out_shape=(half, half), in_specs=[SMEM, SMEM]...  7.38 us
    ppermute x3, starting transfers between devices, on_device(): lax.ppermute(keep, 'col', [(j, (j + 2 * k) % cols) for j in range(cols)])  5.06 us
    pallas_call x1, Pallas kernels, regroup(): pl.pallas_call(regroup_kernel, out_shape=(f32(layers, 8, Y_ROWS, LANES),...  4.87 us
    ppermute x1, starting transfers between devices, on_device(): same = lax.ppermute(own, ('vol', 'col'), pairs)  4.27 us
  transfers between devices with their start and end apart: 11, of which 4 were waited for; matrix products, arithmetic and copies ran while one was open for 1% of the time, Pallas kernels for 22%

profile of v9, /device:TPU:1, one launch (start us, length us, event | category | flops | bytes accessed | tf_op | source)
XLA Modules:
  0.0 100.4 jit_solution(17287359400823293129)
XLA Ops:
  0.6 0.0 copy-start
  0.6 0.0 copy-start.3
  0.7 2.4 %outgoing_rows.1 = (f32[96,1024]{1,0:T(8,128)}, f32[96,1024]{1,0:T(8,128)}) custom-call(f32[8,64,1024]{2,1,0:T(8,128)} %block_ref.3, f32[64,1024]{1,0:T(8,128)} %metric_ref.3), custom_call_target="tpu_custom_call" | custom-call | bytes 100000 | tf_op jit(solution)/shard_map/outgoing_rows/pallas_call | solution.py:248
  3.0 4.0 %collective-permute-start.8 = (f32[96,1024]{1,0:T(8,128)}, f32[96,1024]{1,0:T(8,128)S(1)}, u32[]{:S(2)}, u32[]{:S(2)}) collective-permute-start(f32[96,1024]{1,0:T(8,128)} %get-tuple-element.141), channel_id=1, source_target_pairs={{0,8},{1,9},{2,10},{3,11},{4,12},{5,13},{6,14},{7,15},{8,16},{9,17... | collective-permute-start | bytes 1179656 | tf_op jit(solution)/shard_map/row_halo/ppermute | solution.py:796
  7.0 1.3 %collective-permute-start.9 = (f32[96,1024]{1,0:T(8,128)}, f32[96,1024]{1,0:T(8,128)S(1)}, u32[]{:S(2)}, u32[]{:S(2)}) collective-permute-start(f32[96,1024]{1,0:T(8,128)} %get-tuple-element.145), channel_id=1, source_target_pairs={{8,0},{9,1},{10,2},{11,3},{12,4},{13,5},{14,6},{15,7},{16,8},{17,9... | collective-permute-start | bytes 1179656 | tf_op jit(solution)/shard_map/row_halo/ppermute | solution.py:796
  9.0 0.1 stack.15
  9.1 7.4 %face_sums.1 = (f32[8,32,128]{2,1,0:T(8,128)}, f32[8,32,128]{2,1,0:T(8,128)}) custom-call(s32[1,6]{1,0:T(1,128)S(1)} %bitcast.17, s32[1,1]{1,0:T(1,128)S(6)} %copy.41.count_ref, f32[1,16384]{1,0:T(1,128)} %area_ref, f32[1,16384]{1,0:T(1,128)} %speed_ref.1, s32[1,16384]{1,0:T(1,128)} %node_ref.1), custom_call_target="tpu_custom_call" | custom-call | bytes 700000 | tf_op jit(solution)/shard_map/face_sums/pallas_call | solution.py:211
  16.5 1.0 %collective-permute-start.4 = (f32[8,32,128]{2,1,0:T(8,128)}, f32[8,32,128]{2,1,0:T(8,128)S(1)}, u32[]{:S(2)}, u32[]{:S(2)}) collective-permute-start(f32[8,32,128]{2,1,0:T(8,128)} %get-tuple-element.144), channel_id=1, source_target_pairs={{0,1},{1,0},{2,3},{3,2},{4,5},{5,4},{6,7},{7,6},{8,9},{9,8},{10,11... | collective-permute-start | bytes 393224 | tf_op jit(solution)/shard_map/flux_sum/ppermute | solution.py:801
  17.5 1.2 %collective-permute-done.4 = f32[8,32,128]{2,1,0:T(8,128)S(1)} collective-permute-done((f32[8,32,128]{2,1,0:T(8,128)}, f32[8,32,128]{2,1,0:T(8,128)S(1)}, u32[]{:S(2)}, u32[]{:S(2)}) %collective-permute-start.4) | collective-permute-done | bytes 131104 | tf_op jit(solution)/shard_map/flux_sum/ppermute | solution.py:801
  18.7 0.9 add.135
  19.6 0.0 copy-start.1
  19.6 1.4 %collective-permute-start.5 = (f32[8,32,128]{2,1,0:T(8,128)S(1)}, f32[8,32,128]{2,1,0:T(8,128)S(1)}, u32[]{:S(2)}, u32[]{:S(2)}) collective-permute-start(f32[8,32,128]{2,1,0:T(8,128)S(1)} %add.135), channel_id=1, source_target_pairs={{0,2},{1,3},{2,4},{3,5},{4,6},{5,7},{6,0},{7,1},{8,10},{9,11},{10,... | collective-permute-start | bytes 393224 | tf_op jit(solution)/shard_map/flux_sum/ppermute | solution.py:803
  21.0 2.6 %collective-permute-start.6 = (f32[8,32,128]{2,1,0:T(8,128)S(1)}, f32[8,32,128]{2,1,0:T(8,128)S(1)}, u32[]{:S(2)}, u32[]{:S(2)}) collective-permute-start(f32[8,32,128]{2,1,0:T(8,128)S(1)} %add.135), channel_id=1, source_target_pairs={{0,4},{1,5},{2,6},{3,7},{4,0},{5,1},{6,2},{7,3},{8,12},{9,13},{10,... | collective-permute-start | bytes 393224 | tf_op jit(solution)/shard_map/flux_sum/ppermute | solution.py:803
  23.6 1.1 %collective-permute-start.7 = (f32[8,32,128]{2,1,0:T(8,128)S(1)}, f32[8,32,128]{2,1,0:T(8,128)S(1)}, u32[]{:S(2)}, u32[]{:S(2)}) collective-permute-start(f32[8,32,128]{2,1,0:T(8,128)S(1)} %add.135), channel_id=1, source_target_pairs={{0,6},{1,7},{2,0},{3,1},{4,2},{5,3},{6,4},{7,5},{8,14},{9,15},{10,... | collective-permute-start | bytes 393224 | tf_op jit(solution)/shard_map/flux_sum/ppermute | solution.py:803
  24.7 0.0 collective-permute-done.8.before_ref
  24.7 0.0 collective-permute-done.9.after_ref
  24.7 0.0 copy-done
  24.7 0.0 copy-done.3
  24.7 4.9 %regroup.1 = (f32[8,8,80,128]{3,2,1,0:T(8,128)}, f32[8,128,128]{2,1,0:T(8,128)S(1)}) custom-call(f32[8,64,1024]{2,1,0:T(8,128)S(1)} %copy-done, f32[64,1024]{1,0:T(8,128)S(1)} %copy-done.3, f32[96,1024]{1,0:T(8,128)S(1)} %collective-permute-done.8.before_ref, f32[96,1024]{1,0:T(8,128)S(1)} %collective-permute-done.9.after_ref), custom_call_target="tpu_custom_call" | custom-call | bytes 15000000 | tf_op jit(solution)/shard_map/regroup/pallas_call | solution.py:140
  29.6 0.0 collective-permute-done.5
  29.6 0.1 collective-permute-done.6
  29.7 0.0 collective-permute-done.7
  29.7 3.9 %collective-permute-start.13 = (f32[8,8,80,128]{3,2,1,0:T(8,128)}, f32[8,8,80,128]{3,2,1,0:T(8,128)}, u32[]{:S(2)}, u32[]{:S(2)}) collective-permute-start(f32[8,8,80,128]{3,2,1,0:T(8,128)} %get-tuple-element.154), channel_id=1, source_target_pairs={{0,1},{1,2},{2,3},{3,4},{4,5},{5,6},{6,7},{8,9},{9,10},{10,11},{11... | collective-permute-start | bytes 7864328 | tf_op jit(solution)/shard_map/depth_halo/ppermute | solution.py:796
  33.7 2.0 %collective-permute-start.14 = (f32[8,8,80,128]{3,2,1,0:T(8,128)}, f32[8,8,80,128]{3,2,1,0:T(8,128)}, u32[]{:S(2)}, u32[]{:S(2)}) collective-permute-start(f32[8,8,80,128]{3,2,1,0:T(8,128)} %get-tuple-element.154), channel_id=1, source_target_pairs={{1,0},{2,1},{3,2},{4,3},{5,4},{6,5},{7,6},{9,8},{10,9},{11,10},{12... | collective-permute-start | bytes 7864328 | tf_op jit(solution)/shard_map/depth_halo/ppermute | solution.py:796
  35.6 4.3 %collective-permute-start.11 = (f32[8,32,128]{2,1,0:T(8,128)S(1)}, f32[8,32,128]{2,1,0:T(8,128)S(1)}, u32[]{:S(2)}, u32[]{:S(2)}) collective-permute-start(f32[8,32,128]{2,1,0:T(8,128)S(1)} %add_add_fusion.own_ref), channel_id=1, source_target_pairs={{1,9},{3,11},{5,13},{7,15},{8,0},{9,17},{10,2},{11,19},{12,4},{13,... | collective-permute-start | bytes 393224 | tf_op jit(solution)/shard_map/flux_halo/ppermute | solution.py:819
  39.9 0.1 collective-permute-start.10
  40.0 1.8 %collective-permute-done.11.same_ref = f32[8,32,128]{2,1,0:T(8,128)S(1)} collective-permute-done((f32[8,32,128]{2,1,0:T(8,128)S(1)}, f32[8,32,128]{2,1,0:T(8,128)S(1)}, u32[]{:S(2)}, u32[]{:S(2)}) %collective-permute-start.11) | collective-permute-done | bytes 131104 | tf_op jit(solution)/shard_map/flux_halo/ppermute | solution.py:819
  41.8 0.7 collective-permute-start.12
  42.5 0.0 collective-permute-done.10.other_ref
  42.5 1.0 collective-permute-done.12.cross_ref
  43.5 7.5 %surface_basis.1 = (f32[10,8,16,8,128]{4,3,2,1,0:T(8,128)S(1)}, f32[16,8,128]{2,1,0:T(8,128)S(1)}) custom-call(s32[1,6]{1,0:T(1,128)S(1)} %bitcast.18, f32[8,32,128]{2,1,0:T(8,128)S(1)} %add_add_fusion.own_ref, f32[8,32,128]{2,1,0:T(8,128)S(1)} %collective-permute-done.10.other_ref, f32[8,32,128]{2,1,0:T(8,128)S(1)} %collective-permute-done.11.same_ref, ...), custom_call_target="tpu_custom_call" | custom-call | bytes 700000 | tf_op jit(solution)/shard_map/surface_basis/pallas_call | solution.py:330
  51.0 16.1 %all_to_all.5.sums_ref = f32[16,8,128]{2,1,0:T(8,128)S(1)} all-to-all(f32[16,8,128]{2,1,0:T(8,128)S(1)} %get-tuple-element.152), channel_id=1, replica_groups=mesh['vol'=16,'col'=8] {'vol'}, dimensions={0} | all-to-all | bytes 131072 | tf_op jit(solution)/shard_map/gather_sums/all_to_all | solution.py:827
  67.1 0.0 copy-done.1
  67.1 0.0 copy-start.2
  67.1 0.0 copy-start.4
  67.1 2.3 %surface_solve.1 = (f32[8,80,128]{2,1,0:T(8,128)}, s32[1,1]{1,0:T(1,128)}) custom-call(f32[10,8,16,8,128]{4,3,2,1,0:T(8,128)S(1)} %get-tuple-element.151.part_ref, f32[16,8,128]{2,1,0:T(8,128)S(1)} %all_to_all.5.sums_ref, f32[20,16,128]{2,1,0:T(8,128)S(1)} %copy-done.1), custom_call_target="tpu_custom_call" | custom-call | bytes 300000 | tf_op jit(solution)/shard_map/surface_solve/pallas_call | solution.py:407
  70.0 0.0 collective-permute-done.13
  70.1 0.0 collective-permute-done.14
  70.1 0.0 copy-done.2
  70.1 0.0 copy-done.4
  70.1 30.2 %conditional.1 = ((f32[64,1024]{1,0:T(8,128)}, f32[8,64,1024]{2,1,0:T(8,128)})) conditional(s32[]{:T(128)} %bitcast.9, (s32[]{:T(128)}, f32[8,32,128]{2,1,0:T(8,128)S(1)}, f32[8,32,128]{2,1,0:T(8,128)S(1)}, f32[64,1024]{1,0:T(8,128)S(1)}, s32[1,6]{1,0:T(1,128)S(1)}, /*index=5*/f32[8,8,80,128]{3,2,1,0:T(8,128)}, f32[8,8,80,128]{3,2,1,0:T(8,128)}, ...), branch_computations={%region_0.9_spmd, %region_9.10_spmd} | conditional | flops 3516806 | bytes 15280337 | solution.py:842
  70.3 0.0 copy-start.5
  70.3 2.1 %surface_change.3.change_ref = f32[8,8,64,128]{3,2,1,0:T(8,128)S(1)} custom-call(s32[1,6]{1,0:T(1,128)S(1)} %get-tuple-element.118.where_ref, f32[8,80,128]{2,1,0:T(8,128)} %get-tuple-element.122.speed_ref), custom_call_target="tpu_custom_call" | custom-call | bytes 800000 | tf_op jit(solution)/shard_map/cond/branch_1_fun/surface_change/pallas_call | solution.py:557
  72.5 0.0 copy-done.5
  72.5 27.8 %base_sweeps.3 = (f32[64,1024]{1,0:T(8,128)}, f32[8,64,1024]{2,1,0:T(8,128)}) custom-call(s32[1,6]{1,0:T(1,128)S(1)} %get-tuple-element.118.where_ref, f32[8,8,80,128]{3,2,1,0:T(8,128)} %get-tuple-element.119.wide_ref, f32[8,8,80,128]{3,2,1,0:T(8,128)} %get-tuple-element.120.zlow_ref, f32[8,8,80,128]{3,2,1,0:T(8,128)} %get-tuple-element.121.zhigh_ref, ...), custom_call_target="tpu_custom_call" | custom-call | bytes 2500000 | tf_op jit(solution)/shard_map/cond/branch_1_fun/base_sweeps/pallas_call | solution.py:707
  (1 shorter events, 0.0 us)
Async XLA Ops:
  0.6 24.1 %copy-start = (f32[8,64,1024]{2,1,0:T(8,128)S(1)}, f32[8,64,1024]{2,1,0:T(8,128)}, u32[]{:S(2)}) copy-start(f32[8,64,1024]{2,1,0:T(8,128)} %block_ref.3) | copy-start | bytes 6291460
  0.6 24.1 %copy-start.3 = (f32[64,1024]{1,0:T(8,128)S(1)}, f32[64,1024]{1,0:T(8,128)}, u32[]{:S(2)}) copy-start(f32[64,1024]{1,0:T(8,128)} %metric_ref.3) | copy-start | bytes 786436
  3.0 21.6 %collective-permute-start.8 = (f32[96,1024]{1,0:T(8,128)}, f32[96,1024]{1,0:T(8,128)S(1)}, u32[]{:S(2)}, u32[]{:S(2)}) collective-permute-start(f32[96,1024]{1,0:T(8,128)} %get-tuple-element.141), channel_id=1, source_target_pairs={{0,8},{1,9},{2,10},{3,11},{4,12},{5,13},{6,14},{7,15},{8,16},{9,17... | collective-permute-start | bytes 1179656 | tf_op jit(solution)/shard_map/row_halo/ppermute | solution.py:796
  7.0 17.7 %collective-permute-start.9 = (f32[96,1024]{1,0:T(8,128)}, f32[96,1024]{1,0:T(8,128)S(1)}, u32[]{:S(2)}, u32[]{:S(2)}) collective-permute-start(f32[96,1024]{1,0:T(8,128)} %get-tuple-element.145), channel_id=1, source_target_pairs={{8,0},{9,1},{10,2},{11,3},{12,4},{13,5},{14,6},{15,7},{16,8},{17,9... | collective-permute-start | bytes 1179656 | tf_op jit(solution)/shard_map/row_halo/ppermute | solution.py:796
  16.5 2.2 %collective-permute-start.4 = (f32[8,32,128]{2,1,0:T(8,128)}, f32[8,32,128]{2,1,0:T(8,128)S(1)}, u32[]{:S(2)}, u32[]{:S(2)}) collective-permute-start(f32[8,32,128]{2,1,0:T(8,128)} %get-tuple-element.144), channel_id=1, source_target_pairs={{0,1},{1,0},{2,3},{3,2},{4,5},{5,4},{6,7},{7,6},{8,9},{9,8},{10,11... | collective-permute-start | bytes 393224 | tf_op jit(solution)/shard_map/flux_sum/ppermute | solution.py:801
  19.6 47.5 %copy-start.1 = (f32[20,16,128]{2,1,0:T(8,128)S(1)}, f32[20,16,128]{2,1,0:T(8,128)}, u32[]{:S(2)}) copy-start(f32[20,16,128]{2,1,0:T(8,128)} %constant.115.clone.weights_ref) | copy-start | bytes 491524
  19.6 10.0 %collective-permute-start.5 = (f32[8,32,128]{2,1,0:T(8,128)S(1)}, f32[8,32,128]{2,1,0:T(8,128)S(1)}, u32[]{:S(2)}, u32[]{:S(2)}) collective-permute-start(f32[8,32,128]{2,1,0:T(8,128)S(1)} %add.135), channel_id=1, source_target_pairs={{0,2},{1,3},{2,4},{3,5},{4,6},{5,7},{6,0},{7,1},{8,10},{9,11},{10,... | collective-permute-start | bytes 393224 | tf_op jit(solution)/shard_map/flux_sum/ppermute | solution.py:803
  21.0 8.7 %collective-permute-start.6 = (f32[8,32,128]{2,1,0:T(8,128)S(1)}, f32[8,32,128]{2,1,0:T(8,128)S(1)}, u32[]{:S(2)}, u32[]{:S(2)}) collective-permute-start(f32[8,32,128]{2,1,0:T(8,128)S(1)} %add.135), channel_id=1, source_target_pairs={{0,4},{1,5},{2,6},{3,7},{4,0},{5,1},{6,2},{7,3},{8,12},{9,13},{10,... | collective-permute-start | bytes 393224 | tf_op jit(solution)/shard_map/flux_sum/ppermute | solution.py:803
  23.6 6.1 %collective-permute-start.7 = (f32[8,32,128]{2,1,0:T(8,128)S(1)}, f32[8,32,128]{2,1,0:T(8,128)S(1)}, u32[]{:S(2)}, u32[]{:S(2)}) collective-permute-start(f32[8,32,128]{2,1,0:T(8,128)S(1)} %add.135), channel_id=1, source_target_pairs={{0,6},{1,7},{2,0},{3,1},{4,2},{5,3},{6,4},{7,5},{8,14},{9,15},{10,... | collective-permute-start | bytes 393224 | tf_op jit(solution)/shard_map/flux_sum/ppermute | solution.py:803
  29.7 40.3 %collective-permute-start.13 = (f32[8,8,80,128]{3,2,1,0:T(8,128)}, f32[8,8,80,128]{3,2,1,0:T(8,128)}, u32[]{:S(2)}, u32[]{:S(2)}) collective-permute-start(f32[8,8,80,128]{3,2,1,0:T(8,128)} %get-tuple-element.154), channel_id=1, source_target_pairs={{0,1},{1,2},{2,3},{3,4},{4,5},{5,6},{6,7},{8,9},{9,10},{10,11},{11... | collective-permute-start | bytes 7864328 | tf_op jit(solution)/shard_map/depth_halo/ppermute | solution.py:796
  33.7 36.4 %collective-permute-start.14 = (f32[8,8,80,128]{3,2,1,0:T(8,128)}, f32[8,8,80,128]{3,2,1,0:T(8,128)}, u32[]{:S(2)}, u32[]{:S(2)}) collective-permute-start(f32[8,8,80,128]{3,2,1,0:T(8,128)} %get-tuple-element.154), channel_id=1, source_target_pairs={{1,0},{2,1},{3,2},{4,3},{5,4},{6,5},{7,6},{9,8},{10,9},{11,10},{12... | collective-permute-start | bytes 7864328 | tf_op jit(solution)/shard_map/depth_halo/ppermute | solution.py:796
  35.6 6.2 %collective-permute-start.11 = (f32[8,32,128]{2,1,0:T(8,128)S(1)}, f32[8,32,128]{2,1,0:T(8,128)S(1)}, u32[]{:S(2)}, u32[]{:S(2)}) collective-permute-start(f32[8,32,128]{2,1,0:T(8,128)S(1)} %add_add_fusion.own_ref), channel_id=1, source_target_pairs={{1,9},{3,11},{5,13},{7,15},{8,0},{9,17},{10,2},{11,19},{12,4},{13,... | collective-permute-start | bytes 393224 | tf_op jit(solution)/shard_map/flux_halo/ppermute | solution.py:819
  39.9 2.6 %collective-permute-start.10 = (f32[8,32,128]{2,1,0:T(8,128)S(1)}, f32[8,32,128]{2,1,0:T(8,128)S(1)}, u32[]{:S(2)}, u32[]{:S(2)}) collective-permute-start(f32[8,32,128]{2,1,0:T(8,128)S(1)} %add_add_fusion.own_ref), channel_id=1, source_target_pairs={{0,1},{1,0},{2,3},{3,2},{4,5},{5,4},{6,7},{7,6},{8,9},{9,8},{10,11... | collective-permute-start | bytes 393224 | tf_op jit(solution)/shard_map/flux_halo/ppermute | solution.py:812
  41.8 1.7 %collective-permute-start.12 = (f32[8,32,128]{2,1,0:T(8,128)S(1)}, f32[8,32,128]{2,1,0:T(8,128)S(1)}, u32[]{:S(2)}, u32[]{:S(2)}) collective-permute-start(f32[8,32,128]{2,1,0:T(8,128)S(1)} %collective-permute-done.11.same_ref), channel_id=1, source_target_pairs={{0,1},{1,0},{2,3},{3,2},{4,5},{5,4},{6,7},{7,6},{8,9},{9,8},{10,11... | collective-permute-start | bytes 393224 | tf_op jit(solution)/shard_map/flux_halo/ppermute | solution.py:820
  67.1 3.0 %copy-start.2 = (bf16[1024,1024]{1,0:T(8,128)(2,1)S(1)}, bf16[1024,1024]{1,0:T(8,128)(2,1)}, u32[]{:S(2)}) copy-start(bf16[1024,1024]{1,0:T(8,128)(2,1)} %constant.114.clone) | copy-start | bytes 6291460
  67.1 3.0 %copy-start.4 = (f32[64,1024]{1,0:T(8,128)S(1)}, f32[64,1024]{1,0:T(8,128)}, u32[]{:S(2)}) copy-start(f32[64,1024]{1,0:T(8,128)} %metric_ref.3) | copy-start | bytes 786436
  70.3 2.1 %copy-start.5 = (f32[8,80,128]{2,1,0:T(8,128)S(1)}, f32[8,80,128]{2,1,0:T(8,128)}, u32[]{:S(2)}) copy-start(f32[8,80,128]{2,1,0:T(8,128)} %get-tuple-element.122.speed_ref) | copy-start | bytes 983044 | tf_op jit(solution)/shard_map/cond

commit v10 on v9

--- a/solution.py
+++ b/solution.py
@@ -220,7 +220,7 @@
             pltpu.VMEM((512, 256), jnp.float32),
             pltpu.SemaphoreType.DMA((3,)),
         ],
-        compiler_params=params(56),
+        compiler_params=params(50),
         cost_estimate=cost(7),
         name="face_sums",
     )(where, count, area, speed, node)

time: 101 us -> 98.7 us (0.977)
  Pallas kernels: 54.3 us -> 53 us
    pallas_call x1, Pallas kernels: 7.38 us -> 6.08 us  [face_sums(): pl.pallas_call(face_kernel, out_shape=(half, half), in_specs=[SMEM, SMEM]...]
  transfers between devices with their start and end apart: 11 -> 11, of which waited for: 4 -> 4; matrix products, arithmetic and copies ran while one was open for 1% -> 0% of each run, Pallas kernels for 22% -> 21%
where the time goes in v10:
time: 98.7 us; the launch traced here: 98.1 us
  Pallas kernels  53 us (54%)
  starting transfers between devices  22.3 us (23%)
  blocking collectives  16.1 us (16%)
  waiting for transfers between devices  3.9 us (4%)
  between operations  2.31 us (2%)
    pallas_call x1, Pallas kernels, base_sweeps(): pl.pallas_call(base_kernel, out_shape=(f32(rows, 8 * LANES), f32(layers,...  27.8 us
    all_to_all x1, blocking collectives, on_device(): gathered = lax.all_to_all(spread, 'vol', 0, 0)  16.1 us
    ppermute x4, starting transfers between devices, moved(): return lax.ppermute(x, ('vol', 'col'), pairs)  11.2 us
    pallas_call x1, Pallas kernels, surface_basis(): pl.pallas_call(basis_kernel, out_shape=(f32(ITERS, 8, GROUPS, SUB, LANES)...  7.48 us
    pallas_call x1, Pallas kernels, face_sums(): pl.pallas_call(face_kernel, out_shape=(half, half), in_specs=[SMEM, SMEM]...  6.08 us
    ppermute x3, starting transfers between devices, on_device(): lax.ppermute(keep, 'col', [(j, (j + 2 * k) % cols) for j in range(cols)])  5.05 us
    pallas_call x1, Pallas kernels, regroup(): pl.pallas_call(regroup_kernel, out_shape=(f32(layers, 8, Y_ROWS, LANES),...  4.88 us
    ppermute x1, starting transfers between devices, on_device(): same = lax.ppermute(own, ('vol', 'col'), pairs)  4.28 us
  transfers between devices with their start and end apart: 11, of which 4 were waited for; matrix products, arithmetic and copies ran while one was open for 0% of the time, Pallas kernels for 21%

profile of v10, /device:TPU:1, one launch (start us, length us, event | category | flops | bytes accessed | tf_op | source)
XLA Modules:
  0.0 98.1 jit_solution(190937121579563177)
XLA Ops:
  0.6 0.0 copy-start
  0.6 0.0 copy-start.2
  0.7 0.0 copy-start.3
  0.7 0.0 copy-start.4
  0.7 0.0 copy-start.6
  0.7 2.4 %outgoing_rows.1 = (f32[96,1024]{1,0:T(8,128)}, f32[96,1024]{1,0:T(8,128)}) custom-call(f32[8,64,1024]{2,1,0:T(8,128)} %block_ref.3, f32[64,1024]{1,0:T(8,128)} %metric_ref.3), custom_call_target="tpu_custom_call" | custom-call | bytes 100000 | tf_op jit(solution)/shard_map/outgoing_rows/pallas_call | solution.py:248
  3.1 4.0 %collective-permute-start.8 = (f32[96,1024]{1,0:T(8,128)}, f32[96,1024]{1,0:T(8,128)S(1)}, u32[]{:S(2)}, u32[]{:S(2)}) collective-permute-start(f32[96,1024]{1,0:T(8,128)} %get-tuple-element.141), channel_id=1, source_target_pairs={{0,8},{1,9},{2,10},{3,11},{4,12},{5,13},{6,14},{7,15},{8,16},{9,17... | collective-permute-start | bytes 1179656 | tf_op jit(solution)/shard_map/row_halo/ppermute | solution.py:796
  7.0 1.3 %collective-permute-start.9 = (f32[96,1024]{1,0:T(8,128)}, f32[96,1024]{1,0:T(8,128)S(1)}, u32[]{:S(2)}, u32[]{:S(2)}) collective-permute-start(f32[96,1024]{1,0:T(8,128)} %get-tuple-element.145), channel_id=1, source_target_pairs={{8,0},{9,1},{10,2},{11,3},{12,4},{13,5},{14,6},{15,7},{16,8},{17,9... | collective-permute-start | bytes 1179656 | tf_op jit(solution)/shard_map/row_halo/ppermute | solution.py:796
  9.0 0.1 stack.15
  9.1 0.0 copy-done.2
  9.1 0.0 copy-done.3
  9.1 0.0 copy-done.4
  9.1 6.1 %face_sums.1 = (f32[8,32,128]{2,1,0:T(8,128)S(1)}, f32[8,32,128]{2,1,0:T(8,128)S(1)}) custom-call(s32[1,6]{1,0:T(1,128)S(1)} %bitcast.17, s32[1,1]{1,0:T(1,128)S(6)} %copy.41.count_ref, f32[1,16384]{1,0:T(1,128)S(1)} %copy-done.2, f32[1,16384]{1,0:T(1,128)S(1)} %copy-done.3, s32[1,16384]{1,0:T(1,128)S(1)} %copy-done.4), custom_call_target="tpu_custom_call" | custom-call | bytes 700000 | tf_op jit(solution)/shard_map/face_sums/pallas_call | solution.py:211
  15.2 1.0 %collective-permute-start.4 = (f32[8,32,128]{2,1,0:T(8,128)S(1)}, f32[8,32,128]{2,1,0:T(8,128)S(1)}, u32[]{:S(2)}, u32[]{:S(2)}) collective-permute-start(f32[8,32,128]{2,1,0:T(8,128)S(1)} %get-tuple-element.144), channel_id=1, source_target_pairs={{0,1},{1,0},{2,3},{3,2},{4,5},{5,4},{6,7},{7,6},{8,9},{9,8},{10,11... | collective-permute-start | bytes 393224 | tf_op jit(solution)/shard_map/flux_sum/ppermute | solution.py:801
  16.2 1.0 %collective-permute-done.4 = f32[8,32,128]{2,1,0:T(8,128)S(1)} collective-permute-done((f32[8,32,128]{2,1,0:T(8,128)S(1)}, f32[8,32,128]{2,1,0:T(8,128)S(1)}, u32[]{:S(2)}, u32[]{:S(2)}) %collective-permute-start.4) | collective-permute-done | bytes 131104 | tf_op jit(solution)/shard_map/flux_sum/ppermute | solution.py:801
  17.2 0.0 copy-start.1
  17.2 1.3 %collective-permute-start.5 = (f32[8,32,128]{2,1,0:T(8,128)S(1)}, f32[8,32,128]{2,1,0:T(8,128)S(1)}, u32[]{:S(2)}, u32[]{:S(2)}) collective-permute-start(f32[8,32,128]{2,1,0:T(8,128)S(1)} %add.135), channel_id=1, source_target_pairs={{0,2},{1,3},{2,4},{3,5},{4,6},{5,7},{6,0},{7,1},{8,10},{9,11},{10,... | collective-permute-start | bytes 393224 | tf_op jit(solution)/shard_map/flux_sum/ppermute | solution.py:803
  18.6 2.6 %collective-permute-start.6 = (f32[8,32,128]{2,1,0:T(8,128)S(1)}, f32[8,32,128]{2,1,0:T(8,128)S(1)}, u32[]{:S(2)}, u32[]{:S(2)}) collective-permute-start(f32[8,32,128]{2,1,0:T(8,128)S(1)} %add.135), channel_id=1, source_target_pairs={{0,4},{1,5},{2,6},{3,7},{4,0},{5,1},{6,2},{7,3},{8,12},{9,13},{10,... | collective-permute-start | bytes 393224 | tf_op jit(solution)/shard_map/flux_sum/ppermute | solution.py:803
  21.2 1.1 %collective-permute-start.7 = (f32[8,32,128]{2,1,0:T(8,128)S(1)}, f32[8,32,128]{2,1,0:T(8,128)S(1)}, u32[]{:S(2)}, u32[]{:S(2)}) collective-permute-start(f32[8,32,128]{2,1,0:T(8,128)S(1)} %add.135), channel_id=1, source_target_pairs={{0,6},{1,7},{2,0},{3,1},{4,2},{5,3},{6,4},{7,5},{8,14},{9,15},{10,... | collective-permute-start | bytes 393224 | tf_op jit(solution)/shard_map/flux_sum/ppermute | solution.py:803
  22.3 0.0 collective-permute-done.8.before_ref
  22.3 0.0 collective-permute-done.9.after_ref
  22.3 0.0 copy-done
  22.3 0.0 copy-done.6
  22.3 4.9 %regroup.1 = (f32[8,8,80,128]{3,2,1,0:T(8,128)}, f32[8,128,128]{2,1,0:T(8,128)S(1)}) custom-call(f32[8,64,1024]{2,1,0:T(8,128)S(1)} %copy-done, f32[64,1024]{1,0:T(8,128)S(1)} %copy-done.6, f32[96,1024]{1,0:T(8,128)S(1)} %collective-permute-done.8.before_ref, f32[96,1024]{1,0:T(8,128)S(1)} %collective-permute-done.9.after_ref), custom_call_target="tpu_custom_call" | custom-call | bytes 15000000 | tf_op jit(solution)/shard_map/regroup/pallas_call | solution.py:140
  27.2 0.0 collective-permute-done.5
  27.2 0.1 collective-permute-done.6
  27.3 0.0 collective-permute-done.7
  27.3 3.9 %collective-permute-start.13 = (f32[8,8,80,128]{3,2,1,0:T(8,128)}, f32[8,8,80,128]{3,2,1,0:T(8,128)}, u32[]{:S(2)}, u32[]{:S(2)}) collective-permute-start(f32[8,8,80,128]{3,2,1,0:T(8,128)} %get-tuple-element.154), channel_id=1, source_target_pairs={{0,1},{1,2},{2,3},{3,4},{4,5},{5,6},{6,7},{8,9},{9,10},{10,11},{11... | collective-permute-start | bytes 7864328 | tf_op jit(solution)/shard_map/depth_halo/ppermute | solution.py:796
  31.3 2.0 %collective-permute-start.14 = (f32[8,8,80,128]{3,2,1,0:T(8,128)}, f32[8,8,80,128]{3,2,1,0:T(8,128)}, u32[]{:S(2)}, u32[]{:S(2)}) collective-permute-start(f32[8,8,80,128]{3,2,1,0:T(8,128)} %get-tuple-element.154), channel_id=1, source_target_pairs={{1,0},{2,1},{3,2},{4,3},{5,4},{6,5},{7,6},{9,8},{10,9},{11,10},{12... | collective-permute-start | bytes 7864328 | tf_op jit(solution)/shard_map/depth_halo/ppermute | solution.py:796
  33.3 4.3 %collective-permute-start.11 = (f32[8,32,128]{2,1,0:T(8,128)S(1)}, f32[8,32,128]{2,1,0:T(8,128)S(1)}, u32[]{:S(2)}, u32[]{:S(2)}) collective-permute-start(f32[8,32,128]{2,1,0:T(8,128)S(1)} %add_add_fusion.own_ref), channel_id=1, source_target_pairs={{1,9},{3,11},{5,13},{7,15},{8,0},{9,17},{10,2},{11,19},{12,4},{13,... | collective-permute-start | bytes 393224 | tf_op jit(solution)/shard_map/flux_halo/ppermute | solution.py:819
  37.6 0.1 collective-permute-start.10
  37.6 1.8 %collective-permute-done.11.same_ref = f32[8,32,128]{2,1,0:T(8,128)S(1)} collective-permute-done((f32[8,32,128]{2,1,0:T(8,128)S(1)}, f32[8,32,128]{2,1,0:T(8,128)S(1)}, u32[]{:S(2)}, u32[]{:S(2)}) %collective-permute-start.11) | collective-permute-done | bytes 131104 | tf_op jit(solution)/shard_map/flux_halo/ppermute | solution.py:819
  39.5 0.7 collective-permute-start.12
  40.1 0.0 collective-permute-done.10.other_ref
  40.1 1.0 %collective-permute-done.12.cross_ref = f32[8,32,128]{2,1,0:T(8,128)S(1)} collective-permute-done((f32[8,32,128]{2,1,0:T(8,128)S(1)}, f32[8,32,128]{2,1,0:T(8,128)S(1)}, u32[]{:S(2)}, u32[]{:S(2)}) %collective-permute-start.12) | collective-permute-done | bytes 131104 | tf_op jit(solution)/shard_map/flux_halo/ppermute | solution.py:820
  41.1 7.5 %surface_basis.1 = (f32[10,8,16,8,128]{4,3,2,1,0:T(8,128)S(1)}, f32[16,8,128]{2,1,0:T(8,128)S(1)}) custom-call(s32[1,6]{1,0:T(1,128)S(1)} %bitcast.18, f32[8,32,128]{2,1,0:T(8,128)S(1)} %add_add_fusion.own_ref, f32[8,32,128]{2,1,0:T(8,128)S(1)} %collective-permute-done.10.other_ref, f32[8,32,128]{2,1,0:T(8,128)S(1)} %collective-permute-done.11.same_ref, ...), custom_call_target="tpu_custom_call" | custom-call | bytes 700000 | tf_op jit(solution)/shard_map/surface_basis/pallas_call | solution.py:330
  48.6 16.1 %all_to_all.5.sums_ref = f32[16,8,128]{2,1,0:T(8,128)S(1)} all-to-all(f32[16,8,128]{2,1,0:T(8,128)S(1)} %get-tuple-element.152), channel_id=1, replica_groups=mesh['vol'=16,'col'=8] {'vol'}, dimensions={0} | all-to-all | bytes 131072 | tf_op jit(solution)/shard_map/gather_sums/all_to_all | solution.py:827
  64.7 0.0 copy-done.1
  64.7 0.0 copy-start.5
  64.7 0.0 copy-start.7
  64.7 2.3 %surface_solve.1 = (f32[8,80,128]{2,1,0:T(8,128)}, s32[1,1]{1,0:T(1,128)}) custom-call(f32[10,8,16,8,128]{4,3,2,1,0:T(8,128)S(1)} %get-tuple-element.151.part_ref, f32[16,8,128]{2,1,0:T(8,128)S(1)} %all_to_all.5.sums_ref, f32[20,16,128]{2,1,0:T(8,128)S(1)} %copy-done.1), custom_call_target="tpu_custom_call" | custom-call | bytes 300000 | tf_op jit(solution)/shard_map/surface_solve/pallas_call | solution.py:407
  67.7 0.0 collective-permute-done.13
  67.7 0.0 collective-permute-done.14
  67.7 0.0 copy-done.5
  67.7 0.0 copy-done.7
  67.7 30.2 %conditional.1 = ((f32[64,1024]{1,0:T(8,128)}, f32[8,64,1024]{2,1,0:T(8,128)})) conditional(s32[]{:T(128)} %bitcast.9, (s32[]{:T(128)}, f32[8,32,128]{2,1,0:T(8,128)S(1)}, f32[8,32,128]{2,1,0:T(8,128)S(1)}, f32[64,1024]{1,0:T(8,128)S(1)}, s32[1,6]{1,0:T(1,128)S(1)}, /*index=5*/f32[8,8,80,128]{3,2,1,0:T(8,128)}, f32[8,8,80,128]{3,2,1,0:T(8,128)}, ...), branch_computations={%region_0.9_spmd, %region_9.10_spmd} | conditional | flops 3516806 | bytes 15280337 | solution.py:842
  68.0 0.0 copy-start.8
  68.0 2.1 %surface_change.3.change_ref = f32[8,8,64,128]{3,2,1,0:T(8,128)S(1)} custom-call(s32[1,6]{1,0:T(1,128)S(1)} %get-tuple-element.118.where_ref, f32[8,80,128]{2,1,0:T(8,128)} %get-tuple-element.122.speed_ref), custom_call_target="tpu_custom_call" | custom-call | bytes 800000 | tf_op jit(solution)/shard_map/cond/branch_1_fun/surface_change/pallas_call | solution.py:557
  70.1 0.0 copy-done.8
  70.1 27.8 %base_sweeps.3 = (f32[64,1024]{1,0:T(8,128)}, f32[8,64,1024]{2,1,0:T(8,128)}) custom-call(s32[1,6]{1,0:T(1,128)S(1)} %get-tuple-element.118.where_ref, f32[8,8,80,128]{3,2,1,0:T(8,128)} %get-tuple-element.119.wide_ref, f32[8,8,80,128]{3,2,1,0:T(8,128)} %get-tuple-element.120.zlow_ref, f32[8,8,80,128]{3,2,1,0:T(8,128)} %get-tuple-element.121.zhigh_ref, ...), custom_call_target="tpu_custom_call" | custom-call | bytes 2500000 | tf_op jit(solution)/shard_map/cond/branch_1_fun/base_sweeps/pallas_call | solution.py:707
  (2 shorter events, 0.1 us)
Async XLA Ops:
  0.6 21.7 %copy-start = (f32[8,64,1024]{2,1,0:T(8,128)S(1)}, f32[8,64,1024]{2,1,0:T(8,128)}, u32[]{:S(2)}) copy-start(f32[8,64,1024]{2,1,0:T(8,128)} %block_ref.3) | copy-start | bytes 6291460
  0.6 8.4 %copy-start.2 = (f32[1,16384]{1,0:T(1,128)S(1)}, f32[1,16384]{1,0:T(1,128)}, u32[]{:S(2)}) copy-start(f32[1,16384]{1,0:T(1,128)} %area_ref) | copy-start | bytes 196612
  0.7 8.4 %copy-start.3 = (f32[1,16384]{1,0:T(1,128)S(1)}, f32[1,16384]{1,0:T(1,128)}, u32[]{:S(2)}) copy-start(f32[1,16384]{1,0:T(1,128)} %speed_ref.1) | copy-start | bytes 196612
  0.7 8.4 %copy-start.4 = (s32[1,16384]{1,0:T(1,128)S(1)}, s32[1,16384]{1,0:T(1,128)}, u32[]{:S(2)}) copy-start(s32[1,16384]{1,0:T(1,128)} %node_ref.1) | copy-start | bytes 196612
  0.7 21.6 %copy-start.6 = (f32[64,1024]{1,0:T(8,128)S(1)}, f32[64,1024]{1,0:T(8,128)}, u32[]{:S(2)}) copy-start(f32[64,1024]{1,0:T(8,128)} %metric_ref.3) | copy-start | bytes 786436
  3.1 19.2 %collective-permute-start.8 = (f32[96,1024]{1,0:T(8,128)}, f32[96,1024]{1,0:T(8,128)S(1)}, u32[]{:S(2)}, u32[]{:S(2)}) collective-permute-start(f32[96,1024]{1,0:T(8,128)} %get-tuple-element.141), channel_id=1, source_target_pairs={{0,8},{1,9},{2,10},{3,11},{4,12},{5,13},{6,14},{7,15},{8,16},{9,17... | collective-permute-start | bytes 1179656 | tf_op jit(solution)/shard_map/row_halo/ppermute | solution.py:796
  7.0 15.3 %collective-permute-start.9 = (f32[96,1024]{1,0:T(8,128)}, f32[96,1024]{1,0:T(8,128)S(1)}, u32[]{:S(2)}, u32[]{:S(2)}) collective-permute-start(f32[96,1024]{1,0:T(8,128)} %get-tuple-element.145), channel_id=1, source_target_pairs={{8,0},{9,1},{10,2},{11,3},{12,4},{13,5},{14,6},{15,7},{16,8},{17,9... | collective-permute-start | bytes 1179656 | tf_op jit(solution)/shard_map/row_halo/ppermute | solution.py:796
  15.2 2.0 %collective-permute-start.4 = (f32[8,32,128]{2,1,0:T(8,128)S(1)}, f32[8,32,128]{2,1,0:T(8,128)S(1)}, u32[]{:S(2)}, u32[]{:S(2)}) collective-permute-start(f32[8,32,128]{2,1,0:T(8,128)S(1)} %get-tuple-element.144), channel_id=1, source_target_pairs={{0,1},{1,0},{2,3},{3,2},{4,5},{5,4},{6,7},{7,6},{8,9},{9,8},{10,11... | collective-permute-start | bytes 393224 | tf_op jit(solution)/shard_map/flux_sum/ppermute | solution.py:801
  17.2 47.5 %copy-start.1 = (f32[20,16,128]{2,1,0:T(8,128)S(1)}, f32[20,16,128]{2,1,0:T(8,128)}, u32[]{:S(2)}) copy-start(f32[20,16,128]{2,1,0:T(8,128)} %constant.115.clone.weights_ref) | copy-start | bytes 491524
  17.2 10.0 %collective-permute-start.5 = (f32[8,32,128]{2,1,0:T(8,128)S(1)}, f32[8,32,128]{2,1,0:T(8,128)S(1)}, u32[]{:S(2)}, u32[]{:S(2)}) collective-permute-start(f32[8,32,128]{2,1,0:T(8,128)S(1)} %add.135), channel_id=1, source_target_pairs={{0,2},{1,3},{2,4},{3,5},{4,6},{5,7},{6,0},{7,1},{8,10},{9,11},{10,... | collective-permute-start | bytes 393224 | tf_op jit(solution)/shard_map/flux_sum/ppermute | solution.py:803
  18.6 8.7 %collective-permute-start.6 = (f32[8,32,128]{2,1,0:T(8,128)S(1)}, f32[8,32,128]{2,1,0:T(8,128)S(1)}, u32[]{:S(2)}, u32[]{:S(2)}) collective-permute-start(f32[8,32,128]{2,1,0:T(8,128)S(1)} %add.135), channel_id=1, source_target_pairs={{0,4},{1,5},{2,6},{3,7},{4,0},{5,1},{6,2},{7,3},{8,12},{9,13},{10,... | collective-permute-start | bytes 393224 | tf_op jit(solution)/shard_map/flux_sum/ppermute | solution.py:803
  21.2 6.1 %collective-permute-start.7 = (f32[8,32,128]{2,1,0:T(8,128)S(1)}, f32[8,32,128]{2,1,0:T(8,128)S(1)}, u32[]{:S(2)}, u32[]{:S(2)}) collective-permute-start(f32[8,32,128]{2,1,0:T(8,128)S(1)} %add.135), channel_id=1, source_target_pairs={{0,6},{1,7},{2,0},{3,1},{4,2},{5,3},{6,4},{7,5},{8,14},{9,15},{10,... | collective-permute-start | bytes 393224 | tf_op jit(solution)/shard_map/flux_sum/ppermute | solution.py:803
  27.3 40.3 %collective-permute-start.13 = (f32[8,8,80,128]{3,2,1,0:T(8,128)}, f32[8,8,80,128]{3,2,1,0:T(8,128)}, u32[]{:S(2)}, u32[]{:S(2)}) collective-permute-start(f32[8,8,80,128]{3,2,1,0:T(8,128)} %get-tuple-element.154), channel_id=1, source_target_pairs={{0,1},{1,2},{2,3},{3,4},{4,5},{5,6},{6,7},{8,9},{9,10},{10,11},{11... | collective-permute-start | bytes 7864328 | tf_op jit(solution)/shard_map/depth_halo/ppermute | solution.py:796
  31.3 36.4 %collective-permute-start.14 = (f32[8,8,80,128]{3,2,1,0:T(8,128)}, f32[8,8,80,128]{3,2,1,0:T(8,128)}, u32[]{:S(2)}, u32[]{:S(2)}) collective-permute-start(f32[8,8,80,128]{3,2,1,0:T(8,128)} %get-tuple-element.154), channel_id=1, source_target_pairs={{1,0},{2,1},{3,2},{4,3},{5,4},{6,5},{7,6},{9,8},{10,9},{11,10},{12... | collective-permute-start | bytes 7864328 | tf_op jit(solution)/shard_map/depth_halo/ppermute | solution.py:796
  33.3 6.2 %collective-permute-start.11 = (f32[8,32,128]{2,1,0:T(8,128)S(1)}, f32[8,32,128]{2,1,0:T(8,128)S(1)}, u32[]{:S(2)}, u32[]{:S(2)}) collective-permute-start(f32[8,32,128]{2,1,0:T(8,128)S(1)} %add_add_fusion.own_ref), channel_id=1, source_target_pairs={{1,9},{3,11},{5,13},{7,15},{8,0},{9,17},{10,2},{11,19},{12,4},{13,... | collective-permute-start | bytes 393224 | tf_op jit(solution)/shard_map/flux_halo/ppermute | solution.py:819
  37.6 2.6 %collective-permute-start.10 = (f32[8,32,128]{2,1,0:T(8,128)S(1)}, f32[8,32,128]{2,1,0:T(8,128)S(1)}, u32[]{:S(2)}, u32[]{:S(2)}) collective-permute-start(f32[8,32,128]{2,1,0:T(8,128)S(1)} %add_add_fusion.own_ref), channel_id=1, source_target_pairs={{0,1},{1,0},{2,3},{3,2},{4,5},{5,4},{6,7},{7,6},{8,9},{9,8},{10,11... | collective-permute-start | bytes 393224 | tf_op jit(solution)/shard_map/flux_halo/ppermute | solution.py:812
  39.5 1.7 %collective-permute-start.12 = (f32[8,32,128]{2,1,0:T(8,128)S(1)}, f32[8,32,128]{2,1,0:T(8,128)S(1)}, u32[]{:S(2)}, u32[]{:S(2)}) collective-permute-start(f32[8,32,128]{2,1,0:T(8,128)S(1)} %collective-permute-done.11.same_ref), channel_id=1, source_target_pairs={{0,1},{1,0},{2,3},{3,2},{4,5},{5,4},{6,7},{7,6},{8,9},{9,8},{10,11... | collective-permute-start | bytes 393224 | tf_op jit(solution)/shard_map/flux_halo/ppermute | solution.py:820
  64.7 3.0 %copy-start.5 = (bf16[1024,1024]{1,0:T(8,128)(2,1)S(1)}, bf16[1024,1024]{1,0:T(8,128)(2,1)}, u32[]{:S(2)}) copy-start(bf16[1024,1024]{1,0:T(8,128)(2,1)} %constant.114.clone) | copy-start | bytes 6291460
  64.7 3.0 %copy-start.7 = (f32[64,1024]{1,0:T(8,128)S(1)}, f32[64,1024]{1,0:T(8,128)}, u32[]{:S(2)}) copy-start(f32[64,1024]{1,0:T(8,128)} %metric_ref.3) | copy-start | bytes 786436
  68.0 2.1 %copy-start.8 = (f32[8,80,128]{2,1,0:T(8,128)S(1)}, f32[8,80,128]{2,1,0:T(8,128)}, u32[]{:S(2)}) copy-start(f32[8,80,128]{2,1,0:T(8,128)} %get-tuple-element.122.speed_ref) | copy-start | bytes 983044 | tf_op jit(solution)/shard_map/cond

commit v11 on v10

--- a/solution.py
+++ b/solution.py
@@ -220,7 +220,7 @@
             pltpu.VMEM((512, 256), jnp.float32),
             pltpu.SemaphoreType.DMA((3,)),
         ],
-        compiler_params=params(50),
+        compiler_params=params(32),
         cost_estimate=cost(7),
         name="face_sums",
     )(where, count, area, speed, node)

time: 98.7 us -> 98.7 us (level)
  no operation moved by 1% of the time
where the time goes in v11:
time: 98.7 us; the launch traced here: 98.1 us
  Pallas kernels  53 us (54%)
  starting transfers between devices  22.3 us (23%)
  blocking collectives  16.1 us (16%)
  waiting for transfers between devices  3.9 us (4%)
  between operations  2.31 us (2%)
    pallas_call x1, Pallas kernels, base_sweeps(): pl.pallas_call(base_kernel, out_shape=(f32(rows, 8 * LANES), f32(layers,...  27.8 us
    all_to_all x1, blocking collectives, on_device(): gathered = lax.all_to_all(spread, 'vol', 0, 0)  16.1 us
    ppermute x4, starting transfers between devices, moved(): return lax.ppermute(x, ('vol', 'col'), pairs)  11.2 us
    pallas_call x1, Pallas kernels, surface_basis(): pl.pallas_call(basis_kernel, out_shape=(f32(ITERS, 8, GROUPS, SUB, LANES)...  7.48 us
    pallas_call x1, Pallas kernels, face_sums(): pl.pallas_call(face_kernel, out_shape=(half, half), in_specs=[SMEM, SMEM]...  6.08 us
    ppermute x3, starting transfers between devices, on_device(): lax.ppermute(keep, 'col', [(j, (j + 2 * k) % cols) for j in range(cols)])  5.05 us
    pallas_call x1, Pallas kernels, regroup(): pl.pallas_call(regroup_kernel, out_shape=(f32(layers, 8, Y_ROWS, LANES),...  4.88 us
    ppermute x1, starting transfers between devices, on_device(): same = lax.ppermute(own, ('vol', 'col'), pairs)  4.28 us
  transfers between devices with their start and end apart: 11, of which 4 were waited for; matrix products, arithmetic and copies ran while one was open for 0% of the time, Pallas kernels for 21%

profile of v11, /device:TPU:1, one launch (start us, length us, event | category | flops | bytes accessed | tf_op | source)
XLA Modules:
  0.0 98.1 jit_solution(4272494431580643926)
XLA Ops:
  0.6 0.0 copy-start
  0.6 0.0 copy-start.2
  0.7 0.0 copy-start.3
  0.7 0.0 copy-start.4
  0.7 0.0 copy-start.6
  0.7 2.4 %outgoing_rows.1 = (f32[96,1024]{1,0:T(8,128)}, f32[96,1024]{1,0:T(8,128)}) custom-call(f32[8,64,1024]{2,1,0:T(8,128)} %block_ref.3, f32[64,1024]{1,0:T(8,128)} %metric_ref.3), custom_call_target="tpu_custom_call" | custom-call | bytes 100000 | tf_op jit(solution)/shard_map/outgoing_rows/pallas_call | solution.py:248
  3.1 4.0 %collective-permute-start.8 = (f32[96,1024]{1,0:T(8,128)}, f32[96,1024]{1,0:T(8,128)S(1)}, u32[]{:S(2)}, u32[]{:S(2)}) collective-permute-start(f32[96,1024]{1,0:T(8,128)} %get-tuple-element.141), channel_id=1, source_target_pairs={{0,8},{1,9},{2,10},{3,11},{4,12},{5,13},{6,14},{7,15},{8,16},{9,17... | collective-permute-start | bytes 1179656 | tf_op jit(solution)/shard_map/row_halo/ppermute | solution.py:796
  7.0 1.3 %collective-permute-start.9 = (f32[96,1024]{1,0:T(8,128)}, f32[96,1024]{1,0:T(8,128)S(1)}, u32[]{:S(2)}, u32[]{:S(2)}) collective-permute-start(f32[96,1024]{1,0:T(8,128)} %get-tuple-element.145), channel_id=1, source_target_pairs={{8,0},{9,1},{10,2},{11,3},{12,4},{13,5},{14,6},{15,7},{16,8},{17,9... | collective-permute-start | bytes 1179656 | tf_op jit(solution)/shard_map/row_halo/ppermute | solution.py:796
  9.0 0.1 stack.15
  9.1 0.0 copy-done.2
  9.1 0.0 copy-done.3
  9.1 0.0 copy-done.4
  9.1 6.1 %face_sums.1 = (f32[8,32,128]{2,1,0:T(8,128)S(1)}, f32[8,32,128]{2,1,0:T(8,128)S(1)}) custom-call(s32[1,6]{1,0:T(1,128)S(1)} %bitcast.17, s32[1,1]{1,0:T(1,128)S(6)} %copy.41.count_ref, f32[1,16384]{1,0:T(1,128)S(1)} %copy-done.2, f32[1,16384]{1,0:T(1,128)S(1)} %copy-done.3, s32[1,16384]{1,0:T(1,128)S(1)} %copy-done.4), custom_call_target="tpu_custom_call" | custom-call | bytes 700000 | tf_op jit(solution)/shard_map/face_sums/pallas_call | solution.py:211
  15.2 1.0 %collective-permute-start.4 = (f32[8,32,128]{2,1,0:T(8,128)S(1)}, f32[8,32,128]{2,1,0:T(8,128)S(1)}, u32[]{:S(2)}, u32[]{:S(2)}) collective-permute-start(f32[8,32,128]{2,1,0:T(8,128)S(1)} %get-tuple-element.144), channel_id=1, source_target_pairs={{0,1},{1,0},{2,3},{3,2},{4,5},{5,4},{6,7},{7,6},{8,9},{9,8},{10,11... | collective-permute-start | bytes 393224 | tf_op jit(solution)/shard_map/flux_sum/ppermute | solution.py:801
  16.2 1.0 %collective-permute-done.4 = f32[8,32,128]{2,1,0:T(8,128)S(1)} collective-permute-done((f32[8,32,128]{2,1,0:T(8,128)S(1)}, f32[8,32,128]{2,1,0:T(8,128)S(1)}, u32[]{:S(2)}, u32[]{:S(2)}) %collective-permute-start.4) | collective-permute-done | bytes 131104 | tf_op jit(solution)/shard_map/flux_sum/ppermute | solution.py:801
  17.2 0.0 copy-start.1
  17.2 1.3 %collective-permute-start.5 = (f32[8,32,128]{2,1,0:T(8,128)S(1)}, f32[8,32,128]{2,1,0:T(8,128)S(1)}, u32[]{:S(2)}, u32[]{:S(2)}) collective-permute-start(f32[8,32,128]{2,1,0:T(8,128)S(1)} %add.135), channel_id=1, source_target_pairs={{0,2},{1,3},{2,4},{3,5},{4,6},{5,7},{6,0},{7,1},{8,10},{9,11},{10,... | collective-permute-start | bytes 393224 | tf_op jit(solution)/shard_map/flux_sum/ppermute | solution.py:803
  18.6 2.6 %collective-permute-start.6 = (f32[8,32,128]{2,1,0:T(8,128)S(1)}, f32[8,32,128]{2,1,0:T(8,128)S(1)}, u32[]{:S(2)}, u32[]{:S(2)}) collective-permute-start(f32[8,32,128]{2,1,0:T(8,128)S(1)} %add.135), channel_id=1, source_target_pairs={{0,4},{1,5},{2,6},{3,7},{4,0},{5,1},{6,2},{7,3},{8,12},{9,13},{10,... | collective-permute-start | bytes 393224 | tf_op jit(solution)/shard_map/flux_sum/ppermute | solution.py:803
  21.2 1.1 %collective-permute-start.7 = (f32[8,32,128]{2,1,0:T(8,128)S(1)}, f32[8,32,128]{2,1,0:T(8,128)S(1)}, u32[]{:S(2)}, u32[]{:S(2)}) collective-permute-start(f32[8,32,128]{2,1,0:T(8,128)S(1)} %add.135), channel_id=1, source_target_pairs={{0,6},{1,7},{2,0},{3,1},{4,2},{5,3},{6,4},{7,5},{8,14},{9,15},{10,... | collective-permute-start | bytes 393224 | tf_op jit(solution)/shard_map/flux_sum/ppermute | solution.py:803
  22.3 0.0 collective-permute-done.8.before_ref
  22.3 0.0 collective-permute-done.9.after_ref
  22.3 0.0 copy-done
  22.3 0.0 copy-done.6
  22.3 4.9 %regroup.1 = (f32[8,8,80,128]{3,2,1,0:T(8,128)}, f32[8,128,128]{2,1,0:T(8,128)S(1)}) custom-call(f32[8,64,1024]{2,1,0:T(8,128)S(1)} %copy-done, f32[64,1024]{1,0:T(8,128)S(1)} %copy-done.6, f32[96,1024]{1,0:T(8,128)S(1)} %collective-permute-done.8.before_ref, f32[96,1024]{1,0:T(8,128)S(1)} %collective-permute-done.9.after_ref), custom_call_target="tpu_custom_call" | custom-call | bytes 15000000 | tf_op jit(solution)/shard_map/regroup/pallas_call | solution.py:140
  27.2 0.0 collective-permute-done.5
  27.2 0.1 collective-permute-done.6
  27.3 0.0 collective-permute-done.7
  27.3 3.9 %collective-permute-start.13 = (f32[8,8,80,128]{3,2,1,0:T(8,128)}, f32[8,8,80,128]{3,2,1,0:T(8,128)}, u32[]{:S(2)}, u32[]{:S(2)}) collective-permute-start(f32[8,8,80,128]{3,2,1,0:T(8,128)} %get-tuple-element.154), channel_id=1, source_target_pairs={{0,1},{1,2},{2,3},{3,4},{4,5},{5,6},{6,7},{8,9},{9,10},{10,11},{11... | collective-permute-start | bytes 7864328 | tf_op jit(solution)/shard_map/depth_halo/ppermute | solution.py:796
  31.3 2.0 %collective-permute-start.14 = (f32[8,8,80,128]{3,2,1,0:T(8,128)}, f32[8,8,80,128]{3,2,1,0:T(8,128)}, u32[]{:S(2)}, u32[]{:S(2)}) collective-permute-start(f32[8,8,80,128]{3,2,1,0:T(8,128)} %get-tuple-element.154), channel_id=1, source_target_pairs={{1,0},{2,1},{3,2},{4,3},{5,4},{6,5},{7,6},{9,8},{10,9},{11,10},{12... | collective-permute-start | bytes 7864328 | tf_op jit(solution)/shard_map/depth_halo/ppermute | solution.py:796
  33.3 4.3 %collective-permute-start.11 = (f32[8,32,128]{2,1,0:T(8,128)S(1)}, f32[8,32,128]{2,1,0:T(8,128)S(1)}, u32[]{:S(2)}, u32[]{:S(2)}) collective-permute-start(f32[8,32,128]{2,1,0:T(8,128)S(1)} %add_add_fusion.own_ref), channel_id=1, source_target_pairs={{1,9},{3,11},{5,13},{7,15},{8,0},{9,17},{10,2},{11,19},{12,4},{13,... | collective-permute-start | bytes 393224 | tf_op jit(solution)/shard_map/flux_halo/ppermute | solution.py:819
  37.6 0.1 collective-permute-start.10
  37.6 1.8 %collective-permute-done.11.same_ref = f32[8,32,128]{2,1,0:T(8,128)S(1)} collective-permute-done((f32[8,32,128]{2,1,0:T(8,128)S(1)}, f32[8,32,128]{2,1,0:T(8,128)S(1)}, u32[]{:S(2)}, u32[]{:S(2)}) %collective-permute-start.11) | collective-permute-done | bytes 131104 | tf_op jit(solution)/shard_map/flux_halo/ppermute | solution.py:819
  39.5 0.7 collective-permute-start.12
  40.1 0.0 collective-permute-done.10.other_ref
  40.1 1.0 %collective-permute-done.12.cross_ref = f32[8,32,128]{2,1,0:T(8,128)S(1)} collective-permute-done((f32[8,32,128]{2,1,0:T(8,128)S(1)}, f32[8,32,128]{2,1,0:T(8,128)S(1)}, u32[]{:S(2)}, u32[]{:S(2)}) %collective-permute-start.12) | collective-permute-done | bytes 131104 | tf_op jit(solution)/shard_map/flux_halo/ppermute | solution.py:820
  41.1 7.5 %surface_basis.1 = (f32[10,8,16,8,128]{4,3,2,1,0:T(8,128)S(1)}, f32[16,8,128]{2,1,0:T(8,128)S(1)}) custom-call(s32[1,6]{1,0:T(1,128)S(1)} %bitcast.18, f32[8,32,128]{2,1,0:T(8,128)S(1)} %add_add_fusion.own_ref, f32[8,32,128]{2,1,0:T(8,128)S(1)} %collective-permute-done.10.other_ref, f32[8,32,128]{2,1,0:T(8,128)S(1)} %collective-permute-done.11.same_ref, ...), custom_call_target="tpu_custom_call" | custom-call | bytes 700000 | tf_op jit(solution)/shard_map/surface_basis/pallas_call | solution.py:330
  48.6 16.1 %all_to_all.5.sums_ref = f32[16,8,128]{2,1,0:T(8,128)S(1)} all-to-all(f32[16,8,128]{2,1,0:T(8,128)S(1)} %get-tuple-element.152), channel_id=1, replica_groups=mesh['vol'=16,'col'=8] {'vol'}, dimensions={0} | all-to-all | bytes 131072 | tf_op jit(solution)/shard_map/gather_sums/all_to_all | solution.py:827
  64.7 0.0 copy-done.1
  64.7 0.0 copy-start.5
  64.7 0.0 copy-start.7
  64.7 2.3 %surface_solve.1 = (f32[8,80,128]{2,1,0:T(8,128)}, s32[1,1]{1,0:T(1,128)}) custom-call(f32[10,8,16,8,128]{4,3,2,1,0:T(8,128)S(1)} %get-tuple-element.151.part_ref, f32[16,8,128]{2,1,0:T(8,128)S(1)} %all_to_all.5.sums_ref, f32[20,16,128]{2,1,0:T(8,128)S(1)} %copy-done.1), custom_call_target="tpu_custom_call" | custom-call | bytes 300000 | tf_op jit(solution)/shard_map/surface_solve/pallas_call | solution.py:407
  67.7 0.0 collective-permute-done.13
  67.7 0.0 collective-permute-done.14
  67.7 0.0 copy-done.5
  67.7 0.0 copy-done.7
  67.7 30.2 %conditional.1 = ((f32[64,1024]{1,0:T(8,128)}, f32[8,64,1024]{2,1,0:T(8,128)})) conditional(s32[]{:T(128)} %bitcast.9, (s32[]{:T(128)}, f32[8,32,128]{2,1,0:T(8,128)S(1)}, f32[8,32,128]{2,1,0:T(8,128)S(1)}, f32[64,1024]{1,0:T(8,128)S(1)}, s32[1,6]{1,0:T(1,128)S(1)}, /*index=5*/f32[8,8,80,128]{3,2,1,0:T(8,128)}, f32[8,8,80,128]{3,2,1,0:T(8,128)}, ...), branch_computations={%region_0.9_spmd, %region_9.10_spmd} | conditional | flops 3516806 | bytes 15280337 | solution.py:842
  68.0 0.0 copy-start.8
  68.0 2.1 %surface_change.3.change_ref = f32[8,8,64,128]{3,2,1,0:T(8,128)S(1)} custom-call(s32[1,6]{1,0:T(1,128)S(1)} %get-tuple-element.118.where_ref, f32[8,80,128]{2,1,0:T(8,128)} %get-tuple-element.122.speed_ref), custom_call_target="tpu_custom_call" | custom-call | bytes 800000 | tf_op jit(solution)/shard_map/cond/branch_1_fun/surface_change/pallas_call | solution.py:557
  70.1 0.0 copy-done.8
  70.1 27.8 %base_sweeps.3 = (f32[64,1024]{1,0:T(8,128)}, f32[8,64,1024]{2,1,0:T(8,128)}) custom-call(s32[1,6]{1,0:T(1,128)S(1)} %get-tuple-element.118.where_ref, f32[8,8,80,128]{3,2,1,0:T(8,128)} %get-tuple-element.119.wide_ref, f32[8,8,80,128]{3,2,1,0:T(8,128)} %get-tuple-element.120.zlow_ref, f32[8,8,80,128]{3,2,1,0:T(8,128)} %get-tuple-element.121.zhigh_ref, ...), custom_call_target="tpu_custom_call" | custom-call | bytes 2500000 | tf_op jit(solution)/shard_map/cond/branch_1_fun/base_sweeps/pallas_call | solution.py:707
  (2 shorter events, 0.1 us)
Async XLA Ops:
  0.6 21.7 %copy-start = (f32[8,64,1024]{2,1,0:T(8,128)S(1)}, f32[8,64,1024]{2,1,0:T(8,128)}, u32[]{:S(2)}) copy-start(f32[8,64,1024]{2,1,0:T(8,128)} %block_ref.3) | copy-start | bytes 6291460
  0.6 8.4 %copy-start.2 = (f32[1,16384]{1,0:T(1,128)S(1)}, f32[1,16384]{1,0:T(1,128)}, u32[]{:S(2)}) copy-start(f32[1,16384]{1,0:T(1,128)} %area_ref) | copy-start | bytes 196612
  0.7 8.4 %copy-start.3 = (f32[1,16384]{1,0:T(1,128)S(1)}, f32[1,16384]{1,0:T(1,128)}, u32[]{:S(2)}) copy-start(f32[1,16384]{1,0:T(1,128)} %speed_ref.1) | copy-start | bytes 196612
  0.7 8.4 %copy-start.4 = (s32[1,16384]{1,0:T(1,128)S(1)}, s32[1,16384]{1,0:T(1,128)}, u32[]{:S(2)}) copy-start(s32[1,16384]{1,0:T(1,128)} %node_ref.1) | copy-start | bytes 196612
  0.7 21.6 %copy-start.6 = (f32[64,1024]{1,0:T(8,128)S(1)}, f32[64,1024]{1,0:T(8,128)}, u32[]{:S(2)}) copy-start(f32[64,1024]{1,0:T(8,128)} %metric_ref.3) | copy-start | bytes 786436
  3.1 19.2 %collective-permute-start.8 = (f32[96,1024]{1,0:T(8,128)}, f32[96,1024]{1,0:T(8,128)S(1)}, u32[]{:S(2)}, u32[]{:S(2)}) collective-permute-start(f32[96,1024]{1,0:T(8,128)} %get-tuple-element.141), channel_id=1, source_target_pairs={{0,8},{1,9},{2,10},{3,11},{4,12},{5,13},{6,14},{7,15},{8,16},{9,17... | collective-permute-start | bytes 1179656 | tf_op jit(solution)/shard_map/row_halo/ppermute | solution.py:796
  7.0 15.3 %collective-permute-start.9 = (f32[96,1024]{1,0:T(8,128)}, f32[96,1024]{1,0:T(8,128)S(1)}, u32[]{:S(2)}, u32[]{:S(2)}) collective-permute-start(f32[96,1024]{1,0:T(8,128)} %get-tuple-element.145), channel_id=1, source_target_pairs={{8,0},{9,1},{10,2},{11,3},{12,4},{13,5},{14,6},{15,7},{16,8},{17,9... | collective-permute-start | bytes 1179656 | tf_op jit(solution)/shard_map/row_halo/ppermute | solution.py:796
  15.2 2.0 %collective-permute-start.4 = (f32[8,32,128]{2,1,0:T(8,128)S(1)}, f32[8,32,128]{2,1,0:T(8,128)S(1)}, u32[]{:S(2)}, u32[]{:S(2)}) collective-permute-start(f32[8,32,128]{2,1,0:T(8,128)S(1)} %get-tuple-element.144), channel_id=1, source_target_pairs={{0,1},{1,0},{2,3},{3,2},{4,5},{5,4},{6,7},{7,6},{8,9},{9,8},{10,11... | collective-permute-start | bytes 393224 | tf_op jit(solution)/shard_map/flux_sum/ppermute | solution.py:801
  17.2 47.5 %copy-start.1 = (f32[20,16,128]{2,1,0:T(8,128)S(1)}, f32[20,16,128]{2,1,0:T(8,128)}, u32[]{:S(2)}) copy-start(f32[20,16,128]{2,1,0:T(8,128)} %constant.115.clone.weights_ref) | copy-start | bytes 491524
  17.2 10.0 %collective-permute-start.5 = (f32[8,32,128]{2,1,0:T(8,128)S(1)}, f32[8,32,128]{2,1,0:T(8,128)S(1)}, u32[]{:S(2)}, u32[]{:S(2)}) collective-permute-start(f32[8,32,128]{2,1,0:T(8,128)S(1)} %add.135), channel_id=1, source_target_pairs={{0,2},{1,3},{2,4},{3,5},{4,6},{5,7},{6,0},{7,1},{8,10},{9,11},{10,... | collective-permute-start | bytes 393224 | tf_op jit(solution)/shard_map/flux_sum/ppermute | solution.py:803
  18.6 8.7 %collective-permute-start.6 = (f32[8,32,128]{2,1,0:T(8,128)S(1)}, f32[8,32,128]{2,1,0:T(8,128)S(1)}, u32[]{:S(2)}, u32[]{:S(2)}) collective-permute-start(f32[8,32,128]{2,1,0:T(8,128)S(1)} %add.135), channel_id=1, source_target_pairs={{0,4},{1,5},{2,6},{3,7},{4,0},{5,1},{6,2},{7,3},{8,12},{9,13},{10,... | collective-permute-start | bytes 393224 | tf_op jit(solution)/shard_map/flux_sum/ppermute | solution.py:803
  21.2 6.1 %collective-permute-start.7 = (f32[8,32,128]{2,1,0:T(8,128)S(1)}, f32[8,32,128]{2,1,0:T(8,128)S(1)}, u32[]{:S(2)}, u32[]{:S(2)}) collective-permute-start(f32[8,32,128]{2,1,0:T(8,128)S(1)} %add.135), channel_id=1, source_target_pairs={{0,6},{1,7},{2,0},{3,1},{4,2},{5,3},{6,4},{7,5},{8,14},{9,15},{10,... | collective-permute-start | bytes 393224 | tf_op jit(solution)/shard_map/flux_sum/ppermute | solution.py:803
  27.3 40.3 %collective-permute-start.13 = (f32[8,8,80,128]{3,2,1,0:T(8,128)}, f32[8,8,80,128]{3,2,1,0:T(8,128)}, u32[]{:S(2)}, u32[]{:S(2)}) collective-permute-start(f32[8,8,80,128]{3,2,1,0:T(8,128)} %get-tuple-element.154), channel_id=1, source_target_pairs={{0,1},{1,2},{2,3},{3,4},{4,5},{5,6},{6,7},{8,9},{9,10},{10,11},{11... | collective-permute-start | bytes 7864328 | tf_op jit(solution)/shard_map/depth_halo/ppermute | solution.py:796
  31.3 36.4 %collective-permute-start.14 = (f32[8,8,80,128]{3,2,1,0:T(8,128)}, f32[8,8,80,128]{3,2,1,0:T(8,128)}, u32[]{:S(2)}, u32[]{:S(2)}) collective-permute-start(f32[8,8,80,128]{3,2,1,0:T(8,128)} %get-tuple-element.154), channel_id=1, source_target_pairs={{1,0},{2,1},{3,2},{4,3},{5,4},{6,5},{7,6},{9,8},{10,9},{11,10},{12... | collective-permute-start | bytes 7864328 | tf_op jit(solution)/shard_map/depth_halo/ppermute | solution.py:796
  33.3 6.2 %collective-permute-start.11 = (f32[8,32,128]{2,1,0:T(8,128)S(1)}, f32[8,32,128]{2,1,0:T(8,128)S(1)}, u32[]{:S(2)}, u32[]{:S(2)}) collective-permute-start(f32[8,32,128]{2,1,0:T(8,128)S(1)} %add_add_fusion.own_ref), channel_id=1, source_target_pairs={{1,9},{3,11},{5,13},{7,15},{8,0},{9,17},{10,2},{11,19},{12,4},{13,... | collective-permute-start | bytes 393224 | tf_op jit(solution)/shard_map/flux_halo/ppermute | solution.py:819
  37.6 2.6 %collective-permute-start.10 = (f32[8,32,128]{2,1,0:T(8,128)S(1)}, f32[8,32,128]{2,1,0:T(8,128)S(1)}, u32[]{:S(2)}, u32[]{:S(2)}) collective-permute-start(f32[8,32,128]{2,1,0:T(8,128)S(1)} %add_add_fusion.own_ref), channel_id=1, source_target_pairs={{0,1},{1,0},{2,3},{3,2},{4,5},{5,4},{6,7},{7,6},{8,9},{9,8},{10,11... | collective-permute-start | bytes 393224 | tf_op jit(solution)/shard_map/flux_halo/ppermute | solution.py:812
  39.5 1.7 %collective-permute-start.12 = (f32[8,32,128]{2,1,0:T(8,128)S(1)}, f32[8,32,128]{2,1,0:T(8,128)S(1)}, u32[]{:S(2)}, u32[]{:S(2)}) collective-permute-start(f32[8,32,128]{2,1,0:T(8,128)S(1)} %collective-permute-done.11.same_ref), channel_id=1, source_target_pairs={{0,1},{1,0},{2,3},{3,2},{4,5},{5,4},{6,7},{7,6},{8,9},{9,8},{10,11... | collective-permute-start | bytes 393224 | tf_op jit(solution)/shard_map/flux_halo/ppermute | solution.py:820
  64.7 3.0 %copy-start.5 = (bf16[1024,1024]{1,0:T(8,128)(2,1)S(1)}, bf16[1024,1024]{1,0:T(8,128)(2,1)}, u32[]{:S(2)}) copy-start(bf16[1024,1024]{1,0:T(8,128)(2,1)} %constant.114.clone) | copy-start | bytes 6291460
  64.7 3.0 %copy-start.7 = (f32[64,1024]{1,0:T(8,128)S(1)}, f32[64,1024]{1,0:T(8,128)}, u32[]{:S(2)}) copy-start(f32[64,1024]{1,0:T(8,128)} %metric_ref.3) | copy-start | bytes 786436
  68.0 2.1 %copy-start.8 = (f32[8,80,128]{2,1,0:T(8,128)S(1)}, f32[8,80,128]{2,1,0:T(8,128)}, u32[]{:S(2)}) copy-start(f32[8,80,128]{2,1,0:T(8,128)} %get-tuple-element.122.speed_ref) | copy-start | bytes 983044 | tf_op jit(solution)/shard_map/cond
